TPU v7x, 32 devices: a whole 2x2x4 slice. The times are simulated.
32 devices in a mesh: grp: 2 (over x), orb: 16 (over z, y, core).
Axes of the slice: x: 2, y: 2, z: 4, core: 2. Of those that a mesh axis runs over, the one named last changes fastest.
Arguments:
- three_centre: bfloat16 [16, 64, 16, 4096], P('orb'), may hold values from -0.59765625 to 0.59765625
- green_occ: bfloat16 [32, 4096], P(('grp', 'orb')), parts along dimension 0, may hold values from -0.75 to 0.75
- green_virt: bfloat16 [32, 4096], P(('grp', 'orb')), parts along dimension 0, may hold values from -0.75 to 0.75
- pair_atoms: int32 [16, 2], P('orb'), may hold values from 0 to 15
- basis_count: int32 [16], P('orb'), may hold values from 32 to 64
- chi_target: int32 [16, 256], P('orb'), may hold values from 0 to 63, as said below
Outputs:
- chi_blocks: float32 [128, 4096], P(('grp', 'orb')), parts along dimension 0
There are 2 independent parts, one for each index of `grp`. A program takes and returns all parts, laid end to end along the dimension named above; an argument that names none is the same for every part. Nothing has to cross between parts.
Inputs may be any that keep to these rules, and one draw needn't show every extreme that they name: `chi_target`: block c belongs to device c // 4. Of the 256 entries of one device, at most 32 name blocks of any one device; one device receives exactly 32 from every device.
All inputs are finite; a program needn't handle non-finite values.
Results may differ from a plain program's by a relative error of at most 0.0041.
Values may be sent and summed in bfloat16 or wider, within the bound.
No kernel may reach another device: no remote copies, remote signals or barrier semaphores. Data moves between devices by JAX's collectives and lax.ppermute only.
A program may use at most 128 MiB of HBM per device.

v0:
```python
import jax
import jax.numpy as jnp
from jax import lax
from jax.sharding import PartitionSpec as P

CB_DEV = 4


def local(three_centre, green_occ, green_virt, pair_atoms, basis_count, chi_target):
    block_size = three_centre.shape[1]
    aux_count = three_centre.shape[2]
    lane_ids = jnp.arange(block_size, dtype=jnp.int32)
    present = lane_ids[None, :] < basis_count[:, None]
    valid_entries = (present[:, :, None] & present[:, None, :]).reshape(
        present.shape[0], block_size * block_size
    )
    zero_value = jnp.zeros((), jnp.bfloat16)
    occ_masked = jnp.where(valid_entries, green_occ, zero_value)
    virt_masked = jnp.where(valid_entries, green_virt, zero_value)
    occ_table, virt_table = (
        lax.all_gather(occ_masked, "orb", axis=0, tiled=True),
        lax.all_gather(virt_masked, "orb", axis=0, tiled=True),
    )
    atom_count = occ_table.shape[0]
    atom_ids = jnp.arange(atom_count, dtype=jnp.int32)
    grouping = max(1, 128 // block_size)
    spread_eye = jnp.eye(grouping, dtype=jnp.bfloat16)
    chooser = (atom_ids[None, :] == pair_atoms[0][:, None]).astype(jnp.bfloat16)
    occ_block = jnp.dot(chooser[0:1], occ_table, preferred_element_type=jnp.float32)
    occ_block = occ_block.astype(jnp.bfloat16).reshape(block_size, block_size)
    virt_block = jnp.dot(chooser[1:2], virt_table, preferred_element_type=jnp.float32)
    virt_block = virt_block.astype(jnp.bfloat16).reshape(block_size, block_size)
    integrals = three_centre[0]
    occ_side = jnp.dot(
        occ_block, integrals.reshape(block_size, -1), preferred_element_type=jnp.float32
    )
    occ_side = occ_side.astype(jnp.bfloat16)
    spread_virt = jnp.kron(spread_eye, virt_block)
    virt_side = jnp.dot(
        integrals.reshape(-1, block_size * grouping),
        spread_virt,
        preferred_element_type=jnp.float32,
    )
    virt_side = virt_side.astype(jnp.bfloat16)
    pair_chi = lax.dot_general(
        occ_side.reshape(block_size, -1, block_size),
        virt_side.reshape(block_size, -1, block_size),
        (((0, 2), (0, 2)), ((), ())),
        preferred_element_type=jnp.float32,
    )
    contribution = pair_chi.reshape(aux_count, block_size, aux_count, block_size)
    contribution = contribution.transpose(0, 2, 1, 3).reshape(
        aux_count * aux_count, block_size * block_size
    )
    targets = chi_target.reshape(-1)
    local_rows = targets
    local_rows = jnp.where(
        (local_rows >= 0) & (local_rows < CB_DEV * lax.axis_size("orb")),
        local_rows,
        CB_DEV * lax.axis_size("orb"),
    )
    empty_rows = jnp.zeros((CB_DEV * lax.axis_size("orb"), block_size * block_size), jnp.float32)
    return lax.psum_scatter(
        empty_rows.at[local_rows].add(contribution, mode="drop"),
        "orb",
        scatter_dimension=0,
        tiled=True,
    )


def solution(mesh):
    in_specs = (
        P("orb", None, None, None),
        P(("grp", "orb"), None),
        P(("grp", "orb"), None),
        P("orb", None),
        P("orb"),
        P("orb", None),
    )
    out_specs = P(("grp", "orb"), None)
    return jax.shard_map(local, mesh=mesh, in_specs=in_specs, out_specs=out_specs, check_vma=False)
```

profile of v0, /device:TPU:0, one launch (start us, length us, event | category | flops | bytes accessed | tf_op | source)
XLA Modules:
  0.0 305.6 jit_solution(14330117869527604896)
XLA Ops:
  6.5 0.0 all-reduce.3.cloned.1.call-start
  7.2 0.1 and.37
  7.3 0.1 and.38
  7.4 0.1 and.40
  7.5 0.8 select_bitcast_fusion.1
  8.3 23.8 %all-gather.1 = bf16[16,1,4096]{2,1,0:T(2,128)(2,1)S(1)} all-gather(bf16[1,1,4096]{2,1,0:T(2,128)(2,1)S(1)} %get-tuple-element.6), channel_id=1, replica_groups=mesh['grp'=2,'orb'=16] {'orb'}, dimensions={0}, use_global_device_ids=true | all-gather | bytes 139264 | tf_op jit(solution)/shard_map/all_gather | solution.py:22
  32.1 0.7 iota_compare_fusion
  32.8 0.3 fusion.12
  33.1 0.1 mul.33
  33.2 0.1 broadcast_multiply_fusion
  33.3 0.1 mul.36
  33.4 13.5 %reshape_squeeze.7 = bf16[32768,128]{1,0:T(8,128)(2,1)} reshape(bf16[1,64,16,4096]{3,2,1,0:T(8,128)(2,1)} %param.6) | data formatting | bytes 16777216 | tf_op jit(solution)/shard_map/reshape;squeeze | solution.py:40
  46.9 9.0 %fusion = bf16[32768,128]{0,1:T(8,128)(2,1)} fusion(bf16[128,128]{1,0:T(8,128)(2,1)S(1)} %mul.36, bf16[32768,128]{1,0:T(8,128)(2,1)} %reshape_squeeze.7), kind=kOutput, calls=%fused_computation.3 | convolution fusion | flops 1077936128 | bytes 16809984 | tf_op jit(solution)/shard_map/dot_general | solution.py:39
  55.8 11.9 %copy.13 = bf16[32768,128]{1,0:T(8,128)(2,1)} copy(bf16[32768,128]{0,1:T(8,128)(2,1)} %fusion) | data formatting | bytes 16777216 | tf_op jit(solution)/shard_map/convert_element_type | solution.py:44
  67.8 20.9 %reshape.149 = bf16[64,1024,64]{2,1,0:T(8,128)(2,1)} reshape(bf16[32768,128]{1,0:T(8,128)(2,1)} %copy.13) | data formatting | bytes 16777216 | tf_op jit(solution)/shard_map/reshape | solution.py:47
  88.7 18.3 %all-gather = bf16[16,1,4096]{2,1,0:T(2,128)(2,1)S(1)} all-gather(bf16[1,1,4096]{2,1,0:T(2,128)(2,1)S(1)} %get-tuple-element.5), channel_id=1, replica_groups=mesh['grp'=2,'orb'=16] {'orb'}, dimensions={0}, use_global_device_ids=true | all-gather | bytes 139264 | tf_op jit(solution)/shard_map/all_gather | solution.py:21
  107.0 0.3 fusion.15
  107.3 0.1 reshape.146
  107.4 12.0 %copy.27 = bf16[8,8,16,4096]{3,1,2,0:T(8,128)(2,1)} copy(bf16[8,8,16,4096]{3,2,1,0:T(8,128)(2,1)} %bitcast.61) | data formatting | bytes 16777216
  119.4 8.9 %convolution_convert_fusion = bf16[64,65536]{1,0:T(8,128)(2,1)} fusion(bf16[64,64]{1,0:T(8,128)(2,1)S(1)} %reshape.146, bf16[64,65536]{1,0:T(8,128)(2,1)} %bitcast.60), kind=kOutput, calls=%fused_computation.1 | convolution fusion | flops 541065216 | bytes 16785408 | tf_op jit(solution)/shard_map/dot_general | solution.py:34
  128.3 18.2 %reshape.147 = bf16[64,1024,64]{2,1,0:T(8,128)(2,1)} reshape(bf16[64,65536]{1,0:T(8,128)(2,1)} %convolution_convert_fusion) | data formatting | bytes 16777216 | tf_op jit(solution)/shard_map/reshape | solution.py:46
  146.4 42.5 %fusion.5 = f32[16,16,64,64]{3,2,1,0:T(8,128)} fusion(bf16[16,64,64,64]{3,1,0,2:T(8,128)(2,1)} %bitcast.62, bf16[16,64,64,64,1]{3,1,0,2,4:T(8,128)(2,1)} %bitcast.63), kind=kOutput, calls=%fused_computation.8 | convolution fusion | flops 8589934592 | bytes 20971520 | tf_op jit(solution)/shard_map/dot_general | solution.py:45
  188.9 0.0 copy-start
  189.0 0.0 copy-start.1
  189.0 7.9 %reshape.155 = f32[256,4096]{1,0:T(8,128)} reshape(f32[16,16,64,64]{3,2,1,0:T(8,128)} %fusion.5) | data formatting | bytes 8388608 | tf_op jit(solution)/shard_map/reshape | solution.py:52
  196.9 0.0 copy-done
  196.9 8.5 %scatter_custom_fusion = f32[64,4096]{1,0:T(8,128)} fusion(s32[256]{0:T(256)S(1)} %bitcast.66, f32[256,4096]{1,0:T(8,128)} %reshape.155, f32[]{:T(128)} %constant.4.clone.1), kind=kCustom, calls=%fused_computation.9 | custom fusion | flops 1048576 | bytes 1049088 | tf_op jit(solution)/shard_map/scatter-add | solution.py:64
  205.4 0.0 all-reduce.3.cloned.1.call-update
  205.4 0.0 copy-done.1
  205.4 0.6 dynamic-slice
  206.7 90.6 %all-reduce.3.cloned.1.call-done = f32[64,4096]{1,0:T(8,128)} async-done(((f32[64,4096]{1,0:T(8,128)}), f32[64,4096]{1,0:T(8,128)}) %all-reduce.3.cloned.1.call-update) | async-done | bytes 1048592
  297.2 1.5 constant_dynamic-slice_fusion
  (6 shorter events, 0.0 us)
Async XLA Ops:
  6.5 290.7 %all-reduce.3.cloned.1.call-start = ((), (), s32[]{:S(2)}) async-start(), calls=%async_computation | async-start | bytes 2097152
  188.9 7.9 %copy-start = (s32[1,256]{1,0:T(1,128)S(1)}, s32[1,256]{1,0:T(1,128)}, u32[]{:S(2)}) copy-start(s32[1,256]{1,0:T(1,128)} %param.11) | copy-start | bytes 3076
  189.0 16.5 %copy-start.1 = (u32[32]{0:T(128)S(1)}, u32[32]{0:T(128)}, u32[]{:S(2)}) copy-start(u32[32]{0:T(128)} %constant.17) | copy-start | bytes 388
Sparse Core Ops, SparseCore 0:
  205.5 91.6 all-reduce.2
where the time goes:
time: 307 us; the launch traced here: 306 us
  waiting for transfers between devices  90.6 us (30%)
  local copies, waits for them, and re-layouts  87.1 us (28%)
  matrix products  60.9 us (20%)
  blocking collectives  42.1 us (14%)
  between operations  14.8 us (5%)
  other arithmetic  10.2 us (3%)
    unnamed x2, waiting for transfers between devices  90.6 us
    dot_general x1, matrix products, local(): lax.dot_general(occ_side.reshape(block_size, -1, block_size), virt_side.r...  42.5 us
    all_gather x1, blocking collectives, local(): lax.all_gather(virt_masked, 'orb', axis=0, tiled=True)  23.8 us
    reshape x1, local copies, waits for them, and re-layouts, local(): virt_side.reshape(block_size, -1, block_size)  20.9 us
    all_gather x1, blocking collectives, local(): lax.all_gather(occ_masked, 'orb', axis=0, tiled=True)  18.3 us
    reshape x1, local copies, waits for them, and re-layouts, local(): occ_side.reshape(block_size, -1, block_size)  18.2 us
    unnamed x7, local copies, waits for them, and re-layouts  14.1 us
    another operation x1, local copies, waits for them, and re-layouts, local(): integrals.reshape(-1, block_size * grouping)  13.5 us
  transfers between devices with their start and end apart: 1, of which 1 were waited for; matrix products, arithmetic and copies ran while one was open for 0% of the time, Pallas kernels for 0%

commit v1 on v0

v1 whole, which is shorter than its diff:
```python
import functools

import jax
import jax.numpy as jnp
from jax import lax
from jax.experimental import pallas as pl
from jax.experimental.pallas import tpu as pltpu
from jax.sharding import PartitionSpec as P

CB_DEV = 4
LAM = 4
PARTS = 4


def relayout_kernel(b_ref, d_ref, e_ref):
    lam, aux, width = b_ref.shape
    bs = d_ref.shape[0] // aux
    rows = aux * aux
    row = lax.broadcasted_iota(jnp.int32, (rows, rows), 0)
    col = lax.broadcasted_iota(jnp.int32, (rows, rows), 1)
    perm = (col == (row % aux) * aux + row // aux).astype(jnp.bfloat16)
    half = aux // 2
    for h in range(2):
        part = b_ref[...].astype(jnp.float32)[:, h * half:(h + 1) * half, :]
        e_ref[h] = part.reshape(lam * half, width).astype(jnp.bfloat16)
    for blk in range(bs // aux):
        pieces = []
        for p in range(aux):
            at = (blk * aux + p) * bs
            pieces.append(jnp.concatenate([b_ref[i, :, at:at + bs] for i in range(lam)], axis=-1))
        stacked = jnp.concatenate(pieces, axis=0)
        moved = jnp.dot(perm, stacked, preferred_element_type=jnp.float32).astype(jnp.bfloat16)
        for a in range(aux):
            d_ref[a * bs + blk * aux:a * bs + (blk + 1) * aux, :] = moved[a * aux:(a + 1) * aux]


def relayout(integrals, part):
    bs, aux, width = integrals.shape
    steps = bs // LAM // PARTS
    lams = bs // PARTS
    return pl.pallas_call(
        relayout_kernel,
        grid=(steps,),
        in_specs=[pl.BlockSpec((LAM, aux, width), lambda i: (part * steps + i, 0, 0))],
        out_specs=[
            pl.BlockSpec((aux * bs, LAM * bs), lambda i: (0, i)),
            pl.BlockSpec((2, LAM * aux // 2, width), lambda i: (0, i, 0)),
        ],
        out_shape=[
            jax.ShapeDtypeStruct((aux * bs, lams * bs), jnp.bfloat16),
            jax.ShapeDtypeStruct((2, lams * aux // 2, width), jnp.bfloat16),
        ],
        compiler_params=pltpu.CompilerParams(vmem_limit_bytes=32 << 20),
        cost_estimate=pl.CostEstimate(
            flops=2 * bs * aux * width * 256 // PARTS,
            bytes_accessed=6 * bs * aux * width // PARTS,
            transcendentals=0,
        ),
    )(integrals)


def chi_kernel(bs, aux, ids_ref, tgt_ref, table_ref, *refs):
    d_parts, e_parts = refs[:PARTS], refs[PARTS:2 * PARTS]
    keep_ref, send_ref = refs[2 * PARTS:2 * PARTS + 2]
    dbuf, ebuf, obuf, outb, acc, d_sem, e_sem = refs[2 * PARTS + 2:]
    half = aux // 2
    width = bs * bs
    d_w = width // PARTS
    e_w = bs * half // PARTS

    def d_copy(i):
        return pltpu.make_async_copy(d_parts[i], dbuf.at[:, pl.ds(i * d_w, d_w)], d_sem.at[i])

    def e_copy(i):
        return pltpu.make_async_copy(e_parts[i], ebuf.at[:, pl.ds(i * e_w, e_w), :], e_sem.at[i])

    for i in range(PARTS):
        d_copy(i).start()
    for i in range(PARTS):
        e_copy(i).start()

    occ = table_ref[ids_ref[0]][:, :bs]
    virt = table_ref[ids_ref[1]][:, bs:]

    wide = LAM * bs
    rep = (
        lax.broadcasted_iota(jnp.int32, (wide, bs), 0) % bs == lax.broadcasted_iota(jnp.int32, (wide, bs), 1)
    ).astype(jnp.bfloat16)
    spread = jnp.dot(rep, virt, preferred_element_type=jnp.float32).astype(jnp.bfloat16)
    spread = jnp.concatenate([spread] * LAM, axis=1)
    same = (
        lax.broadcasted_iota(jnp.int32, (wide, wide), 0) // bs == lax.broadcasted_iota(jnp.int32, (wide, wide), 1) // bs
    )
    virt_w = jnp.where(same, spread, jnp.zeros((), jnp.bfloat16))

    tall = bs * half
    rep_o = (
        lax.broadcasted_iota(jnp.int32, (tall, bs), 0) // half == lax.broadcasted_iota(jnp.int32, (tall, bs), 1)
    ).astype(jnp.bfloat16)
    rep_t = (
        lax.broadcasted_iota(jnp.int32, (bs, tall), 1) // half == lax.broadcasted_iota(jnp.int32, (bs, tall), 0)
    ).astype(jnp.bfloat16)
    spread_o = jnp.dot(rep_o, occ, preferred_element_type=jnp.float32).astype(jnp.bfloat16)
    spread_o = jnp.dot(spread_o, rep_t, preferred_element_type=jnp.float32)
    same_o = (
        lax.broadcasted_iota(jnp.int32, (tall, tall), 0) % half
        == lax.broadcasted_iota(jnp.int32, (tall, tall), 1) % half
    )
    occ_w = jnp.where(same_o, spread_o, 0.0).astype(jnp.bfloat16)

    acc[...] = jnp.zeros_like(acc)

    for i in range(PARTS):
        d_copy(i).wait()
        for j in range(d_w // wide):
            at = i * d_w + j * wide
            got = jnp.dot(dbuf[:, at:at + wide], virt_w, preferred_element_type=jnp.float32)
            dbuf[:, at:at + wide] = got.astype(jnp.bfloat16)
    for i in range(PARTS):
        e_copy(i).wait()

    group = 4 * bs
    lanes = 2 * bs

    @pl.loop(0, width // group)
    def _(j):
        cols = pl.ds(pl.multiple_of(j * group, group), group)
        sides = []
        for h in range(2):
            got = jnp.dot(occ_w, ebuf[h, :, cols], preferred_element_type=jnp.float32)
            sides.append(got.reshape(bs, half, group))
        both = jnp.concatenate(sides, axis=1).astype(jnp.bfloat16)
        for p in range(4):
            rows = pl.ds(pl.multiple_of(j * (4 * aux) + p * aux, aux), aux)
            for q in range(bs // 2):
                obuf[rows, q * lanes:(q + 1) * lanes] = jnp.concatenate(
                    [both[2 * q, :, p * bs:(p + 1) * bs], both[2 * q + 1, :, p * bs:(p + 1) * bs]], axis=-1
                )

    low = lax.broadcasted_iota(jnp.int32, (bs, lanes), 1) < bs
    rows_at = aux * aux
    for n in range(aux // 4):
        for m in range(aux * bs // rows_at):
            got = lax.dot_general(
                obuf[m * rows_at:(m + 1) * rows_at, :],
                dbuf[n * group:(n + 1) * group, :],
                (((1,), (1,)), ((), ())),
                preferred_element_type=jnp.float32,
            )
            for t in range(2):
                outb[t, m * rows_at:(m + 1) * rows_at, :] = got[:, t * lanes:(t + 1) * lanes]

        @pl.loop(0, aux)
        def _(a):
            for t in range(2):
                value = outb[t, pl.ds(a, bs, stride=aux), :]
                first = tgt_ref[a * aux + n * 4 + 2 * t]
                second = tgt_ref[a * aux + n * 4 + 2 * t + 1]
                acc[first] += jnp.where(low, value, 0.0)
                acc[second] += jnp.where(low, 0.0, value)

    pairs = keep_ref.shape[0]

    def joined(i):
        one, two = acc[2 * i], acc[2 * i + 1]
        return jnp.where(low, one, two) + pltpu.roll(jnp.where(low, two, one), bs, 1)

    @pl.loop(0, pairs)
    def _(i):
        keep_ref[i] = joined(i)
        send_ref[i] = joined(pairs + i).astype(jnp.bfloat16)


def chi_blocks_of(ids, targets, table, d_parts, e_parts, bs, aux, blocks):
    half = aux // 2
    width = bs * bs
    pairs = blocks // 4
    any_spec = pl.BlockSpec(memory_space=pl.ANY)
    vmem = pl.BlockSpec(memory_space=pltpu.VMEM)
    smem = pl.BlockSpec(memory_space=pltpu.SMEM)
    return pl.pallas_call(
        functools.partial(chi_kernel, bs, aux),
        in_specs=[smem, smem, vmem] + [any_spec] * (2 * PARTS),
        out_specs=[vmem, vmem],
        out_shape=[
            jax.ShapeDtypeStruct((pairs, bs, 2 * bs), jnp.float32),
            jax.ShapeDtypeStruct((pairs, bs, 2 * bs), jnp.bfloat16),
        ],
        scratch_shapes=[
            pltpu.VMEM((aux * bs, width), jnp.bfloat16),
            pltpu.VMEM((2, bs * half, width), jnp.bfloat16),
            pltpu.VMEM((aux * bs, width), jnp.bfloat16),
            pltpu.VMEM((2, aux * bs, 2 * bs), jnp.float32),
            pltpu.VMEM((blocks, bs, 2 * bs), jnp.float32),
            pltpu.SemaphoreType.DMA((PARTS,)),
            pltpu.SemaphoreType.DMA((PARTS,)),
        ],
        compiler_params=pltpu.CompilerParams(vmem_limit_bytes=60 << 20),
        cost_estimate=pl.CostEstimate(
            flops=2 * (aux * bs) ** 2 * width * 2, bytes_accessed=4 * aux * bs * width, transcendentals=0
        ),
    )(ids, targets, table, *d_parts, *e_parts)


def local(orb, three_centre, green_occ, green_virt, pair_atoms, basis_count, chi_target):
    bs, aux = three_centre.shape[1], three_centre.shape[2]
    bits = orb.bit_length() - 1
    me = lax.axis_index("orb")

    def exchange(value, bit):
        return lax.ppermute(value, "orb", [(i, i ^ (1 << bit)) for i in range(orb)])

    lane = lax.broadcasted_iota(jnp.int32, (bs, 2 * bs), 1) % bs
    row = lax.broadcasted_iota(jnp.int32, (bs, 2 * bs), 0)
    both = jnp.concatenate([green_occ.reshape(bs, bs), green_virt.reshape(bs, bs)], axis=1)
    valid = (lane < basis_count[0]) & (row < basis_count[0])
    table = jnp.where(valid, both, jnp.zeros((), both.dtype))[None]

    for bit in reversed(range(bits)):
        table = jnp.concatenate([table, exchange(table, bit)], axis=0)

    def slot(rel):
        place = jnp.zeros_like(rel)
        for k, bit in enumerate(reversed(range(bits))):
            place = place + (((rel >> bit) & 1) << k)
        return place

    ids = slot(pair_atoms[0] ^ me)
    targets = chi_target[0]
    place = slot((targets // CB_DEV) ^ me) * CB_DEV + targets % CB_DEV

    d_parts, e_parts = zip(*[relayout(three_centre[0], i) for i in range(PARTS)])
    keep, send = chi_blocks_of(ids, place, table, d_parts, e_parts, bs, aux, orb * CB_DEV)
    for bit in range(bits):
        total = keep + exchange(send, bit).astype(jnp.float32)
        rest = total.shape[0] // 2
        if bit + 1 < bits:
            keep, send = total[:rest], total[rest:].astype(jnp.bfloat16)
    total = total.reshape(CB_DEV // 2, bs, 2, bs).transpose(0, 2, 1, 3)
    return total.reshape(CB_DEV, bs * bs)


def solution(mesh):
    in_specs = (
        P("orb", None, None, None),
        P(("grp", "orb"), None),
        P(("grp", "orb"), None),
        P("orb", None),
        P("orb"),
        P("orb", None),
    )
    out_specs = P(("grp", "orb"), None)
    return jax.shard_map(
        functools.partial(local, mesh.shape["orb"]), mesh=mesh, in_specs=in_specs, out_specs=out_specs, check_vma=False
    )
```

time: 307 us -> 92.4 us (0.30)
  waiting for transfers between devices: 90.6 us -> 18.2 us
  local copies, waits for them, and re-layouts: 87.1 us -> 19.3 us
  matrix products: 60.9 us -> 0 us
  blocking collectives: 42.1 us -> 0 us
  Pallas kernels: 0 us -> 39.7 us
  between operations: 14.8 us -> 0.86 us
  starting transfers between devices: 0.01 us -> 10.1 us
  other arithmetic: 10.2 us -> 3.9 us
    unnamed x2 -> x0, waiting for transfers between devices: 90.6 us -> none
    dot_general x5 -> x0, matrix products: 60.9 us -> none  [the longest x1 42.5 us: local(): lax.dot_general(occ_side.reshape(block_size, -1, block_size), virt_side.r...]
    reshape x4 -> x2, local copies, waits for them, and re-layouts: 47.1 us -> 0.86 us  [the longest x1 0.74 us: local(): return total.reshape(CB_DEV, bs * bs)]
    all_gather x2 -> x0, blocking collectives: 42.1 us -> none  [the longest x1 23.8 us: local(): lax.all_gather(virt_masked, 'orb', axis=0, tiled=True)]
    pallas_call x0 -> x5, Pallas kernels: none -> 39.7 us  [the longest x1 31.3 us: chi_blocks_of(): pl.pallas_call(functools.partial(chi_kernel, bs, aux), in_specs=[smem, sm...]
    ppermute x0 -> x8, waiting for transfers between devices: none -> 18.2 us  [exchange(): return lax.ppermute(value, 'orb', [(i, i ^ 1 << bit) for i in range(orb)])]
    another operation x1 -> x0, local copies, waits for them, and re-layouts: 13.5 us -> none  [local(): integrals.reshape(-1, block_size * grouping)]
    convert_element_type x1 -> x0, local copies, waits for them, and re-layouts: 11.9 us -> none  [local(): virt_side = virt_side.astype(jnp.bfloat16)]
  transfers between devices with their start and end apart: 1 -> 8, of which waited for: 1 -> 6; matrix products, arithmetic and copies ran while one was open for 0% -> 1% of each run, Pallas kernels for 0% -> 9%
where the time goes in v1:
time: 92.4 us; the launch traced here: 92 us
  Pallas kernels  39.7 us (43%)
  local copies, waits for them, and re-layouts  19.3 us (21%)
  waiting for transfers between devices  18.2 us (20%)
  starting transfers between devices  10.1 us (11%)
  other arithmetic  3.9 us (4%)
    pallas_call x1, Pallas kernels, chi_blocks_of(): pl.pallas_call(functools.partial(chi_kernel, bs, aux), in_specs=[smem, sm...  31.3 us
    ppermute x8, waiting for transfers between devices, exchange(): return lax.ppermute(value, 'orb', [(i, i ^ 1 << bit) for i in range(orb)])  18.2 us
    unnamed x29, local copies, waits for them, and re-layouts  18.2 us
    ppermute x8, starting transfers between devices, exchange(): return lax.ppermute(value, 'orb', [(i, i ^ 1 << bit) for i in range(orb)])  10.1 us
    pallas_call x4, Pallas kernels, relayout(): pl.pallas_call(relayout_kernel, grid=(steps,), in_specs=[pl.BlockSpec((LA...  8.45 us
  transfers between devices with their start and end apart: 8, of which 6 were waited for; matrix products, arithmetic and copies ran while one was open for 1% of the time, Pallas kernels for 9%

profile of v1, /device:TPU:0, one launch (start us, length us, event | category | flops | bytes accessed | tf_op | source)
XLA Modules:
  0.0 92.0 jit_solution(8918927795768064888)
XLA Ops:
  0.7 0.8 reduce
  1.4 0.1 concatenate.29
  1.5 0.8 reduce.1
  2.3 0.1 concatenate.30
  2.4 0.1 constant_dynamic-update-slice_fusion.4
  2.5 4.1 %collective-permute-start = (bf16[1,64,128]{2,1,0:T(8,128)(2,1)S(1)}, bf16[1,64,128]{2,1,0:T(8,128)(2,1)S(1)}, u32[]{:S(2)}, u32[]{:S(2)}) collective-permute-start(bf16[1,64,128]{2,1,0:T(8,128)(2,1)S(1)} %get-tuple-element.26), channel_id=1, source_target_pairs={{0,8},{1,9},{2,10},{3,11},{4,12},{5,13},{6,14},{7,15},{8,0},{9,1},... | collective-permute-start | bytes 49160 | tf_op jit(solution)/shard_map/ppermute | solution.py:211
  6.6 3.4 %copy-done = bf16[1,64,16,4096]{3,2,1,0:T(8,128)(2,1)S(1)} copy-done((bf16[1,64,16,4096]{3,2,1,0:T(8,128)(2,1)S(1)}, bf16[1,64,16,4096]{3,2,1,0:T(8,128)(2,1)}, u32[]{:S(2)}) %copy-start) | copy-done | bytes 8388632
  10.0 2.1 %shard_map.67 = (bf16[1024,1024]{1,0:T(8,128)(2,1)S(1)}, bf16[2,128,4096]{2,1,0:T(8,128)(2,1)S(1)}) custom-call(bf16[64,16,4096]{2,1,0:T(8,128)(2,1)S(1)} %bitcast.10), custom_call_target="tpu_custom_call" | custom-call | flops 536870912 | bytes 6291456 | tf_op jit(solution)/shard_map/pallas_call | solution.py:41
  12.1 0.0 copy-start.2
  12.1 1.4 %copy-done.2 = bf16[1024,1024]{1,0:T(8,128)(2,1)} copy-done((bf16[1024,1024]{1,0:T(8,128)(2,1)}, bf16[1024,1024]{1,0:T(8,128)(2,1)S(1)}, u32[]{:S(2)}) %copy-start.2) | copy-done | bytes 2097176
  13.4 1.3 %copy-done.3 = bf16[2,128,4096]{2,1,0:T(8,128)(2,1)} copy-done((bf16[2,128,4096]{2,1,0:T(8,128)(2,1)}, bf16[2,128,4096]{2,1,0:T(8,128)(2,1)S(1)}, u32[]{:S(2)}) %copy-start.3) | copy-done | bytes 2097176
  14.8 2.1 %shard_map.66 = (bf16[1024,1024]{1,0:T(8,128)(2,1)S(1)}, bf16[2,128,4096]{2,1,0:T(8,128)(2,1)S(1)}) custom-call(bf16[64,16,4096]{2,1,0:T(8,128)(2,1)S(1)} %bitcast.11), custom_call_target="tpu_custom_call" | custom-call | flops 536870912 | bytes 6291456 | tf_op jit(solution)/shard_map/pallas_call | solution.py:41
  16.9 0.0 copy-start.4
  16.9 1.3 %copy-done.4 = bf16[1024,1024]{1,0:T(8,128)(2,1)} copy-done((bf16[1024,1024]{1,0:T(8,128)(2,1)}, bf16[1024,1024]{1,0:T(8,128)(2,1)S(1)}, u32[]{:S(2)}) %copy-start.4) | copy-done | bytes 2097176
  18.2 1.3 %copy-done.5 = bf16[2,128,4096]{2,1,0:T(8,128)(2,1)} copy-done((bf16[2,128,4096]{2,1,0:T(8,128)(2,1)}, bf16[2,128,4096]{2,1,0:T(8,128)(2,1)S(1)}, u32[]{:S(2)}) %copy-start.5) | copy-done | bytes 2097176
  19.5 0.0 copy-done.12
  19.5 0.5 add_bitcast_fusion.ids_ref
  20.0 0.0 copy-done.10
  20.0 0.6 fusion.2.tgt_ref
  20.6 3.4 %copy-done.1 = bf16[1,64,16,4096]{3,2,1,0:T(8,128)(2,1)S(1)} copy-done((bf16[1,64,16,4096]{3,2,1,0:T(8,128)(2,1)S(1)}, bf16[1,64,16,4096]{3,2,1,0:T(8,128)(2,1)}, u32[]{:S(2)}) %copy-start.1) | copy-done | bytes 8388632
  24.0 2.1 %shard_map.65 = (bf16[1024,1024]{1,0:T(8,128)(2,1)S(1)}, bf16[2,128,4096]{2,1,0:T(8,128)(2,1)S(1)}) custom-call(bf16[64,16,4096]{2,1,0:T(8,128)(2,1)S(1)} %bitcast.12), custom_call_target="tpu_custom_call" | custom-call | flops 536870912 | bytes 6291456 | tf_op jit(solution)/shard_map/pallas_call | solution.py:41
  26.1 0.0 copy-start.6
  26.1 1.3 %copy-done.6 = bf16[1024,1024]{1,0:T(8,128)(2,1)} copy-done((bf16[1024,1024]{1,0:T(8,128)(2,1)}, bf16[1024,1024]{1,0:T(8,128)(2,1)S(1)}, u32[]{:S(2)}) %copy-start.6) | copy-done | bytes 2097176
  27.4 1.3 %copy-done.7 = bf16[2,128,4096]{2,1,0:T(8,128)(2,1)} copy-done((bf16[2,128,4096]{2,1,0:T(8,128)(2,1)}, bf16[2,128,4096]{2,1,0:T(8,128)(2,1)S(1)}, u32[]{:S(2)}) %copy-start.7) | copy-done | bytes 2097176
  28.8 0.0 collective-permute-done
  28.8 1.6 %collective-permute-start.1 = (bf16[2,64,128]{2,1,0:T(8,128)(2,1)S(1)}, bf16[2,64,128]{2,1,0:T(8,128)(2,1)S(1)}, u32[]{:S(2)}, u32[]{:S(2)}) collective-permute-start(bf16[2,64,128]{2,1,0:T(8,128)(2,1)S(1)} %pad_maximum_fusion.2), channel_id=1, source_target_pairs={{0,4},{1,5},{2,6},{3,7},{4,0},{5,1},{6,2},{7,3},{8,12},{9,13},{10,... | collective-permute-start | bytes 98312 | tf_op jit(solution)/shard_map/ppermute | solution.py:211
  30.4 2.1 %shard_map.64 = (bf16[1024,1024]{1,0:T(8,128)(2,1)S(1)}, bf16[2,128,4096]{2,1,0:T(8,128)(2,1)S(1)}) custom-call(bf16[64,16,4096]{2,1,0:T(8,128)(2,1)S(1)} %bitcast.13), custom_call_target="tpu_custom_call" | custom-call | flops 536870912 | bytes 6291456 | tf_op jit(solution)/shard_map/pallas_call | solution.py:41
  32.5 0.0 copy-start.8
  32.5 1.3 %copy-done.8 = bf16[1024,1024]{1,0:T(8,128)(2,1)} copy-done((bf16[1024,1024]{1,0:T(8,128)(2,1)}, bf16[1024,1024]{1,0:T(8,128)(2,1)S(1)}, u32[]{:S(2)}) %copy-start.8) | copy-done | bytes 2097176
  33.9 1.4 %copy-done.9 = bf16[2,128,4096]{2,1,0:T(8,128)(2,1)} copy-done((bf16[2,128,4096]{2,1,0:T(8,128)(2,1)}, bf16[2,128,4096]{2,1,0:T(8,128)(2,1)S(1)}, u32[]{:S(2)}) %copy-start.9) | copy-done | bytes 2097176
  35.3 0.0 collective-permute-done.1
  35.3 1.6 %collective-permute-start.2 = (bf16[4,64,128]{2,1,0:T(8,128)(2,1)S(1)}, bf16[4,64,128]{2,1,0:T(8,128)(2,1)S(1)}, u32[]{:S(2)}, u32[]{:S(2)}) collective-permute-start(bf16[4,64,128]{2,1,0:T(8,128)(2,1)S(1)} %pad_maximum_fusion.1), channel_id=1, source_target_pairs={{0,2},{1,3},{2,0},{3,1},{4,6},{5,7},{6,4},{7,5},{8,10},{9,11},{10,... | collective-permute-start | bytes 196616 | tf_op jit(solution)/shard_map/ppermute | solution.py:211
  36.9 2.7 %collective-permute-done.2 = bf16[4,64,128]{2,1,0:T(8,128)(2,1)S(1)} collective-permute-done((bf16[4,64,128]{2,1,0:T(8,128)(2,1)S(1)}, bf16[4,64,128]{2,1,0:T(8,128)(2,1)S(1)}, u32[]{:S(2)}, u32[]{:S(2)}) %collective-permute-start.2) | collective-permute-done | bytes 65568 | tf_op jit(solution)/shard_map/ppermute | solution.py:211
  39.6 0.1 collective-permute-start.3
  39.7 1.3 %collective-permute-done.3 = bf16[8,64,128]{2,1,0:T(8,128)(2,1)S(1)} collective-permute-done((bf16[8,64,128]{2,1,0:T(8,128)(2,1)S(1)}, bf16[8,64,128]{2,1,0:T(8,128)(2,1)S(1)}, u32[]{:S(2)}, u32[]{:S(2)}) %collective-permute-start.3) | collective-permute-done | bytes 131104 | tf_op jit(solution)/shard_map/ppermute | solution.py:211
  41.1 0.7 copy-done.11
  41.8 31.3 %shard_map.68 = (f32[16,64,128]{2,1,0:T(8,128)}, bf16[16,64,128]{2,1,0:T(8,128)(2,1)}) custom-call(s32[2]{0:T(128)} %add_bitcast_fusion.ids_ref, s32[256]{0:T(256)} %fusion.2.tgt_ref, bf16[16,64,128]{2,1,0:T(8,128)(2,1)} %copy-done.11, bf16[1024,1024]{1,0:T(8,128)(2,1)} %copy-done.8, bf16[1024,1024]{1,0:T(8,128)(2,1)} %copy-done.6, ...), custom_call_target="tpu_custom_call" | custom-call | flops 17179869184 | bytes 16777216 | tf_op jit(solution)/shard_map/pallas_call | solution.py:181
  73.0 0.2 collective-permute-start.4
  73.3 1.6 %collective-permute-done.4 = bf16[16,64,128]{2,1,0:T(8,128)(2,1)S(1)} collective-permute-done((bf16[16,64,128]{2,1,0:T(8,128)(2,1)}, bf16[16,64,128]{2,1,0:T(8,128)(2,1)S(1)}, u32[]{:S(2)}, u32[]{:S(2)}) %collective-permute-start.4) | collective-permute-done | bytes 262176 | tf_op jit(solution)/shard_map/ppermute | solution.py:211
  74.9 1.1 %convert_add_fusion = f32[16,64,128]{2,1,0:T(8,128)S(1)} fusion(f32[16,64,128]{2,1,0:T(8,128)} %get-tuple-element.23, bf16[16,64,128]{2,1,0:T(8,128)(2,1)S(1)} %collective-permute-done.4), kind=kLoop, calls=%fused_computation | loop fusion | flops 262144 | bytes 1310720 | tf_op jit(solution)/shard_map/add | solution.py:235
  76.0 1.6 %collective-permute-start.5 = (bf16[8,64,128]{2,1,0:T(8,128)(2,1)S(1)}, bf16[8,64,128]{2,1,0:T(8,128)(2,1)S(1)}, u32[]{:S(2)}, u32[]{:S(2)}) collective-permute-start(bf16[8,64,128]{2,1,0:T(8,128)(2,1)S(1)} %slice.39), channel_id=1, source_target_pairs={{0,2},{1,3},{2,0},{3,1},{4,6},{5,7},{6,4},{7,5},{8,10},{9,11},{10,... | collective-permute-start | bytes 393224 | tf_op jit(solution)/shard_map/ppermute | solution.py:211
  77.6 4.0 %collective-permute-done.5 = bf16[8,64,128]{2,1,0:T(8,128)(2,1)S(1)} collective-permute-done((bf16[8,64,128]{2,1,0:T(8,128)(2,1)S(1)}, bf16[8,64,128]{2,1,0:T(8,128)(2,1)S(1)}, u32[]{:S(2)}, u32[]{:S(2)}) %collective-permute-start.5) | collective-permute-done | bytes 131104 | tf_op jit(solution)/shard_map/ppermute | solution.py:211
  81.7 0.5 collective-permute-start.6
  82.2 3.8 %collective-permute-done.6 = bf16[4,64,128]{2,1,0:T(8,128)(2,1)S(1)} collective-permute-done((bf16[4,64,128]{2,1,0:T(8,128)(2,1)S(1)}, bf16[4,64,128]{2,1,0:T(8,128)(2,1)S(1)}, u32[]{:S(2)}, u32[]{:S(2)}) %collective-permute-start.6) | collective-permute-done | bytes 65568 | tf_op jit(solution)/shard_map/ppermute | solution.py:211
  86.0 0.4 collective-permute-start.7
  86.4 4.7 %collective-permute-done.7 = bf16[2,64,128]{2,1,0:T(8,128)(2,1)S(1)} collective-permute-done((bf16[2,64,128]{2,1,0:T(8,128)(2,1)S(1)}, bf16[2,64,128]{2,1,0:T(8,128)(2,1)S(1)}, u32[]{:S(2)}, u32[]{:S(2)}) %collective-permute-start.7) | collective-permute-done | bytes 32800 | tf_op jit(solution)/shard_map/ppermute | solution.py:211
  91.2 0.1 reshape.155
  91.3 0.7 reshape.156
  (26 shorter events, 0.2 us)
Async XLA Ops:
  2.5 26.3 %collective-permute-start = (bf16[1,64,128]{2,1,0:T(8,128)(2,1)S(1)}, bf16[1,64,128]{2,1,0:T(8,128)(2,1)S(1)}, u32[]{:S(2)}, u32[]{:S(2)}) collective-permute-start(bf16[1,64,128]{2,1,0:T(8,128)(2,1)S(1)} %get-tuple-element.26), channel_id=1, source_target_pairs={{0,8},{1,9},{2,10},{3,11},{4,12},{5,13},{6,14},{7,15},{8,0},{9,1},... | collective-permute-start | bytes 49160 | tf_op jit(solution)/shard_map/ppermute | solution.py:211
  6.6 3.4 %copy-start = (bf16[1,64,16,4096]{3,2,1,0:T(8,128)(2,1)S(1)}, bf16[1,64,16,4096]{3,2,1,0:T(8,128)(2,1)}, u32[]{:S(2)}) copy-start(bf16[1,64,16,4096]{3,2,1,0:T(8,128)(2,1)} %param.6) | copy-start | bytes 25165828
  12.1 1.4 %copy-start.2 = (bf16[1024,1024]{1,0:T(8,128)(2,1)}, bf16[1024,1024]{1,0:T(8,128)(2,1)S(1)}, u32[]{:S(2)}) copy-start(bf16[1024,1024]{1,0:T(8,128)(2,1)S(1)} %get-tuple-element.18.refs_3_) | copy-start | bytes 6291460
  13.4 1.3 %copy-start.3 = (bf16[2,128,4096]{2,1,0:T(8,128)(2,1)}, bf16[2,128,4096]{2,1,0:T(8,128)(2,1)S(1)}, u32[]{:S(2)}) copy-start(bf16[2,128,4096]{2,1,0:T(8,128)(2,1)S(1)} %get-tuple-element.22.refs_7_) | copy-start | bytes 6291460
  14.8 4.8 %copy-start.12 = (s32[1,2]{1,0:T(1,128)S(1)}, s32[1,2]{1,0:T(1,128)}, u32[]{:S(2)}) copy-start(s32[1,2]{1,0:T(1,128)} %param.9) | copy-start | bytes 28
  14.8 5.3 %copy-start.10 = (s32[1,256]{1,0:T(1,128)S(1)}, s32[1,256]{1,0:T(1,128)}, u32[]{:S(2)}) copy-start(s32[1,256]{1,0:T(1,128)} %param.11) | copy-start | bytes 3076
  16.9 1.3 %copy-start.4 = (bf16[1024,1024]{1,0:T(8,128)(2,1)}, bf16[1024,1024]{1,0:T(8,128)(2,1)S(1)}, u32[]{:S(2)}) copy-start(bf16[1024,1024]{1,0:T(8,128)(2,1)S(1)} %get-tuple-element.17.refs_2_) | copy-start | bytes 6291460
  18.2 1.3 %copy-start.5 = (bf16[2,128,4096]{2,1,0:T(8,128)(2,1)}, bf16[2,128,4096]{2,1,0:T(8,128)(2,1)S(1)}, u32[]{:S(2)}) copy-start(bf16[2,128,4096]{2,1,0:T(8,128)(2,1)S(1)} %get-tuple-element.21.refs_6_) | copy-start | bytes 6291460
  20.6 3.4 %copy-start.1 = (bf16[1,64,16,4096]{3,2,1,0:T(8,128)(2,1)S(1)}, bf16[1,64,16,4096]{3,2,1,0:T(8,128)(2,1)}, u32[]{:S(2)}) copy-start(bf16[1,64,16,4096]{3,2,1,0:T(8,128)(2,1)} %param.6) | copy-start | bytes 25165828
  26.1 1.3 %copy-start.6 = (bf16[1024,1024]{1,0:T(8,128)(2,1)}, bf16[1024,1024]{1,0:T(8,128)(2,1)S(1)}, u32[]{:S(2)}) copy-start(bf16[1024,1024]{1,0:T(8,128)(2,1)S(1)} %get-tuple-element.16.refs_1_) | copy-start | bytes 6291460
  27.4 1.3 %copy-start.7 = (bf16[2,128,4096]{2,1,0:T(8,128)(2,1)}, bf16[2,128,4096]{2,1,0:T(8,128)(2,1)S(1)}, u32[]{:S(2)}) copy-start(bf16[2,128,4096]{2,1,0:T(8,128)(2,1)S(1)} %get-tuple-element.20.refs_5_) | copy-start | bytes 6291460
  28.8 6.5 %collective-permute-start.1 = (bf16[2,64,128]{2,1,0:T(8,128)(2,1)S(1)}, bf16[2,64,128]{2,1,0:T(8,128)(2,1)S(1)}, u32[]{:S(2)}, u32[]{:S(2)}) collective-permute-start(bf16[2,64,128]{2,1,0:T(8,128)(2,1)S(1)} %pad_maximum_fusion.2), channel_id=1, source_target_pairs={{0,4},{1,5},{2,6},{3,7},{4,0},{5,1},{6,2},{7,3},{8,12},{9,13},{10,... | collective-permute-start | bytes 98312 | tf_op jit(solution)/shard_map/ppermute | solution.py:211
  32.5 1.3 %copy-start.8 = (bf16[1024,1024]{1,0:T(8,128)(2,1)}, bf16[1024,1024]{1,0:T(8,128)(2,1)S(1)}, u32[]{:S(2)}) copy-start(bf16[1024,1024]{1,0:T(8,128)(2,1)S(1)} %get-tuple-element.15.refs_0_) | copy-start | bytes 6291460
  33.9 1.4 %copy-start.9 = (bf16[2,128,4096]{2,1,0:T(8,128)(2,1)}, bf16[2,128,4096]{2,1,0:T(8,128)(2,1)S(1)}, u32[]{:S(2)}) copy-start(bf16[2,128,4096]{2,1,0:T(8,128)(2,1)S(1)} %get-tuple-element.19.refs_4_) | copy-start | bytes 6291460
  35.3 4.3 %collective-permute-start.2 = (bf16[4,64,128]{2,1,0:T(8,128)(2,1)S(1)}, bf16[4,64,128]{2,1,0:T(8,128)(2,1)S(1)}, u32[]{:S(2)}, u32[]{:S(2)}) collective-permute-start(bf16[4,64,128]{2,1,0:T(8,128)(2,1)S(1)} %pad_maximum_fusion.1), channel_id=1, source_target_pairs={{0,2},{1,3},{2,0},{3,1},{4,6},{5,7},{6,4},{7,5},{8,10},{9,11},{10,... | collective-permute-start | bytes 196616 | tf_op jit(solution)/shard_map/ppermute | solution.py:211
  39.6 1.4 %collective-permute-start.3 = (bf16[8,64,128]{2,1,0:T(8,128)(2,1)S(1)}, bf16[8,64,128]{2,1,0:T(8,128)(2,1)S(1)}, u32[]{:S(2)}, u32[]{:S(2)}) collective-permute-start(bf16[8,64,128]{2,1,0:T(8,128)(2,1)S(1)} %pad_maximum_fusion), channel_id=1, source_target_pairs={{0,1},{1,0},{2,3},{3,2},{4,5},{5,4},{6,7},{7,6},{8,9},{9,8},{10,11... | collective-permute-start | bytes 393224 | tf_op jit(solution)/shard_map/ppermute | solution.py:211
  41.1 0.7 copy-start.11
  73.0 1.8 %collective-permute-start.4 = (bf16[16,64,128]{2,1,0:T(8,128)(2,1)}, bf16[16,64,128]{2,1,0:T(8,128)(2,1)S(1)}, u32[]{:S(2)}, u32[]{:S(2)}) collective-permute-start(bf16[16,64,128]{2,1,0:T(8,128)(2,1)} %get-tuple-element.24), channel_id=1, source_target_pairs={{0,1},{1,0},{2,3},{3,2},{4,5},{5,4},{6,7},{7,6},{8,9},{9,8},{10,11... | collective-permute-start | bytes 786440 | tf_op jit(solution)/shard_map/ppermute | solution.py:211
  76.0 5.6 %collective-permute-start.5 = (bf16[8,64,128]{2,1,0:T(8,128)(2,1)S(1)}, bf16[8,64,128]{2,1,0:T(8,128)(2,1)S(1)}, u32[]{:S(2)}, u32[]{:S(2)}) collective-permute-start(bf16[8,64,128]{2,1,0:T(8,128)(2,1)S(1)} %slice.39), channel_id=1, source_target_pairs={{0,2},{1,3},{2,0},{3,1},{4,6},{5,7},{6,4},{7,5},{8,10},{9,11},{10,... | collective-permute-start | bytes 393224 | tf_op jit(solution)/shard_map/ppermute | solution.py:211
  81.7 4.3 %collective-permute-start.6 = (bf16[4,64,128]{2,1,0:T(8,128)(2,1)S(1)}, bf16[4,64,128]{2,1,0:T(8,128)(2,1)S(1)}, u32[]{:S(2)}, u32[]{:S(2)}) collective-permute-start(bf16[4,64,128]{2,1,0:T(8,128)(2,1)S(1)} %slice.40), channel_id=1, source_target_pairs={{0,4},{1,5},{2,6},{3,7},{4,0},{5,1},{6,2},{7,3},{8,12},{9,13},{10,... | collective-permute-start | bytes 196616 | tf_op jit(solution)/shard_map/ppermute | solution.py:211
  86.0 5.1 %collective-permute-start.7 = (bf16[2,64,128]{2,1,0:T(8,128)(2,1)S(1)}, bf16[2,64,128]{2,1,0:T(8,128)(2,1)S(1)}, u32[]{:S(2)}, u32[]{:S(2)}) collective-permute-start(bf16[2,64,128]{2,1,0:T(8,128)(2,1)S(1)} %slice.41), channel_id=1, source_target_pairs={{0,8},{1,9},{2,10},{3,11},{4,12},{5,13},{6,14},{7,15},{8,0},{9,1},... | collective-permute-start | bytes 98312 | tf_op jit(solution)/shard_map/ppermute | solution.py:211

commit v2 on v1

v2 whole, which is shorter than its diff:
```python
import functools

import jax
import jax.numpy as jnp
from jax import lax
from jax.experimental import pallas as pl
from jax.experimental.pallas import tpu as pltpu
from jax.sharding import PartitionSpec as P

CB_DEV = 4
LAM = 4
PARTS = 4
VMEM = 60 << 20


def pack_kernel(count_ref, occ_ref, virt_ref, out_ref, rows_ref):
    lanes = out_ref.shape[2]
    half = out_ref.shape[1] // 2
    for i in range(half):
        rows_ref[i:i + 1, :] = occ_ref[:, i * lanes:(i + 1) * lanes].astype(jnp.float32)
        rows_ref[half + i:half + i + 1, :] = virt_ref[:, i * lanes:(i + 1) * lanes].astype(jnp.float32)
    bs = lanes // 2
    row = lax.broadcasted_iota(jnp.int32, rows_ref.shape, 0)
    lane = lax.broadcasted_iota(jnp.int32, rows_ref.shape, 1)
    count = count_ref[0]
    valid = (2 * (row % half) + lane // bs < count) & (lane % bs < count)
    out_ref[0] = jnp.where(valid, rows_ref[...], 0.0).astype(jnp.bfloat16)


def packed(basis_count, green_occ, green_virt, bs):
    vmem = pl.BlockSpec(memory_space=pltpu.VMEM)
    return pl.pallas_call(
        pack_kernel,
        in_specs=[pl.BlockSpec(memory_space=pltpu.SMEM), vmem, vmem],
        out_specs=vmem,
        out_shape=jax.ShapeDtypeStruct((1, bs, 2 * bs), jnp.bfloat16),
        scratch_shapes=[pltpu.VMEM((bs, 2 * bs), jnp.float32)],
    )(basis_count, green_occ, green_virt)


def relayout_kernel(b_ref, d_ref):
    lam, aux, width = b_ref.shape
    bs = d_ref.shape[0] // aux
    rows = aux * aux
    row = lax.broadcasted_iota(jnp.int32, (rows, rows), 0)
    col = lax.broadcasted_iota(jnp.int32, (rows, rows), 1)
    perm = (col == (row % aux) * aux + row // aux).astype(jnp.bfloat16)
    for blk in range(bs // aux):
        pieces = []
        for p in range(aux):
            at = (blk * aux + p) * bs
            pieces.append(jnp.concatenate([b_ref[i, :, at:at + bs] for i in range(lam)], axis=-1))
        stacked = jnp.concatenate(pieces, axis=0)
        moved = jnp.dot(perm, stacked, preferred_element_type=jnp.float32).astype(jnp.bfloat16)
        for a in range(aux):
            d_ref[a * bs + blk * aux:a * bs + (blk + 1) * aux, :] = moved[a * aux:(a + 1) * aux]


def relayout(integrals, part):
    bs, aux, width = integrals.shape
    steps = bs // LAM // PARTS
    return pl.pallas_call(
        relayout_kernel,
        grid=(steps,),
        in_specs=[pl.BlockSpec((LAM, aux, width), lambda i: (part * steps + i, 0, 0))],
        out_specs=pl.BlockSpec((aux * bs, LAM * bs), lambda i: (0, i)),
        out_shape=jax.ShapeDtypeStruct((aux * bs, bs // PARTS * bs), jnp.bfloat16),
        compiler_params=pltpu.CompilerParams(vmem_limit_bytes=VMEM),
        cost_estimate=pl.CostEstimate(
            flops=2 * bs * aux * width * 256 // PARTS,
            bytes_accessed=4 * bs * aux * width // PARTS,
            transcendentals=0,
        ),
    )(integrals)


def chi_kernel(bs, aux, sends, ids_ref, tgt_ref, table_ref, b_ref, *refs):
    d_parts, refs = refs[:PARTS], refs[PARTS:]
    keep_ref, send_refs, refs = refs[0], refs[1:1 + sends], refs[1 + sends:]
    dbuf, bbuf, obuf, out0, out1, d_sem, b_sem, *accs = refs
    low_acc, high_acc = accs[0], accs[-1]
    half = aux // 2
    width = bs * bs
    wide = LAM * bs
    per = width // PARTS // wide

    def d_copy(part, j):
        src = d_parts[part].at[:, pl.ds(pl.multiple_of(j * wide, wide), wide)]
        at = pl.multiple_of((part * per + j) * wide, wide)
        return pltpu.make_async_copy(src, dbuf.at[:, pl.ds(at, wide)], d_sem.at[part * per + j])

    def b_copy(j):
        cols = pl.ds(pl.multiple_of(j * wide, wide), wide)
        return pltpu.make_async_copy(b_ref.at[:, :, cols], bbuf.at[:, :, cols], b_sem.at[j])

    for part in range(PARTS):
        for j in range(per):
            d_copy(part, j).start()
            b_copy(part * per + j).start()

    occ = table_ref[ids_ref[0], :bs // 2]
    virt = table_ref[ids_ref[1], bs // 2:]

    def spread_rows(block, of_row, count):
        shape = (count, bs // 2)
        pick = of_row(lax.broadcasted_iota(jnp.int32, shape, 0)) // 2 == lax.broadcasted_iota(jnp.int32, shape, 1)
        got = jnp.dot(pick.astype(jnp.bfloat16), block, preferred_element_type=jnp.float32)
        odd = of_row(lax.broadcasted_iota(jnp.int32, (count, bs), 0)) % 2 == 1
        return jnp.where(odd, got[:, bs:], got[:, :bs])

    spread = spread_rows(virt, lambda i: i % bs, wide)
    spread = jnp.concatenate([spread] * LAM, axis=1)
    same = (
        lax.broadcasted_iota(jnp.int32, (wide, wide), 0) // bs == lax.broadcasted_iota(jnp.int32, (wide, wide), 1) // bs
    )
    virt_w = jnp.where(same, spread, 0.0).astype(jnp.bfloat16)

    tall = bs * half
    rep_t = (
        lax.broadcasted_iota(jnp.int32, (bs, tall), 1) // half == lax.broadcasted_iota(jnp.int32, (bs, tall), 0)
    ).astype(jnp.bfloat16)
    spread_o = spread_rows(occ, lambda i: i // half, tall).astype(jnp.bfloat16)
    spread_o = jnp.dot(spread_o, rep_t, preferred_element_type=jnp.float32)
    same_o = (
        lax.broadcasted_iota(jnp.int32, (tall, tall), 0) % half
        == lax.broadcasted_iota(jnp.int32, (tall, tall), 1) % half
    )
    occ_w = jnp.where(same_o, spread_o, 0.0).astype(jnp.bfloat16)

    for ref in accs:
        ref[...] = jnp.zeros_like(ref)

    lanes = 2 * bs
    for part in range(PARTS):

        @pl.loop(0, per)
        def _(i):
            j = part * per + i
            d_copy(part, i).wait()
            b_copy(j).wait()
            cols = pl.ds(pl.multiple_of(j * wide, wide), wide)
            got = jnp.dot(dbuf[:, cols], virt_w, preferred_element_type=jnp.float32)
            dbuf[:, cols] = got.astype(jnp.bfloat16)
            block = bbuf[:, :, cols].astype(jnp.float32)
            sides = []
            for h in range(2):
                side = block[:, h * half:(h + 1) * half, :].reshape(tall, wide).astype(jnp.bfloat16)
                got = jnp.dot(occ_w, side, preferred_element_type=jnp.float32)
                sides.append(got.reshape(bs, half, wide))
            both = jnp.concatenate(sides, axis=1).astype(jnp.bfloat16)
            for p in range(LAM):
                rows = pl.ds(pl.multiple_of(j * (LAM * aux) + p * aux, aux), aux)
                for q in range(bs // 2):
                    obuf[rows, q * lanes:(q + 1) * lanes] = jnp.concatenate(
                        [both[2 * q, :, p * bs:(p + 1) * bs], both[2 * q + 1, :, p * bs:(p + 1) * bs]], axis=-1
                    )

    low = lax.broadcasted_iota(jnp.int32, (bs, lanes), 1) < bs
    shared = len(accs) == 1
    outs = (out0, out1)
    group = 4 * bs

    def scatter(n):
        for a in range(aux):
            for t in range(2):
                value = outs[n % 2][t, pl.ds(a, bs, stride=aux), :]
                first = tgt_ref[a * aux + n * 4 + 2 * t]
                second = tgt_ref[a * aux + n * 4 + 2 * t + 1]
                low_acc[first] += jnp.where(low, value, 0.0) if shared else value
                high_acc[second] += jnp.where(low, 0.0, value) if shared else value

    for n in range(aux // 4):
        if n:
            scatter(n - 1)
        got = lax.dot_general(
            obuf[...],
            dbuf[n * group:(n + 1) * group, :],
            (((1,), (1,)), ((), ())),
            preferred_element_type=jnp.float32,
        )
        for t in range(2):
            outs[n % 2][t] = got[:, t * lanes:(t + 1) * lanes]
    scatter(aux // 4 - 1)

    pairs = keep_ref.shape[0]

    def joined(i):
        if shared:
            one, two = low_acc[2 * i], low_acc[2 * i + 1]
            return jnp.where(low, one, two) + pltpu.roll(jnp.where(low, two, one), bs, 1)
        left = jnp.where(low, low_acc[2 * i], high_acc[2 * i + 1])
        right = jnp.where(low, low_acc[2 * i + 1], high_acc[2 * i])
        return left + pltpu.roll(right, bs, 1)

    @pl.loop(0, pairs)
    def _(i):
        keep_ref[i] = joined(i)
        for k, send_ref in enumerate(send_refs):
            send_ref[i] = joined((k + 1) * pairs + i).astype(jnp.bfloat16)


def chi_blocks_of(ids, targets, table, integrals, d_parts, blocks, sends):
    bs, aux, width = integrals.shape
    pairs = blocks // 2 // (sends + 1)
    any_spec = pl.BlockSpec(memory_space=pl.ANY)
    vmem = pl.BlockSpec(memory_space=pltpu.VMEM)
    smem = pl.BlockSpec(memory_space=pltpu.SMEM)
    acc = pltpu.VMEM((blocks, bs, 2 * bs), jnp.float32)
    chunks = width // (LAM * bs)
    return pl.pallas_call(
        functools.partial(chi_kernel, bs, aux, sends),
        in_specs=[smem, smem, vmem] + [any_spec] * (1 + PARTS),
        out_specs=[vmem] * (1 + sends),
        out_shape=[jax.ShapeDtypeStruct((pairs, bs, 2 * bs), jnp.float32)]
        + [jax.ShapeDtypeStruct((pairs, bs, 2 * bs), jnp.bfloat16)] * sends,
        scratch_shapes=[
            pltpu.VMEM((aux * bs, width), jnp.bfloat16),
            pltpu.VMEM((bs, aux, width), jnp.bfloat16),
            pltpu.VMEM((aux * bs, width), jnp.bfloat16),
            pltpu.VMEM((2, aux * bs, 2 * bs), jnp.float32),
            pltpu.VMEM((2, aux * bs, 2 * bs), jnp.float32),
            pltpu.SemaphoreType.DMA((chunks,)),
            pltpu.SemaphoreType.DMA((chunks,)),
        ]
        + [acc] * (2 if blocks <= 128 else 1),
        compiler_params=pltpu.CompilerParams(vmem_limit_bytes=VMEM),
        cost_estimate=pl.CostEstimate(
            flops=2 * (aux * bs) ** 2 * width * 2, bytes_accessed=4 * aux * bs * width, transcendentals=0
        ),
    )(ids, targets, table, integrals, *d_parts)


def gather_rounds(bits):
    rounds = []
    while bits:
        step = min(2, bits)
        bits -= step
        rounds.append((bits, step))
    return rounds


def sum_rounds(bits):
    rounds, at = [], 0
    while at < bits:
        step = 1 if at < 2 else min(2, bits - at)
        rounds.append((at, step))
        at += step
    return rounds


def local(orb, three_centre, green_occ, green_virt, pair_atoms, basis_count, chi_target):
    bs = three_centre.shape[1]
    bits = orb.bit_length() - 1
    me = lax.axis_index("orb")

    def exchange(value, flip):
        return lax.ppermute(value, "orb", [(i, i ^ flip) for i in range(orb)])

    table = packed(basis_count, green_occ, green_virt, bs)
    ids = jnp.zeros_like(pair_atoms[0])
    rel = pair_atoms[0] ^ me
    count = 1
    for shift, step in gather_rounds(bits):
        table = jnp.concatenate([table] + [exchange(table, v << shift) for v in range(1, 1 << step)], axis=0)
        ids = ids + ((rel >> shift) & ((1 << step) - 1)) * count
        count <<= step

    targets = chi_target[0]
    rel = (targets // CB_DEV) ^ me
    place = jnp.zeros_like(targets)
    for shift, step in sum_rounds(bits):
        place = (place << step) | ((rel >> shift) & ((1 << step) - 1))
    place = place * CB_DEV + targets % CB_DEV

    d_parts = [relayout(three_centre[0], i) for i in range(PARTS)]
    rounds = sum_rounds(bits)
    total, *sends = chi_blocks_of(ids, place, table, three_centre[0], d_parts, orb * CB_DEV, (1 << rounds[0][1]) - 1)
    for k, (shift, step) in enumerate(rounds):
        if k:
            rest = total.shape[0] >> step
            sends = [total[v * rest:(v + 1) * rest].astype(jnp.bfloat16) for v in range(1, 1 << step)]
            total = total[:rest]
        for v, send in enumerate(sends):
            total = total + exchange(send, (v + 1) << shift).astype(jnp.float32)
    total = total.reshape(CB_DEV // 2, bs, 2, bs).transpose(0, 2, 1, 3)
    return total.reshape(CB_DEV, bs * bs)


def solution(mesh):
    in_specs = (
        P("orb", None, None, None),
        P(("grp", "orb"), None),
        P(("grp", "orb"), None),
        P("orb", None),
        P("orb"),
        P("orb", None),
    )
    out_specs = P(("grp", "orb"), None)
    return jax.shard_map(
        functools.partial(local, mesh.shape["orb"]), mesh=mesh, in_specs=in_specs, out_specs=out_specs, check_vma=False
    )
```

time: 92.4 us -> 80.3 us (0.87)
  local copies, waits for them, and re-layouts: 19.3 us -> 2.44 us
  Pallas kernels: 39.7 us -> 46.7 us
  waiting for transfers between devices: 18.2 us -> 14.2 us
  starting transfers between devices: 10.1 us -> 13.5 us
  other arithmetic: 3.9 us -> 2.25 us
    unnamed x29 -> x14, local copies, waits for them, and re-layouts: 18.2 us -> 1.52 us
    pallas_call x4, Pallas kernels: 8.45 us -> 18.6 us  [relayout(): pl.pallas_call(relayout_kernel, grid=(steps,), in_specs=[pl.BlockSpec((LA...]
    ppermute x8 -> x11, waiting for transfers between devices: 18.2 us -> 14.2 us  [exchange(): return lax.ppermute(value, 'orb', [(i, i ^ flip) for i in range(orb)])]
    ppermute x8 -> x11, starting transfers between devices: 10.1 us -> 13.5 us  [exchange(): return lax.ppermute(value, 'orb', [(i, i ^ flip) for i in range(orb)])]
    pallas_call x1 -> x2, Pallas kernels: 31.3 us -> 28.1 us  [the longest x1 26.7 us: chi_blocks_of(): pl.pallas_call(functools.partial(chi_kernel, bs, aux, sends), in_specs=[s...]
    unnamed x3 -> x0, other arithmetic: 1.63 us -> none
    add x6 -> x4, other arithmetic: 2.23 us -> 2.2 us  [the longest x2 1.13 us: local(): total = total + exchange(send, v + 1 << shift).astype(jnp.float32)]
  transfers between devices with their start and end apart: 8 -> 11, of which waited for: 6 -> 6; matrix products, arithmetic and copies ran while one was open for 1% -> 2% of each run, Pallas kernels for 9% -> 23%
where the time goes in v2:
time: 80.3 us; the launch traced here: 79.8 us
  Pallas kernels  46.7 us (58%)
  waiting for transfers between devices  14.2 us (18%)
  starting transfers between devices  13.5 us (17%)
  local copies, waits for them, and re-layouts  2.44 us (3%)
  other arithmetic  2.25 us (3%)
    pallas_call x1, Pallas kernels, chi_blocks_of(): pl.pallas_call(functools.partial(chi_kernel, bs, aux, sends), in_specs=[s...  26.7 us
    pallas_call x4, Pallas kernels, relayout(): pl.pallas_call(relayout_kernel, grid=(steps,), in_specs=[pl.BlockSpec((LA...  18.6 us
    ppermute x11, waiting for transfers between devices, exchange(): return lax.ppermute(value, 'orb', [(i, i ^ flip) for i in range(orb)])  14.2 us
    ppermute x11, starting transfers between devices, exchange(): return lax.ppermute(value, 'orb', [(i, i ^ flip) for i in range(orb)])  13.5 us
  transfers between devices with their start and end apart: 11, of which 6 were waited for; matrix products, arithmetic and copies ran while one was open for 2% of the time, Pallas kernels for 23%

profile of v2, /device:TPU:0, one launch (start us, length us, event | category | flops | bytes accessed | tf_op | source)
XLA Modules:
  0.0 79.8 jit_solution(15056511293142901234)
XLA Ops:
  0.7 1.4 %shard_map.64 = bf16[1,64,128]{2,1,0:T(8,128)(2,1)} custom-call(s32[1]{0:T(128)S(6)} %copy.14.count_ref, bf16[1,4096]{1,0:T(2,128)(2,1)} %occ_ref.1, bf16[1,4096]{1,0:T(2,128)(2,1)} %virt_ref.1), custom_call_target="tpu_custom_call" | custom-call | tf_op jit(solution)/shard_map/pallas_call | solution.py:32
  2.0 5.0 %collective-permute-start.2 = (bf16[1,64,128]{2,1,0:T(8,128)(2,1)}, bf16[1,64,128]{2,1,0:T(8,128)(2,1)S(1)}, u32[]{:S(2)}, u32[]{:S(2)}) collective-permute-start(bf16[1,64,128]{2,1,0:T(8,128)(2,1)} %shard_map.64), channel_id=1, source_target_pairs={{0,12},{1,13},{2,14},{3,15},{4,8},{5,9},{6,10},{7,11},{8,4},{9,5},... | collective-permute-start | bytes 49160 | tf_op jit(solution)/shard_map/ppermute | solution.py:257
  7.1 0.0 collective-permute-start.1
  7.1 0.6 collective-permute-start
  7.6 0.8 constant_dynamic-update-slice_fusion.6
  8.4 4.6 %shard_map.68.refs_3_ = bf16[1024,1024]{1,0:T(8,128)(2,1)} custom-call(bf16[64,16,4096]{2,1,0:T(8,128)(2,1)} %bitcast.7), custom_call_target="tpu_custom_call" | custom-call | flops 536870912 | bytes 4194304 | tf_op jit(solution)/shard_map/pallas_call | solution.py:62
  13.0 4.7 %shard_map.67.refs_2_ = bf16[1024,1024]{1,0:T(8,128)(2,1)} custom-call(bf16[64,16,4096]{2,1,0:T(8,128)(2,1)} %bitcast.8), custom_call_target="tpu_custom_call" | custom-call | flops 536870912 | bytes 4194304 | tf_op jit(solution)/shard_map/pallas_call | solution.py:62
  17.7 0.0 copy-start.3
  17.7 0.0 copy-start.2
  17.7 4.6 %shard_map.66.refs_1_ = bf16[1024,1024]{1,0:T(8,128)(2,1)} custom-call(bf16[64,16,4096]{2,1,0:T(8,128)(2,1)} %bitcast.9), custom_call_target="tpu_custom_call" | custom-call | flops 536870912 | bytes 4194304 | tf_op jit(solution)/shard_map/pallas_call | solution.py:62
  22.3 0.0 copy-done.3
  22.3 0.5 add_bitcast_fusion.ids_ref
  22.8 0.0 copy-done.2
  22.8 0.6 fusion.2.tgt_ref
  23.4 0.0 copy-start
  23.4 4.7 %shard_map.65.refs_0_ = bf16[1024,1024]{1,0:T(8,128)(2,1)} custom-call(bf16[64,16,4096]{2,1,0:T(8,128)(2,1)} %bitcast.10), custom_call_target="tpu_custom_call" | custom-call | flops 536870912 | bytes 4194304 | tf_op jit(solution)/shard_map/pallas_call | solution.py:62
  28.1 0.0 collective-permute-done.2
  28.1 0.0 collective-permute-done.1
  28.1 0.0 collective-permute-done
  28.1 0.0 copy-done
  28.1 0.5 collective-permute-start.5
  28.6 1.4 %collective-permute-start.4 = (bf16[4,64,128]{2,1,0:T(8,128)(2,1)S(1)}, bf16[4,64,128]{2,1,0:T(8,128)(2,1)S(1)}, u32[]{:S(2)}, u32[]{:S(2)}) collective-permute-start(bf16[4,64,128]{2,1,0:T(8,128)(2,1)S(1)} %pad_maximum_fusion), channel_id=1, source_target_pairs={{0,2},{1,3},{2,0},{3,1},{4,6},{5,7},{6,4},{7,5},{8,10},{9,11},{10,... | collective-permute-start | bytes 196616 | tf_op jit(solution)/shard_map/ppermute | solution.py:257
  30.0 0.1 collective-permute-start.3
  30.1 1.2 %collective-permute-done.3 = bf16[4,64,128]{2,1,0:T(8,128)(2,1)S(1)} collective-permute-done((bf16[4,64,128]{2,1,0:T(8,128)(2,1)S(1)}, bf16[4,64,128]{2,1,0:T(8,128)(2,1)S(1)}, u32[]{:S(2)}, u32[]{:S(2)}) %collective-permute-start.3) | collective-permute-done | bytes 65568 | tf_op jit(solution)/shard_map/ppermute | solution.py:257
  31.3 2.6 %collective-permute-done.4 = bf16[4,64,128]{2,1,0:T(8,128)(2,1)S(1)} collective-permute-done((bf16[4,64,128]{2,1,0:T(8,128)(2,1)S(1)}, bf16[4,64,128]{2,1,0:T(8,128)(2,1)S(1)}, u32[]{:S(2)}, u32[]{:S(2)}) %collective-permute-start.4) | collective-permute-done | bytes 65568 | tf_op jit(solution)/shard_map/ppermute | solution.py:257
  33.9 0.0 collective-permute-done.5
  33.9 0.0 copy-start.1
  33.9 0.7 copy-done.1
  34.6 26.7 %shard_map.69 = (f32[16,64,128]{2,1,0:T(8,128)}, bf16[16,64,128]{2,1,0:T(8,128)(2,1)}) custom-call(s32[2]{0:T(128)} %add_bitcast_fusion.ids_ref, s32[256]{0:T(256)} %fusion.2.tgt_ref, bf16[16,64,128]{2,1,0:T(8,128)(2,1)} %copy-done.1, bf16[64,16,4096]{2,1,0:T(8,128)(2,1)} %bitcast.11, bf16[1024,1024]{1,0:T(8,128)(2,1)} %shard_map.65.refs_0_, ...), custom_call_target="tpu_custom_call" | custom-call | flops 17179869184 | bytes 16777216 | tf_op jit(solution)/shard_map/pallas_call | solution.py:210
  61.3 0.2 collective-permute-start.6
  61.5 1.6 %collective-permute-done.6 = bf16[16,64,128]{2,1,0:T(8,128)(2,1)S(1)} collective-permute-done((bf16[16,64,128]{2,1,0:T(8,128)(2,1)}, bf16[16,64,128]{2,1,0:T(8,128)(2,1)S(1)}, u32[]{:S(2)}, u32[]{:S(2)}) %collective-permute-start.6) | collective-permute-done | bytes 262176 | tf_op jit(solution)/shard_map/ppermute | solution.py:257
  63.1 1.1 %convert_add_fusion = f32[16,64,128]{2,1,0:T(8,128)S(1)} fusion(f32[16,64,128]{2,1,0:T(8,128)} %get-tuple-element.7, bf16[16,64,128]{2,1,0:T(8,128)(2,1)S(1)} %collective-permute-done.6), kind=kLoop, calls=%fused_computation | loop fusion | flops 262144 | bytes 1310720 | tf_op jit(solution)/shard_map/add | solution.py:284
  64.3 1.1 %collective-permute-start.7 = (bf16[8,64,128]{2,1,0:T(8,128)(2,1)S(1)}, bf16[8,64,128]{2,1,0:T(8,128)(2,1)S(1)}, u32[]{:S(2)}, u32[]{:S(2)}) collective-permute-start(bf16[8,64,128]{2,1,0:T(8,128)(2,1)S(1)} %slice.41), channel_id=1, source_target_pairs={{0,2},{1,3},{2,0},{3,1},{4,6},{5,7},{6,4},{7,5},{8,10},{9,11},{10,... | collective-permute-start | bytes 393224 | tf_op jit(solution)/shard_map/ppermute | solution.py:257
  65.4 4.5 %collective-permute-done.7 = bf16[8,64,128]{2,1,0:T(8,128)(2,1)S(1)} collective-permute-done((bf16[8,64,128]{2,1,0:T(8,128)(2,1)S(1)}, bf16[8,64,128]{2,1,0:T(8,128)(2,1)S(1)}, u32[]{:S(2)}, u32[]{:S(2)}) %collective-permute-start.7) | collective-permute-done | bytes 131104 | tf_op jit(solution)/shard_map/ppermute | solution.py:257
  69.9 1.7 %collective-permute-start.8 = (bf16[2,64,128]{2,1,0:T(8,128)(2,1)S(1)}, bf16[2,64,128]{2,1,0:T(8,128)(2,1)S(1)}, u32[]{:S(2)}, u32[]{:S(2)}) collective-permute-start(bf16[2,64,128]{2,1,0:T(8,128)(2,1)S(1)} %get-tuple-element.11), channel_id=1, source_target_pairs={{0,4},{1,5},{2,6},{3,7},{4,0},{5,1},{6,2},{7,3},{8,12},{9,13},{10,... | collective-permute-start | bytes 98312 | tf_op jit(solution)/shard_map/ppermute | solution.py:257
  71.6 2.4 %collective-permute-start.10 = (bf16[2,64,128]{2,1,0:T(8,128)(2,1)S(1)}, bf16[2,64,128]{2,1,0:T(8,128)(2,1)S(1)}, u32[]{:S(2)}, u32[]{:S(2)}) collective-permute-start(bf16[2,64,128]{2,1,0:T(8,128)(2,1)S(1)} %get-tuple-element.12), channel_id=1, source_target_pairs={{0,12},{1,13},{2,14},{3,15},{4,8},{5,9},{6,10},{7,11},{8,4},{9,5},... | collective-permute-start | bytes 98312 | tf_op jit(solution)/shard_map/ppermute | solution.py:257
  74.0 0.5 collective-permute-start.9
  74.5 0.0 collective-permute-done.8
  74.5 3.0 %collective-permute-done.10 = bf16[2,64,128]{2,1,0:T(8,128)(2,1)S(1)} collective-permute-done((bf16[2,64,128]{2,1,0:T(8,128)(2,1)S(1)}, bf16[2,64,128]{2,1,0:T(8,128)(2,1)S(1)}, u32[]{:S(2)}, u32[]{:S(2)}) %collective-permute-start.10) | collective-permute-done | bytes 32800 | tf_op jit(solution)/shard_map/ppermute | solution.py:257
  77.6 1.3 %collective-permute-done.9 = bf16[2,64,128]{2,1,0:T(8,128)(2,1)S(1)} collective-permute-done((bf16[2,64,128]{2,1,0:T(8,128)(2,1)S(1)}, bf16[2,64,128]{2,1,0:T(8,128)(2,1)S(1)}, u32[]{:S(2)}, u32[]{:S(2)}) %collective-permute-start.9) | collective-permute-done | bytes 32800 | tf_op jit(solution)/shard_map/ppermute | solution.py:257
  78.9 0.1 reshape.18
  79.0 0.7 reshape.19
  (12 shorter events, 0.2 us)
Async XLA Ops:
  2.0 26.0 %collective-permute-start.2 = (bf16[1,64,128]{2,1,0:T(8,128)(2,1)}, bf16[1,64,128]{2,1,0:T(8,128)(2,1)S(1)}, u32[]{:S(2)}, u32[]{:S(2)}) collective-permute-start(bf16[1,64,128]{2,1,0:T(8,128)(2,1)} %shard_map.64), channel_id=1, source_target_pairs={{0,12},{1,13},{2,14},{3,15},{4,8},{5,9},{6,10},{7,11},{8,4},{9,5},... | collective-permute-start | bytes 49160 | tf_op jit(solution)/shard_map/ppermute | solution.py:257
  7.1 21.0 %collective-permute-start.1 = (bf16[1,64,128]{2,1,0:T(8,128)(2,1)}, bf16[1,64,128]{2,1,0:T(8,128)(2,1)S(1)}, u32[]{:S(2)}, u32[]{:S(2)}) collective-permute-start(bf16[1,64,128]{2,1,0:T(8,128)(2,1)} %shard_map.64), channel_id=1, source_target_pairs={{0,8},{1,9},{2,10},{3,11},{4,12},{5,13},{6,14},{7,15},{8,0},{9,1},... | collective-permute-start | bytes 49160 | tf_op jit(solution)/shard_map/ppermute | solution.py:257
  7.1 21.0 %collective-permute-start = (bf16[1,64,128]{2,1,0:T(8,128)(2,1)}, bf16[1,64,128]{2,1,0:T(8,128)(2,1)S(1)}, u32[]{:S(2)}, u32[]{:S(2)}) collective-permute-start(bf16[1,64,128]{2,1,0:T(8,128)(2,1)} %shard_map.64), channel_id=1, source_target_pairs={{0,4},{1,5},{2,6},{3,7},{4,0},{5,1},{6,2},{7,3},{8,12},{9,13},{10,... | collective-permute-start | bytes 49160 | tf_op jit(solution)/shard_map/ppermute | solution.py:257
  17.7 4.6 %copy-start.3 = (s32[1,2]{1,0:T(1,128)S(1)}, s32[1,2]{1,0:T(1,128)}, u32[]{:S(2)}) copy-start(s32[1,2]{1,0:T(1,128)} %param.9) | copy-start | bytes 28
  17.7 5.1 %copy-start.2 = (s32[1,256]{1,0:T(1,128)S(1)}, s32[1,256]{1,0:T(1,128)}, u32[]{:S(2)}) copy-start(s32[1,256]{1,0:T(1,128)} %param.11) | copy-start | bytes 3076
  23.4 4.7 %copy-start = (bf16[1,64,128]{2,1,0:T(8,128)(2,1)S(1)}, bf16[1,64,128]{2,1,0:T(8,128)(2,1)}, u32[]{:S(2)}) copy-start(bf16[1,64,128]{2,1,0:T(8,128)(2,1)} %shard_map.64) | copy-start | bytes 49156
  28.1 5.8 %collective-permute-start.5 = (bf16[4,64,128]{2,1,0:T(8,128)(2,1)S(1)}, bf16[4,64,128]{2,1,0:T(8,128)(2,1)S(1)}, u32[]{:S(2)}, u32[]{:S(2)}) collective-permute-start(bf16[4,64,128]{2,1,0:T(8,128)(2,1)S(1)} %pad_maximum_fusion), channel_id=1, source_target_pairs={{0,3},{1,2},{2,1},{3,0},{4,7},{5,6},{6,5},{7,4},{8,11},{9,10},{10,... | collective-permute-start | bytes 196616 | tf_op jit(solution)/shard_map/ppermute | solution.py:257
  28.6 5.3 %collective-permute-start.4 = (bf16[4,64,128]{2,1,0:T(8,128)(2,1)S(1)}, bf16[4,64,128]{2,1,0:T(8,128)(2,1)S(1)}, u32[]{:S(2)}, u32[]{:S(2)}) collective-permute-start(bf16[4,64,128]{2,1,0:T(8,128)(2,1)S(1)} %pad_maximum_fusion), channel_id=1, source_target_pairs={{0,2},{1,3},{2,0},{3,1},{4,6},{5,7},{6,4},{7,5},{8,10},{9,11},{10,... | collective-permute-start | bytes 196616 | tf_op jit(solution)/shard_map/ppermute | solution.py:257
  30.0 1.3 %collective-permute-start.3 = (bf16[4,64,128]{2,1,0:T(8,128)(2,1)S(1)}, bf16[4,64,128]{2,1,0:T(8,128)(2,1)S(1)}, u32[]{:S(2)}, u32[]{:S(2)}) collective-permute-start(bf16[4,64,128]{2,1,0:T(8,128)(2,1)S(1)} %pad_maximum_fusion), channel_id=1, source_target_pairs={{0,1},{1,0},{2,3},{3,2},{4,5},{5,4},{6,7},{7,6},{8,9},{9,8},{10,11... | collective-permute-start | bytes 196616 | tf_op jit(solution)/shard_map/ppermute | solution.py:257
  33.9 0.7 copy-start.1
  61.3 1.8 %collective-permute-start.6 = (bf16[16,64,128]{2,1,0:T(8,128)(2,1)}, bf16[16,64,128]{2,1,0:T(8,128)(2,1)S(1)}, u32[]{:S(2)}, u32[]{:S(2)}) collective-permute-start(bf16[16,64,128]{2,1,0:T(8,128)(2,1)} %get-tuple-element.8), channel_id=1, source_target_pairs={{0,1},{1,0},{2,3},{3,2},{4,5},{5,4},{6,7},{7,6},{8,9},{9,8},{10,11... | collective-permute-start | bytes 786440 | tf_op jit(solution)/shard_map/ppermute | solution.py:257
  64.3 5.6 %collective-permute-start.7 = (bf16[8,64,128]{2,1,0:T(8,128)(2,1)S(1)}, bf16[8,64,128]{2,1,0:T(8,128)(2,1)S(1)}, u32[]{:S(2)}, u32[]{:S(2)}) collective-permute-start(bf16[8,64,128]{2,1,0:T(8,128)(2,1)S(1)} %slice.41), channel_id=1, source_target_pairs={{0,2},{1,3},{2,0},{3,1},{4,6},{5,7},{6,4},{7,5},{8,10},{9,11},{10,... | collective-permute-start | bytes 393224 | tf_op jit(solution)/shard_map/ppermute | solution.py:257
  69.9 4.6 %collective-permute-start.8 = (bf16[2,64,128]{2,1,0:T(8,128)(2,1)S(1)}, bf16[2,64,128]{2,1,0:T(8,128)(2,1)S(1)}, u32[]{:S(2)}, u32[]{:S(2)}) collective-permute-start(bf16[2,64,128]{2,1,0:T(8,128)(2,1)S(1)} %get-tuple-element.11), channel_id=1, source_target_pairs={{0,4},{1,5},{2,6},{3,7},{4,0},{5,1},{6,2},{7,3},{8,12},{9,13},{10,... | collective-permute-start | bytes 98312 | tf_op jit(solution)/shard_map/ppermute | solution.py:257
  71.6 6.0 %collective-permute-start.10 = (bf16[2,64,128]{2,1,0:T(8,128)(2,1)S(1)}, bf16[2,64,128]{2,1,0:T(8,128)(2,1)S(1)}, u32[]{:S(2)}, u32[]{:S(2)}) collective-permute-start(bf16[2,64,128]{2,1,0:T(8,128)(2,1)S(1)} %get-tuple-element.12), channel_id=1, source_target_pairs={{0,12},{1,13},{2,14},{3,15},{4,8},{5,9},{6,10},{7,11},{8,4},{9,5},... | collective-permute-start | bytes 98312 | tf_op jit(solution)/shard_map/ppermute | solution.py:257
  74.0 4.8 %collective-permute-start.9 = (bf16[2,64,128]{2,1,0:T(8,128)(2,1)S(1)}, bf16[2,64,128]{2,1,0:T(8,128)(2,1)S(1)}, u32[]{:S(2)}, u32[]{:S(2)}) collective-permute-start(bf16[2,64,128]{2,1,0:T(8,128)(2,1)S(1)} %get-tuple-element.13), channel_id=1, source_target_pairs={{0,8},{1,9},{2,10},{3,11},{4,12},{5,13},{6,14},{7,15},{8,0},{9,1},... | collective-permute-start | bytes 98312 | tf_op jit(solution)/shard_map/ppermute | solution.py:257

commit v3 on v2

v3 whole, which is shorter than its diff:
```python
import functools

import jax
import jax.numpy as jnp
from jax import lax
from jax.experimental import pallas as pl
from jax.experimental.pallas import tpu as pltpu
from jax.sharding import PartitionSpec as P

CB_DEV = 4
LAM = 4
PARTS = 4
GRANT = 8 << 20


def pack_kernel(count_ref, occ_ref, virt_ref, out_ref, rows_ref):
    lanes = out_ref.shape[2]
    half = out_ref.shape[1] // 2
    for i in range(half):
        rows_ref[i:i + 1, :] = occ_ref[:, i * lanes:(i + 1) * lanes].astype(jnp.float32)
        rows_ref[half + i:half + i + 1, :] = virt_ref[:, i * lanes:(i + 1) * lanes].astype(jnp.float32)
    bs = lanes // 2
    row = lax.broadcasted_iota(jnp.int32, rows_ref.shape, 0)
    lane = lax.broadcasted_iota(jnp.int32, rows_ref.shape, 1)
    count = count_ref[0]
    valid = (2 * (row % half) + lane // bs < count) & (lane % bs < count)
    out_ref[0] = jnp.where(valid, rows_ref[...], 0.0).astype(jnp.bfloat16)


def packed(basis_count, green_occ, green_virt, bs):
    vmem = pl.BlockSpec(memory_space=pltpu.VMEM)
    return pl.pallas_call(
        pack_kernel,
        in_specs=[pl.BlockSpec(memory_space=pltpu.SMEM), vmem, vmem],
        out_specs=vmem,
        out_shape=jax.ShapeDtypeStruct((1, bs, 2 * bs), jnp.bfloat16),
        scratch_shapes=[pltpu.VMEM((bs, 2 * bs), jnp.float32)],
    )(basis_count, green_occ, green_virt)


def relayout_kernel(part, b_ref, d_ref):
    bs, aux, _ = b_ref.shape
    wide = LAM * bs
    rows = aux * aux
    row = lax.broadcasted_iota(jnp.int32, (rows, rows), 0)
    col = lax.broadcasted_iota(jnp.int32, (rows, rows), 1)
    perm = (col == (row % aux) * aux + row // aux).astype(jnp.bfloat16)

    @pl.loop(0, bs // PARTS // LAM)
    def _(i):
        first = part * (bs // PARTS) + i * LAM
        cols = pl.ds(pl.multiple_of(i * wide, wide), wide)
        for blk in range(bs // aux):
            pieces = []
            for p in range(aux):
                at = (blk * aux + p) * bs
                pieces.append(jnp.concatenate([b_ref[first + k, :, at:at + bs] for k in range(LAM)], axis=-1))
            stacked = jnp.concatenate(pieces, axis=0)
            moved = jnp.dot(perm, stacked, preferred_element_type=jnp.float32).astype(jnp.bfloat16)
            for a in range(aux):
                d_ref[a * bs + blk * aux:a * bs + (blk + 1) * aux, cols] = moved[a * aux:(a + 1) * aux]


def in_vmem(count):
    return [pl.BlockSpec(memory_space=pltpu.VMEM)] * count


def in_smem(count):
    return [pl.BlockSpec(memory_space=pltpu.SMEM)] * count


def relayout(integrals, part):
    bs, aux, width = integrals.shape
    return pl.pallas_call(
        functools.partial(relayout_kernel, part),
        in_specs=in_vmem(1),
        out_specs=in_vmem(1)[0],
        out_shape=jax.ShapeDtypeStruct((aux * bs, bs // PARTS * bs), jnp.bfloat16),
        compiler_params=pltpu.CompilerParams(vmem_limit_bytes=GRANT),
        cost_estimate=pl.CostEstimate(
            flops=2 * bs * aux * width * 256 // PARTS,
            bytes_accessed=4 * bs * aux * width // PARTS,
            transcendentals=0,
        ),
    )(integrals)


def spread_rows(block, of_row, count, bs):
    shape = (count, bs // 2)
    pick = of_row(lax.broadcasted_iota(jnp.int32, shape, 0)) // 2 == lax.broadcasted_iota(jnp.int32, shape, 1)
    got = jnp.dot(pick.astype(jnp.bfloat16), block, preferred_element_type=jnp.float32)
    odd = of_row(lax.broadcasted_iota(jnp.int32, (count, bs), 0)) % 2 == 1
    return jnp.where(odd, got[:, bs:], got[:, :bs])


def virt_kernel(bs, ids_ref, table_ref, *refs):
    d_parts, v_ref = refs[:PARTS], refs[PARTS]
    wide = LAM * bs
    spread = spread_rows(table_ref[ids_ref[1], bs // 2:], lambda i: i % bs, wide, bs)
    spread = jnp.concatenate([spread] * LAM, axis=1)
    same = (
        lax.broadcasted_iota(jnp.int32, (wide, wide), 0) // bs == lax.broadcasted_iota(jnp.int32, (wide, wide), 1) // bs
    )
    virt_w = jnp.where(same, spread, 0.0).astype(jnp.bfloat16)
    each = d_parts[0].shape[1]
    for part in range(PARTS):
        for at in range(0, each, wide):
            got = jnp.dot(d_parts[part][:, at:at + wide], virt_w, preferred_element_type=jnp.float32)
            v_ref[:, part * each + at:part * each + at + wide] = got.astype(jnp.bfloat16)


def occ_kernel(ids_ref, table_ref, b_ref, o_ref):
    bs, aux, width = b_ref.shape
    half = aux // 2
    wide = LAM * bs
    lanes = 2 * bs
    tall = bs * half
    rep_t = (
        lax.broadcasted_iota(jnp.int32, (bs, tall), 1) // half == lax.broadcasted_iota(jnp.int32, (bs, tall), 0)
    ).astype(jnp.bfloat16)
    spread = spread_rows(table_ref[ids_ref[0], :bs // 2], lambda i: i // half, tall, bs).astype(jnp.bfloat16)
    spread = jnp.dot(spread, rep_t, preferred_element_type=jnp.float32)
    same = (
        lax.broadcasted_iota(jnp.int32, (tall, tall), 0) % half
        == lax.broadcasted_iota(jnp.int32, (tall, tall), 1) % half
    )
    occ_w = jnp.where(same, spread, 0.0).astype(jnp.bfloat16)

    @pl.loop(0, width // wide, unroll=2)
    def _(j):
        cols = pl.ds(pl.multiple_of(j * wide, wide), wide)
        block = b_ref[:, :, cols].astype(jnp.float32)
        sides = []
        for h in range(2):
            side = block[:, h * half:(h + 1) * half, :].reshape(tall, wide).astype(jnp.bfloat16)
            got = jnp.dot(occ_w, side, preferred_element_type=jnp.float32)
            sides.append(got.reshape(bs, half, wide))
        both = jnp.concatenate(sides, axis=1).astype(jnp.bfloat16)
        for p in range(LAM):
            rows = pl.ds(pl.multiple_of(j * (LAM * aux) + p * aux, aux), aux)
            for q in range(bs // 2):
                o_ref[rows, q * lanes:(q + 1) * lanes] = jnp.concatenate(
                    [both[2 * q, :, p * bs:(p + 1) * bs], both[2 * q + 1, :, p * bs:(p + 1) * bs]], axis=-1
                )


def chi_kernel(bs, sends, tgt_ref, o_ref, v_ref, *refs):
    keep_ref, send_refs, refs = refs[0], refs[1:1 + sends], refs[1 + sends:]
    out0, out1, *accs = refs
    low_acc, high_acc = accs[0], accs[-1]
    aux = o_ref.shape[0] // bs
    lanes = 2 * bs
    for ref in accs:
        ref[...] = jnp.zeros_like(ref)
    low = lax.broadcasted_iota(jnp.int32, (bs, lanes), 1) < bs
    shared = len(accs) == 1
    outs = (out0, out1)
    group = 4 * bs

    def scatter(n):
        for a in range(aux):
            for t in range(2):
                value = outs[n % 2][t, pl.ds(a, bs, stride=aux), :]
                first = tgt_ref[a * aux + n * 4 + 2 * t]
                second = tgt_ref[a * aux + n * 4 + 2 * t + 1]
                low_acc[first] += jnp.where(low, value, 0.0) if shared else value
                high_acc[second] += jnp.where(low, 0.0, value) if shared else value

    for n in range(aux // 4):
        if n:
            scatter(n - 1)
        got = lax.dot_general(
            o_ref[...],
            v_ref[n * group:(n + 1) * group, :],
            (((1,), (1,)), ((), ())),
            preferred_element_type=jnp.float32,
        )
        for t in range(2):
            outs[n % 2][t] = got[:, t * lanes:(t + 1) * lanes]
    scatter(aux // 4 - 1)

    pairs = keep_ref.shape[0]

    def joined(i):
        if shared:
            one, two = low_acc[2 * i], low_acc[2 * i + 1]
            return jnp.where(low, one, two) + pltpu.roll(jnp.where(low, two, one), bs, 1)
        left = jnp.where(low, low_acc[2 * i], high_acc[2 * i + 1])
        right = jnp.where(low, low_acc[2 * i + 1], high_acc[2 * i])
        return left + pltpu.roll(right, bs, 1)

    @pl.loop(0, pairs)
    def _(i):
        keep_ref[i] = joined(i)
        for k, send_ref in enumerate(send_refs):
            send_ref[i] = joined((k + 1) * pairs + i).astype(jnp.bfloat16)


def chi_blocks_of(ids, targets, table, integrals, d_parts, blocks, sends):
    bs, aux, width = integrals.shape
    pairs = blocks // 2 // (sends + 1)
    side = jax.ShapeDtypeStruct((aux * bs, width), jnp.bfloat16)
    params = pltpu.CompilerParams(vmem_limit_bytes=GRANT)
    cost = pl.CostEstimate(flops=2 * (aux * bs) ** 2 * width, bytes_accessed=4 * aux * bs * width, transcendentals=0)
    virt_side = pl.pallas_call(
        functools.partial(virt_kernel, bs),
        in_specs=in_smem(1) + in_vmem(1 + PARTS),
        out_specs=in_vmem(1)[0],
        out_shape=side,
        compiler_params=params,
        cost_estimate=cost,
    )(ids, table, *d_parts)
    occ_side = pl.pallas_call(
        occ_kernel,
        in_specs=in_smem(1) + in_vmem(2),
        out_specs=in_vmem(1)[0],
        out_shape=side,
        compiler_params=params,
        cost_estimate=cost,
    )(ids, table, integrals)
    accs = 2 if blocks <= 128 else 1
    acc = pltpu.VMEM((blocks, bs, 2 * bs), jnp.float32)
    out = pltpu.VMEM((2, aux * bs, 2 * bs), jnp.float32)
    return pl.pallas_call(
        functools.partial(chi_kernel, bs, sends),
        in_specs=in_smem(1) + in_vmem(2),
        out_specs=in_vmem(1 + sends),
        out_shape=[jax.ShapeDtypeStruct((pairs, bs, 2 * bs), jnp.float32)]
        + [jax.ShapeDtypeStruct((pairs, bs, 2 * bs), jnp.bfloat16)] * sends,
        scratch_shapes=[out, out] + [acc] * accs,
        compiler_params=pltpu.CompilerParams(vmem_limit_bytes=GRANT + 4 * (accs * blocks + 2 * aux * 2) * bs * 2 * bs),
        cost_estimate=cost,
    )(targets, occ_side, virt_side)


def gather_rounds(bits):
    rounds = []
    while bits:
        step = min(2, bits)
        bits -= step
        rounds.append((bits, step))
    return rounds


def sum_rounds(bits):
    rounds, at = [], 0
    while at < bits:
        step = 1 if at < 2 else min(2, bits - at)
        rounds.append((at, step))
        at += step
    return rounds


def local(orb, three_centre, green_occ, green_virt, pair_atoms, basis_count, chi_target):
    bs = three_centre.shape[1]
    bits = orb.bit_length() - 1
    me = lax.axis_index("orb")

    def exchange(value, flip):
        return lax.ppermute(value, "orb", [(i, i ^ flip) for i in range(orb)])

    table = packed(basis_count, green_occ, green_virt, bs)
    ids = jnp.zeros_like(pair_atoms[0])
    rel = pair_atoms[0] ^ me
    count = 1
    for shift, step in gather_rounds(bits):
        table = jnp.concatenate([table] + [exchange(table, v << shift) for v in range(1, 1 << step)], axis=0)
        ids = ids + ((rel >> shift) & ((1 << step) - 1)) * count
        count <<= step

    targets = chi_target[0]
    rel = (targets // CB_DEV) ^ me
    place = jnp.zeros_like(targets)
    for shift, step in sum_rounds(bits):
        place = (place << step) | ((rel >> shift) & ((1 << step) - 1))
    place = place * CB_DEV + targets % CB_DEV

    d_parts = [relayout(three_centre[0], i) for i in range(PARTS)]
    rounds = sum_rounds(bits)
    total, *sends = chi_blocks_of(ids, place, table, three_centre[0], d_parts, orb * CB_DEV, (1 << rounds[0][1]) - 1)
    for k, (shift, step) in enumerate(rounds):
        if k:
            rest = total.shape[0] >> step
            sends = [total[v * rest:(v + 1) * rest].astype(jnp.bfloat16) for v in range(1, 1 << step)]
            total = total[:rest]
        for v, send in enumerate(sends):
            total = total + exchange(send, (v + 1) << shift).astype(jnp.float32)
    total = total.reshape(CB_DEV // 2, bs, 2, bs).transpose(0, 2, 1, 3)
    return total.reshape(CB_DEV, bs * bs)


def solution(mesh):
    in_specs = (
        P("orb", None, None, None),
        P(("grp", "orb"), None),
        P(("grp", "orb"), None),
        P("orb", None),
        P("orb"),
        P("orb", None),
    )
    out_specs = P(("grp", "orb"), None)
    return jax.shard_map(
        functools.partial(local, mesh.shape["orb"]), mesh=mesh, in_specs=in_specs, out_specs=out_specs, check_vma=False
    )
```

time: 80.3 us -> 76 us (0.946)
  Pallas kernels: 46.7 us -> 32.6 us
  local copies, waits for them, and re-layouts: 2.44 us -> 14.5 us
  other arithmetic: 2.25 us -> 0.15 us
    pallas_call x5 -> x7, Pallas kernels: 45.3 us -> 31.3 us  [the longest x1 12.7 us: chi_blocks_of(): pl.pallas_call(functools.partial(chi_kernel, bs, sends), in_specs=in_smem...]
    unnamed x14 -> x26, local copies, waits for them, and re-layouts: 1.52 us -> 13.6 us
    add x2, other arithmetic: 1.13 us -> 0.07 us  [local(): total = total + exchange(send, v + 1 << shift).astype(jnp.float32)]
  transfers between devices with their start and end apart: 11 -> 11, of which waited for: 6 -> 6; matrix products, arithmetic and copies ran while one was open for 2% -> 1% of each run, Pallas kernels for 23% -> 9%
where the time goes in v3:
time: 76 us; the launch traced here: 75.5 us
  Pallas kernels  32.6 us (43%)
  local copies, waits for them, and re-layouts  14.5 us (19%)
  waiting for transfers between devices  14.1 us (19%)
  starting transfers between devices  13.3 us (18%)
  between operations  0.87 us (1%)
    ppermute x11, waiting for transfers between devices, exchange(): return lax.ppermute(value, 'orb', [(i, i ^ flip) for i in range(orb)])  14.1 us
    unnamed x26, local copies, waits for them, and re-layouts  13.6 us
    ppermute x11, starting transfers between devices, exchange(): return lax.ppermute(value, 'orb', [(i, i ^ flip) for i in range(orb)])  13.3 us
    pallas_call x1, Pallas kernels, chi_blocks_of(): pl.pallas_call(functools.partial(chi_kernel, bs, sends), in_specs=in_smem...  12.7 us
    pallas_call x1, Pallas kernels, chi_blocks_of(): pl.pallas_call(occ_kernel, in_specs=in_smem(1) + in_vmem(2), out_specs=in...  8.66 us
    pallas_call x4, Pallas kernels, relayout(): pl.pallas_call(functools.partial(relayout_kernel, part), in_specs=in_vmem...  6.76 us
    pallas_call x1, Pallas kernels, chi_blocks_of(): pl.pallas_call(functools.partial(virt_kernel, bs), in_specs=in_smem(1) +...  3.17 us
  transfers between devices with their start and end apart: 11, of which 6 were waited for; matrix products, arithmetic and copies ran while one was open for 1% of the time, Pallas kernels for 9%

profile of v3, /device:TPU:0, one launch (start us, length us, event | category | flops | bytes accessed | tf_op | source)
XLA Modules:
  0.0 75.5 jit_solution(11731126738860239631)
XLA Ops:
  0.7 1.4 %shard_map.64 = bf16[1,64,128]{2,1,0:T(8,128)(2,1)} custom-call(s32[1]{0:T(128)S(6)} %copy.14.count_ref, bf16[1,4096]{1,0:T(2,128)(2,1)} %occ_ref.1, bf16[1,4096]{1,0:T(2,128)(2,1)} %virt_ref.1), custom_call_target="tpu_custom_call" | custom-call | tf_op jit(solution)/shard_map/pallas_call | solution.py:32
  2.0 5.0 %collective-permute-start.2 = (bf16[1,64,128]{2,1,0:T(8,128)(2,1)}, bf16[1,64,128]{2,1,0:T(8,128)(2,1)S(1)}, u32[]{:S(2)}, u32[]{:S(2)}) collective-permute-start(bf16[1,64,128]{2,1,0:T(8,128)(2,1)} %shard_map.64), channel_id=1, source_target_pairs={{0,12},{1,13},{2,14},{3,15},{4,8},{5,9},{6,10},{7,11},{8,4},{9,5},... | collective-permute-start | bytes 49160 | tf_op jit(solution)/shard_map/ppermute | solution.py:260
  7.1 0.0 collective-permute-start.1
  7.1 0.6 collective-permute-start
  7.6 0.8 constant_dynamic-update-slice_fusion.6
  8.4 3.4 %copy-done = bf16[1,64,16,4096]{3,2,1,0:T(8,128)(2,1)S(1)} copy-done((bf16[1,64,16,4096]{3,2,1,0:T(8,128)(2,1)S(1)}, bf16[1,64,16,4096]{3,2,1,0:T(8,128)(2,1)}, u32[]{:S(2)}) %copy-start) | copy-done | bytes 8388632
  11.8 1.7 %shard_map.69.refs_3_ = bf16[1024,1024]{1,0:T(8,128)(2,1)S(1)} custom-call(bf16[64,16,4096]{2,1,0:T(8,128)(2,1)S(1)} %bitcast.7), custom_call_target="tpu_custom_call" | custom-call | flops 536870912 | bytes 4194304 | tf_op jit(solution)/shard_map/pallas_call | solution.py:74
  13.5 1.7 %shard_map.68.refs_2_ = bf16[1024,1024]{1,0:T(8,128)(2,1)S(1)} custom-call(bf16[64,16,4096]{2,1,0:T(8,128)(2,1)S(1)} %bitcast.8), custom_call_target="tpu_custom_call" | custom-call | flops 536870912 | bytes 4194304 | tf_op jit(solution)/shard_map/pallas_call | solution.py:74
  15.2 0.0 copy-start.3
  15.2 1.3 %copy-done.3 = bf16[1024,1024]{1,0:T(8,128)(2,1)} copy-done((bf16[1024,1024]{1,0:T(8,128)(2,1)}, bf16[1024,1024]{1,0:T(8,128)(2,1)S(1)}, u32[]{:S(2)}) %copy-start.3) | copy-done | bytes 2097176
  16.5 1.7 %shard_map.67.refs_1_ = bf16[1024,1024]{1,0:T(8,128)(2,1)S(1)} custom-call(bf16[64,16,4096]{2,1,0:T(8,128)(2,1)S(1)} %bitcast.9), custom_call_target="tpu_custom_call" | custom-call | flops 536870912 | bytes 4194304 | tf_op jit(solution)/shard_map/pallas_call | solution.py:74
  18.2 0.0 copy-start.5
  18.2 1.3 %copy-done.5 = bf16[1024,1024]{1,0:T(8,128)(2,1)} copy-done((bf16[1024,1024]{1,0:T(8,128)(2,1)}, bf16[1024,1024]{1,0:T(8,128)(2,1)S(1)}, u32[]{:S(2)}) %copy-start.5) | copy-done | bytes 2097176
  19.5 0.0 copy-done.9
  19.5 0.0 copy-done.8
  19.5 0.0 copy-start.1
  19.5 3.4 %copy-done.1 = bf16[1,64,16,4096]{3,2,1,0:T(8,128)(2,1)S(1)} copy-done((bf16[1,64,16,4096]{3,2,1,0:T(8,128)(2,1)S(1)}, bf16[1,64,16,4096]{3,2,1,0:T(8,128)(2,1)}, u32[]{:S(2)}) %copy-start.1) | copy-done | bytes 8388632
  22.9 1.7 %shard_map.66.refs_0_ = bf16[1024,1024]{1,0:T(8,128)(2,1)S(1)} custom-call(bf16[64,16,4096]{2,1,0:T(8,128)(2,1)S(1)} %bitcast.10), custom_call_target="tpu_custom_call" | custom-call | flops 536870912 | bytes 4194304 | tf_op jit(solution)/shard_map/pallas_call | solution.py:74
  24.6 0.0 collective-permute-done.2
  24.6 0.0 collective-permute-done.1
  24.6 0.0 collective-permute-done
  24.7 0.0 copy-done.7
  24.7 0.5 collective-permute-start.5
  25.2 1.4 %collective-permute-start.4 = (bf16[4,64,128]{2,1,0:T(8,128)(2,1)S(1)}, bf16[4,64,128]{2,1,0:T(8,128)(2,1)S(1)}, u32[]{:S(2)}, u32[]{:S(2)}) collective-permute-start(bf16[4,64,128]{2,1,0:T(8,128)(2,1)S(1)} %pad_maximum_fusion), channel_id=1, source_target_pairs={{0,2},{1,3},{2,0},{3,1},{4,6},{5,7},{6,4},{7,5},{8,10},{9,11},{10,... | collective-permute-start | bytes 196616 | tf_op jit(solution)/shard_map/ppermute | solution.py:260
  26.6 0.1 collective-permute-start.3
  26.7 1.2 %collective-permute-done.3 = bf16[4,64,128]{2,1,0:T(8,128)(2,1)S(1)} collective-permute-done((bf16[4,64,128]{2,1,0:T(8,128)(2,1)S(1)}, bf16[4,64,128]{2,1,0:T(8,128)(2,1)S(1)}, u32[]{:S(2)}, u32[]{:S(2)}) %collective-permute-start.3) | collective-permute-done | bytes 65568 | tf_op jit(solution)/shard_map/ppermute | solution.py:260
  27.8 2.6 %collective-permute-done.4 = bf16[4,64,128]{2,1,0:T(8,128)(2,1)S(1)} collective-permute-done((bf16[4,64,128]{2,1,0:T(8,128)(2,1)S(1)}, bf16[4,64,128]{2,1,0:T(8,128)(2,1)S(1)}, u32[]{:S(2)}, u32[]{:S(2)}) %collective-permute-start.4) | collective-permute-done | bytes 65568 | tf_op jit(solution)/shard_map/ppermute | solution.py:260
  30.5 0.0 collective-permute-done.5
  30.5 0.0 copy-start.2
  30.5 3.4 %copy-done.2 = bf16[1,64,16,4096]{3,2,1,0:T(8,128)(2,1)S(1)} copy-done((bf16[1,64,16,4096]{3,2,1,0:T(8,128)(2,1)S(1)}, bf16[1,64,16,4096]{3,2,1,0:T(8,128)(2,1)}, u32[]{:S(2)}) %copy-start.2) | copy-done | bytes 8388632
  33.9 8.7 %shard_map.65.o_ref = bf16[1024,4096]{1,0:T(8,128)(2,1)S(1)} custom-call(s32[2]{0:T(128)S(1)} %add_bitcast_fusion.ids_ref, bf16[16,64,128]{2,1,0:T(8,128)(2,1)S(1)} %constant_dynamic-update-slice_fusion.table_ref, bf16[64,16,4096]{2,1,0:T(8,128)(2,1)S(1)} %bitcast.11), custom_call_target="tpu_custom_call" | custom-call | flops 8589934592 | bytes 16777216 | tf_op jit(solution)/shard_map/pallas_call | solution.py:213
  42.6 0.0 copy-done.4
  42.6 0.0 copy-done.6
  42.6 3.2 %shard_map.70.v_ref = bf16[1024,4096]{1,0:T(8,128)(2,1)S(1)} custom-call(s32[2]{0:T(128)S(1)} %add_bitcast_fusion.ids_ref, bf16[16,64,128]{2,1,0:T(8,128)(2,1)S(1)} %constant_dynamic-update-slice_fusion.table_ref, bf16[1024,1024]{1,0:T(8,128)(2,1)S(1)} %shard_map.66.refs_0_, bf16[1024,1024]{1,0:T(8,128)(2,1)S(1)} %copy-done.6, ...), custom_call_target="tpu_custom_call" | custom-call | flops 8589934592 | bytes 16777216 | tf_op jit(solution)/shard_map/pallas_call | solution.py:205
  45.8 12.7 %shard_map.71 = (f32[16,64,128]{2,1,0:T(8,128)S(1)}, bf16[16,64,128]{2,1,0:T(8,128)(2,1)S(1)}) custom-call(s32[256]{0:T(256)S(1)} %fusion.2.tgt_ref, bf16[1024,4096]{1,0:T(8,128)(2,1)S(1)} %shard_map.65.o_ref, bf16[1024,4096]{1,0:T(8,128)(2,1)S(1)} %shard_map.70.v_ref), custom_call_target="tpu_custom_call" | custom-call | flops 8589934592 | bytes 16777216 | tf_op jit(solution)/shard_map/pallas_call | solution.py:224
  58.4 0.2 collective-permute-start.6
  58.6 1.4 %collective-permute-done.6 = bf16[16,64,128]{2,1,0:T(8,128)(2,1)S(1)} collective-permute-done((bf16[16,64,128]{2,1,0:T(8,128)(2,1)S(1)}, bf16[16,64,128]{2,1,0:T(8,128)(2,1)S(1)}, u32[]{:S(2)}, u32[]{:S(2)}) %collective-permute-start.6) | collective-permute-done | bytes 262176 | tf_op jit(solution)/shard_map/ppermute | solution.py:260
  60.0 0.1 convert_add_fusion
  60.1 1.1 %collective-permute-start.7 = (bf16[8,64,128]{2,1,0:T(8,128)(2,1)S(1)}, bf16[8,64,128]{2,1,0:T(8,128)(2,1)S(1)}, u32[]{:S(2)}, u32[]{:S(2)}) collective-permute-start(bf16[8,64,128]{2,1,0:T(8,128)(2,1)S(1)} %slice.41), channel_id=1, source_target_pairs={{0,2},{1,3},{2,0},{3,1},{4,6},{5,7},{6,4},{7,5},{8,10},{9,11},{10,... | collective-permute-start | bytes 393224 | tf_op jit(solution)/shard_map/ppermute | solution.py:260
  61.2 4.5 %collective-permute-done.7 = bf16[8,64,128]{2,1,0:T(8,128)(2,1)S(1)} collective-permute-done((bf16[8,64,128]{2,1,0:T(8,128)(2,1)S(1)}, bf16[8,64,128]{2,1,0:T(8,128)(2,1)S(1)}, u32[]{:S(2)}, u32[]{:S(2)}) %collective-permute-start.7) | collective-permute-done | bytes 131104 | tf_op jit(solution)/shard_map/ppermute | solution.py:260
  65.8 1.6 %collective-permute-start.8 = (bf16[2,64,128]{2,1,0:T(8,128)(2,1)S(1)}, bf16[2,64,128]{2,1,0:T(8,128)(2,1)S(1)}, u32[]{:S(2)}, u32[]{:S(2)}) collective-permute-start(bf16[2,64,128]{2,1,0:T(8,128)(2,1)S(1)} %get-tuple-element.11), channel_id=1, source_target_pairs={{0,4},{1,5},{2,6},{3,7},{4,0},{5,1},{6,2},{7,3},{8,12},{9,13},{10,... | collective-permute-start | bytes 98312 | tf_op jit(solution)/shard_map/ppermute | solution.py:260
  67.4 2.4 %collective-permute-start.10 = (bf16[2,64,128]{2,1,0:T(8,128)(2,1)S(1)}, bf16[2,64,128]{2,1,0:T(8,128)(2,1)S(1)}, u32[]{:S(2)}, u32[]{:S(2)}) collective-permute-start(bf16[2,64,128]{2,1,0:T(8,128)(2,1)S(1)} %get-tuple-element.12), channel_id=1, source_target_pairs={{0,12},{1,13},{2,14},{3,15},{4,8},{5,9},{6,10},{7,11},{8,4},{9,5},... | collective-permute-start | bytes 98312 | tf_op jit(solution)/shard_map/ppermute | solution.py:260
  69.8 0.5 collective-permute-start.9
  70.3 0.0 collective-permute-done.8
  70.3 3.0 %collective-permute-done.10 = bf16[2,64,128]{2,1,0:T(8,128)(2,1)S(1)} collective-permute-done((bf16[2,64,128]{2,1,0:T(8,128)(2,1)S(1)}, bf16[2,64,128]{2,1,0:T(8,128)(2,1)S(1)}, u32[]{:S(2)}, u32[]{:S(2)}) %collective-permute-start.10) | collective-permute-done | bytes 32800 | tf_op jit(solution)/shard_map/ppermute | solution.py:260
  73.3 1.3 %collective-permute-done.9 = bf16[2,64,128]{2,1,0:T(8,128)(2,1)S(1)} collective-permute-done((bf16[2,64,128]{2,1,0:T(8,128)(2,1)S(1)}, bf16[2,64,128]{2,1,0:T(8,128)(2,1)S(1)}, u32[]{:S(2)}, u32[]{:S(2)}) %collective-permute-start.9) | collective-permute-done | bytes 32800 | tf_op jit(solution)/shard_map/ppermute | solution.py:260
  74.7 0.1 reshape.18
  74.8 0.7 reshape.19
  (20 shorter events, 0.2 us)
Async XLA Ops:
  2.0 22.6 %collective-permute-start.2 = (bf16[1,64,128]{2,1,0:T(8,128)(2,1)}, bf16[1,64,128]{2,1,0:T(8,128)(2,1)S(1)}, u32[]{:S(2)}, u32[]{:S(2)}) collective-permute-start(bf16[1,64,128]{2,1,0:T(8,128)(2,1)} %shard_map.64), channel_id=1, source_target_pairs={{0,12},{1,13},{2,14},{3,15},{4,8},{5,9},{6,10},{7,11},{8,4},{9,5},... | collective-permute-start | bytes 49160 | tf_op jit(solution)/shard_map/ppermute | solution.py:260
  7.1 17.6 %collective-permute-start.1 = (bf16[1,64,128]{2,1,0:T(8,128)(2,1)}, bf16[1,64,128]{2,1,0:T(8,128)(2,1)S(1)}, u32[]{:S(2)}, u32[]{:S(2)}) collective-permute-start(bf16[1,64,128]{2,1,0:T(8,128)(2,1)} %shard_map.64), channel_id=1, source_target_pairs={{0,8},{1,9},{2,10},{3,11},{4,12},{5,13},{6,14},{7,15},{8,0},{9,1},... | collective-permute-start | bytes 49160 | tf_op jit(solution)/shard_map/ppermute | solution.py:260
  7.1 17.6 %collective-permute-start = (bf16[1,64,128]{2,1,0:T(8,128)(2,1)}, bf16[1,64,128]{2,1,0:T(8,128)(2,1)S(1)}, u32[]{:S(2)}, u32[]{:S(2)}) collective-permute-start(bf16[1,64,128]{2,1,0:T(8,128)(2,1)} %shard_map.64), channel_id=1, source_target_pairs={{0,4},{1,5},{2,6},{3,7},{4,0},{5,1},{6,2},{7,3},{8,12},{9,13},{10,... | collective-permute-start | bytes 49160 | tf_op jit(solution)/shard_map/ppermute | solution.py:260
  8.4 3.4 %copy-start = (bf16[1,64,16,4096]{3,2,1,0:T(8,128)(2,1)S(1)}, bf16[1,64,16,4096]{3,2,1,0:T(8,128)(2,1)}, u32[]{:S(2)}) copy-start(bf16[1,64,16,4096]{3,2,1,0:T(8,128)(2,1)} %param.6) | copy-start | bytes 25165828
  15.2 1.3 %copy-start.3 = (bf16[1024,1024]{1,0:T(8,128)(2,1)}, bf16[1024,1024]{1,0:T(8,128)(2,1)S(1)}, u32[]{:S(2)}) copy-start(bf16[1024,1024]{1,0:T(8,128)(2,1)S(1)} %shard_map.68.refs_2_) | copy-start | bytes 6291460
  16.5 3.0 %copy-start.9 = (s32[1,2]{1,0:T(1,128)S(1)}, s32[1,2]{1,0:T(1,128)}, u32[]{:S(2)}) copy-start(s32[1,2]{1,0:T(1,128)} %param.9) | copy-start | bytes 28
  16.5 3.0 %copy-start.8 = (s32[1,256]{1,0:T(1,128)S(1)}, s32[1,256]{1,0:T(1,128)}, u32[]{:S(2)}) copy-start(s32[1,256]{1,0:T(1,128)} %param.11) | copy-start | bytes 3076
  18.2 1.3 %copy-start.5 = (bf16[1024,1024]{1,0:T(8,128)(2,1)}, bf16[1024,1024]{1,0:T(8,128)(2,1)S(1)}, u32[]{:S(2)}) copy-start(bf16[1024,1024]{1,0:T(8,128)(2,1)S(1)} %shard_map.67.refs_1_) | copy-start | bytes 6291460
  19.5 3.4 %copy-start.1 = (bf16[1,64,16,4096]{3,2,1,0:T(8,128)(2,1)S(1)}, bf16[1,64,16,4096]{3,2,1,0:T(8,128)(2,1)}, u32[]{:S(2)}) copy-start(bf16[1,64,16,4096]{3,2,1,0:T(8,128)(2,1)} %param.6) | copy-start | bytes 25165828
  22.9 1.7 %copy-start.7 = (bf16[1,64,128]{2,1,0:T(8,128)(2,1)S(1)}, bf16[1,64,128]{2,1,0:T(8,128)(2,1)}, u32[]{:S(2)}) copy-start(bf16[1,64,128]{2,1,0:T(8,128)(2,1)} %shard_map.64) | copy-start | bytes 49156
  24.7 5.8 %collective-permute-start.5 = (bf16[4,64,128]{2,1,0:T(8,128)(2,1)S(1)}, bf16[4,64,128]{2,1,0:T(8,128)(2,1)S(1)}, u32[]{:S(2)}, u32[]{:S(2)}) collective-permute-start(bf16[4,64,128]{2,1,0:T(8,128)(2,1)S(1)} %pad_maximum_fusion), channel_id=1, source_target_pairs={{0,3},{1,2},{2,1},{3,0},{4,7},{5,6},{6,5},{7,4},{8,11},{9,10},{10,... | collective-permute-start | bytes 196616 | tf_op jit(solution)/shard_map/ppermute | solution.py:260
  25.2 5.3 %collective-permute-start.4 = (bf16[4,64,128]{2,1,0:T(8,128)(2,1)S(1)}, bf16[4,64,128]{2,1,0:T(8,128)(2,1)S(1)}, u32[]{:S(2)}, u32[]{:S(2)}) collective-permute-start(bf16[4,64,128]{2,1,0:T(8,128)(2,1)S(1)} %pad_maximum_fusion), channel_id=1, source_target_pairs={{0,2},{1,3},{2,0},{3,1},{4,6},{5,7},{6,4},{7,5},{8,10},{9,11},{10,... | collective-permute-start | bytes 196616 | tf_op jit(solution)/shard_map/ppermute | solution.py:260
  26.6 1.3 %collective-permute-start.3 = (bf16[4,64,128]{2,1,0:T(8,128)(2,1)S(1)}, bf16[4,64,128]{2,1,0:T(8,128)(2,1)S(1)}, u32[]{:S(2)}, u32[]{:S(2)}) collective-permute-start(bf16[4,64,128]{2,1,0:T(8,128)(2,1)S(1)} %pad_maximum_fusion), channel_id=1, source_target_pairs={{0,1},{1,0},{2,3},{3,2},{4,5},{5,4},{6,7},{7,6},{8,9},{9,8},{10,11... | collective-permute-start | bytes 196616 | tf_op jit(solution)/shard_map/ppermute | solution.py:260
  30.5 3.4 %copy-start.2 = (bf16[1,64,16,4096]{3,2,1,0:T(8,128)(2,1)S(1)}, bf16[1,64,16,4096]{3,2,1,0:T(8,128)(2,1)}, u32[]{:S(2)}) copy-start(bf16[1,64,16,4096]{3,2,1,0:T(8,128)(2,1)} %param.6) | copy-start | bytes 25165828
  33.9 8.7 %copy-start.4 = (bf16[1024,1024]{1,0:T(8,128)(2,1)S(1)}, bf16[1024,1024]{1,0:T(8,128)(2,1)}, u32[]{:S(2)}) copy-start(bf16[1024,1024]{1,0:T(8,128)(2,1)} %copy-done.3) | copy-start | bytes 6291460
  33.9 8.7 %copy-start.6 = (bf16[1024,1024]{1,0:T(8,128)(2,1)S(1)}, bf16[1024,1024]{1,0:T(8,128)(2,1)}, u32[]{:S(2)}) copy-start(bf16[1024,1024]{1,0:T(8,128)(2,1)} %copy-done.5) | copy-start | bytes 6291460
  58.4 1.6 %collective-permute-start.6 = (bf16[16,64,128]{2,1,0:T(8,128)(2,1)S(1)}, bf16[16,64,128]{2,1,0:T(8,128)(2,1)S(1)}, u32[]{:S(2)}, u32[]{:S(2)}) collective-permute-start(bf16[16,64,128]{2,1,0:T(8,128)(2,1)S(1)} %get-tuple-element.8), channel_id=1, source_target_pairs={{0,1},{1,0},{2,3},{3,2},{4,5},{5,4},{6,7},{7,6},{8,9},{9,8},{10,11... | collective-permute-start | bytes 786440 | tf_op jit(solution)/shard_map/ppermute | solution.py:260
  60.1 5.6 %collective-permute-start.7 = (bf16[8,64,128]{2,1,0:T(8,128)(2,1)S(1)}, bf16[8,64,128]{2,1,0:T(8,128)(2,1)S(1)}, u32[]{:S(2)}, u32[]{:S(2)}) collective-permute-start(bf16[8,64,128]{2,1,0:T(8,128)(2,1)S(1)} %slice.41), channel_id=1, source_target_pairs={{0,2},{1,3},{2,0},{3,1},{4,6},{5,7},{6,4},{7,5},{8,10},{9,11},{10,... | collective-permute-start | bytes 393224 | tf_op jit(solution)/shard_map/ppermute | solution.py:260
  65.8 4.5 %collective-permute-start.8 = (bf16[2,64,128]{2,1,0:T(8,128)(2,1)S(1)}, bf16[2,64,128]{2,1,0:T(8,128)(2,1)S(1)}, u32[]{:S(2)}, u32[]{:S(2)}) collective-permute-start(bf16[2,64,128]{2,1,0:T(8,128)(2,1)S(1)} %get-tuple-element.11), channel_id=1, source_target_pairs={{0,4},{1,5},{2,6},{3,7},{4,0},{5,1},{6,2},{7,3},{8,12},{9,13},{10,... | collective-permute-start | bytes 98312 | tf_op jit(solution)/shard_map/ppermute | solution.py:260
  67.4 6.0 %collective-permute-start.10 = (bf16[2,64,128]{2,1,0:T(8,128)(2,1)S(1)}, bf16[2,64,128]{2,1,0:T(8,128)(2,1)S(1)}, u32[]{:S(2)}, u32[]{:S(2)}) collective-permute-start(bf16[2,64,128]{2,1,0:T(8,128)(2,1)S(1)} %get-tuple-element.12), channel_id=1, source_target_pairs={{0,12},{1,13},{2,14},{3,15},{4,8},{5,9},{6,10},{7,11},{8,4},{9,5},... | collective-permute-start | bytes 98312 | tf_op jit(solution)/shard_map/ppermute | solution.py:260
  69.8 4.8 %collective-permute-start.9 = (bf16[2,64,128]{2,1,0:T(8,128)(2,1)S(1)}, bf16[2,64,128]{2,1,0:T(8,128)(2,1)S(1)}, u32[]{:S(2)}, u32[]{:S(2)}) collective-permute-start(bf16[2,64,128]{2,1,0:T(8,128)(2,1)S(1)} %get-tuple-element.13), channel_id=1, source_target_pairs={{0,8},{1,9},{2,10},{3,11},{4,12},{5,13},{6,14},{7,15},{8,0},{9,1},... | collective-permute-start | bytes 98312 | tf_op jit(solution)/shard_map/ppermute | solution.py:260

commit v4 on v3

--- a/solution.py
+++ b/solution.py
@@ -13,7 +13,8 @@
 GRANT = 8 << 20
 
 
-def pack_kernel(count_ref, occ_ref, virt_ref, out_ref, rows_ref):
+def pack_kernel(owner_rounds, table_rounds, me_ref, count_ref, pair_ref, tgt_ref, occ_ref, virt_ref, *refs):
+    out_ref, ids_ref, place_ref, rows_ref = refs
     lanes = out_ref.shape[2]
     half = out_ref.shape[1] // 2
     for i in range(half):
@@ -26,19 +27,38 @@
     valid = (2 * (row % half) + lane // bs < count) & (lane % bs < count)
     out_ref[0] = jnp.where(valid, rows_ref[...], 0.0).astype(jnp.bfloat16)
 
-
-def packed(basis_count, green_occ, green_virt, bs):
-    vmem = pl.BlockSpec(memory_space=pltpu.VMEM)
+    me = me_ref[0]
+    rel = pair_ref[...] ^ me
+    ids, weight = jnp.zeros_like(rel), 1
+    for shift, step in table_rounds:
+        ids = ids + ((rel >> shift) & ((1 << step) - 1)) * weight
+        weight <<= step
+    ids_ref[...] = ids
+
+    targets = tgt_ref[...]
+    rel = (targets // CB_DEV) ^ me
+    place = jnp.zeros_like(targets)
+    for shift, step in owner_rounds:
+        place = (place << step) | ((rel >> shift) & ((1 << step) - 1))
+    place_ref[...] = place * CB_DEV + targets % CB_DEV
+
+
+def packed(me, basis_count, pair_atoms, chi_target, green_occ, green_virt, bs, bits):
     return pl.pallas_call(
-        pack_kernel,
-        in_specs=[pl.BlockSpec(memory_space=pltpu.SMEM), vmem, vmem],
-        out_specs=vmem,
-        out_shape=jax.ShapeDtypeStruct((1, bs, 2 * bs), jnp.bfloat16),
+        functools.partial(pack_kernel, sum_rounds(bits), gather_rounds(bits)),
+        in_specs=in_smem(2) + in_vmem(4),
+        out_specs=in_vmem(3),
+        out_shape=[
+            jax.ShapeDtypeStruct((1, bs, 2 * bs), jnp.bfloat16),
+            jax.ShapeDtypeStruct(pair_atoms.shape, jnp.int32),
+            jax.ShapeDtypeStruct(chi_target.shape, jnp.int32),
+        ],
         scratch_shapes=[pltpu.VMEM((bs, 2 * bs), jnp.float32)],
-    )(basis_count, green_occ, green_virt)
-
-
-def relayout_kernel(part, b_ref, d_ref):
+        compiler_params=pltpu.CompilerParams(vmem_limit_bytes=2 << 20),
+    )(me, basis_count, pair_atoms, chi_target, green_occ, green_virt)
+
+
+def relayout_kernel(part, b_ref, _, d_ref):
     bs, aux, _ = b_ref.shape
     wide = LAM * bs
     rows = aux * aux
@@ -69,11 +89,11 @@
     return [pl.BlockSpec(memory_space=pltpu.SMEM)] * count
 
 
-def relayout(integrals, part):
+def relayout(integrals, part, after):
     bs, aux, width = integrals.shape
     return pl.pallas_call(
         functools.partial(relayout_kernel, part),
-        in_specs=in_vmem(1),
+        in_specs=in_vmem(1) + [pl.BlockSpec(memory_space=pl.ANY)],
         out_specs=in_vmem(1)[0],
         out_shape=jax.ShapeDtypeStruct((aux * bs, bs // PARTS * bs), jnp.bfloat16),
         compiler_params=pltpu.CompilerParams(vmem_limit_bytes=GRANT),
@@ -82,7 +102,7 @@
             bytes_accessed=4 * bs * aux * width // PARTS,
             transcendentals=0,
         ),
-    )(integrals)
+    )(integrals, after)
 
 
 def spread_rows(block, of_row, count, bs):
@@ -93,10 +113,18 @@
     return jnp.where(odd, got[:, bs:], got[:, :bs])
 
 
-def virt_kernel(bs, ids_ref, table_ref, *refs):
-    d_parts, v_ref = refs[:PARTS], refs[PARTS]
+def green_block(tables, slot):
+    count = tables[0].shape[0]
+    block = tables[0][slot % count].astype(jnp.float32)
+    for k in range(1, len(tables)):
+        block = jnp.where(slot // count == k, tables[k][slot % count].astype(jnp.float32), block)
+    return block.astype(jnp.bfloat16)
+
+
+def virt_kernel(bs, pieces, ids_ref, *refs):
+    tables, d_parts, v_ref = refs[:pieces], refs[pieces:pieces + PARTS], refs[-1]
     wide = LAM * bs
-    spread = spread_rows(table_ref[ids_ref[1], bs // 2:], lambda i: i % bs, wide, bs)
+    spread = spread_rows(green_block(tables, ids_ref[1])[bs // 2:], lambda i: i % bs, wide, bs)
     spread = jnp.concatenate([spread] * LAM, axis=1)
     same = (
         lax.broadcasted_iota(jnp.int32, (wide, wide), 0) // bs == lax.broadcasted_iota(jnp.int32, (wide, wide), 1) // bs
@@ -109,16 +137,17 @@
             v_ref[:, part * each + at:part * each + at + wide] = got.astype(jnp.bfloat16)
 
 
-def occ_kernel(ids_ref, table_ref, b_ref, o_ref):
+def occ_kernel(pieces, ids_ref, *refs):
+    tables, (b_ref, o_ref) = refs[:pieces], refs[pieces:]
     bs, aux, width = b_ref.shape
     half = aux // 2
-    wide = LAM * bs
+    wide = 8 * bs
     lanes = 2 * bs
     tall = bs * half
     rep_t = (
         lax.broadcasted_iota(jnp.int32, (bs, tall), 1) // half == lax.broadcasted_iota(jnp.int32, (bs, tall), 0)
     ).astype(jnp.bfloat16)
-    spread = spread_rows(table_ref[ids_ref[0], :bs // 2], lambda i: i // half, tall, bs).astype(jnp.bfloat16)
+    spread = spread_rows(green_block(tables, ids_ref[0])[:bs // 2], lambda i: i // half, tall, bs).astype(jnp.bfloat16)
     spread = jnp.dot(spread, rep_t, preferred_element_type=jnp.float32)
     same = (
         lax.broadcasted_iota(jnp.int32, (tall, tall), 0) % half
@@ -126,7 +155,7 @@
     )
     occ_w = jnp.where(same, spread, 0.0).astype(jnp.bfloat16)
 
-    @pl.loop(0, width // wide, unroll=2)
+    @pl.loop(0, width // wide)
     def _(j):
         cols = pl.ds(pl.multiple_of(j * wide, wide), wide)
         block = b_ref[:, :, cols].astype(jnp.float32)
@@ -136,8 +165,8 @@
             got = jnp.dot(occ_w, side, preferred_element_type=jnp.float32)
             sides.append(got.reshape(bs, half, wide))
         both = jnp.concatenate(sides, axis=1).astype(jnp.bfloat16)
-        for p in range(LAM):
-            rows = pl.ds(pl.multiple_of(j * (LAM * aux) + p * aux, aux), aux)
+        for p in range(wide // bs):
+            rows = pl.ds(pl.multiple_of(j * (wide // bs * aux) + p * aux, aux), aux)
             for q in range(bs // 2):
                 o_ref[rows, q * lanes:(q + 1) * lanes] = jnp.concatenate(
                     [both[2 * q, :, p * bs:(p + 1) * bs], both[2 * q + 1, :, p * bs:(p + 1) * bs]], axis=-1
@@ -196,28 +225,28 @@
             send_ref[i] = joined((k + 1) * pairs + i).astype(jnp.bfloat16)
 
 
-def chi_blocks_of(ids, targets, table, integrals, d_parts, blocks, sends):
+def chi_blocks_of(ids, targets, tables, integrals, d_parts, blocks, sends):
     bs, aux, width = integrals.shape
     pairs = blocks // 2 // (sends + 1)
     side = jax.ShapeDtypeStruct((aux * bs, width), jnp.bfloat16)
     params = pltpu.CompilerParams(vmem_limit_bytes=GRANT)
     cost = pl.CostEstimate(flops=2 * (aux * bs) ** 2 * width, bytes_accessed=4 * aux * bs * width, transcendentals=0)
     virt_side = pl.pallas_call(
-        functools.partial(virt_kernel, bs),
-        in_specs=in_smem(1) + in_vmem(1 + PARTS),
+        functools.partial(virt_kernel, bs, len(tables)),
+        in_specs=in_smem(1) + in_vmem(len(tables) + PARTS),
         out_specs=in_vmem(1)[0],
         out_shape=side,
         compiler_params=params,
         cost_estimate=cost,
-    )(ids, table, *d_parts)
+    )(ids, *tables, *d_parts)
     occ_side = pl.pallas_call(
-        occ_kernel,
-        in_specs=in_smem(1) + in_vmem(2),
+        functools.partial(occ_kernel, len(tables)),
+        in_specs=in_smem(1) + in_vmem(len(tables) + 1),
         out_specs=in_vmem(1)[0],
         out_shape=side,
         compiler_params=params,
         cost_estimate=cost,
-    )(ids, table, integrals)
+    )(ids, *tables, integrals)
     accs = 2 if blocks <= 128 else 1
     acc = pltpu.VMEM((blocks, bs, 2 * bs), jnp.float32)
     out = pltpu.VMEM((2, aux * bs, 2 * bs), jnp.float32)
@@ -234,12 +263,7 @@
 
 
 def gather_rounds(bits):
-    rounds = []
-    while bits:
-        step = min(2, bits)
-        bits -= step
-        rounds.append((bits, step))
-    return rounds
+    return [(shift, step) for shift, step in reversed(sum_rounds(bits))]
 
 
 def sum_rounds(bits):
@@ -259,25 +283,21 @@
     def exchange(value, flip):
         return lax.ppermute(value, "orb", [(i, i ^ flip) for i in range(orb)])
 
-    table = packed(basis_count, green_occ, green_virt, bs)
-    ids = jnp.zeros_like(pair_atoms[0])
-    rel = pair_atoms[0] ^ me
-    count = 1
-    for shift, step in gather_rounds(bits):
-        table = jnp.concatenate([table] + [exchange(table, v << shift) for v in range(1, 1 << step)], axis=0)
-        ids = ids + ((rel >> shift) & ((1 << step) - 1)) * count
-        count <<= step
-
-    targets = chi_target[0]
-    rel = (targets // CB_DEV) ^ me
-    place = jnp.zeros_like(targets)
-    for shift, step in sum_rounds(bits):
-        place = (place << step) | ((rel >> shift) & ((1 << step) - 1))
-    place = place * CB_DEV + targets % CB_DEV
-
-    d_parts = [relayout(three_centre[0], i) for i in range(PARTS)]
+    integrals = three_centre[0]
+    table, ids, place = packed(
+        me[None].astype(jnp.int32), basis_count, pair_atoms, chi_target, green_occ, green_virt, bs, bits
+    )
+    rounds = gather_rounds(bits)
+    tables, after = [table], [table]
+    for shift, step in rounds:
+        table = tables[0] if len(tables) == 1 else jnp.concatenate(tables, axis=0)
+        tables = [table] + [exchange(table, v << shift) for v in range(1, 1 << step)]
+        after.append(tables[-1])
+    d_parts = [relayout(integrals, i, after[max(0, i - PARTS + len(rounds))]) for i in range(PARTS)]
     rounds = sum_rounds(bits)
-    total, *sends = chi_blocks_of(ids, place, table, three_centre[0], d_parts, orb * CB_DEV, (1 << rounds[0][1]) - 1)
+    total, *sends = chi_blocks_of(
+        ids[0], place[0], tables, integrals, d_parts, orb * CB_DEV, (1 << rounds[0][1]) - 1
+    )
     for k, (shift, step) in enumerate(rounds):
         if k:
             rest = total.shape[0] >> step

time: 76 us -> 67.5 us (0.89)
  local copies, waits for them, and re-layouts: 14.5 us -> 7.09 us
  waiting for transfers between devices: 14.1 us -> 12.2 us
  starting transfers between devices: 13.3 us -> 14.2 us
    unnamed x26 -> x16, local copies, waits for them, and re-layouts: 13.6 us -> 6.17 us
    ppermute x11 -> x10, waiting for transfers between devices: 14.1 us -> 12.2 us  [exchange(): return lax.ppermute(value, 'orb', [(i, i ^ flip) for i in range(orb)])]
    ppermute x11 -> x10, starting transfers between devices: 13.3 us -> 14.2 us  [exchange(): return lax.ppermute(value, 'orb', [(i, i ^ flip) for i in range(orb)])]
  transfers between devices with their start and end apart: 11 -> 10, of which waited for: 6 -> 5; matrix products, arithmetic and copies ran while one was open for 1% -> 0% of each run, Pallas kernels for 9% -> 10%
where the time goes in v4:
time: 67.5 us; the launch traced here: 67.1 us
  Pallas kernels  32.7 us (48%)
  starting transfers between devices  14.2 us (21%)
  waiting for transfers between devices  12.2 us (18%)
  local copies, waits for them, and re-layouts  7.09 us (11%)
  between operations  0.83 us (1%)
    ppermute x10, starting transfers between devices, exchange(): return lax.ppermute(value, 'orb', [(i, i ^ flip) for i in range(orb)])  14.2 us
    pallas_call x1, Pallas kernels, chi_blocks_of(): pl.pallas_call(functools.partial(chi_kernel, bs, sends), in_specs=in_smem...  12.7 us
    ppermute x10, waiting for transfers between devices, exchange(): return lax.ppermute(value, 'orb', [(i, i ^ flip) for i in range(orb)])  12.2 us
    pallas_call x1, Pallas kernels, chi_blocks_of(): pl.pallas_call(functools.partial(occ_kernel, len(tables)), in_specs=in_sm...  9.99 us
    pallas_call x4, Pallas kernels, relayout(): pl.pallas_call(functools.partial(relayout_kernel, part), in_specs=in_vmem...  6.77 us
    unnamed x16, local copies, waits for them, and re-layouts  6.17 us
    pallas_call x1, Pallas kernels, chi_blocks_of(): pl.pallas_call(functools.partial(virt_kernel, bs, len(tables)), in_specs=...  3.17 us
  transfers between devices with their start and end apart: 10, of which 5 were waited for; matrix products, arithmetic and copies ran while one was open for 0% of the time, Pallas kernels for 10%

profile of v4, /device:TPU:0, one launch (start us, length us, event | category | flops | bytes accessed | tf_op | source)
XLA Modules:
  0.0 67.1 jit_solution(3866618032474601263)
XLA Ops:
  0.7 0.0 copy-start.2
  0.7 0.7 %copy-done.2 = bf16[1,4096]{1,0:T(2,128)(2,1)S(1)} copy-done((bf16[1,4096]{1,0:T(2,128)(2,1)S(1)}, bf16[1,4096]{1,0:T(2,128)(2,1)}, u32[]{:S(2)}) %copy-start.2) | copy-done | bytes 8216
  1.4 0.0 copy-start.3
  1.4 0.7 %copy-done.3 = bf16[1,4096]{1,0:T(2,128)(2,1)S(1)} copy-done((bf16[1,4096]{1,0:T(2,128)(2,1)S(1)}, bf16[1,4096]{1,0:T(2,128)(2,1)}, u32[]{:S(2)}) %copy-start.3) | copy-done | bytes 8216
  2.1 0.0 copy-start.4
  2.1 0.7 %copy-done.4 = s32[1,256]{1,0:T(1,128)S(1)} copy-done((s32[1,256]{1,0:T(1,128)S(1)}, s32[1,256]{1,0:T(1,128)}, u32[]{:S(2)}) %copy-start.4) | copy-done | bytes 1048
  2.8 0.0 copy-start.5
  2.8 0.7 copy-done.5
  3.4 0.1 shard_map.64
  3.5 5.1 %collective-permute-start.2 = (bf16[1,64,128]{2,1,0:T(8,128)(2,1)S(1)}, bf16[1,64,128]{2,1,0:T(8,128)(2,1)S(1)}, u32[]{:S(2)}, u32[]{:S(2)}) collective-permute-start(bf16[1,64,128]{2,1,0:T(8,128)(2,1)S(1)} %get-tuple-element.12._), channel_id=1, source_target_pairs={{0,12},{1,13},{2,14},{3,15},{4,8},{5,9},{6,10},{7,11},{8,4},{9,5},... | collective-permute-start | bytes 49160 | tf_op jit(solution)/shard_map/ppermute | solution.py:284
  8.6 0.0 collective-permute-start.1
  8.6 0.6 collective-permute-start
  9.2 0.0 copy-start
  9.2 3.4 %copy-done = bf16[1,64,16,4096]{3,2,1,0:T(8,128)(2,1)S(1)} copy-done((bf16[1,64,16,4096]{3,2,1,0:T(8,128)(2,1)S(1)}, bf16[1,64,16,4096]{3,2,1,0:T(8,128)(2,1)}, u32[]{:S(2)}) %copy-start) | copy-done | bytes 8388632
  12.6 0.0 copy-start.1
  12.6 1.7 %shard_map.67.refs_3_ = bf16[1024,1024]{1,0:T(8,128)(2,1)S(1)} custom-call(bf16[64,16,4096]{2,1,0:T(8,128)(2,1)S(1)} %bitcast.7, bf16[1,64,128]{2,1,0:T(8,128)(2,1)S(1)} %get-tuple-element.12._), custom_call_target="tpu_custom_call" | custom-call | flops 536870912 | bytes 4194304 | tf_op jit(solution)/shard_map/pallas_call | solution.py:94
  14.3 0.0 collective-permute-done.2._
  14.3 0.0 collective-permute-done.1
  14.3 0.0 collective-permute-done
  14.4 1.7 %collective-permute-start.3 = (bf16[4,64,128]{2,1,0:T(8,128)(2,1)S(1)}, bf16[4,64,128]{2,1,0:T(8,128)(2,1)S(1)}, u32[]{:S(2)}, u32[]{:S(2)}) collective-permute-start(bf16[4,64,128]{2,1,0:T(8,128)(2,1)S(1)} %pad_maximum_fusion), channel_id=1, source_target_pairs={{0,2},{1,3},{2,0},{3,1},{4,6},{5,7},{6,4},{7,5},{8,10},{9,11},{10,... | collective-permute-start | bytes 196616 | tf_op jit(solution)/shard_map/ppermute | solution.py:284
  16.1 2.6 %collective-permute-done.3._ = bf16[4,64,128]{2,1,0:T(8,128)(2,1)S(1)} collective-permute-done((bf16[4,64,128]{2,1,0:T(8,128)(2,1)S(1)}, bf16[4,64,128]{2,1,0:T(8,128)(2,1)S(1)}, u32[]{:S(2)}, u32[]{:S(2)}) %collective-permute-start.3) | collective-permute-done | bytes 65568 | tf_op jit(solution)/shard_map/ppermute | solution.py:284
  18.7 0.1 collective-permute-start.4
  18.8 0.0 copy-done.1
  18.8 1.7 %shard_map.66.refs_2_ = bf16[1024,1024]{1,0:T(8,128)(2,1)S(1)} custom-call(bf16[64,16,4096]{2,1,0:T(8,128)(2,1)S(1)} %bitcast.8, bf16[1,64,128]{2,1,0:T(8,128)(2,1)S(1)} %get-tuple-element.12._), custom_call_target="tpu_custom_call" | custom-call | flops 536870912 | bytes 4194304 | tf_op jit(solution)/shard_map/pallas_call | solution.py:94
  20.5 1.7 %shard_map.68.refs_4_ = bf16[1024,1024]{1,0:T(8,128)(2,1)S(1)} custom-call(bf16[64,16,4096]{2,1,0:T(8,128)(2,1)S(1)} %bitcast.9, bf16[1,64,128]{2,1,0:T(8,128)(2,1)S(1)} %collective-permute-done.2._), custom_call_target="tpu_custom_call" | custom-call | flops 536870912 | bytes 4194304 | tf_op jit(solution)/shard_map/pallas_call | solution.py:94
  22.2 1.7 %shard_map.69.refs_5_ = bf16[1024,1024]{1,0:T(8,128)(2,1)S(1)} custom-call(bf16[64,16,4096]{2,1,0:T(8,128)(2,1)S(1)} %bitcast.10, bf16[4,64,128]{2,1,0:T(8,128)(2,1)S(1)} %collective-permute-done.3._), custom_call_target="tpu_custom_call" | custom-call | flops 536870912 | bytes 4194304 | tf_op jit(solution)/shard_map/pallas_call | solution.py:94
  23.9 0.0 collective-permute-done.4.refs_1_
  23.9 10.0 %shard_map.65.o_ref = bf16[1024,4096]{1,0:T(8,128)(2,1)S(1)} custom-call(s32[2]{0:T(128)S(1)} %bitcast.13, bf16[8,64,128]{2,1,0:T(8,128)(2,1)S(1)} %constant_dynamic-update-slice_fusion.refs_0_, bf16[8,64,128]{2,1,0:T(8,128)(2,1)S(1)} %collective-permute-done.4.refs_1_, bf16[64,16,4096]{2,1,0:T(8,128)(2,1)S(1)} %bitcast.11), custom_call_target="tpu_custom_call" | custom-call | flops 8589934592 | bytes 16777216 | tf_op jit(solution)/shard_map/pallas_call | solution.py:242
  33.9 3.2 %shard_map.70.v_ref = bf16[1024,4096]{1,0:T(8,128)(2,1)S(1)} custom-call(s32[2]{0:T(128)S(1)} %bitcast.14, bf16[8,64,128]{2,1,0:T(8,128)(2,1)S(1)} %constant_dynamic-update-slice_fusion.refs_0_, bf16[8,64,128]{2,1,0:T(8,128)(2,1)S(1)} %collective-permute-done.4.refs_1_, bf16[1024,1024]{1,0:T(8,128)(2,1)S(1)} %shard_map.66.refs_2_, ...), custom_call_target="tpu_custom_call" | custom-call | flops 8589934592 | bytes 16777216 | tf_op jit(solution)/shard_map/pallas_call | solution.py:234
  37.1 12.7 %shard_map.71 = (f32[16,64,128]{2,1,0:T(8,128)S(1)}, bf16[16,64,128]{2,1,0:T(8,128)(2,1)S(1)}) custom-call(s32[256]{0:T(256)S(1)} %bitcast.12, bf16[1024,4096]{1,0:T(8,128)(2,1)S(1)} %shard_map.65.o_ref, bf16[1024,4096]{1,0:T(8,128)(2,1)S(1)} %shard_map.70.v_ref), custom_call_target="tpu_custom_call" | custom-call | flops 8589934592 | bytes 16777216 | tf_op jit(solution)/shard_map/pallas_call | solution.py:253
  49.8 0.6 collective-permute-start.5
  50.4 1.2 %collective-permute-done.5 = bf16[16,64,128]{2,1,0:T(8,128)(2,1)S(1)} collective-permute-done((bf16[16,64,128]{2,1,0:T(8,128)(2,1)S(1)}, bf16[16,64,128]{2,1,0:T(8,128)(2,1)S(1)}, u32[]{:S(2)}, u32[]{:S(2)}) %collective-permute-start.5) | collective-permute-done | bytes 262176 | tf_op jit(solution)/shard_map/ppermute | solution.py:284
  51.5 0.1 convert_add_fusion
  51.6 1.7 %collective-permute-start.6 = (bf16[8,64,128]{2,1,0:T(8,128)(2,1)S(1)}, bf16[8,64,128]{2,1,0:T(8,128)(2,1)S(1)}, u32[]{:S(2)}, u32[]{:S(2)}) collective-permute-start(bf16[8,64,128]{2,1,0:T(8,128)(2,1)S(1)} %slice.41), channel_id=1, source_target_pairs={{0,2},{1,3},{2,0},{3,1},{4,6},{5,7},{6,4},{7,5},{8,10},{9,11},{10,... | collective-permute-start | bytes 393224 | tf_op jit(solution)/shard_map/ppermute | solution.py:284
  53.4 4.1 %collective-permute-done.6 = bf16[8,64,128]{2,1,0:T(8,128)(2,1)S(1)} collective-permute-done((bf16[8,64,128]{2,1,0:T(8,128)(2,1)S(1)}, bf16[8,64,128]{2,1,0:T(8,128)(2,1)S(1)}, u32[]{:S(2)}, u32[]{:S(2)}) %collective-permute-start.6) | collective-permute-done | bytes 131104 | tf_op jit(solution)/shard_map/ppermute | solution.py:284
  57.5 1.4 %collective-permute-start.7 = (bf16[2,64,128]{2,1,0:T(8,128)(2,1)S(1)}, bf16[2,64,128]{2,1,0:T(8,128)(2,1)S(1)}, u32[]{:S(2)}, u32[]{:S(2)}) collective-permute-start(bf16[2,64,128]{2,1,0:T(8,128)(2,1)S(1)} %get-tuple-element.17), channel_id=1, source_target_pairs={{0,4},{1,5},{2,6},{3,7},{4,0},{5,1},{6,2},{7,3},{8,12},{9,13},{10,... | collective-permute-start | bytes 98312 | tf_op jit(solution)/shard_map/ppermute | solution.py:284
  59.0 2.4 %collective-permute-start.9 = (bf16[2,64,128]{2,1,0:T(8,128)(2,1)S(1)}, bf16[2,64,128]{2,1,0:T(8,128)(2,1)S(1)}, u32[]{:S(2)}, u32[]{:S(2)}) collective-permute-start(bf16[2,64,128]{2,1,0:T(8,128)(2,1)S(1)} %get-tuple-element.18), channel_id=1, source_target_pairs={{0,12},{1,13},{2,14},{3,15},{4,8},{5,9},{6,10},{7,11},{8,4},{9,5},... | collective-permute-start | bytes 98312 | tf_op jit(solution)/shard_map/ppermute | solution.py:284
  61.4 0.5 collective-permute-start.8
  61.9 0.0 collective-permute-done.7
  61.9 3.2 %collective-permute-done.9 = bf16[2,64,128]{2,1,0:T(8,128)(2,1)S(1)} collective-permute-done((bf16[2,64,128]{2,1,0:T(8,128)(2,1)S(1)}, bf16[2,64,128]{2,1,0:T(8,128)(2,1)S(1)}, u32[]{:S(2)}, u32[]{:S(2)}) %collective-permute-start.9) | collective-permute-done | bytes 32800 | tf_op jit(solution)/shard_map/ppermute | solution.py:284
  65.1 1.1 %collective-permute-done.8 = bf16[2,64,128]{2,1,0:T(8,128)(2,1)S(1)} collective-permute-done((bf16[2,64,128]{2,1,0:T(8,128)(2,1)S(1)}, bf16[2,64,128]{2,1,0:T(8,128)(2,1)S(1)}, u32[]{:S(2)}, u32[]{:S(2)}) %collective-permute-start.8) | collective-permute-done | bytes 32800 | tf_op jit(solution)/shard_map/ppermute | solution.py:284
  66.2 0.1 reshape.6
  66.4 0.7 %reshape.7 = f32[4,4096]{1,0:T(4,128)} reshape(f32[2,2,64,64]{3,2,1,0:T(8,128)S(1)} %copy.7) | data formatting | bytes 131072 | tf_op jit(solution)/shard_map/reshape | solution.py:309
  (11 shorter events, 0.1 us)
Async XLA Ops:
  0.7 0.7 %copy-start.2 = (bf16[1,4096]{1,0:T(2,128)(2,1)S(1)}, bf16[1,4096]{1,0:T(2,128)(2,1)}, u32[]{:S(2)}) copy-start(bf16[1,4096]{1,0:T(2,128)(2,1)} %occ_ref.1) | copy-start | bytes 24580
  1.4 0.7 %copy-start.3 = (bf16[1,4096]{1,0:T(2,128)(2,1)S(1)}, bf16[1,4096]{1,0:T(2,128)(2,1)}, u32[]{:S(2)}) copy-start(bf16[1,4096]{1,0:T(2,128)(2,1)} %virt_ref.1) | copy-start | bytes 24580
  2.1 0.7 %copy-start.4 = (s32[1,256]{1,0:T(1,128)S(1)}, s32[1,256]{1,0:T(1,128)}, u32[]{:S(2)}) copy-start(s32[1,256]{1,0:T(1,128)} %tgt_ref.1) | copy-start | bytes 3076
  2.8 0.7 copy-start.5
  3.5 10.8 %collective-permute-start.2 = (bf16[1,64,128]{2,1,0:T(8,128)(2,1)S(1)}, bf16[1,64,128]{2,1,0:T(8,128)(2,1)S(1)}, u32[]{:S(2)}, u32[]{:S(2)}) collective-permute-start(bf16[1,64,128]{2,1,0:T(8,128)(2,1)S(1)} %get-tuple-element.12._), channel_id=1, source_target_pairs={{0,12},{1,13},{2,14},{3,15},{4,8},{5,9},{6,10},{7,11},{8,4},{9,5},... | collective-permute-start | bytes 49160 | tf_op jit(solution)/shard_map/ppermute | solution.py:284
  8.6 5.7 %collective-permute-start.1 = (bf16[1,64,128]{2,1,0:T(8,128)(2,1)S(1)}, bf16[1,64,128]{2,1,0:T(8,128)(2,1)S(1)}, u32[]{:S(2)}, u32[]{:S(2)}) collective-permute-start(bf16[1,64,128]{2,1,0:T(8,128)(2,1)S(1)} %get-tuple-element.12._), channel_id=1, source_target_pairs={{0,8},{1,9},{2,10},{3,11},{4,12},{5,13},{6,14},{7,15},{8,0},{9,1},... | collective-permute-start | bytes 49160 | tf_op jit(solution)/shard_map/ppermute | solution.py:284
  8.6 5.8 %collective-permute-start = (bf16[1,64,128]{2,1,0:T(8,128)(2,1)S(1)}, bf16[1,64,128]{2,1,0:T(8,128)(2,1)S(1)}, u32[]{:S(2)}, u32[]{:S(2)}) collective-permute-start(bf16[1,64,128]{2,1,0:T(8,128)(2,1)S(1)} %get-tuple-element.12._), channel_id=1, source_target_pairs={{0,4},{1,5},{2,6},{3,7},{4,0},{5,1},{6,2},{7,3},{8,12},{9,13},{10,... | collective-permute-start | bytes 49160 | tf_op jit(solution)/shard_map/ppermute | solution.py:284
  9.2 3.4 %copy-start = (bf16[1,64,16,4096]{3,2,1,0:T(8,128)(2,1)S(1)}, bf16[1,64,16,4096]{3,2,1,0:T(8,128)(2,1)}, u32[]{:S(2)}) copy-start(bf16[1,64,16,4096]{3,2,1,0:T(8,128)(2,1)} %param.6) | copy-start | bytes 25165828
  12.6 6.2 %copy-start.1 = (bf16[1,64,16,4096]{3,2,1,0:T(8,128)(2,1)S(1)}, bf16[1,64,16,4096]{3,2,1,0:T(8,128)(2,1)}, u32[]{:S(2)}) copy-start(bf16[1,64,16,4096]{3,2,1,0:T(8,128)(2,1)} %param.6) | copy-start | bytes 25165828
  14.4 4.3 %collective-permute-start.3 = (bf16[4,64,128]{2,1,0:T(8,128)(2,1)S(1)}, bf16[4,64,128]{2,1,0:T(8,128)(2,1)S(1)}, u32[]{:S(2)}, u32[]{:S(2)}) collective-permute-start(bf16[4,64,128]{2,1,0:T(8,128)(2,1)S(1)} %pad_maximum_fusion), channel_id=1, source_target_pairs={{0,2},{1,3},{2,0},{3,1},{4,6},{5,7},{6,4},{7,5},{8,10},{9,11},{10,... | collective-permute-start | bytes 196616 | tf_op jit(solution)/shard_map/ppermute | solution.py:284
  18.7 5.2 %collective-permute-start.4 = (bf16[8,64,128]{2,1,0:T(8,128)(2,1)S(1)}, bf16[8,64,128]{2,1,0:T(8,128)(2,1)S(1)}, u32[]{:S(2)}, u32[]{:S(2)}) collective-permute-start(bf16[8,64,128]{2,1,0:T(8,128)(2,1)S(1)} %constant_dynamic-update-slice_fusion.refs_0_), channel_id=1, source_target_pairs={{0,1},{1,0},{2,3},{3,2},{4,5},{5,4},{6,7},{7,6},{8,9},{9,8},{10,11... | collective-permute-start | bytes 393224 | tf_op jit(solution)/shard_map/ppermute | solution.py:284
  49.8 1.7 %collective-permute-start.5 = (bf16[16,64,128]{2,1,0:T(8,128)(2,1)S(1)}, bf16[16,64,128]{2,1,0:T(8,128)(2,1)S(1)}, u32[]{:S(2)}, u32[]{:S(2)}) collective-permute-start(bf16[16,64,128]{2,1,0:T(8,128)(2,1)S(1)} %get-tuple-element.14), channel_id=1, source_target_pairs={{0,1},{1,0},{2,3},{3,2},{4,5},{5,4},{6,7},{7,6},{8,9},{9,8},{10,11... | collective-permute-start | bytes 786440 | tf_op jit(solution)/shard_map/ppermute | solution.py:284
  51.6 5.8 %collective-permute-start.6 = (bf16[8,64,128]{2,1,0:T(8,128)(2,1)S(1)}, bf16[8,64,128]{2,1,0:T(8,128)(2,1)S(1)}, u32[]{:S(2)}, u32[]{:S(2)}) collective-permute-start(bf16[8,64,128]{2,1,0:T(8,128)(2,1)S(1)} %slice.41), channel_id=1, source_target_pairs={{0,2},{1,3},{2,0},{3,1},{4,6},{5,7},{6,4},{7,5},{8,10},{9,11},{10,... | collective-permute-start | bytes 393224 | tf_op jit(solution)/shard_map/ppermute | solution.py:284
  57.5 4.4 %collective-permute-start.7 = (bf16[2,64,128]{2,1,0:T(8,128)(2,1)S(1)}, bf16[2,64,128]{2,1,0:T(8,128)(2,1)S(1)}, u32[]{:S(2)}, u32[]{:S(2)}) collective-permute-start(bf16[2,64,128]{2,1,0:T(8,128)(2,1)S(1)} %get-tuple-element.17), channel_id=1, source_target_pairs={{0,4},{1,5},{2,6},{3,7},{4,0},{5,1},{6,2},{7,3},{8,12},{9,13},{10,... | collective-permute-start | bytes 98312 | tf_op jit(solution)/shard_map/ppermute | solution.py:284
  59.0 6.1 %collective-permute-start.9 = (bf16[2,64,128]{2,1,0:T(8,128)(2,1)S(1)}, bf16[2,64,128]{2,1,0:T(8,128)(2,1)S(1)}, u32[]{:S(2)}, u32[]{:S(2)}) collective-permute-start(bf16[2,64,128]{2,1,0:T(8,128)(2,1)S(1)} %get-tuple-element.18), channel_id=1, source_target_pairs={{0,12},{1,13},{2,14},{3,15},{4,8},{5,9},{6,10},{7,11},{8,4},{9,5},... | collective-permute-start | bytes 98312 | tf_op jit(solution)/shard_map/ppermute | solution.py:284
  61.4 4.8 %collective-permute-start.8 = (bf16[2,64,128]{2,1,0:T(8,128)(2,1)S(1)}, bf16[2,64,128]{2,1,0:T(8,128)(2,1)S(1)}, u32[]{:S(2)}, u32[]{:S(2)}) collective-permute-start(bf16[2,64,128]{2,1,0:T(8,128)(2,1)S(1)} %get-tuple-element.19), channel_id=1, source_target_pairs={{0,8},{1,9},{2,10},{3,11},{4,12},{5,13},{6,14},{7,15},{8,0},{9,1},... | collective-permute-start | bytes 98312 | tf_op jit(solution)/shard_map/ppermute | solution.py:284

commit v5 on v4

--- a/solution.py
+++ b/solution.py
@@ -13,8 +13,14 @@
 GRANT = 8 << 20
 
 
-def pack_kernel(owner_rounds, table_rounds, me_ref, count_ref, pair_ref, tgt_ref, occ_ref, virt_ref, *refs):
-    out_ref, ids_ref, place_ref, rows_ref = refs
+def pack_kernel(owner_rounds, table_rounds, me_ref, count_ref, *refs):
+    sources, (out_ref, ids_ref, place_ref), (rows_ref, *held, sems) = refs[:4], refs[4:7], refs[7:]
+    copies = [pltpu.make_async_copy(src, dst, sems.at[k]) for k, (src, dst) in enumerate(zip(sources, held))]
+    for copy in copies:
+        copy.start()
+    for copy in copies:
+        copy.wait()
+    pair_ref, tgt_ref, occ_ref, virt_ref = held
     lanes = out_ref.shape[2]
     half = out_ref.shape[1] // 2
     for i in range(half):
@@ -46,35 +52,46 @@
 def packed(me, basis_count, pair_atoms, chi_target, green_occ, green_virt, bs, bits):
     return pl.pallas_call(
         functools.partial(pack_kernel, sum_rounds(bits), gather_rounds(bits)),
-        in_specs=in_smem(2) + in_vmem(4),
+        in_specs=in_smem(2) + [pl.BlockSpec(memory_space=pl.ANY)] * 4,
         out_specs=in_vmem(3),
         out_shape=[
             jax.ShapeDtypeStruct((1, bs, 2 * bs), jnp.bfloat16),
             jax.ShapeDtypeStruct(pair_atoms.shape, jnp.int32),
             jax.ShapeDtypeStruct(chi_target.shape, jnp.int32),
         ],
-        scratch_shapes=[pltpu.VMEM((bs, 2 * bs), jnp.float32)],
-        compiler_params=pltpu.CompilerParams(vmem_limit_bytes=2 << 20),
+        scratch_shapes=[pltpu.VMEM((bs, 2 * bs), jnp.float32)]
+        + [pltpu.VMEM(x.shape, x.dtype) for x in (pair_atoms, chi_target, green_occ, green_virt)]
+        + [pltpu.SemaphoreType.DMA((4,))],
+        compiler_params=pltpu.CompilerParams(vmem_limit_bytes=60 << 20),
     )(me, basis_count, pair_atoms, chi_target, green_occ, green_virt)
 
 
-def relayout_kernel(part, b_ref, _, d_ref):
-    bs, aux, _ = b_ref.shape
+def relayout_kernel(part, b_hbm, *refs):
+    d_ref, b_ref, sems = refs[-3:]
+    lams, aux, width = b_ref.shape
+    bs = d_ref.shape[0] // aux
     wide = LAM * bs
+
+    def copy(i):
+        held = pl.ds(i * LAM, LAM)
+        return pltpu.make_async_copy(b_hbm.at[pl.ds(part * lams + i * LAM, LAM)], b_ref.at[held], sems.at[i])
+
+    for i in range(lams // LAM):
+        copy(i).start()
     rows = aux * aux
     row = lax.broadcasted_iota(jnp.int32, (rows, rows), 0)
     col = lax.broadcasted_iota(jnp.int32, (rows, rows), 1)
     perm = (col == (row % aux) * aux + row // aux).astype(jnp.bfloat16)
 
-    @pl.loop(0, bs // PARTS // LAM)
+    @pl.loop(0, lams // LAM)
     def _(i):
-        first = part * (bs // PARTS) + i * LAM
+        copy(i).wait()
         cols = pl.ds(pl.multiple_of(i * wide, wide), wide)
         for blk in range(bs // aux):
             pieces = []
             for p in range(aux):
                 at = (blk * aux + p) * bs
-                pieces.append(jnp.concatenate([b_ref[first + k, :, at:at + bs] for k in range(LAM)], axis=-1))
+                pieces.append(jnp.concatenate([b_ref[i * LAM + k, :, at:at + bs] for k in range(LAM)], axis=-1))
             stacked = jnp.concatenate(pieces, axis=0)
             moved = jnp.dot(perm, stacked, preferred_element_type=jnp.float32).astype(jnp.bfloat16)
             for a in range(aux):
@@ -91,18 +108,24 @@
 
 def relayout(integrals, part, after):
     bs, aux, width = integrals.shape
+    lams = bs // PARTS
+    hidden = pl.BlockSpec(memory_space=pl.ANY)
     return pl.pallas_call(
         functools.partial(relayout_kernel, part),
-        in_specs=in_vmem(1) + [pl.BlockSpec(memory_space=pl.ANY)],
+        in_specs=[hidden] * (1 + len(after)),
         out_specs=in_vmem(1)[0],
-        out_shape=jax.ShapeDtypeStruct((aux * bs, bs // PARTS * bs), jnp.bfloat16),
-        compiler_params=pltpu.CompilerParams(vmem_limit_bytes=GRANT),
+        out_shape=jax.ShapeDtypeStruct((aux * bs, lams * bs), jnp.bfloat16),
+        scratch_shapes=[
+            pltpu.VMEM((lams, aux, width), integrals.dtype),
+            pltpu.SemaphoreType.DMA((lams // LAM,)),
+        ],
+        compiler_params=pltpu.CompilerParams(vmem_limit_bytes=48 << 20),
         cost_estimate=pl.CostEstimate(
             flops=2 * bs * aux * width * 256 // PARTS,
             bytes_accessed=4 * bs * aux * width // PARTS,
             transcendentals=0,
         ),
-    )(integrals, after)
+    )(integrals, *after)
 
 
 def spread_rows(block, of_row, count, bs):
@@ -138,11 +161,18 @@
 
 
 def occ_kernel(pieces, ids_ref, *refs):
-    tables, (b_ref, o_ref) = refs[:pieces], refs[pieces:]
+    tables, (b_hbm, o_ref, b_ref, sems) = refs[:pieces], refs[pieces:]
     bs, aux, width = b_ref.shape
     half = aux // 2
-    wide = 8 * bs
+    wide = LAM * bs
     lanes = 2 * bs
+
+    def copy(j):
+        cols = pl.ds(pl.multiple_of(j * wide, wide), wide)
+        return pltpu.make_async_copy(b_hbm.at[:, :, cols], b_ref.at[:, :, cols], sems.at[j])
+
+    for j in range(width // wide):
+        copy(j).start()
     tall = bs * half
     rep_t = (
         lax.broadcasted_iota(jnp.int32, (bs, tall), 1) // half == lax.broadcasted_iota(jnp.int32, (bs, tall), 0)
@@ -155,22 +185,25 @@
     )
     occ_w = jnp.where(same, spread, 0.0).astype(jnp.bfloat16)
 
-    @pl.loop(0, width // wide)
+    low = lax.broadcasted_iota(jnp.int32, (bs // 2, half, lanes), 2) < bs
+
+    @pl.loop(0, width // wide, unroll=2)
     def _(j):
+        copy(j).wait()
         cols = pl.ds(pl.multiple_of(j * wide, wide), wide)
         block = b_ref[:, :, cols].astype(jnp.float32)
-        sides = []
         for h in range(2):
             side = block[:, h * half:(h + 1) * half, :].reshape(tall, wide).astype(jnp.bfloat16)
-            got = jnp.dot(occ_w, side, preferred_element_type=jnp.float32)
-            sides.append(got.reshape(bs, half, wide))
-        both = jnp.concatenate(sides, axis=1).astype(jnp.bfloat16)
-        for p in range(wide // bs):
-            rows = pl.ds(pl.multiple_of(j * (wide // bs * aux) + p * aux, aux), aux)
-            for q in range(bs // 2):
-                o_ref[rows, q * lanes:(q + 1) * lanes] = jnp.concatenate(
-                    [both[2 * q, :, p * bs:(p + 1) * bs], both[2 * q + 1, :, p * bs:(p + 1) * bs]], axis=-1
-                )
+            got = jnp.dot(occ_w, side, preferred_element_type=jnp.float32).reshape(bs // 2, 2, half, wide)
+            for t in range(wide // lanes):
+                even = got[:, 0, :, t * lanes:(t + 1) * lanes]
+                odd = got[:, 1, :, t * lanes:(t + 1) * lanes]
+                turned = pltpu.roll(jnp.where(low, odd, even), bs, 2)
+                tile = jnp.concatenate([jnp.where(low, even, turned), jnp.where(low, turned, odd)], axis=1)
+                tile = tile.astype(jnp.bfloat16)
+                at = h * tall + (j * (wide // bs) + 2 * t) * half
+                for q in range(bs // 2):
+                    o_ref[pl.ds(pl.multiple_of(at, aux), aux), q * lanes:(q + 1) * lanes] = tile[q]
 
 
 def chi_kernel(bs, sends, tgt_ref, o_ref, v_ref, *refs):
@@ -178,6 +211,7 @@
     out0, out1, *accs = refs
     low_acc, high_acc = accs[0], accs[-1]
     aux = o_ref.shape[0] // bs
+    half = aux // 2
     lanes = 2 * bs
     for ref in accs:
         ref[...] = jnp.zeros_like(ref)
@@ -189,7 +223,7 @@
     def scatter(n):
         for a in range(aux):
             for t in range(2):
-                value = outs[n % 2][t, pl.ds(a, bs, stride=aux), :]
+                value = outs[n % 2][t, pl.ds(a // half * (half * bs) + a % half, bs, stride=half), :]
                 first = tgt_ref[a * aux + n * 4 + 2 * t]
                 second = tgt_ref[a * aux + n * 4 + 2 * t + 1]
                 low_acc[first] += jnp.where(low, value, 0.0) if shared else value
@@ -241,10 +275,14 @@
     )(ids, *tables, *d_parts)
     occ_side = pl.pallas_call(
         functools.partial(occ_kernel, len(tables)),
-        in_specs=in_smem(1) + in_vmem(len(tables) + 1),
+        in_specs=in_smem(1) + in_vmem(len(tables)) + [pl.BlockSpec(memory_space=pl.ANY)],
         out_specs=in_vmem(1)[0],
         out_shape=side,
-        compiler_params=params,
+        scratch_shapes=[
+            pltpu.VMEM(integrals.shape, integrals.dtype),
+            pltpu.SemaphoreType.DMA((width // (LAM * bs),)),
+        ],
+        compiler_params=pltpu.CompilerParams(vmem_limit_bytes=40 << 20),
         cost_estimate=cost,
     )(ids, *tables, integrals)
     accs = 2 if blocks <= 128 else 1
@@ -288,12 +326,15 @@
         me[None].astype(jnp.int32), basis_count, pair_atoms, chi_target, green_occ, green_virt, bs, bits
     )
     rounds = gather_rounds(bits)
-    tables, after = [table], [table]
-    for shift, step in rounds:
+    tables, d_parts = [table], []
+    for k, (shift, step) in enumerate(rounds):
+        after = tables[-1:] if k else []
         table = tables[0] if len(tables) == 1 else jnp.concatenate(tables, axis=0)
+        if k and len(d_parts) == k:
+            table, d_parts[-1] = lax.optimization_barrier((table, d_parts[-1]))
         tables = [table] + [exchange(table, v << shift) for v in range(1, 1 << step)]
-        after.append(tables[-1])
-    d_parts = [relayout(integrals, i, after[max(0, i - PARTS + len(rounds))]) for i in range(PARTS)]
+        parts = [i for i in range(PARTS) if min(i, len(rounds) - 1) == k]
+        d_parts += [relayout(integrals, i, after) for i in parts]
     rounds = sum_rounds(bits)
     total, *sends = chi_blocks_of(
         ids[0], place[0], tables, integrals, d_parts, orb * CB_DEV, (1 << rounds[0][1]) - 1

time: 67.5 us -> 65.7 us (0.973)
  local copies, waits for them, and re-layouts: 7.09 us -> 0.92 us
  Pallas kernels: 32.7 us -> 38.8 us
  starting transfers between devices: 14.2 us -> 13.1 us
    unnamed x16 -> x6, local copies, waits for them, and re-layouts: 6.17 us -> 0.01 us
    pallas_call x4, Pallas kernels: 6.77 us -> 10.9 us  [relayout(): pl.pallas_call(functools.partial(relayout_kernel, part), in_specs=[hidden...]
    pallas_call x1, Pallas kernels: 9.99 us -> 11.5 us  [chi_blocks_of(): pl.pallas_call(functools.partial(occ_kernel, len(tables)), in_specs=in_sm...]
    pallas_call x1, Pallas kernels: 0.05 us -> 1.44 us  [packed(): pl.pallas_call(functools.partial(pack_kernel, sum_rounds(bits), gather_ro...]
    ppermute x10, starting transfers between devices: 14.2 us -> 13.1 us  [exchange(): return lax.ppermute(value, 'orb', [(i, i ^ flip) for i in range(orb)])]
    pallas_call x1, Pallas kernels: 12.7 us -> 11.7 us  [chi_blocks_of(): pl.pallas_call(functools.partial(chi_kernel, bs, sends), in_specs=in_smem...]
  transfers between devices with their start and end apart: 10 -> 10, of which waited for: 5 -> 6; matrix products, arithmetic and copies ran while one was open for 0% -> 0% of each run, Pallas kernels for 10% -> 17%
where the time goes in v5:
time: 65.7 us; the launch traced here: 65.4 us
  Pallas kernels  38.8 us (59%)
  starting transfers between devices  13.1 us (20%)
  waiting for transfers between devices  11.7 us (18%)
  local copies, waits for them, and re-layouts  0.92 us (1%)
  between operations  0.85 us (1%)
    ppermute x10, starting transfers between devices, exchange(): return lax.ppermute(value, 'orb', [(i, i ^ flip) for i in range(orb)])  13.1 us
    pallas_call x1, Pallas kernels, chi_blocks_of(): pl.pallas_call(functools.partial(chi_kernel, bs, sends), in_specs=in_smem...  11.7 us
    ppermute x10, waiting for transfers between devices, exchange(): return lax.ppermute(value, 'orb', [(i, i ^ flip) for i in range(orb)])  11.7 us
    pallas_call x1, Pallas kernels, chi_blocks_of(): pl.pallas_call(functools.partial(occ_kernel, len(tables)), in_specs=in_sm...  11.5 us
    pallas_call x4, Pallas kernels, relayout(): pl.pallas_call(functools.partial(relayout_kernel, part), in_specs=[hidden...  10.9 us
    pallas_call x1, Pallas kernels, chi_blocks_of(): pl.pallas_call(functools.partial(virt_kernel, bs, len(tables)), in_specs=...  3.17 us
    pallas_call x1, Pallas kernels, packed(): pl.pallas_call(functools.partial(pack_kernel, sum_rounds(bits), gather_ro...  1.44 us
  transfers between devices with their start and end apart: 10, of which 6 were waited for; matrix products, arithmetic and copies ran while one was open for 0% of the time, Pallas kernels for 17%

profile of v5, /device:TPU:0, one launch (start us, length us, event | category | flops | bytes accessed | tf_op | source)
XLA Modules:
  0.0 65.4 jit_solution(13883292369077363865)
XLA Ops:
  0.7 1.4 %shard_map.64 = (bf16[1,64,128]{2,1,0:T(8,128)(2,1)}, s32[1,2]{1,0:T(1,128)}, s32[1,256]{1,0:T(1,128)}) custom-call(s32[1]{0:T(128)} %bitcast.me_ref, s32[1]{0:T(128)S(6)} %copy.8.count_ref, s32[1,2]{1,0:T(1,128)} %refs_0_.1, s32[1,256]{1,0:T(1,128)} %refs_1_.1, bf16[1,4096]{1,0:T(2,128)(2,1)} %refs_2_.1, bf16[1,4096]{1,0:T(2,128)(2,1)} %refs_3_.1), custom_call_target="tpu_custom_call" | custom-call | tf_op jit(solution)/shard_map/pallas_call | solution.py:53
  2.1 5.1 %collective-permute-start.2 = (bf16[1,64,128]{2,1,0:T(8,128)(2,1)}, bf16[1,64,128]{2,1,0:T(8,128)(2,1)S(1)}, u32[]{:S(2)}, u32[]{:S(2)}) collective-permute-start(bf16[1,64,128]{2,1,0:T(8,128)(2,1)} %get-tuple-element.16), channel_id=1, source_target_pairs={{0,12},{1,13},{2,14},{3,15},{4,8},{5,9},{6,10},{7,11},{8,4},{9,5},... | collective-permute-start | bytes 49160 | tf_op jit(solution)/shard_map/ppermute | solution.py:322
  7.2 0.0 collective-permute-start.1
  7.2 0.6 collective-permute-start
  7.9 0.0 copy-start.2
  7.9 2.7 %shard_map.65.refs_2_ = bf16[1024,1024]{1,0:T(8,128)(2,1)S(1)} custom-call(bf16[64,16,4096]{2,1,0:T(8,128)(2,1)} %bitcast.10), custom_call_target="tpu_custom_call" | custom-call | flops 536870912 | bytes 4194304 | tf_op jit(solution)/shard_map/pallas_call | solution.py:113
  10.6 0.0 collective-permute-done.2.refs_0_
  10.6 1.4 %collective-permute-done.1 = bf16[1,64,128]{2,1,0:T(8,128)(2,1)S(1)} collective-permute-done((bf16[1,64,128]{2,1,0:T(8,128)(2,1)}, bf16[1,64,128]{2,1,0:T(8,128)(2,1)S(1)}, u32[]{:S(2)}, u32[]{:S(2)}) %collective-permute-start.1) | collective-permute-done | bytes 16416 | tf_op jit(solution)/shard_map/ppermute | solution.py:322
  12.1 0.0 collective-permute-done
  12.1 0.0 copy-done.2
  12.1 1.6 %collective-permute-start.3 = (bf16[4,64,128]{2,1,0:T(8,128)(2,1)S(1)}, bf16[4,64,128]{2,1,0:T(8,128)(2,1)S(1)}, u32[]{:S(2)}, u32[]{:S(2)}) collective-permute-start(bf16[4,64,128]{2,1,0:T(8,128)(2,1)S(1)} %pad_maximum_fusion.1), channel_id=1, source_target_pairs={{0,2},{1,3},{2,0},{3,1},{4,6},{5,7},{6,4},{7,5},{8,10},{9,11},{10,... | collective-permute-start | bytes 196616 | tf_op jit(solution)/shard_map/ppermute | solution.py:322
  13.7 2.7 %shard_map.66.refs_3_ = bf16[1024,1024]{1,0:T(8,128)(2,1)S(1)} custom-call(bf16[64,16,4096]{2,1,0:T(8,128)(2,1)} %bitcast.11, bf16[1,64,128]{2,1,0:T(8,128)(2,1)S(1)} %collective-permute-done.2.refs_0_), custom_call_target="tpu_custom_call" | custom-call | flops 536870912 | bytes 4194304 | tf_op jit(solution)/shard_map/pallas_call | solution.py:113
  16.4 0.0 collective-permute-done.3.refs_0_
  16.4 0.1 collective-permute-start.4
  16.5 2.7 %shard_map.69.refs_5_ = bf16[1024,1024]{1,0:T(8,128)(2,1)S(1)} custom-call(bf16[64,16,4096]{2,1,0:T(8,128)(2,1)} %bitcast.12, bf16[4,64,128]{2,1,0:T(8,128)(2,1)S(1)} %collective-permute-done.3.refs_0_), custom_call_target="tpu_custom_call" | custom-call | flops 536870912 | bytes 4194304 | tf_op jit(solution)/shard_map/pallas_call | solution.py:113
  19.3 0.0 copy-start.1
  19.3 2.7 %shard_map.68.refs_4_ = bf16[1024,1024]{1,0:T(8,128)(2,1)S(1)} custom-call(bf16[64,16,4096]{2,1,0:T(8,128)(2,1)} %bitcast.13, bf16[4,64,128]{2,1,0:T(8,128)(2,1)S(1)} %collective-permute-done.3.refs_0_), custom_call_target="tpu_custom_call" | custom-call | flops 536870912 | bytes 4194304 | tf_op jit(solution)/shard_map/pallas_call | solution.py:113
  22.0 0.0 collective-permute-done.4.refs_1_
  22.0 0.0 copy-done.1
  22.0 11.5 %shard_map.67.o_ref = bf16[1024,4096]{1,0:T(8,128)(2,1)S(1)} custom-call(s32[2]{0:T(128)S(1)} %bitcast.8, bf16[8,64,128]{2,1,0:T(8,128)(2,1)S(1)} %pad_maximum_fusion.refs_0_, bf16[8,64,128]{2,1,0:T(8,128)(2,1)S(1)} %collective-permute-done.4.refs_1_, bf16[64,16,4096]{2,1,0:T(8,128)(2,1)} %bitcast.14), custom_call_target="tpu_custom_call" | custom-call | flops 8589934592 | bytes 16777216 | tf_op jit(solution)/shard_map/pallas_call | solution.py:276
  33.5 0.0 copy-start
  33.5 3.2 %shard_map.70.v_ref = bf16[1024,4096]{1,0:T(8,128)(2,1)S(1)} custom-call(s32[2]{0:T(128)S(1)} %bitcast.9, bf16[8,64,128]{2,1,0:T(8,128)(2,1)S(1)} %pad_maximum_fusion.refs_0_, bf16[8,64,128]{2,1,0:T(8,128)(2,1)S(1)} %collective-permute-done.4.refs_1_, bf16[1024,1024]{1,0:T(8,128)(2,1)S(1)} %shard_map.65.refs_2_, bf16[1024,1024]{1,0:T(8,128)(2,1)S(1)} %shard_map.66.refs_3_, ...), custom_call_target="tpu_custom_call" | custom-call | flops 8589934592 | bytes 16777216 | tf_op jit(solution)/shard_map/pallas_call | solution.py:268
  36.7 0.0 copy-done
  36.7 11.7 %shard_map.71 = (f32[16,64,128]{2,1,0:T(8,128)S(1)}, bf16[16,64,128]{2,1,0:T(8,128)(2,1)S(1)}) custom-call(s32[256]{0:T(256)S(1)} %bitcast.7, bf16[1024,4096]{1,0:T(8,128)(2,1)S(1)} %shard_map.67.o_ref, bf16[1024,4096]{1,0:T(8,128)(2,1)S(1)} %shard_map.70.v_ref), custom_call_target="tpu_custom_call" | custom-call | flops 8589934592 | bytes 16777216 | tf_op jit(solution)/shard_map/pallas_call | solution.py:291
  48.5 0.6 collective-permute-start.5
  49.0 1.2 %collective-permute-done.5 = bf16[16,64,128]{2,1,0:T(8,128)(2,1)S(1)} collective-permute-done((bf16[16,64,128]{2,1,0:T(8,128)(2,1)S(1)}, bf16[16,64,128]{2,1,0:T(8,128)(2,1)S(1)}, u32[]{:S(2)}, u32[]{:S(2)}) %collective-permute-start.5) | collective-permute-done | bytes 262176 | tf_op jit(solution)/shard_map/ppermute | solution.py:322
  50.2 0.1 convert_add_fusion
  50.3 1.6 %collective-permute-start.6 = (bf16[8,64,128]{2,1,0:T(8,128)(2,1)S(1)}, bf16[8,64,128]{2,1,0:T(8,128)(2,1)S(1)}, u32[]{:S(2)}, u32[]{:S(2)}) collective-permute-start(bf16[8,64,128]{2,1,0:T(8,128)(2,1)S(1)} %slice.41), channel_id=1, source_target_pairs={{0,2},{1,3},{2,0},{3,1},{4,6},{5,7},{6,4},{7,5},{8,10},{9,11},{10,... | collective-permute-start | bytes 393224 | tf_op jit(solution)/shard_map/ppermute | solution.py:322
  51.9 4.2 %collective-permute-done.6 = bf16[8,64,128]{2,1,0:T(8,128)(2,1)S(1)} collective-permute-done((bf16[8,64,128]{2,1,0:T(8,128)(2,1)S(1)}, bf16[8,64,128]{2,1,0:T(8,128)(2,1)S(1)}, u32[]{:S(2)}, u32[]{:S(2)}) %collective-permute-start.6) | collective-permute-done | bytes 131104 | tf_op jit(solution)/shard_map/ppermute | solution.py:322
  56.2 0.1 collective-permute-start.7
  56.2 3.5 %collective-permute-start.9 = (bf16[2,64,128]{2,1,0:T(8,128)(2,1)S(1)}, bf16[2,64,128]{2,1,0:T(8,128)(2,1)S(1)}, u32[]{:S(2)}, u32[]{:S(2)}) collective-permute-start(bf16[2,64,128]{2,1,0:T(8,128)(2,1)S(1)} %get-tuple-element.26), channel_id=1, source_target_pairs={{0,12},{1,13},{2,14},{3,15},{4,8},{5,9},{6,10},{7,11},{8,4},{9,5},... | collective-permute-start | bytes 98312 | tf_op jit(solution)/shard_map/ppermute | solution.py:322
  59.7 0.0 collective-permute-start.8
  59.7 0.4 collective-permute-done.7
  60.1 2.2 %collective-permute-done.9 = bf16[2,64,128]{2,1,0:T(8,128)(2,1)S(1)} collective-permute-done((bf16[2,64,128]{2,1,0:T(8,128)(2,1)S(1)}, bf16[2,64,128]{2,1,0:T(8,128)(2,1)S(1)}, u32[]{:S(2)}, u32[]{:S(2)}) %collective-permute-start.9) | collective-permute-done | bytes 32800 | tf_op jit(solution)/shard_map/ppermute | solution.py:322
  62.3 2.2 %collective-permute-done.8 = bf16[2,64,128]{2,1,0:T(8,128)(2,1)S(1)} collective-permute-done((bf16[2,64,128]{2,1,0:T(8,128)(2,1)S(1)}, bf16[2,64,128]{2,1,0:T(8,128)(2,1)S(1)}, u32[]{:S(2)}, u32[]{:S(2)}) %collective-permute-start.8) | collective-permute-done | bytes 32800 | tf_op jit(solution)/shard_map/ppermute | solution.py:322
  64.6 0.1 reshape.6
  64.7 0.7 %reshape.7 = f32[4,4096]{1,0:T(4,128)} reshape(f32[2,2,64,64]{3,2,1,0:T(8,128)S(1)} %copy.7) | data formatting | bytes 131072 | tf_op jit(solution)/shard_map/reshape | solution.py:350
  (7 shorter events, 0.1 us)
Async XLA Ops:
  2.1 8.5 %collective-permute-start.2 = (bf16[1,64,128]{2,1,0:T(8,128)(2,1)}, bf16[1,64,128]{2,1,0:T(8,128)(2,1)S(1)}, u32[]{:S(2)}, u32[]{:S(2)}) collective-permute-start(bf16[1,64,128]{2,1,0:T(8,128)(2,1)} %get-tuple-element.16), channel_id=1, source_target_pairs={{0,12},{1,13},{2,14},{3,15},{4,8},{5,9},{6,10},{7,11},{8,4},{9,5},... | collective-permute-start | bytes 49160 | tf_op jit(solution)/shard_map/ppermute | solution.py:322
  7.2 4.8 %collective-permute-start.1 = (bf16[1,64,128]{2,1,0:T(8,128)(2,1)}, bf16[1,64,128]{2,1,0:T(8,128)(2,1)S(1)}, u32[]{:S(2)}, u32[]{:S(2)}) collective-permute-start(bf16[1,64,128]{2,1,0:T(8,128)(2,1)} %get-tuple-element.16), channel_id=1, source_target_pairs={{0,8},{1,9},{2,10},{3,11},{4,12},{5,13},{6,14},{7,15},{8,0},{9,1},... | collective-permute-start | bytes 49160 | tf_op jit(solution)/shard_map/ppermute | solution.py:322
  7.2 4.8 %collective-permute-start = (bf16[1,64,128]{2,1,0:T(8,128)(2,1)}, bf16[1,64,128]{2,1,0:T(8,128)(2,1)S(1)}, u32[]{:S(2)}, u32[]{:S(2)}) collective-permute-start(bf16[1,64,128]{2,1,0:T(8,128)(2,1)} %get-tuple-element.16), channel_id=1, source_target_pairs={{0,4},{1,5},{2,6},{3,7},{4,0},{5,1},{6,2},{7,3},{8,12},{9,13},{10,... | collective-permute-start | bytes 49160 | tf_op jit(solution)/shard_map/ppermute | solution.py:322
  7.9 4.2 %copy-start.2 = (bf16[1,64,128]{2,1,0:T(8,128)(2,1)S(1)}, bf16[1,64,128]{2,1,0:T(8,128)(2,1)}, u32[]{:S(2)}) copy-start(bf16[1,64,128]{2,1,0:T(8,128)(2,1)} %get-tuple-element.16) | copy-start | bytes 49156
  12.1 4.3 %collective-permute-start.3 = (bf16[4,64,128]{2,1,0:T(8,128)(2,1)S(1)}, bf16[4,64,128]{2,1,0:T(8,128)(2,1)S(1)}, u32[]{:S(2)}, u32[]{:S(2)}) collective-permute-start(bf16[4,64,128]{2,1,0:T(8,128)(2,1)S(1)} %pad_maximum_fusion.1), channel_id=1, source_target_pairs={{0,2},{1,3},{2,0},{3,1},{4,6},{5,7},{6,4},{7,5},{8,10},{9,11},{10,... | collective-permute-start | bytes 196616 | tf_op jit(solution)/shard_map/ppermute | solution.py:322
  16.4 5.6 %collective-permute-start.4 = (bf16[8,64,128]{2,1,0:T(8,128)(2,1)S(1)}, bf16[8,64,128]{2,1,0:T(8,128)(2,1)S(1)}, u32[]{:S(2)}, u32[]{:S(2)}) collective-permute-start(bf16[8,64,128]{2,1,0:T(8,128)(2,1)S(1)} %pad_maximum_fusion.refs_0_), channel_id=1, source_target_pairs={{0,1},{1,0},{2,3},{3,2},{4,5},{5,4},{6,7},{7,6},{8,9},{9,8},{10,11... | collective-permute-start | bytes 393224 | tf_op jit(solution)/shard_map/ppermute | solution.py:322
  19.3 2.8 %copy-start.1 = (s32[1,2]{1,0:T(1,128)S(1)}, s32[1,2]{1,0:T(1,128)}, u32[]{:S(2)}) copy-start(s32[1,2]{1,0:T(1,128)} %get-tuple-element.15) | copy-start | bytes 28
  33.5 3.2 %copy-start = (s32[1,256]{1,0:T(1,128)S(1)}, s32[1,256]{1,0:T(1,128)}, u32[]{:S(2)}) copy-start(s32[1,256]{1,0:T(1,128)} %get-tuple-element.14) | copy-start | bytes 3076
  48.5 1.7 %collective-permute-start.5 = (bf16[16,64,128]{2,1,0:T(8,128)(2,1)S(1)}, bf16[16,64,128]{2,1,0:T(8,128)(2,1)S(1)}, u32[]{:S(2)}, u32[]{:S(2)}) collective-permute-start(bf16[16,64,128]{2,1,0:T(8,128)(2,1)S(1)} %get-tuple-element.22), channel_id=1, source_target_pairs={{0,1},{1,0},{2,3},{3,2},{4,5},{5,4},{6,7},{7,6},{8,9},{9,8},{10,11... | collective-permute-start | bytes 786440 | tf_op jit(solution)/shard_map/ppermute | solution.py:322
  50.3 5.8 %collective-permute-start.6 = (bf16[8,64,128]{2,1,0:T(8,128)(2,1)S(1)}, bf16[8,64,128]{2,1,0:T(8,128)(2,1)S(1)}, u32[]{:S(2)}, u32[]{:S(2)}) collective-permute-start(bf16[8,64,128]{2,1,0:T(8,128)(2,1)S(1)} %slice.41), channel_id=1, source_target_pairs={{0,2},{1,3},{2,0},{3,1},{4,6},{5,7},{6,4},{7,5},{8,10},{9,11},{10,... | collective-permute-start | bytes 393224 | tf_op jit(solution)/shard_map/ppermute | solution.py:322
  56.2 4.0 %collective-permute-start.7 = (bf16[2,64,128]{2,1,0:T(8,128)(2,1)S(1)}, bf16[2,64,128]{2,1,0:T(8,128)(2,1)S(1)}, u32[]{:S(2)}, u32[]{:S(2)}) collective-permute-start(bf16[2,64,128]{2,1,0:T(8,128)(2,1)S(1)} %get-tuple-element.25), channel_id=1, source_target_pairs={{0,4},{1,5},{2,6},{3,7},{4,0},{5,1},{6,2},{7,3},{8,12},{9,13},{10,... | collective-permute-start | bytes 98312 | tf_op jit(solution)/shard_map/ppermute | solution.py:322
  56.2 6.1 %collective-permute-start.9 = (bf16[2,64,128]{2,1,0:T(8,128)(2,1)S(1)}, bf16[2,64,128]{2,1,0:T(8,128)(2,1)S(1)}, u32[]{:S(2)}, u32[]{:S(2)}) collective-permute-start(bf16[2,64,128]{2,1,0:T(8,128)(2,1)S(1)} %get-tuple-element.26), channel_id=1, source_target_pairs={{0,12},{1,13},{2,14},{3,15},{4,8},{5,9},{6,10},{7,11},{8,4},{9,5},... | collective-permute-start | bytes 98312 | tf_op jit(solution)/shard_map/ppermute | solution.py:322
  59.7 4.8 %collective-permute-start.8 = (bf16[2,64,128]{2,1,0:T(8,128)(2,1)S(1)}, bf16[2,64,128]{2,1,0:T(8,128)(2,1)S(1)}, u32[]{:S(2)}, u32[]{:S(2)}) collective-permute-start(bf16[2,64,128]{2,1,0:T(8,128)(2,1)S(1)} %get-tuple-element.27), channel_id=1, source_target_pairs={{0,8},{1,9},{2,10},{3,11},{4,12},{5,13},{6,14},{7,15},{8,0},{9,1},... | collective-permute-start | bytes 98312 | tf_op jit(solution)/shard_map/ppermute | solution.py:322

commit v6 on v5

--- a/solution.py
+++ b/solution.py
@@ -66,36 +66,45 @@
     )(me, basis_count, pair_atoms, chi_target, green_occ, green_virt)
 
 
+def halves_joined(one, two, low, lanes):
+    turned = pltpu.roll(jnp.where(low, two, one), lanes // 2, one.ndim - 1)
+    return jnp.where(low, one, turned), jnp.where(low, turned, two)
+
+
 def relayout_kernel(part, b_hbm, *refs):
     d_ref, b_ref, sems = refs[-3:]
-    lams, aux, width = b_ref.shape
-    bs = d_ref.shape[0] // aux
-    wide = LAM * bs
-
-    def copy(i):
-        held = pl.ds(i * LAM, LAM)
-        return pltpu.make_async_copy(b_hbm.at[pl.ds(part * lams + i * LAM, LAM)], b_ref.at[held], sems.at[i])
-
-    for i in range(lams // LAM):
-        copy(i).start()
+    tiles, lams, aux, lanes = b_ref.shape
+    per = aux // 2
+
+    def copy(c):
+        held = pl.ds(pl.multiple_of(c * lanes, lanes), lanes)
+        return pltpu.make_async_copy(b_hbm.at[pl.ds(part * lams, lams), :, held], b_ref.at[c], sems.at[c])
+
+    for c in range(tiles):
+        copy(c).start()
     rows = aux * aux
     row = lax.broadcasted_iota(jnp.int32, (rows, rows), 0)
     col = lax.broadcasted_iota(jnp.int32, (rows, rows), 1)
     perm = (col == (row % aux) * aux + row // aux).astype(jnp.bfloat16)
-
-    @pl.loop(0, lams // LAM)
-    def _(i):
-        copy(i).wait()
-        cols = pl.ds(pl.multiple_of(i * wide, wide), wide)
-        for blk in range(bs // aux):
-            pieces = []
-            for p in range(aux):
-                at = (blk * aux + p) * bs
-                pieces.append(jnp.concatenate([b_ref[i * LAM + k, :, at:at + bs] for k in range(LAM)], axis=-1))
-            stacked = jnp.concatenate(pieces, axis=0)
-            moved = jnp.dot(perm, stacked, preferred_element_type=jnp.float32).astype(jnp.bfloat16)
+    low = lax.broadcasted_iota(jnp.int32, (per, aux, lanes), 2) < lanes // 2
+
+    @pl.loop(0, tiles // per)
+    def _(blk):
+        for c in range(per):
+            copy(blk * per + c).wait()
+        held = b_ref[pl.ds(blk * per, per)].astype(jnp.float32)
+        for i in range(0, lams, LAM):
+            columns = []
+            for k in range(0, LAM, 2):
+                even, odd = halves_joined(held[:, i + k], held[:, i + k + 1], low, lanes)
+                columns.append(jnp.stack([even, odd], axis=1).reshape(rows, lanes).astype(jnp.bfloat16))
+            moved = jnp.dot(perm, jnp.concatenate(columns, axis=1), preferred_element_type=jnp.float32)
+            moved = moved.astype(jnp.bfloat16)
             for a in range(aux):
-                d_ref[a * bs + blk * aux:a * bs + (blk + 1) * aux, cols] = moved[a * aux:(a + 1) * aux]
+                for t in range(LAM // 2):
+                    d_ref[a * (tiles // per) + blk, i // 2 + t] = moved[
+                        a * aux:(a + 1) * aux, t * lanes:(t + 1) * lanes
+                    ]
 
 
 def in_vmem(count):
@@ -114,10 +123,10 @@
         functools.partial(relayout_kernel, part),
         in_specs=[hidden] * (1 + len(after)),
         out_specs=in_vmem(1)[0],
-        out_shape=jax.ShapeDtypeStruct((aux * bs, lams * bs), jnp.bfloat16),
+        out_shape=jax.ShapeDtypeStruct((bs, lams // 2, aux, 2 * bs), jnp.bfloat16),
         scratch_shapes=[
-            pltpu.VMEM((lams, aux, width), integrals.dtype),
-            pltpu.SemaphoreType.DMA((lams // LAM,)),
+            pltpu.VMEM((bs // 2, lams, aux, 2 * bs), integrals.dtype),
+            pltpu.SemaphoreType.DMA((bs // 2,)),
         ],
         compiler_params=pltpu.CompilerParams(vmem_limit_bytes=48 << 20),
         cost_estimate=pl.CostEstimate(
@@ -153,26 +162,31 @@
         lax.broadcasted_iota(jnp.int32, (wide, wide), 0) // bs == lax.broadcasted_iota(jnp.int32, (wide, wide), 1) // bs
     )
     virt_w = jnp.where(same, spread, 0.0).astype(jnp.bfloat16)
-    each = d_parts[0].shape[1]
+    blocks, each, rows, lanes = d_parts[0].shape
     for part in range(PARTS):
-        for at in range(0, each, wide):
-            got = jnp.dot(d_parts[part][:, at:at + wide], virt_w, preferred_element_type=jnp.float32)
-            v_ref[:, part * each + at:part * each + at + wide] = got.astype(jnp.bfloat16)
+        for at in range(0, each, 2):
+            block = flat(d_parts[part], slice(None), [at, at + 1])
+            got = jnp.dot(block, virt_w, preferred_element_type=jnp.float32).astype(jnp.bfloat16)
+            for t in range(2):
+                v_ref[:, part * each + at + t] = got[:, t * lanes:(t + 1) * lanes].reshape(blocks, rows, lanes)
+
+
+def flat(ref, blocks, tiles):
+    got = [ref[blocks, t] for t in tiles]
+    return jnp.concatenate([x.reshape(x.shape[0] * x.shape[1], x.shape[2]) for x in got], axis=1)
 
 
 def occ_kernel(pieces, ids_ref, *refs):
-    tables, (b_hbm, o_ref, b_ref, sems) = refs[:pieces], refs[pieces:]
-    bs, aux, width = b_ref.shape
+    tables, (b_hbm, o_ref, b_ref, sems, *results) = refs[:pieces], refs[pieces:]
+    tiles, bs, aux, lanes = b_ref.shape
     half = aux // 2
-    wide = LAM * bs
-    lanes = 2 * bs
-
-    def copy(j):
-        cols = pl.ds(pl.multiple_of(j * wide, wide), wide)
-        return pltpu.make_async_copy(b_hbm.at[:, :, cols], b_ref.at[:, :, cols], sems.at[j])
-
-    for j in range(width // wide):
-        copy(j).start()
+
+    def copy(c):
+        cols = pl.ds(pl.multiple_of(c * lanes, lanes), lanes)
+        return pltpu.make_async_copy(b_hbm.at[:, :, cols], b_ref.at[c], sems.at[c])
+
+    for c in range(tiles):
+        copy(c).start()
     tall = bs * half
     rep_t = (
         lax.broadcasted_iota(jnp.int32, (bs, tall), 1) // half == lax.broadcasted_iota(jnp.int32, (bs, tall), 0)
@@ -184,35 +198,47 @@
         == lax.broadcasted_iota(jnp.int32, (tall, tall), 1) % half
     )
     occ_w = jnp.where(same, spread, 0.0).astype(jnp.bfloat16)
-
-    low = lax.broadcasted_iota(jnp.int32, (bs // 2, half, lanes), 2) < bs
-
-    @pl.loop(0, width // wide, unroll=2)
+    low = lax.broadcasted_iota(jnp.int32, (bs // 2, half, lanes), 2) < lanes // 2
+
+    def product(j, h):
+        sides = []
+        for t in range(2):
+            block = b_ref[2 * j + t].astype(jnp.float32)[:, h * half:(h + 1) * half]
+            sides.append(block.reshape(tall, lanes).astype(jnp.bfloat16))
+        results[h][...] = jnp.dot(occ_w, jnp.concatenate(sides, axis=1), preferred_element_type=jnp.float32)
+
+    def placed(j, h):
+        for t in range(2):
+            got = results[h][:, t * lanes:(t + 1) * lanes].reshape(bs // 2, 2, half, lanes)
+            pair = halves_joined(got[:, 0], got[:, 1], low, lanes)
+            o_ref[h * tiles + 2 * j + t] = jnp.concatenate(pair, axis=1).astype(jnp.bfloat16)
+
+    def arrived(j):
+        for t in range(2):
+            copy(2 * j + t).wait()
+
+    arrived(0)
+    product(0, 0)
+    product(0, 1)
+    placed(0, 0)
+
+    @pl.loop(1, tiles // 2)
     def _(j):
-        copy(j).wait()
-        cols = pl.ds(pl.multiple_of(j * wide, wide), wide)
-        block = b_ref[:, :, cols].astype(jnp.float32)
-        for h in range(2):
-            side = block[:, h * half:(h + 1) * half, :].reshape(tall, wide).astype(jnp.bfloat16)
-            got = jnp.dot(occ_w, side, preferred_element_type=jnp.float32).reshape(bs // 2, 2, half, wide)
-            for t in range(wide // lanes):
-                even = got[:, 0, :, t * lanes:(t + 1) * lanes]
-                odd = got[:, 1, :, t * lanes:(t + 1) * lanes]
-                turned = pltpu.roll(jnp.where(low, odd, even), bs, 2)
-                tile = jnp.concatenate([jnp.where(low, even, turned), jnp.where(low, turned, odd)], axis=1)
-                tile = tile.astype(jnp.bfloat16)
-                at = h * tall + (j * (wide // bs) + 2 * t) * half
-                for q in range(bs // 2):
-                    o_ref[pl.ds(pl.multiple_of(at, aux), aux), q * lanes:(q + 1) * lanes] = tile[q]
+        arrived(j)
+        placed(j - 1, 1)
+        product(j, 0)
+        placed(j, 0)
+        product(j, 1)
+
+    placed(tiles // 2 - 1, 1)
 
 
 def chi_kernel(bs, sends, tgt_ref, o_ref, v_ref, *refs):
     keep_ref, send_refs, refs = refs[0], refs[1:1 + sends], refs[1 + sends:]
     out0, out1, *accs = refs
     low_acc, high_acc = accs[0], accs[-1]
-    aux = o_ref.shape[0] // bs
+    tiles, aux, lanes = o_ref.shape[1:]
     half = aux // 2
-    lanes = 2 * bs
     for ref in accs:
         ref[...] = jnp.zeros_like(ref)
     low = lax.broadcasted_iota(jnp.int32, (bs, lanes), 1) < bs
@@ -233,8 +259,8 @@
         if n:
             scatter(n - 1)
         got = lax.dot_general(
-            o_ref[...],
-            v_ref[n * group:(n + 1) * group, :],
+            flat(o_ref, slice(None), range(tiles)),
+            flat(v_ref, slice(n * group // aux, (n + 1) * group // aux), range(tiles)),
             (((1,), (1,)), ((), ())),
             preferred_element_type=jnp.float32,
         )
@@ -262,7 +288,7 @@
 def chi_blocks_of(ids, targets, tables, integrals, d_parts, blocks, sends):
     bs, aux, width = integrals.shape
     pairs = blocks // 2 // (sends + 1)
-    side = jax.ShapeDtypeStruct((aux * bs, width), jnp.bfloat16)
+    side = jax.ShapeDtypeStruct((bs, bs // 2, aux, 2 * bs), jnp.bfloat16)
     params = pltpu.CompilerParams(vmem_limit_bytes=GRANT)
     cost = pl.CostEstimate(flops=2 * (aux * bs) ** 2 * width, bytes_accessed=4 * aux * bs * width, transcendentals=0)
     virt_side = pl.pallas_call(
@@ -279,9 +305,10 @@
         out_specs=in_vmem(1)[0],
         out_shape=side,
         scratch_shapes=[
-            pltpu.VMEM(integrals.shape, integrals.dtype),
-            pltpu.SemaphoreType.DMA((width // (LAM * bs),)),
-        ],
+            pltpu.VMEM((bs // 2, bs, aux, 2 * bs), integrals.dtype),
+            pltpu.SemaphoreType.DMA((bs // 2,)),
+        ]
+        + [pltpu.VMEM((bs * aux // 2, 4 * bs), jnp.float32)] * 2,
         compiler_params=pltpu.CompilerParams(vmem_limit_bytes=40 << 20),
         cost_estimate=cost,
     )(ids, *tables, integrals)

time: 65.7 us -> 65.4 us (level)
    pallas_call x1, Pallas kernels: 11.5 us -> 10.4 us  [chi_blocks_of(): pl.pallas_call(functools.partial(occ_kernel, len(tables)), in_specs=in_sm...]
    pallas_call x4, Pallas kernels: 10.9 us -> 11.8 us  [relayout(): pl.pallas_call(functools.partial(relayout_kernel, part), in_specs=[hidden...]
  transfers between devices with their start and end apart: 10 -> 10, of which waited for: 6 -> 6; matrix products, arithmetic and copies ran while one was open for 0% -> 0% of each run, Pallas kernels for 17% -> 18%
where the time goes in v6:
time: 65.4 us; the launch traced here: 65 us
  Pallas kernels  38.5 us (59%)
  starting transfers between devices  12.9 us (20%)
  waiting for transfers between devices  11.7 us (18%)
  local copies, waits for them, and re-layouts  0.92 us (1%)
  between operations  0.85 us (1%)
    ppermute x10, starting transfers between devices, exchange(): return lax.ppermute(value, 'orb', [(i, i ^ flip) for i in range(orb)])  12.9 us
    pallas_call x4, Pallas kernels, relayout(): pl.pallas_call(functools.partial(relayout_kernel, part), in_specs=[hidden...  11.8 us
    pallas_call x1, Pallas kernels, chi_blocks_of(): pl.pallas_call(functools.partial(chi_kernel, bs, sends), in_specs=in_smem...  11.7 us
    ppermute x10, waiting for transfers between devices, exchange(): return lax.ppermute(value, 'orb', [(i, i ^ flip) for i in range(orb)])  11.7 us
    pallas_call x1, Pallas kernels, chi_blocks_of(): pl.pallas_call(functools.partial(occ_kernel, len(tables)), in_specs=in_sm...  10.4 us
    pallas_call x1, Pallas kernels, chi_blocks_of(): pl.pallas_call(functools.partial(virt_kernel, bs, len(tables)), in_specs=...  3.17 us
    pallas_call x1, Pallas kernels, packed(): pl.pallas_call(functools.partial(pack_kernel, sum_rounds(bits), gather_ro...  1.44 us
  transfers between devices with their start and end apart: 10, of which 6 were waited for; matrix products, arithmetic and copies ran while one was open for 0% of the time, Pallas kernels for 18%

profile of v6, /device:TPU:0, one launch (start us, length us, event | category | flops | bytes accessed | tf_op | source)
XLA Modules:
  0.0 65.0 jit_solution(9707718762584680212)
XLA Ops:
  0.7 1.4 %shard_map.64 = (bf16[1,64,128]{2,1,0:T(8,128)(2,1)}, s32[1,2]{1,0:T(1,128)}, s32[1,256]{1,0:T(1,128)}) custom-call(s32[1]{0:T(128)} %bitcast.me_ref, s32[1]{0:T(128)S(6)} %copy.8.count_ref, s32[1,2]{1,0:T(1,128)} %refs_0_.1, s32[1,256]{1,0:T(1,128)} %refs_1_.1, bf16[1,4096]{1,0:T(2,128)(2,1)} %refs_2_.1, bf16[1,4096]{1,0:T(2,128)(2,1)} %refs_3_.1), custom_call_target="tpu_custom_call" | custom-call | tf_op jit(solution)/shard_map/pallas_call | solution.py:53
  2.1 5.1 %collective-permute-start.2 = (bf16[1,64,128]{2,1,0:T(8,128)(2,1)}, bf16[1,64,128]{2,1,0:T(8,128)(2,1)S(1)}, u32[]{:S(2)}, u32[]{:S(2)}) collective-permute-start(bf16[1,64,128]{2,1,0:T(8,128)(2,1)} %get-tuple-element.16), channel_id=1, source_target_pairs={{0,12},{1,13},{2,14},{3,15},{4,8},{5,9},{6,10},{7,11},{8,4},{9,5},... | collective-permute-start | bytes 49160 | tf_op jit(solution)/shard_map/ppermute | solution.py:349
  7.2 0.0 collective-permute-start.1
  7.2 0.6 collective-permute-start
  7.9 0.0 copy-start.2
  7.9 3.0 %shard_map.65.refs_2_ = bf16[64,8,16,128]{3,2,1,0:T(8,128)(2,1)S(1)} custom-call(bf16[64,16,4096]{2,1,0:T(8,128)(2,1)} %bitcast.10), custom_call_target="tpu_custom_call" | custom-call | flops 536870912 | bytes 4194304 | tf_op jit(solution)/shard_map/pallas_call | solution.py:122
  10.8 0.0 collective-permute-done.2.refs_0_
  10.8 1.2 %collective-permute-done.1 = bf16[1,64,128]{2,1,0:T(8,128)(2,1)S(1)} collective-permute-done((bf16[1,64,128]{2,1,0:T(8,128)(2,1)}, bf16[1,64,128]{2,1,0:T(8,128)(2,1)S(1)}, u32[]{:S(2)}, u32[]{:S(2)}) %collective-permute-start.1) | collective-permute-done | bytes 16416 | tf_op jit(solution)/shard_map/ppermute | solution.py:349
  12.1 0.0 collective-permute-done
  12.1 0.0 copy-done.2
  12.1 1.6 %collective-permute-start.3 = (bf16[4,64,128]{2,1,0:T(8,128)(2,1)S(1)}, bf16[4,64,128]{2,1,0:T(8,128)(2,1)S(1)}, u32[]{:S(2)}, u32[]{:S(2)}) collective-permute-start(bf16[4,64,128]{2,1,0:T(8,128)(2,1)S(1)} %pad_maximum_fusion.1), channel_id=1, source_target_pairs={{0,2},{1,3},{2,0},{3,1},{4,6},{5,7},{6,4},{7,5},{8,10},{9,11},{10,... | collective-permute-start | bytes 196616 | tf_op jit(solution)/shard_map/ppermute | solution.py:349
  13.7 2.9 %shard_map.66.refs_3_ = bf16[64,8,16,128]{3,2,1,0:T(8,128)(2,1)S(1)} custom-call(bf16[64,16,4096]{2,1,0:T(8,128)(2,1)} %bitcast.11, bf16[1,64,128]{2,1,0:T(8,128)(2,1)S(1)} %collective-permute-done.2.refs_0_), custom_call_target="tpu_custom_call" | custom-call | flops 536870912 | bytes 4194304 | tf_op jit(solution)/shard_map/pallas_call | solution.py:122
  16.6 0.0 collective-permute-done.3.refs_0_
  16.7 0.1 collective-permute-start.4
  16.7 2.9 %shard_map.69.refs_5_ = bf16[64,8,16,128]{3,2,1,0:T(8,128)(2,1)S(1)} custom-call(bf16[64,16,4096]{2,1,0:T(8,128)(2,1)} %bitcast.12, bf16[4,64,128]{2,1,0:T(8,128)(2,1)S(1)} %collective-permute-done.3.refs_0_), custom_call_target="tpu_custom_call" | custom-call | flops 536870912 | bytes 4194304 | tf_op jit(solution)/shard_map/pallas_call | solution.py:122
  19.7 0.0 copy-start.1
  19.7 2.9 %shard_map.68.refs_4_ = bf16[64,8,16,128]{3,2,1,0:T(8,128)(2,1)S(1)} custom-call(bf16[64,16,4096]{2,1,0:T(8,128)(2,1)} %bitcast.13, bf16[4,64,128]{2,1,0:T(8,128)(2,1)S(1)} %collective-permute-done.3.refs_0_), custom_call_target="tpu_custom_call" | custom-call | flops 536870912 | bytes 4194304 | tf_op jit(solution)/shard_map/pallas_call | solution.py:122
  22.6 0.0 collective-permute-done.4.refs_1_
  22.7 0.0 copy-done.1
  22.7 10.4 %shard_map.67.o_ref = bf16[64,32,16,128]{3,2,1,0:T(8,128)(2,1)S(1)} custom-call(s32[2]{0:T(128)S(1)} %bitcast.8, bf16[8,64,128]{2,1,0:T(8,128)(2,1)S(1)} %pad_maximum_fusion.refs_0_, bf16[8,64,128]{2,1,0:T(8,128)(2,1)S(1)} %collective-permute-done.4.refs_1_, bf16[64,16,4096]{2,1,0:T(8,128)(2,1)} %bitcast.14), custom_call_target="tpu_custom_call" | custom-call | flops 8589934592 | bytes 16777216 | tf_op jit(solution)/shard_map/pallas_call | solution.py:302
  33.1 0.0 copy-start
  33.1 3.2 %shard_map.70.v_ref = bf16[64,32,16,128]{3,2,1,0:T(8,128)(2,1)S(1)} custom-call(s32[2]{0:T(128)S(1)} %bitcast.9, bf16[8,64,128]{2,1,0:T(8,128)(2,1)S(1)} %pad_maximum_fusion.refs_0_, bf16[8,64,128]{2,1,0:T(8,128)(2,1)S(1)} %collective-permute-done.4.refs_1_, bf16[64,8,16,128]{3,2,1,0:T(8,128)(2,1)S(1)} %shard_map.65.refs_2_, ...), custom_call_target="tpu_custom_call" | custom-call | flops 8589934592 | bytes 16777216 | tf_op jit(solution)/shard_map/pallas_call | solution.py:294
  36.3 0.0 copy-done
  36.3 11.7 %shard_map.71 = (f32[16,64,128]{2,1,0:T(8,128)S(1)}, bf16[16,64,128]{2,1,0:T(8,128)(2,1)S(1)}) custom-call(s32[256]{0:T(256)S(1)} %bitcast.7, bf16[64,32,16,128]{3,2,1,0:T(8,128)(2,1)S(1)} %shard_map.67.o_ref, bf16[64,32,16,128]{3,2,1,0:T(8,128)(2,1)S(1)} %shard_map.70.v_ref), custom_call_target="tpu_custom_call" | custom-call | flops 8589934592 | bytes 16777216 | tf_op jit(solution)/shard_map/pallas_call | solution.py:318
  48.0 0.6 collective-permute-start.5
  48.5 1.2 %collective-permute-done.5 = bf16[16,64,128]{2,1,0:T(8,128)(2,1)S(1)} collective-permute-done((bf16[16,64,128]{2,1,0:T(8,128)(2,1)S(1)}, bf16[16,64,128]{2,1,0:T(8,128)(2,1)S(1)}, u32[]{:S(2)}, u32[]{:S(2)}) %collective-permute-start.5) | collective-permute-done | bytes 262176 | tf_op jit(solution)/shard_map/ppermute | solution.py:349
  49.7 0.1 convert_add_fusion
  49.8 1.4 %collective-permute-start.6 = (bf16[8,64,128]{2,1,0:T(8,128)(2,1)S(1)}, bf16[8,64,128]{2,1,0:T(8,128)(2,1)S(1)}, u32[]{:S(2)}, u32[]{:S(2)}) collective-permute-start(bf16[8,64,128]{2,1,0:T(8,128)(2,1)S(1)} %slice.41), channel_id=1, source_target_pairs={{0,2},{1,3},{2,0},{3,1},{4,6},{5,7},{6,4},{7,5},{8,10},{9,11},{10,... | collective-permute-start | bytes 393224 | tf_op jit(solution)/shard_map/ppermute | solution.py:349
  51.2 4.5 %collective-permute-done.6 = bf16[8,64,128]{2,1,0:T(8,128)(2,1)S(1)} collective-permute-done((bf16[8,64,128]{2,1,0:T(8,128)(2,1)S(1)}, bf16[8,64,128]{2,1,0:T(8,128)(2,1)S(1)}, u32[]{:S(2)}, u32[]{:S(2)}) %collective-permute-start.6) | collective-permute-done | bytes 131104 | tf_op jit(solution)/shard_map/ppermute | solution.py:349
  55.7 0.3 collective-permute-start.7
  56.0 3.3 %collective-permute-start.9 = (bf16[2,64,128]{2,1,0:T(8,128)(2,1)S(1)}, bf16[2,64,128]{2,1,0:T(8,128)(2,1)S(1)}, u32[]{:S(2)}, u32[]{:S(2)}) collective-permute-start(bf16[2,64,128]{2,1,0:T(8,128)(2,1)S(1)} %get-tuple-element.26), channel_id=1, source_target_pairs={{0,12},{1,13},{2,14},{3,15},{4,8},{5,9},{6,10},{7,11},{8,4},{9,5},... | collective-permute-start | bytes 98312 | tf_op jit(solution)/shard_map/ppermute | solution.py:349
  59.3 0.0 collective-permute-start.8
  59.3 0.4 collective-permute-done.7
  59.7 2.3 %collective-permute-done.9 = bf16[2,64,128]{2,1,0:T(8,128)(2,1)S(1)} collective-permute-done((bf16[2,64,128]{2,1,0:T(8,128)(2,1)S(1)}, bf16[2,64,128]{2,1,0:T(8,128)(2,1)S(1)}, u32[]{:S(2)}, u32[]{:S(2)}) %collective-permute-start.9) | collective-permute-done | bytes 32800 | tf_op jit(solution)/shard_map/ppermute | solution.py:349
  62.0 2.1 %collective-permute-done.8 = bf16[2,64,128]{2,1,0:T(8,128)(2,1)S(1)} collective-permute-done((bf16[2,64,128]{2,1,0:T(8,128)(2,1)S(1)}, bf16[2,64,128]{2,1,0:T(8,128)(2,1)S(1)}, u32[]{:S(2)}, u32[]{:S(2)}) %collective-permute-start.8) | collective-permute-done | bytes 32800 | tf_op jit(solution)/shard_map/ppermute | solution.py:349
  64.1 0.1 reshape.6
  64.3 0.7 %reshape.7 = f32[4,4096]{1,0:T(4,128)} reshape(f32[2,2,64,64]{3,2,1,0:T(8,128)S(1)} %copy.7) | data formatting | bytes 131072 | tf_op jit(solution)/shard_map/reshape | solution.py:377
  (7 shorter events, 0.1 us)
Async XLA Ops:
  2.1 8.7 %collective-permute-start.2 = (bf16[1,64,128]{2,1,0:T(8,128)(2,1)}, bf16[1,64,128]{2,1,0:T(8,128)(2,1)S(1)}, u32[]{:S(2)}, u32[]{:S(2)}) collective-permute-start(bf16[1,64,128]{2,1,0:T(8,128)(2,1)} %get-tuple-element.16), channel_id=1, source_target_pairs={{0,12},{1,13},{2,14},{3,15},{4,8},{5,9},{6,10},{7,11},{8,4},{9,5},... | collective-permute-start | bytes 49160 | tf_op jit(solution)/shard_map/ppermute | solution.py:349
  7.2 4.8 %collective-permute-start.1 = (bf16[1,64,128]{2,1,0:T(8,128)(2,1)}, bf16[1,64,128]{2,1,0:T(8,128)(2,1)S(1)}, u32[]{:S(2)}, u32[]{:S(2)}) collective-permute-start(bf16[1,64,128]{2,1,0:T(8,128)(2,1)} %get-tuple-element.16), channel_id=1, source_target_pairs={{0,8},{1,9},{2,10},{3,11},{4,12},{5,13},{6,14},{7,15},{8,0},{9,1},... | collective-permute-start | bytes 49160 | tf_op jit(solution)/shard_map/ppermute | solution.py:349
  7.2 4.8 %collective-permute-start = (bf16[1,64,128]{2,1,0:T(8,128)(2,1)}, bf16[1,64,128]{2,1,0:T(8,128)(2,1)S(1)}, u32[]{:S(2)}, u32[]{:S(2)}) collective-permute-start(bf16[1,64,128]{2,1,0:T(8,128)(2,1)} %get-tuple-element.16), channel_id=1, source_target_pairs={{0,4},{1,5},{2,6},{3,7},{4,0},{5,1},{6,2},{7,3},{8,12},{9,13},{10,... | collective-permute-start | bytes 49160 | tf_op jit(solution)/shard_map/ppermute | solution.py:349
  7.9 4.2 %copy-start.2 = (bf16[1,64,128]{2,1,0:T(8,128)(2,1)S(1)}, bf16[1,64,128]{2,1,0:T(8,128)(2,1)}, u32[]{:S(2)}) copy-start(bf16[1,64,128]{2,1,0:T(8,128)(2,1)} %get-tuple-element.16) | copy-start | bytes 49156
  12.1 4.5 %collective-permute-start.3 = (bf16[4,64,128]{2,1,0:T(8,128)(2,1)S(1)}, bf16[4,64,128]{2,1,0:T(8,128)(2,1)S(1)}, u32[]{:S(2)}, u32[]{:S(2)}) collective-permute-start(bf16[4,64,128]{2,1,0:T(8,128)(2,1)S(1)} %pad_maximum_fusion.1), channel_id=1, source_target_pairs={{0,2},{1,3},{2,0},{3,1},{4,6},{5,7},{6,4},{7,5},{8,10},{9,11},{10,... | collective-permute-start | bytes 196616 | tf_op jit(solution)/shard_map/ppermute | solution.py:349
  16.7 6.0 %collective-permute-start.4 = (bf16[8,64,128]{2,1,0:T(8,128)(2,1)S(1)}, bf16[8,64,128]{2,1,0:T(8,128)(2,1)S(1)}, u32[]{:S(2)}, u32[]{:S(2)}) collective-permute-start(bf16[8,64,128]{2,1,0:T(8,128)(2,1)S(1)} %pad_maximum_fusion.refs_0_), channel_id=1, source_target_pairs={{0,1},{1,0},{2,3},{3,2},{4,5},{5,4},{6,7},{7,6},{8,9},{9,8},{10,11... | collective-permute-start | bytes 393224 | tf_op jit(solution)/shard_map/ppermute | solution.py:349
  19.7 3.0 %copy-start.1 = (s32[1,2]{1,0:T(1,128)S(1)}, s32[1,2]{1,0:T(1,128)}, u32[]{:S(2)}) copy-start(s32[1,2]{1,0:T(1,128)} %get-tuple-element.15) | copy-start | bytes 28
  33.1 3.2 %copy-start = (s32[1,256]{1,0:T(1,128)S(1)}, s32[1,256]{1,0:T(1,128)}, u32[]{:S(2)}) copy-start(s32[1,256]{1,0:T(1,128)} %get-tuple-element.14) | copy-start | bytes 3076
  48.0 1.7 %collective-permute-start.5 = (bf16[16,64,128]{2,1,0:T(8,128)(2,1)S(1)}, bf16[16,64,128]{2,1,0:T(8,128)(2,1)S(1)}, u32[]{:S(2)}, u32[]{:S(2)}) collective-permute-start(bf16[16,64,128]{2,1,0:T(8,128)(2,1)S(1)} %get-tuple-element.22), channel_id=1, source_target_pairs={{0,1},{1,0},{2,3},{3,2},{4,5},{5,4},{6,7},{7,6},{8,9},{9,8},{10,11... | collective-permute-start | bytes 786440 | tf_op jit(solution)/shard_map/ppermute | solution.py:349
  49.8 5.8 %collective-permute-start.6 = (bf16[8,64,128]{2,1,0:T(8,128)(2,1)S(1)}, bf16[8,64,128]{2,1,0:T(8,128)(2,1)S(1)}, u32[]{:S(2)}, u32[]{:S(2)}) collective-permute-start(bf16[8,64,128]{2,1,0:T(8,128)(2,1)S(1)} %slice.41), channel_id=1, source_target_pairs={{0,2},{1,3},{2,0},{3,1},{4,6},{5,7},{6,4},{7,5},{8,10},{9,11},{10,... | collective-permute-start | bytes 393224 | tf_op jit(solution)/shard_map/ppermute | solution.py:349
  55.7 4.0 %collective-permute-start.7 = (bf16[2,64,128]{2,1,0:T(8,128)(2,1)S(1)}, bf16[2,64,128]{2,1,0:T(8,128)(2,1)S(1)}, u32[]{:S(2)}, u32[]{:S(2)}) collective-permute-start(bf16[2,64,128]{2,1,0:T(8,128)(2,1)S(1)} %get-tuple-element.25), channel_id=1, source_target_pairs={{0,4},{1,5},{2,6},{3,7},{4,0},{5,1},{6,2},{7,3},{8,12},{9,13},{10,... | collective-permute-start | bytes 98312 | tf_op jit(solution)/shard_map/ppermute | solution.py:349
  56.0 6.1 %collective-permute-start.9 = (bf16[2,64,128]{2,1,0:T(8,128)(2,1)S(1)}, bf16[2,64,128]{2,1,0:T(8,128)(2,1)S(1)}, u32[]{:S(2)}, u32[]{:S(2)}) collective-permute-start(bf16[2,64,128]{2,1,0:T(8,128)(2,1)S(1)} %get-tuple-element.26), channel_id=1, source_target_pairs={{0,12},{1,13},{2,14},{3,15},{4,8},{5,9},{6,10},{7,11},{8,4},{9,5},... | collective-permute-start | bytes 98312 | tf_op jit(solution)/shard_map/ppermute | solution.py:349
  59.3 4.8 %collective-permute-start.8 = (bf16[2,64,128]{2,1,0:T(8,128)(2,1)S(1)}, bf16[2,64,128]{2,1,0:T(8,128)(2,1)S(1)}, u32[]{:S(2)}, u32[]{:S(2)}) collective-permute-start(bf16[2,64,128]{2,1,0:T(8,128)(2,1)S(1)} %get-tuple-element.27), channel_id=1, source_target_pairs={{0,8},{1,9},{2,10},{3,11},{4,12},{5,13},{6,14},{7,15},{8,0},{9,1},... | collective-permute-start | bytes 98312 | tf_op jit(solution)/shard_map/ppermute | solution.py:349

commit v7 on v6

--- a/solution.py
+++ b/solution.py
@@ -13,7 +13,7 @@
 GRANT = 8 << 20
 
 
-def pack_kernel(owner_rounds, table_rounds, me_ref, count_ref, *refs):
+def pack_kernel(place_rounds, table_rounds, me_ref, count_ref, *refs):
     sources, (out_ref, ids_ref, place_ref), (rows_ref, *held, sems) = refs[:4], refs[4:7], refs[7:]
     copies = [pltpu.make_async_copy(src, dst, sems.at[k]) for k, (src, dst) in enumerate(zip(sources, held))]
     for copy in copies:
@@ -44,14 +44,14 @@
     targets = tgt_ref[...]
     rel = (targets // CB_DEV) ^ me
     place = jnp.zeros_like(targets)
-    for shift, step in owner_rounds:
+    for shift, step in place_rounds:
         place = (place << step) | ((rel >> shift) & ((1 << step) - 1))
     place_ref[...] = place * CB_DEV + targets % CB_DEV
 
 
 def packed(me, basis_count, pair_atoms, chi_target, green_occ, green_virt, bs, bits):
     return pl.pallas_call(
-        functools.partial(pack_kernel, sum_rounds(bits), gather_rounds(bits)),
+        functools.partial(pack_kernel, owner_rounds(bits), gather_rounds(bits)),
         in_specs=in_smem(2) + [pl.BlockSpec(memory_space=pl.ANY)] * 4,
         out_specs=in_vmem(3),
         out_shape=[
@@ -72,39 +72,36 @@
 
 
 def relayout_kernel(part, b_hbm, *refs):
-    d_ref, b_ref, sems = refs[-3:]
-    tiles, lams, aux, lanes = b_ref.shape
-    per = aux // 2
-
-    def copy(c):
-        held = pl.ds(pl.multiple_of(c * lanes, lanes), lanes)
-        return pltpu.make_async_copy(b_hbm.at[pl.ds(part * lams, lams), :, held], b_ref.at[c], sems.at[c])
-
-    for c in range(tiles):
-        copy(c).start()
-    rows = aux * aux
-    row = lax.broadcasted_iota(jnp.int32, (rows, rows), 0)
-    col = lax.broadcasted_iota(jnp.int32, (rows, rows), 1)
-    perm = (col == (row % aux) * aux + row // aux).astype(jnp.bfloat16)
-    low = lax.broadcasted_iota(jnp.int32, (per, aux, lanes), 2) < lanes // 2
-
-    @pl.loop(0, tiles // per)
-    def _(blk):
-        for c in range(per):
-            copy(blk * per + c).wait()
-        held = b_ref[pl.ds(blk * per, per)].astype(jnp.float32)
-        for i in range(0, lams, LAM):
-            columns = []
-            for k in range(0, LAM, 2):
-                even, odd = halves_joined(held[:, i + k], held[:, i + k + 1], low, lanes)
-                columns.append(jnp.stack([even, odd], axis=1).reshape(rows, lanes).astype(jnp.bfloat16))
-            moved = jnp.dot(perm, jnp.concatenate(columns, axis=1), preferred_element_type=jnp.float32)
-            moved = moved.astype(jnp.bfloat16)
-            for a in range(aux):
-                for t in range(LAM // 2):
-                    d_ref[a * (tiles // per) + blk, i // 2 + t] = moved[
-                        a * aux:(a + 1) * aux, t * lanes:(t + 1) * lanes
-                    ]
+    d_ref, b_ref, sems, *turns = refs[-5:]
+    lams, aux, width = b_ref.shape
+    lanes = d_ref.shape[3]
+    tiles, half, bs = width // lanes, aux // 2, lanes // 2
+
+    def copy(i):
+        held = pl.ds(2 * i, 2)
+        return pltpu.make_async_copy(b_hbm.at[pl.ds(part * lams + 2 * i, 2)], b_ref.at[held], sems.at[i])
+
+    for i in range(lams // 2):
+        copy(i).start()
+    low = lax.broadcasted_iota(jnp.int32, (aux, lanes), 1) < bs
+
+    def turned(i, turn):
+        for c in range(tiles):
+            one, two = [b_ref[2 * i + k, :, c * lanes:(c + 1) * lanes].astype(jnp.float32) for k in range(2)]
+            for k, joined in enumerate(halves_joined(one, two, low, lanes)):
+                for h in range(2):
+                    at = (h * bs + 2 * c + k) * half
+                    turn[at:at + half, :] = joined[h * half:(h + 1) * half]
+        for a in range(aux):
+            rows = turn[pl.ds(a // half * (bs * half) + a % half, bs, stride=half), :].astype(jnp.bfloat16)
+            d_ref[a * (bs // aux):(a + 1) * (bs // aux), i] = rows.reshape(bs // aux, aux, lanes)
+
+    @pl.loop(0, lams // 4)
+    def _(i):
+        for k, turn in enumerate(turns):
+            copy(2 * i + k).wait()
+        for k, turn in enumerate(turns):
+            turned(2 * i + k, turn)
 
 
 def in_vmem(count):
@@ -125,9 +122,10 @@
         out_specs=in_vmem(1)[0],
         out_shape=jax.ShapeDtypeStruct((bs, lams // 2, aux, 2 * bs), jnp.bfloat16),
         scratch_shapes=[
-            pltpu.VMEM((bs // 2, lams, aux, 2 * bs), integrals.dtype),
-            pltpu.SemaphoreType.DMA((bs // 2,)),
-        ],
+            pltpu.VMEM((lams, aux, width), integrals.dtype),
+            pltpu.SemaphoreType.DMA((lams // 2,)),
+        ]
+        + [pltpu.VMEM((aux * bs, 2 * bs), jnp.float32)] * 2,
         compiler_params=pltpu.CompilerParams(vmem_limit_bytes=48 << 20),
         cost_estimate=pl.CostEstimate(
             flops=2 * bs * aux * width * 256 // PARTS,
@@ -178,15 +176,18 @@
 
 def occ_kernel(pieces, ids_ref, *refs):
     tables, (b_hbm, o_ref, b_ref, sems, *results) = refs[:pieces], refs[pieces:]
-    tiles, bs, aux, lanes = b_ref.shape
-    half = aux // 2
-
-    def copy(c):
-        cols = pl.ds(pl.multiple_of(c * lanes, lanes), lanes)
-        return pltpu.make_async_copy(b_hbm.at[:, :, cols], b_ref.at[c], sems.at[c])
-
-    for c in range(tiles):
-        copy(c).start()
+    bs, aux, width = b_ref.shape
+    half, lanes = aux // 2, 2 * bs
+    tiles = width // lanes
+
+    def columns(j):
+        return pl.ds(pl.multiple_of(j * (2 * lanes), 2 * lanes), 2 * lanes)
+
+    def copy(j):
+        return pltpu.make_async_copy(b_hbm.at[:, :, columns(j)], b_ref.at[:, :, columns(j)], sems.at[j])
+
+    for j in range(tiles // 2):
+        copy(j).start()
     tall = bs * half
     rep_t = (
         lax.broadcasted_iota(jnp.int32, (bs, tall), 1) // half == lax.broadcasted_iota(jnp.int32, (bs, tall), 0)
@@ -201,11 +202,9 @@
     low = lax.broadcasted_iota(jnp.int32, (bs // 2, half, lanes), 2) < lanes // 2
 
     def product(j, h):
-        sides = []
-        for t in range(2):
-            block = b_ref[2 * j + t].astype(jnp.float32)[:, h * half:(h + 1) * half]
-            sides.append(block.reshape(tall, lanes).astype(jnp.bfloat16))
-        results[h][...] = jnp.dot(occ_w, jnp.concatenate(sides, axis=1), preferred_element_type=jnp.float32)
+        block = b_ref[:, :, columns(j)].astype(jnp.float32)[:, h * half:(h + 1) * half]
+        side = block.reshape(tall, 2 * lanes).astype(jnp.bfloat16)
+        results[h][...] = jnp.dot(occ_w, side, preferred_element_type=jnp.float32)
 
     def placed(j, h):
         for t in range(2):
@@ -213,18 +212,14 @@
             pair = halves_joined(got[:, 0], got[:, 1], low, lanes)
             o_ref[h * tiles + 2 * j + t] = jnp.concatenate(pair, axis=1).astype(jnp.bfloat16)
 
-    def arrived(j):
-        for t in range(2):
-            copy(2 * j + t).wait()
-
-    arrived(0)
+    copy(0).wait()
     product(0, 0)
     product(0, 1)
     placed(0, 0)
 
     @pl.loop(1, tiles // 2)
     def _(j):
-        arrived(j)
+        copy(j).wait()
         placed(j - 1, 1)
         product(j, 0)
         placed(j, 0)
@@ -305,8 +300,8 @@
         out_specs=in_vmem(1)[0],
         out_shape=side,
         scratch_shapes=[
-            pltpu.VMEM((bs // 2, bs, aux, 2 * bs), integrals.dtype),
-            pltpu.SemaphoreType.DMA((bs // 2,)),
+            pltpu.VMEM(integrals.shape, integrals.dtype),
+            pltpu.SemaphoreType.DMA((bs // 4,)),
         ]
         + [pltpu.VMEM((bs * aux // 2, 4 * bs), jnp.float32)] * 2,
         compiler_params=pltpu.CompilerParams(vmem_limit_bytes=40 << 20),
@@ -328,16 +323,16 @@
 
 
 def gather_rounds(bits):
-    return [(shift, step) for shift, step in reversed(sum_rounds(bits))]
-
-
-def sum_rounds(bits):
     rounds, at = [], 0
     while at < bits:
         step = 1 if at < 2 else min(2, bits - at)
         rounds.append((at, step))
         at += step
-    return rounds
+    return rounds[::-1]
+
+
+def owner_rounds(bits):
+    return [(bit, 1) for bit in range(bits)]
 
 
 def local(orb, three_centre, green_occ, green_virt, pair_atoms, basis_count, chi_target):
@@ -362,17 +357,22 @@
         tables = [table] + [exchange(table, v << shift) for v in range(1, 1 << step)]
         parts = [i for i in range(PARTS) if min(i, len(rounds) - 1) == k]
         d_parts += [relayout(integrals, i, after) for i in parts]
-    rounds = sum_rounds(bits)
-    total, *sends = chi_blocks_of(
-        ids[0], place[0], tables, integrals, d_parts, orb * CB_DEV, (1 << rounds[0][1]) - 1
-    )
-    for k, (shift, step) in enumerate(rounds):
-        if k:
-            rest = total.shape[0] >> step
-            sends = [total[v * rest:(v + 1) * rest].astype(jnp.bfloat16) for v in range(1, 1 << step)]
-            total = total[:rest]
-        for v, send in enumerate(sends):
-            total = total + exchange(send, (v + 1) << shift).astype(jnp.float32)
+    total, send = chi_blocks_of(ids[0], place[0], tables, integrals, d_parts, orb * CB_DEV, 1)
+    total = total + exchange(send, 1).astype(jnp.float32)
+    total = total.reshape([2] * (bits - 1) + [-1, bs, 2 * bs])
+    halves = [total[..., :bs // 2, :], total[..., bs // 2:, :]]
+    todo = [list(range(1, bits)), list(range(2, bits)) + [1]]
+    left = [list(range(1, bits)) for _ in halves]
+    for k in range(bits - 1):
+        sends, keeps = [], []
+        for part, order, axes in zip(halves, todo, left):
+            axis = axes.index(order[k])
+            axes.remove(order[k])
+            keeps.append(lax.index_in_dim(part, 0, axis, keepdims=False))
+            sends.append(lax.index_in_dim(part, 1, axis, keepdims=False).astype(jnp.bfloat16))
+        came = [exchange(send, 1 << order[k]) for send, order in zip(sends, todo)]
+        halves = [keep + got.astype(jnp.float32) for keep, got in zip(keeps, came)]
+    total = jnp.concatenate(halves, axis=-2)
     total = total.reshape(CB_DEV // 2, bs, 2, bs).transpose(0, 2, 1, 3)
     return total.reshape(CB_DEV, bs * bs)
 

time: 65.4 us -> 66.5 us (1.017)
  Pallas kernels: 38.5 us -> 36.2 us
  waiting for transfers between devices: 11.7 us -> 13.6 us
  starting transfers between devices: 12.9 us -> 14.4 us
    pallas_call x4, Pallas kernels: 11.8 us -> 9.49 us  [relayout(): pl.pallas_call(functools.partial(relayout_kernel, part), in_specs=[hidden...]
    ppermute x10 -> x12, waiting for transfers between devices: 11.7 us -> 13.6 us  [exchange(): return lax.ppermute(value, 'orb', [(i, i ^ flip) for i in range(orb)])]
    ppermute x10 -> x12, starting transfers between devices: 12.9 us -> 14.4 us  [exchange(): return lax.ppermute(value, 'orb', [(i, i ^ flip) for i in range(orb)])]
  transfers between devices with their start and end apart: 10 -> 12, of which waited for: 6 -> 9; matrix products, arithmetic and copies ran while one was open for 0% -> 0% of each run, Pallas kernels for 18% -> 14%
where the time goes in v7:
time: 66.5 us; the launch traced here: 66.2 us
  Pallas kernels  36.2 us (54%)
  starting transfers between devices  14.4 us (22%)
  waiting for transfers between devices  13.6 us (20%)
  local copies, waits for them, and re-layouts  0.93 us (1%)
  between operations  0.88 us (1%)
    ppermute x12, starting transfers between devices, exchange(): return lax.ppermute(value, 'orb', [(i, i ^ flip) for i in range(orb)])  14.4 us
    ppermute x12, waiting for transfers between devices, exchange(): return lax.ppermute(value, 'orb', [(i, i ^ flip) for i in range(orb)])  13.6 us
    pallas_call x1, Pallas kernels, chi_blocks_of(): pl.pallas_call(functools.partial(chi_kernel, bs, sends), in_specs=in_smem...  11.7 us
    pallas_call x1, Pallas kernels, chi_blocks_of(): pl.pallas_call(functools.partial(occ_kernel, len(tables)), in_specs=in_sm...  10.4 us
    pallas_call x4, Pallas kernels, relayout(): pl.pallas_call(functools.partial(relayout_kernel, part), in_specs=[hidden...  9.49 us
    pallas_call x1, Pallas kernels, chi_blocks_of(): pl.pallas_call(functools.partial(virt_kernel, bs, len(tables)), in_specs=...  3.17 us
    pallas_call x1, Pallas kernels, packed(): pl.pallas_call(functools.partial(pack_kernel, owner_rounds(bits), gather_...  1.44 us
  transfers between devices with their start and end apart: 12, of which 9 were waited for; matrix products, arithmetic and copies ran while one was open for 0% of the time, Pallas kernels for 14%

profile of v7, /device:TPU:0, one launch (start us, length us, event | category | flops | bytes accessed | tf_op | source)
XLA Modules:
  0.0 66.2 jit_solution(12279957961954806687)
XLA Ops:
  0.7 1.4 %shard_map.64 = (bf16[1,64,128]{2,1,0:T(8,128)(2,1)}, s32[1,2]{1,0:T(1,128)}, s32[1,256]{1,0:T(1,128)}) custom-call(s32[1]{0:T(128)} %bitcast.me_ref, s32[1]{0:T(128)S(6)} %copy.12.count_ref, s32[1,2]{1,0:T(1,128)} %refs_0_.1, s32[1,256]{1,0:T(1,128)} %refs_1_.1, bf16[1,4096]{1,0:T(2,128)(2,1)} %refs_2_.1, bf16[1,4096]{1,0:T(2,128)(2,1)} %refs_3_.1), custom_call_target="tpu_custom_call" | custom-call | tf_op jit(solution)/shard_map/pallas_call | solution.py:53
  2.1 5.1 %collective-permute-start.2 = (bf16[1,64,128]{2,1,0:T(8,128)(2,1)}, bf16[1,64,128]{2,1,0:T(8,128)(2,1)S(1)}, u32[]{:S(2)}, u32[]{:S(2)}) collective-permute-start(bf16[1,64,128]{2,1,0:T(8,128)(2,1)} %get-tuple-element.16), channel_id=1, source_target_pairs={{0,12},{1,13},{2,14},{3,15},{4,8},{5,9},{6,10},{7,11},{8,4},{9,5},... | collective-permute-start | bytes 49160 | tf_op jit(solution)/shard_map/ppermute | solution.py:344
  7.2 0.0 collective-permute-start.1
  7.2 0.6 collective-permute-start
  7.9 0.0 copy-start.2
  7.9 2.4 %shard_map.65.refs_2_ = bf16[64,8,16,128]{3,2,1,0:T(8,128)(2,1)S(1)} custom-call(bf16[64,16,4096]{2,1,0:T(8,128)(2,1)} %bitcast.51), custom_call_target="tpu_custom_call" | custom-call | flops 536870912 | bytes 4194304 | tf_op jit(solution)/shard_map/pallas_call | solution.py:119
  10.3 0.0 collective-permute-done.2.refs_0_
  10.3 1.8 %collective-permute-done.1 = bf16[1,64,128]{2,1,0:T(8,128)(2,1)S(1)} collective-permute-done((bf16[1,64,128]{2,1,0:T(8,128)(2,1)}, bf16[1,64,128]{2,1,0:T(8,128)(2,1)S(1)}, u32[]{:S(2)}, u32[]{:S(2)}) %collective-permute-start.1) | collective-permute-done | bytes 16416 | tf_op jit(solution)/shard_map/ppermute | solution.py:344
  12.1 0.0 collective-permute-done
  12.1 0.0 copy-done.2
  12.1 1.6 %collective-permute-start.3 = (bf16[4,64,128]{2,1,0:T(8,128)(2,1)S(1)}, bf16[4,64,128]{2,1,0:T(8,128)(2,1)S(1)}, u32[]{:S(2)}, u32[]{:S(2)}) collective-permute-start(bf16[4,64,128]{2,1,0:T(8,128)(2,1)S(1)} %pad_maximum_fusion.1), channel_id=1, source_target_pairs={{0,2},{1,3},{2,0},{3,1},{4,6},{5,7},{6,4},{7,5},{8,10},{9,11},{10,... | collective-permute-start | bytes 196616 | tf_op jit(solution)/shard_map/ppermute | solution.py:344
  13.7 2.4 %shard_map.66.refs_3_ = bf16[64,8,16,128]{3,2,1,0:T(8,128)(2,1)S(1)} custom-call(bf16[64,16,4096]{2,1,0:T(8,128)(2,1)} %bitcast.52, bf16[1,64,128]{2,1,0:T(8,128)(2,1)S(1)} %collective-permute-done.2.refs_0_), custom_call_target="tpu_custom_call" | custom-call | flops 536870912 | bytes 4194304 | tf_op jit(solution)/shard_map/pallas_call | solution.py:119
  16.1 0.4 collective-permute-done.3.refs_0_
  16.4 0.1 collective-permute-start.4
  16.5 2.4 %shard_map.69.refs_5_ = bf16[64,8,16,128]{3,2,1,0:T(8,128)(2,1)S(1)} custom-call(bf16[64,16,4096]{2,1,0:T(8,128)(2,1)} %bitcast.53, bf16[4,64,128]{2,1,0:T(8,128)(2,1)S(1)} %collective-permute-done.3.refs_0_), custom_call_target="tpu_custom_call" | custom-call | flops 536870912 | bytes 4194304 | tf_op jit(solution)/shard_map/pallas_call | solution.py:119
  18.9 0.0 copy-start.1
  18.9 2.4 %shard_map.68.refs_4_ = bf16[64,8,16,128]{3,2,1,0:T(8,128)(2,1)S(1)} custom-call(bf16[64,16,4096]{2,1,0:T(8,128)(2,1)} %bitcast.54, bf16[4,64,128]{2,1,0:T(8,128)(2,1)S(1)} %collective-permute-done.3.refs_0_), custom_call_target="tpu_custom_call" | custom-call | flops 536870912 | bytes 4194304 | tf_op jit(solution)/shard_map/pallas_call | solution.py:119
  21.3 0.0 collective-permute-done.4.refs_1_
  21.3 0.0 copy-done.1
  21.3 10.4 %shard_map.67.o_ref = bf16[64,32,16,128]{3,2,1,0:T(8,128)(2,1)S(1)} custom-call(s32[2]{0:T(128)S(1)} %bitcast.49, bf16[8,64,128]{2,1,0:T(8,128)(2,1)S(1)} %pad_maximum_fusion.refs_0_, bf16[8,64,128]{2,1,0:T(8,128)(2,1)S(1)} %collective-permute-done.4.refs_1_, bf16[64,16,4096]{2,1,0:T(8,128)(2,1)} %bitcast.55), custom_call_target="tpu_custom_call" | custom-call | flops 8589934592 | bytes 16777216 | tf_op jit(solution)/shard_map/pallas_call | solution.py:297
  31.7 0.0 copy-start
  31.7 3.2 %shard_map.70.v_ref = bf16[64,32,16,128]{3,2,1,0:T(8,128)(2,1)S(1)} custom-call(s32[2]{0:T(128)S(1)} %bitcast.50, bf16[8,64,128]{2,1,0:T(8,128)(2,1)S(1)} %pad_maximum_fusion.refs_0_, bf16[8,64,128]{2,1,0:T(8,128)(2,1)S(1)} %collective-permute-done.4.refs_1_, bf16[64,8,16,128]{3,2,1,0:T(8,128)(2,1)S(1)} %shard_map.65.refs_2_, ...), custom_call_target="tpu_custom_call" | custom-call | flops 8589934592 | bytes 16777216 | tf_op jit(solution)/shard_map/pallas_call | solution.py:289
  34.9 0.0 copy-done
  34.9 11.7 %shard_map.71 = (f32[16,64,128]{2,1,0:T(8,128)S(1)}, bf16[16,64,128]{2,1,0:T(8,128)(2,1)S(1)}) custom-call(s32[256]{0:T(256)S(1)} %bitcast.48, bf16[64,32,16,128]{3,2,1,0:T(8,128)(2,1)S(1)} %shard_map.67.o_ref, bf16[64,32,16,128]{3,2,1,0:T(8,128)(2,1)S(1)} %shard_map.70.v_ref), custom_call_target="tpu_custom_call" | custom-call | flops 8589934592 | bytes 16777216 | tf_op jit(solution)/shard_map/pallas_call | solution.py:313
  46.6 0.6 collective-permute-start.5
  47.2 1.2 %collective-permute-done.5 = bf16[16,64,128]{2,1,0:T(8,128)(2,1)S(1)} collective-permute-done((bf16[16,64,128]{2,1,0:T(8,128)(2,1)S(1)}, bf16[16,64,128]{2,1,0:T(8,128)(2,1)S(1)}, u32[]{:S(2)}, u32[]{:S(2)}) %collective-permute-start.5) | collective-permute-done | bytes 262176 | tf_op jit(solution)/shard_map/ppermute | solution.py:344
  48.3 0.1 convert_add_fusion
  48.5 1.6 %collective-permute-start.6 = (bf16[2,2,2,32,128]{4,3,2,1,0:T(8,128)(2,1)S(1)}, bf16[2,2,2,32,128]{4,3,2,1,0:T(8,128)(2,1)S(1)}, u32[]{:S(2)}, u32[]{:S(2)}) collective-permute-start(bf16[2,2,2,32,128]{4,3,2,1,0:T(8,128)(2,1)S(1)} %slice_bitcast_fusion.5), channel_id=1, source_target_pairs={{0,2},{1,3},{2,0},{3,1},{4,6},{5,7},{6,4},{7,5},{8,10},{9,11},{10,... | collective-permute-start | bytes 196616 | tf_op jit(solution)/shard_map/ppermute | solution.py:344
  50.1 0.0 collective-permute-start.9
  50.1 2.8 %collective-permute-done.6 = bf16[2,2,2,32,128]{4,3,2,1,0:T(8,128)(2,1)S(1)} collective-permute-done((bf16[2,2,2,32,128]{4,3,2,1,0:T(8,128)(2,1)S(1)}, bf16[2,2,2,32,128]{4,3,2,1,0:T(8,128)(2,1)S(1)}, u32[]{:S(2)}, u32[]{:S(2)}) %collective-permute-start.6) | collective-permute-done | bytes 65568 | tf_op jit(solution)/shard_map/ppermute | solution.py:344
  52.9 1.4 %collective-permute-done.9 = bf16[2,2,2,32,128]{4,3,2,1,0:T(8,128)(2,1)S(1)} collective-permute-done((bf16[2,2,2,32,128]{4,3,2,1,0:T(8,128)(2,1)S(1)}, bf16[2,2,2,32,128]{4,3,2,1,0:T(8,128)(2,1)S(1)}, u32[]{:S(2)}, u32[]{:S(2)}) %collective-permute-start.9) | collective-permute-done | bytes 65568 | tf_op jit(solution)/shard_map/ppermute | solution.py:344
  54.4 2.1 %collective-permute-start.10 = (bf16[2,2,32,128]{3,2,1,0:T(8,128)(2,1)S(1)}, bf16[2,2,32,128]{3,2,1,0:T(8,128)(2,1)S(1)}, u32[]{:S(2)}, u32[]{:S(2)}) collective-permute-start(bf16[2,2,32,128]{3,2,1,0:T(8,128)(2,1)S(1)} %fusion.5), channel_id=1, source_target_pairs={{0,8},{1,9},{2,10},{3,11},{4,12},{5,13},{6,14},{7,15},{8,0},{9,1},... | collective-permute-start | bytes 98312 | tf_op jit(solution)/shard_map/ppermute | solution.py:344
  56.5 0.6 collective-permute-start.7
  57.0 2.2 %collective-permute-done.10 = bf16[2,2,32,128]{3,2,1,0:T(8,128)(2,1)S(1)} collective-permute-done((bf16[2,2,32,128]{3,2,1,0:T(8,128)(2,1)S(1)}, bf16[2,2,32,128]{3,2,1,0:T(8,128)(2,1)S(1)}, u32[]{:S(2)}, u32[]{:S(2)}) %collective-permute-start.10) | collective-permute-done | bytes 32800 | tf_op jit(solution)/shard_map/ppermute | solution.py:344
  59.3 0.7 %collective-permute-start.11 = (bf16[2,32,128]{2,1,0:T(8,128)(2,1)S(1)}, bf16[2,32,128]{2,1,0:T(8,128)(2,1)S(1)}, u32[]{:S(2)}, u32[]{:S(2)}) collective-permute-start(bf16[2,32,128]{2,1,0:T(8,128)(2,1)S(1)} %fusion.9), channel_id=1, source_target_pairs={{0,2},{1,3},{2,0},{3,1},{4,6},{5,7},{6,4},{7,5},{8,10},{9,11},{10,... | collective-permute-start | bytes 49160 | tf_op jit(solution)/shard_map/ppermute | solution.py:344
  60.0 0.5 collective-permute-done.7
  60.5 1.5 %collective-permute-start.8 = (bf16[2,32,128]{2,1,0:T(8,128)(2,1)S(1)}, bf16[2,32,128]{2,1,0:T(8,128)(2,1)S(1)}, u32[]{:S(2)}, u32[]{:S(2)}) collective-permute-start(bf16[2,32,128]{2,1,0:T(8,128)(2,1)S(1)} %fusion.8), channel_id=1, source_target_pairs={{0,8},{1,9},{2,10},{3,11},{4,12},{5,13},{6,14},{7,15},{8,0},{9,1},... | collective-permute-start | bytes 49160 | tf_op jit(solution)/shard_map/ppermute | solution.py:344
  62.0 1.1 %collective-permute-done.11 = bf16[2,32,128]{2,1,0:T(8,128)(2,1)S(1)} collective-permute-done((bf16[2,32,128]{2,1,0:T(8,128)(2,1)S(1)}, bf16[2,32,128]{2,1,0:T(8,128)(2,1)S(1)}, u32[]{:S(2)}, u32[]{:S(2)}) %collective-permute-start.11) | collective-permute-done | bytes 16416 | tf_op jit(solution)/shard_map/ppermute | solution.py:344
  63.1 2.2 %collective-permute-done.8 = bf16[2,32,128]{2,1,0:T(8,128)(2,1)S(1)} collective-permute-done((bf16[2,32,128]{2,1,0:T(8,128)(2,1)S(1)}, bf16[2,32,128]{2,1,0:T(8,128)(2,1)S(1)}, u32[]{:S(2)}, u32[]{:S(2)}) %collective-permute-start.8) | collective-permute-done | bytes 16416 | tf_op jit(solution)/shard_map/ppermute | solution.py:344
  65.3 0.1 reshape.16
  65.5 0.7 %reshape.17 = f32[4,4096]{1,0:T(4,128)} reshape(f32[2,2,64,64]{3,2,1,0:T(8,128)S(1)} %bitcast.58) | data formatting | bytes 131072 | tf_op jit(solution)/shard_map/reshape | solution.py:377
  (16 shorter events, 0.2 us)
Async XLA Ops:
  2.1 8.2 %collective-permute-start.2 = (bf16[1,64,128]{2,1,0:T(8,128)(2,1)}, bf16[1,64,128]{2,1,0:T(8,128)(2,1)S(1)}, u32[]{:S(2)}, u32[]{:S(2)}) collective-permute-start(bf16[1,64,128]{2,1,0:T(8,128)(2,1)} %get-tuple-element.16), channel_id=1, source_target_pairs={{0,12},{1,13},{2,14},{3,15},{4,8},{5,9},{6,10},{7,11},{8,4},{9,5},... | collective-permute-start | bytes 49160 | tf_op jit(solution)/shard_map/ppermute | solution.py:344
  7.2 4.8 %collective-permute-start.1 = (bf16[1,64,128]{2,1,0:T(8,128)(2,1)}, bf16[1,64,128]{2,1,0:T(8,128)(2,1)S(1)}, u32[]{:S(2)}, u32[]{:S(2)}) collective-permute-start(bf16[1,64,128]{2,1,0:T(8,128)(2,1)} %get-tuple-element.16), channel_id=1, source_target_pairs={{0,8},{1,9},{2,10},{3,11},{4,12},{5,13},{6,14},{7,15},{8,0},{9,1},... | collective-permute-start | bytes 49160 | tf_op jit(solution)/shard_map/ppermute | solution.py:344
  7.2 4.8 %collective-permute-start = (bf16[1,64,128]{2,1,0:T(8,128)(2,1)}, bf16[1,64,128]{2,1,0:T(8,128)(2,1)S(1)}, u32[]{:S(2)}, u32[]{:S(2)}) collective-permute-start(bf16[1,64,128]{2,1,0:T(8,128)(2,1)} %get-tuple-element.16), channel_id=1, source_target_pairs={{0,4},{1,5},{2,6},{3,7},{4,0},{5,1},{6,2},{7,3},{8,12},{9,13},{10,... | collective-permute-start | bytes 49160 | tf_op jit(solution)/shard_map/ppermute | solution.py:344
  7.9 4.2 %copy-start.2 = (bf16[1,64,128]{2,1,0:T(8,128)(2,1)S(1)}, bf16[1,64,128]{2,1,0:T(8,128)(2,1)}, u32[]{:S(2)}) copy-start(bf16[1,64,128]{2,1,0:T(8,128)(2,1)} %get-tuple-element.16) | copy-start | bytes 49156
  12.1 4.3 %collective-permute-start.3 = (bf16[4,64,128]{2,1,0:T(8,128)(2,1)S(1)}, bf16[4,64,128]{2,1,0:T(8,128)(2,1)S(1)}, u32[]{:S(2)}, u32[]{:S(2)}) collective-permute-start(bf16[4,64,128]{2,1,0:T(8,128)(2,1)S(1)} %pad_maximum_fusion.1), channel_id=1, source_target_pairs={{0,2},{1,3},{2,0},{3,1},{4,6},{5,7},{6,4},{7,5},{8,10},{9,11},{10,... | collective-permute-start | bytes 196616 | tf_op jit(solution)/shard_map/ppermute | solution.py:344
  16.4 4.9 %collective-permute-start.4 = (bf16[8,64,128]{2,1,0:T(8,128)(2,1)S(1)}, bf16[8,64,128]{2,1,0:T(8,128)(2,1)S(1)}, u32[]{:S(2)}, u32[]{:S(2)}) collective-permute-start(bf16[8,64,128]{2,1,0:T(8,128)(2,1)S(1)} %pad_maximum_fusion.refs_0_), channel_id=1, source_target_pairs={{0,1},{1,0},{2,3},{3,2},{4,5},{5,4},{6,7},{7,6},{8,9},{9,8},{10,11... | collective-permute-start | bytes 393224 | tf_op jit(solution)/shard_map/ppermute | solution.py:344
  18.9 2.4 %copy-start.1 = (s32[1,2]{1,0:T(1,128)S(1)}, s32[1,2]{1,0:T(1,128)}, u32[]{:S(2)}) copy-start(s32[1,2]{1,0:T(1,128)} %get-tuple-element.15) | copy-start | bytes 28
  31.7 3.2 %copy-start = (s32[1,256]{1,0:T(1,128)S(1)}, s32[1,256]{1,0:T(1,128)}, u32[]{:S(2)}) copy-start(s32[1,256]{1,0:T(1,128)} %get-tuple-element.14) | copy-start | bytes 3076
  46.6 1.7 %collective-permute-start.5 = (bf16[16,64,128]{2,1,0:T(8,128)(2,1)S(1)}, bf16[16,64,128]{2,1,0:T(8,128)(2,1)S(1)}, u32[]{:S(2)}, u32[]{:S(2)}) collective-permute-start(bf16[16,64,128]{2,1,0:T(8,128)(2,1)S(1)} %get-tuple-element.22), channel_id=1, source_target_pairs={{0,1},{1,0},{2,3},{3,2},{4,5},{5,4},{6,7},{7,6},{8,9},{9,8},{10,11... | collective-permute-start | bytes 786440 | tf_op jit(solution)/shard_map/ppermute | solution.py:344
  48.5 4.4 %collective-permute-start.6 = (bf16[2,2,2,32,128]{4,3,2,1,0:T(8,128)(2,1)S(1)}, bf16[2,2,2,32,128]{4,3,2,1,0:T(8,128)(2,1)S(1)}, u32[]{:S(2)}, u32[]{:S(2)}) collective-permute-start(bf16[2,2,2,32,128]{4,3,2,1,0:T(8,128)(2,1)S(1)} %slice_bitcast_fusion.5), channel_id=1, source_target_pairs={{0,2},{1,3},{2,0},{3,1},{4,6},{5,7},{6,4},{7,5},{8,10},{9,11},{10,... | collective-permute-start | bytes 196616 | tf_op jit(solution)/shard_map/ppermute | solution.py:344
  50.1 4.3 %collective-permute-start.9 = (bf16[2,2,2,32,128]{4,3,2,1,0:T(8,128)(2,1)S(1)}, bf16[2,2,2,32,128]{4,3,2,1,0:T(8,128)(2,1)S(1)}, u32[]{:S(2)}, u32[]{:S(2)}) collective-permute-start(bf16[2,2,2,32,128]{4,3,2,1,0:T(8,128)(2,1)S(1)} %slice_bitcast_fusion.3), channel_id=1, source_target_pairs={{0,4},{1,5},{2,6},{3,7},{4,0},{5,1},{6,2},{7,3},{8,12},{9,13},{10,... | collective-permute-start | bytes 196616 | tf_op jit(solution)/shard_map/ppermute | solution.py:344
  54.4 4.9 %collective-permute-start.10 = (bf16[2,2,32,128]{3,2,1,0:T(8,128)(2,1)S(1)}, bf16[2,2,32,128]{3,2,1,0:T(8,128)(2,1)S(1)}, u32[]{:S(2)}, u32[]{:S(2)}) collective-permute-start(bf16[2,2,32,128]{3,2,1,0:T(8,128)(2,1)S(1)} %fusion.5), channel_id=1, source_target_pairs={{0,8},{1,9},{2,10},{3,11},{4,12},{5,13},{6,14},{7,15},{8,0},{9,1},... | collective-permute-start | bytes 98312 | tf_op jit(solution)/shard_map/ppermute | solution.py:344
  56.5 4.0 %collective-permute-start.7 = (bf16[2,2,32,128]{3,2,1,0:T(8,128)(2,1)S(1)}, bf16[2,2,32,128]{3,2,1,0:T(8,128)(2,1)S(1)}, u32[]{:S(2)}, u32[]{:S(2)}) collective-permute-start(bf16[2,2,32,128]{3,2,1,0:T(8,128)(2,1)S(1)} %fusion.4), channel_id=1, source_target_pairs={{0,4},{1,5},{2,6},{3,7},{4,0},{5,1},{6,2},{7,3},{8,12},{9,13},{10,... | collective-permute-start | bytes 98312 | tf_op jit(solution)/shard_map/ppermute | solution.py:344
  59.3 3.8 %collective-permute-start.11 = (bf16[2,32,128]{2,1,0:T(8,128)(2,1)S(1)}, bf16[2,32,128]{2,1,0:T(8,128)(2,1)S(1)}, u32[]{:S(2)}, u32[]{:S(2)}) collective-permute-start(bf16[2,32,128]{2,1,0:T(8,128)(2,1)S(1)} %fusion.9), channel_id=1, source_target_pairs={{0,2},{1,3},{2,0},{3,1},{4,6},{5,7},{6,4},{7,5},{8,10},{9,11},{10,... | collective-permute-start | bytes 49160 | tf_op jit(solution)/shard_map/ppermute | solution.py:344
  60.5 4.8 %collective-permute-start.8 = (bf16[2,32,128]{2,1,0:T(8,128)(2,1)S(1)}, bf16[2,32,128]{2,1,0:T(8,128)(2,1)S(1)}, u32[]{:S(2)}, u32[]{:S(2)}) collective-permute-start(bf16[2,32,128]{2,1,0:T(8,128)(2,1)S(1)} %fusion.8), channel_id=1, source_target_pairs={{0,8},{1,9},{2,10},{3,11},{4,12},{5,13},{6,14},{7,15},{8,0},{9,1},... | collective-permute-start | bytes 49160 | tf_op jit(solution)/shard_map/ppermute | solution.py:344

commit v8 on v7

--- a/solution.py
+++ b/solution.py
@@ -13,7 +13,7 @@
 GRANT = 8 << 20
 
 
-def pack_kernel(place_rounds, table_rounds, me_ref, count_ref, *refs):
+def pack_kernel(pairs, table_rounds, me_ref, count_ref, *refs):
     sources, (out_ref, ids_ref, place_ref), (rows_ref, *held, sems) = refs[:4], refs[4:7], refs[7:]
     copies = [pltpu.make_async_copy(src, dst, sems.at[k]) for k, (src, dst) in enumerate(zip(sources, held))]
     for copy in copies:
@@ -42,16 +42,14 @@
     ids_ref[...] = ids
 
     targets = tgt_ref[...]
-    rel = (targets // CB_DEV) ^ me
-    place = jnp.zeros_like(targets)
-    for shift, step in place_rounds:
-        place = (place << step) | ((rel >> shift) & ((1 << step) - 1))
+    owner = targets // CB_DEV
+    place = ((owner ^ me) & 1) * pairs + (owner >> 1)
     place_ref[...] = place * CB_DEV + targets % CB_DEV
 
 
 def packed(me, basis_count, pair_atoms, chi_target, green_occ, green_virt, bs, bits):
     return pl.pallas_call(
-        functools.partial(pack_kernel, owner_rounds(bits), gather_rounds(bits)),
+        functools.partial(pack_kernel, 1 << (bits - 1), gather_rounds(bits)),
         in_specs=in_smem(2) + [pl.BlockSpec(memory_space=pl.ANY)] * 4,
         out_specs=in_vmem(3),
         out_shape=[
@@ -323,16 +321,7 @@
 
 
 def gather_rounds(bits):
-    rounds, at = [], 0
-    while at < bits:
-        step = 1 if at < 2 else min(2, bits - at)
-        rounds.append((at, step))
-        at += step
-    return rounds[::-1]
-
-
-def owner_rounds(bits):
-    return [(bit, 1) for bit in range(bits)]
+    return [(bit, 1) for bit in reversed(range(bits))]
 
 
 def local(orb, three_centre, green_occ, green_virt, pair_atoms, basis_count, chi_target):
@@ -359,20 +348,11 @@
         d_parts += [relayout(integrals, i, after) for i in parts]
     total, send = chi_blocks_of(ids[0], place[0], tables, integrals, d_parts, orb * CB_DEV, 1)
     total = total + exchange(send, 1).astype(jnp.float32)
-    total = total.reshape([2] * (bits - 1) + [-1, bs, 2 * bs])
-    halves = [total[..., :bs // 2, :], total[..., bs // 2:, :]]
-    todo = [list(range(1, bits)), list(range(2, bits)) + [1]]
-    left = [list(range(1, bits)) for _ in halves]
-    for k in range(bits - 1):
-        sends, keeps = [], []
-        for part, order, axes in zip(halves, todo, left):
-            axis = axes.index(order[k])
-            axes.remove(order[k])
-            keeps.append(lax.index_in_dim(part, 0, axis, keepdims=False))
-            sends.append(lax.index_in_dim(part, 1, axis, keepdims=False).astype(jnp.bfloat16))
-        came = [exchange(send, 1 << order[k]) for send, order in zip(sends, todo)]
-        halves = [keep + got.astype(jnp.float32) for keep, got in zip(keeps, came)]
-    total = jnp.concatenate(halves, axis=-2)
+    groups = [list(range(parity, orb, 2)) for parity in range(2)]
+    came = lax.all_to_all(
+        total.reshape(orb // 2, -1, bs, 2 * bs).astype(jnp.bfloat16), "orb", 0, 0, axis_index_groups=groups, tiled=True
+    )
+    total = came.astype(jnp.float32).sum(axis=0)
     total = total.reshape(CB_DEV // 2, bs, 2, bs).transpose(0, 2, 1, 3)
     return total.reshape(CB_DEV, bs * bs)
 

time: 66.5 us -> 62.8 us (0.944)
  blocking collectives: 0 us -> 14.9 us
  waiting for transfers between devices: 13.6 us -> 1.54 us
  starting transfers between devices: 14.4 us -> 7.96 us
    all_to_all x0 -> x1, blocking collectives: none -> 14.9 us  [local(): lax.all_to_all(total.reshape(orb // 2, -1, bs, 2 * bs).astype(jnp.bfloat1...]
    ppermute x12 -> x5, waiting for transfers between devices: 13.6 us -> 1.54 us  [exchange(): return lax.ppermute(value, 'orb', [(i, i ^ flip) for i in range(orb)])]
    ppermute x12 -> x5, starting transfers between devices: 14.4 us -> 7.96 us  [exchange(): return lax.ppermute(value, 'orb', [(i, i ^ flip) for i in range(orb)])]
  transfers between devices with their start and end apart: 12 -> 5, of which waited for: 9 -> 2; matrix products, arithmetic and copies ran while one was open for 0% -> 0% of each run, Pallas kernels for 14% -> 15%
where the time goes in v8:
time: 62.8 us; the launch traced here: 62.5 us
  Pallas kernels  36.2 us (58%)
  blocking collectives  14.9 us (24%)
  starting transfers between devices  7.96 us (13%)
  waiting for transfers between devices  1.54 us (2%)
  local copies, waits for them, and re-layouts  0.89 us (1%)
  between operations  0.84 us (1%)
    all_to_all x1, blocking collectives, local(): lax.all_to_all(total.reshape(orb // 2, -1, bs, 2 * bs).astype(jnp.bfloat1...  14.9 us
    pallas_call x1, Pallas kernels, chi_blocks_of(): pl.pallas_call(functools.partial(chi_kernel, bs, sends), in_specs=in_smem...  11.7 us
    pallas_call x1, Pallas kernels, chi_blocks_of(): pl.pallas_call(functools.partial(occ_kernel, len(tables)), in_specs=in_sm...  10.4 us
    pallas_call x4, Pallas kernels, relayout(): pl.pallas_call(functools.partial(relayout_kernel, part), in_specs=[hidden...  9.49 us
    ppermute x5, starting transfers between devices, exchange(): return lax.ppermute(value, 'orb', [(i, i ^ flip) for i in range(orb)])  7.96 us
    pallas_call x1, Pallas kernels, chi_blocks_of(): pl.pallas_call(functools.partial(virt_kernel, bs, len(tables)), in_specs=...  3.17 us
    ppermute x5, waiting for transfers between devices, exchange(): return lax.ppermute(value, 'orb', [(i, i ^ flip) for i in range(orb)])  1.54 us
    pallas_call x1, Pallas kernels, packed(): pl.pallas_call(functools.partial(pack_kernel, 1 << bits - 1, gather_round...  1.44 us
  transfers between devices with their start and end apart: 5, of which 2 were waited for; matrix products, arithmetic and copies ran while one was open for 0% of the time, Pallas kernels for 15%

profile of v8, /device:TPU:0, one launch (start us, length us, event | category | flops | bytes accessed | tf_op | source)
XLA Modules:
  0.0 62.5 jit_solution(13909613185563112668)
XLA Ops:
  0.7 1.4 %shard_map.64 = (bf16[1,64,128]{2,1,0:T(8,128)(2,1)}, s32[1,2]{1,0:T(1,128)}, s32[1,256]{1,0:T(1,128)}) custom-call(s32[1]{0:T(128)} %bitcast.me_ref, s32[1]{0:T(128)S(6)} %copy.8.count_ref, s32[1,2]{1,0:T(1,128)} %refs_0_.1, s32[1,256]{1,0:T(1,128)} %refs_1_.1, bf16[1,4096]{1,0:T(2,128)(2,1)} %refs_2_.1, bf16[1,4096]{1,0:T(2,128)(2,1)} %refs_3_.1), custom_call_target="tpu_custom_call" | custom-call | tf_op jit(solution)/shard_map/pallas_call | solution.py:51
  2.1 4.1 %collective-permute-start = (bf16[1,64,128]{2,1,0:T(8,128)(2,1)}, bf16[1,64,128]{2,1,0:T(8,128)(2,1)S(1)}, u32[]{:S(2)}, u32[]{:S(2)}) collective-permute-start(bf16[1,64,128]{2,1,0:T(8,128)(2,1)} %get-tuple-element.18), channel_id=1, source_target_pairs={{0,8},{1,9},{2,10},{3,11},{4,12},{5,13},{6,14},{7,15},{8,0},{9,1},... | collective-permute-start | bytes 49160 | tf_op jit(solution)/shard_map/ppermute | solution.py:333
  6.2 0.0 copy-start.2
  6.2 2.4 %shard_map.65.refs_2_ = bf16[64,8,16,128]{3,2,1,0:T(8,128)(2,1)S(1)} custom-call(bf16[64,16,4096]{2,1,0:T(8,128)(2,1)} %bitcast.11), custom_call_target="tpu_custom_call" | custom-call | flops 536870912 | bytes 4194304 | tf_op jit(solution)/shard_map/pallas_call | solution.py:117
  8.6 0.0 collective-permute-done.refs_0_
  8.6 0.0 copy-done.2
  8.6 1.6 %collective-permute-start.1 = (bf16[2,64,128]{2,1,0:T(8,128)(2,1)S(1)}, bf16[2,64,128]{2,1,0:T(8,128)(2,1)S(1)}, u32[]{:S(2)}, u32[]{:S(2)}) collective-permute-start(bf16[2,64,128]{2,1,0:T(8,128)(2,1)S(1)} %pad_maximum_fusion.2), channel_id=1, source_target_pairs={{0,4},{1,5},{2,6},{3,7},{4,0},{5,1},{6,2},{7,3},{8,12},{9,13},{10,... | collective-permute-start | bytes 98312 | tf_op jit(solution)/shard_map/ppermute | solution.py:333
  10.3 2.4 %shard_map.66.refs_3_ = bf16[64,8,16,128]{3,2,1,0:T(8,128)(2,1)S(1)} custom-call(bf16[64,16,4096]{2,1,0:T(8,128)(2,1)} %bitcast.12, bf16[1,64,128]{2,1,0:T(8,128)(2,1)S(1)} %collective-permute-done.refs_0_), custom_call_target="tpu_custom_call" | custom-call | flops 536870912 | bytes 4194304 | tf_op jit(solution)/shard_map/pallas_call | solution.py:117
  12.6 0.0 collective-permute-done.1.refs_0_
  12.7 1.6 %collective-permute-start.2 = (bf16[4,64,128]{2,1,0:T(8,128)(2,1)S(1)}, bf16[4,64,128]{2,1,0:T(8,128)(2,1)S(1)}, u32[]{:S(2)}, u32[]{:S(2)}) collective-permute-start(bf16[4,64,128]{2,1,0:T(8,128)(2,1)S(1)} %pad_maximum_fusion.1), channel_id=1, source_target_pairs={{0,2},{1,3},{2,0},{3,1},{4,6},{5,7},{6,4},{7,5},{8,10},{9,11},{10,... | collective-permute-start | bytes 196616 | tf_op jit(solution)/shard_map/ppermute | solution.py:333
  14.3 2.4 %shard_map.67.refs_4_ = bf16[64,8,16,128]{3,2,1,0:T(8,128)(2,1)S(1)} custom-call(bf16[64,16,4096]{2,1,0:T(8,128)(2,1)} %bitcast.13, bf16[2,64,128]{2,1,0:T(8,128)(2,1)S(1)} %collective-permute-done.1.refs_0_), custom_call_target="tpu_custom_call" | custom-call | flops 536870912 | bytes 4194304 | tf_op jit(solution)/shard_map/pallas_call | solution.py:117
  16.6 0.4 collective-permute-done.2.refs_0_
  17.0 0.0 copy-start.1
  17.0 0.1 collective-permute-start.3
  17.1 2.4 %shard_map.69.refs_5_ = bf16[64,8,16,128]{3,2,1,0:T(8,128)(2,1)S(1)} custom-call(bf16[64,16,4096]{2,1,0:T(8,128)(2,1)} %bitcast.14, bf16[4,64,128]{2,1,0:T(8,128)(2,1)S(1)} %collective-permute-done.2.refs_0_), custom_call_target="tpu_custom_call" | custom-call | flops 536870912 | bytes 4194304 | tf_op jit(solution)/shard_map/pallas_call | solution.py:117
  19.5 0.0 collective-permute-done.3.refs_1_
  19.5 0.0 copy-done.1
  19.5 10.4 %shard_map.68.o_ref = bf16[64,32,16,128]{3,2,1,0:T(8,128)(2,1)S(1)} custom-call(s32[2]{0:T(128)S(1)} %bitcast.9, bf16[8,64,128]{2,1,0:T(8,128)(2,1)S(1)} %pad_maximum_fusion.refs_0_, bf16[8,64,128]{2,1,0:T(8,128)(2,1)S(1)} %collective-permute-done.3.refs_1_, bf16[64,16,4096]{2,1,0:T(8,128)(2,1)} %bitcast.15), custom_call_target="tpu_custom_call" | custom-call | flops 8589934592 | bytes 16777216 | tf_op jit(solution)/shard_map/pallas_call | solution.py:295
  29.9 0.0 copy-start
  29.9 3.2 %shard_map.70.v_ref = bf16[64,32,16,128]{3,2,1,0:T(8,128)(2,1)S(1)} custom-call(s32[2]{0:T(128)S(1)} %bitcast.10, bf16[8,64,128]{2,1,0:T(8,128)(2,1)S(1)} %pad_maximum_fusion.refs_0_, bf16[8,64,128]{2,1,0:T(8,128)(2,1)S(1)} %collective-permute-done.3.refs_1_, bf16[64,8,16,128]{3,2,1,0:T(8,128)(2,1)S(1)} %shard_map.65.refs_2_, ...), custom_call_target="tpu_custom_call" | custom-call | flops 8589934592 | bytes 16777216 | tf_op jit(solution)/shard_map/pallas_call | solution.py:287
  33.1 0.0 copy-done
  33.1 11.7 %shard_map.71 = (f32[16,64,128]{2,1,0:T(8,128)S(1)}, bf16[16,64,128]{2,1,0:T(8,128)(2,1)S(1)}) custom-call(s32[256]{0:T(256)S(1)} %bitcast.8, bf16[64,32,16,128]{3,2,1,0:T(8,128)(2,1)S(1)} %shard_map.68.o_ref, bf16[64,32,16,128]{3,2,1,0:T(8,128)(2,1)S(1)} %shard_map.70.v_ref), custom_call_target="tpu_custom_call" | custom-call | flops 8589934592 | bytes 16777216 | tf_op jit(solution)/shard_map/pallas_call | solution.py:311
  44.8 0.6 collective-permute-start.4
  45.4 1.2 %collective-permute-done.4 = bf16[16,64,128]{2,1,0:T(8,128)(2,1)S(1)} collective-permute-done((bf16[16,64,128]{2,1,0:T(8,128)(2,1)S(1)}, bf16[16,64,128]{2,1,0:T(8,128)(2,1)S(1)}, u32[]{:S(2)}, u32[]{:S(2)}) %collective-permute-start.4) | collective-permute-done | bytes 262176 | tf_op jit(solution)/shard_map/ppermute | solution.py:333
  46.5 0.1 add_convert_fusion
  46.6 14.9 %all_to_all.5 = bf16[8,2,64,128]{3,2,1,0:T(8,128)(2,1)S(1)} all-to-all(bf16[8,2,64,128]{3,2,1,0:T(8,128)(2,1)S(1)} %bitcast.16), channel_id=1, replica_groups={{0,2,4,6,8,10,12,14},{1,3,5,7,9,11,13,15},{16,18,20,22,24,26,28,30},{17..., dimensions={0} | all-to-all | bytes 524288 | tf_op jit(solution)/shard_map/all_to_all | solution.py:352
  61.6 0.1 reshape.8
  61.7 0.7 %reshape.9 = f32[4,4096]{1,0:T(4,128)} reshape(f32[2,2,64,64]{3,2,1,0:T(8,128)S(1)} %copy.7) | data formatting | bytes 131072 | tf_op jit(solution)/shard_map/reshape | solution.py:357
  (5 shorter events, 0.1 us)
Async XLA Ops:
  2.1 6.5 %collective-permute-start = (bf16[1,64,128]{2,1,0:T(8,128)(2,1)}, bf16[1,64,128]{2,1,0:T(8,128)(2,1)S(1)}, u32[]{:S(2)}, u32[]{:S(2)}) collective-permute-start(bf16[1,64,128]{2,1,0:T(8,128)(2,1)} %get-tuple-element.18), channel_id=1, source_target_pairs={{0,8},{1,9},{2,10},{3,11},{4,12},{5,13},{6,14},{7,15},{8,0},{9,1},... | collective-permute-start | bytes 49160 | tf_op jit(solution)/shard_map/ppermute | solution.py:333
  6.2 2.4 %copy-start.2 = (bf16[1,64,128]{2,1,0:T(8,128)(2,1)S(1)}, bf16[1,64,128]{2,1,0:T(8,128)(2,1)}, u32[]{:S(2)}) copy-start(bf16[1,64,128]{2,1,0:T(8,128)(2,1)} %get-tuple-element.18) | copy-start | bytes 49156
  8.6 4.0 %collective-permute-start.1 = (bf16[2,64,128]{2,1,0:T(8,128)(2,1)S(1)}, bf16[2,64,128]{2,1,0:T(8,128)(2,1)S(1)}, u32[]{:S(2)}, u32[]{:S(2)}) collective-permute-start(bf16[2,64,128]{2,1,0:T(8,128)(2,1)S(1)} %pad_maximum_fusion.2), channel_id=1, source_target_pairs={{0,4},{1,5},{2,6},{3,7},{4,0},{5,1},{6,2},{7,3},{8,12},{9,13},{10,... | collective-permute-start | bytes 98312 | tf_op jit(solution)/shard_map/ppermute | solution.py:333
  12.7 4.3 %collective-permute-start.2 = (bf16[4,64,128]{2,1,0:T(8,128)(2,1)S(1)}, bf16[4,64,128]{2,1,0:T(8,128)(2,1)S(1)}, u32[]{:S(2)}, u32[]{:S(2)}) collective-permute-start(bf16[4,64,128]{2,1,0:T(8,128)(2,1)S(1)} %pad_maximum_fusion.1), channel_id=1, source_target_pairs={{0,2},{1,3},{2,0},{3,1},{4,6},{5,7},{6,4},{7,5},{8,10},{9,11},{10,... | collective-permute-start | bytes 196616 | tf_op jit(solution)/shard_map/ppermute | solution.py:333
  17.0 2.5 %copy-start.1 = (s32[1,2]{1,0:T(1,128)S(1)}, s32[1,2]{1,0:T(1,128)}, u32[]{:S(2)}) copy-start(s32[1,2]{1,0:T(1,128)} %get-tuple-element.17) | copy-start | bytes 28
  17.0 2.5 %collective-permute-start.3 = (bf16[8,64,128]{2,1,0:T(8,128)(2,1)S(1)}, bf16[8,64,128]{2,1,0:T(8,128)(2,1)S(1)}, u32[]{:S(2)}, u32[]{:S(2)}) collective-permute-start(bf16[8,64,128]{2,1,0:T(8,128)(2,1)S(1)} %pad_maximum_fusion.refs_0_), channel_id=1, source_target_pairs={{0,1},{1,0},{2,3},{3,2},{4,5},{5,4},{6,7},{7,6},{8,9},{9,8},{10,11... | collective-permute-start | bytes 393224 | tf_op jit(solution)/shard_map/ppermute | solution.py:333
  29.9 3.2 %copy-start = (s32[1,256]{1,0:T(1,128)S(1)}, s32[1,256]{1,0:T(1,128)}, u32[]{:S(2)}) copy-start(s32[1,256]{1,0:T(1,128)} %get-tuple-element.16) | copy-start | bytes 3076
  44.8 1.7 %collective-permute-start.4 = (bf16[16,64,128]{2,1,0:T(8,128)(2,1)S(1)}, bf16[16,64,128]{2,1,0:T(8,128)(2,1)S(1)}, u32[]{:S(2)}, u32[]{:S(2)}) collective-permute-start(bf16[16,64,128]{2,1,0:T(8,128)(2,1)S(1)} %get-tuple-element.26), channel_id=1, source_target_pairs={{0,1},{1,0},{2,3},{3,2},{4,5},{5,4},{6,7},{7,6},{8,9},{9,8},{10,11... | collective-permute-start | bytes 786440 | tf_op jit(solution)/shard_map/ppermute | solution.py:333

commit v9 on v8

--- a/solution.py
+++ b/solution.py
@@ -13,7 +13,7 @@
 GRANT = 8 << 20
 
 
-def pack_kernel(pairs, table_rounds, me_ref, count_ref, *refs):
+def pack_kernel(quarter, table_rounds, me_ref, count_ref, *refs):
     sources, (out_ref, ids_ref, place_ref), (rows_ref, *held, sems) = refs[:4], refs[4:7], refs[7:]
     copies = [pltpu.make_async_copy(src, dst, sems.at[k]) for k, (src, dst) in enumerate(zip(sources, held))]
     for copy in copies:
@@ -43,13 +43,14 @@
 
     targets = tgt_ref[...]
     owner = targets // CB_DEV
-    place = ((owner ^ me) & 1) * pairs + (owner >> 1)
+    rel = owner ^ me
+    place = ((rel & 1) * 2 + ((rel >> 1) & 1)) * quarter + (owner >> 2)
     place_ref[...] = place * CB_DEV + targets % CB_DEV
 
 
 def packed(me, basis_count, pair_atoms, chi_target, green_occ, green_virt, bs, bits):
     return pl.pallas_call(
-        functools.partial(pack_kernel, 1 << (bits - 1), gather_rounds(bits)),
+        functools.partial(pack_kernel, 1 << (bits - 2), gather_rounds(bits)),
         in_specs=in_smem(2) + [pl.BlockSpec(memory_space=pl.ANY)] * 4,
         out_specs=in_vmem(3),
         out_shape=[
@@ -149,8 +150,27 @@
     return block.astype(jnp.bfloat16)
 
 
-def virt_kernel(bs, pieces, ids_ref, *refs):
-    tables, d_parts, v_ref = refs[:pieces], refs[pieces:pieces + PARTS], refs[-1]
+def flat(ref, blocks, tiles):
+    got = [ref[blocks, t] for t in tiles]
+    return jnp.concatenate([x.reshape(x.shape[0] * x.shape[1], x.shape[2]) for x in got], axis=1)
+
+
+def sides_kernel(pieces, ids_ref, *refs):
+    tables, d_parts, refs = refs[:pieces], refs[pieces:pieces + PARTS], refs[pieces + PARTS:]
+    b_hbm, v_ref, o_ref, b_ref, sems, *results = refs
+    bs, aux, width = b_ref.shape
+    half, lanes = aux // 2, 2 * bs
+    tiles = width // lanes
+
+    def columns(j):
+        return pl.ds(pl.multiple_of(j * (2 * lanes), 2 * lanes), 2 * lanes)
+
+    def copy(j):
+        return pltpu.make_async_copy(b_hbm.at[:, :, columns(j)], b_ref.at[:, :, columns(j)], sems.at[j])
+
+    for j in range(tiles // 2):
+        copy(j).start()
+
     wide = LAM * bs
     spread = spread_rows(green_block(tables, ids_ref[1])[bs // 2:], lambda i: i % bs, wide, bs)
     spread = jnp.concatenate([spread] * LAM, axis=1)
@@ -158,34 +178,14 @@
         lax.broadcasted_iota(jnp.int32, (wide, wide), 0) // bs == lax.broadcasted_iota(jnp.int32, (wide, wide), 1) // bs
     )
     virt_w = jnp.where(same, spread, 0.0).astype(jnp.bfloat16)
-    blocks, each, rows, lanes = d_parts[0].shape
+    each = d_parts[0].shape[1]
     for part in range(PARTS):
         for at in range(0, each, 2):
-            block = flat(d_parts[part], slice(None), [at, at + 1])
-            got = jnp.dot(block, virt_w, preferred_element_type=jnp.float32).astype(jnp.bfloat16)
+            got = jnp.dot(flat(d_parts[part], slice(None), [at, at + 1]), virt_w, preferred_element_type=jnp.float32)
+            got = got.astype(jnp.bfloat16)
             for t in range(2):
-                v_ref[:, part * each + at + t] = got[:, t * lanes:(t + 1) * lanes].reshape(blocks, rows, lanes)
-
-
-def flat(ref, blocks, tiles):
-    got = [ref[blocks, t] for t in tiles]
-    return jnp.concatenate([x.reshape(x.shape[0] * x.shape[1], x.shape[2]) for x in got], axis=1)
-
-
-def occ_kernel(pieces, ids_ref, *refs):
-    tables, (b_hbm, o_ref, b_ref, sems, *results) = refs[:pieces], refs[pieces:]
-    bs, aux, width = b_ref.shape
-    half, lanes = aux // 2, 2 * bs
-    tiles = width // lanes
-
-    def columns(j):
-        return pl.ds(pl.multiple_of(j * (2 * lanes), 2 * lanes), 2 * lanes)
-
-    def copy(j):
-        return pltpu.make_async_copy(b_hbm.at[:, :, columns(j)], b_ref.at[:, :, columns(j)], sems.at[j])
-
-    for j in range(tiles // 2):
-        copy(j).start()
+                v_ref[:, part * each + at + t] = got[:, t * lanes:(t + 1) * lanes].reshape(v_ref.shape[:1] + (aux, lanes))
+
     tall = bs * half
     rep_t = (
         lax.broadcasted_iota(jnp.int32, (bs, tall), 1) // half == lax.broadcasted_iota(jnp.int32, (bs, tall), 0)
@@ -282,29 +282,20 @@
     bs, aux, width = integrals.shape
     pairs = blocks // 2 // (sends + 1)
     side = jax.ShapeDtypeStruct((bs, bs // 2, aux, 2 * bs), jnp.bfloat16)
-    params = pltpu.CompilerParams(vmem_limit_bytes=GRANT)
     cost = pl.CostEstimate(flops=2 * (aux * bs) ** 2 * width, bytes_accessed=4 * aux * bs * width, transcendentals=0)
-    virt_side = pl.pallas_call(
-        functools.partial(virt_kernel, bs, len(tables)),
-        in_specs=in_smem(1) + in_vmem(len(tables) + PARTS),
-        out_specs=in_vmem(1)[0],
-        out_shape=side,
-        compiler_params=params,
-        cost_estimate=cost,
-    )(ids, *tables, *d_parts)
-    occ_side = pl.pallas_call(
-        functools.partial(occ_kernel, len(tables)),
-        in_specs=in_smem(1) + in_vmem(len(tables)) + [pl.BlockSpec(memory_space=pl.ANY)],
-        out_specs=in_vmem(1)[0],
-        out_shape=side,
+    virt_side, occ_side = pl.pallas_call(
+        functools.partial(sides_kernel, len(tables)),
+        in_specs=in_smem(1) + in_vmem(len(tables) + PARTS) + [pl.BlockSpec(memory_space=pl.ANY)],
+        out_specs=in_vmem(2),
+        out_shape=[side, side],
         scratch_shapes=[
             pltpu.VMEM(integrals.shape, integrals.dtype),
             pltpu.SemaphoreType.DMA((bs // 4,)),
         ]
         + [pltpu.VMEM((bs * aux // 2, 4 * bs), jnp.float32)] * 2,
-        compiler_params=pltpu.CompilerParams(vmem_limit_bytes=40 << 20),
+        compiler_params=pltpu.CompilerParams(vmem_limit_bytes=24 << 20),
         cost_estimate=cost,
-    )(ids, *tables, integrals)
+    )(ids, *tables, *d_parts, integrals)
     accs = 2 if blocks <= 128 else 1
     acc = pltpu.VMEM((blocks, bs, 2 * bs), jnp.float32)
     out = pltpu.VMEM((2, aux * bs, 2 * bs), jnp.float32)
@@ -348,9 +339,11 @@
         d_parts += [relayout(integrals, i, after) for i in parts]
     total, send = chi_blocks_of(ids[0], place[0], tables, integrals, d_parts, orb * CB_DEV, 1)
     total = total + exchange(send, 1).astype(jnp.float32)
-    groups = [list(range(parity, orb, 2)) for parity in range(2)]
+    rest = total.shape[0] // 2
+    total = total[:rest] + exchange(total[rest:].astype(jnp.bfloat16), 2).astype(jnp.float32)
+    groups = [list(range(low, orb, 4)) for low in range(4)]
     came = lax.all_to_all(
-        total.reshape(orb // 2, -1, bs, 2 * bs).astype(jnp.bfloat16), "orb", 0, 0, axis_index_groups=groups, tiled=True
+        total.reshape(orb // 4, -1, bs, 2 * bs).astype(jnp.bfloat16), "orb", 0, 0, axis_index_groups=groups, tiled=True
     )
     total = came.astype(jnp.float32).sum(axis=0)
     total = total.reshape(CB_DEV // 2, bs, 2, bs).transpose(0, 2, 1, 3)

time: 62.8 us -> 63.7 us (1.014)
  blocking collectives: 14.9 us -> 10.5 us
  waiting for transfers between devices: 1.54 us -> 5.77 us
  starting transfers between devices: 7.96 us -> 9.57 us
    all_to_all x1, blocking collectives: 14.9 us -> 10.5 us  [local(): lax.all_to_all(total.reshape(orb // 4, -1, bs, 2 * bs).astype(jnp.bfloat1...]
    ppermute x5 -> x6, waiting for transfers between devices: 1.54 us -> 5.77 us  [exchange(): return lax.ppermute(value, 'orb', [(i, i ^ flip) for i in range(orb)])]
    ppermute x5 -> x6, starting transfers between devices: 7.96 us -> 9.57 us  [exchange(): return lax.ppermute(value, 'orb', [(i, i ^ flip) for i in range(orb)])]
    pallas_call x3 -> x2, Pallas kernels: 15 us -> 14.5 us  [the longest x1 13 us: chi_blocks_of(): pl.pallas_call(functools.partial(sides_kernel, len(tables)), in_specs=in_...]
  transfers between devices with their start and end apart: 5 -> 6, of which waited for: 2 -> 3; matrix products, arithmetic and copies ran while one was open for 0% -> 0% of each run, Pallas kernels for 15% -> 15%
where the time goes in v9:
time: 63.7 us; the launch traced here: 63.4 us
  Pallas kernels  35.7 us (56%)
  blocking collectives  10.5 us (16%)
  starting transfers between devices  9.57 us (15%)
  waiting for transfers between devices  5.77 us (9%)
  local copies, waits for them, and re-layouts  0.91 us (1%)
  between operations  0.84 us (1%)
    pallas_call x1, Pallas kernels, chi_blocks_of(): pl.pallas_call(functools.partial(sides_kernel, len(tables)), in_specs=in_...  13 us
    pallas_call x1, Pallas kernels, chi_blocks_of(): pl.pallas_call(functools.partial(chi_kernel, bs, sends), in_specs=in_smem...  11.7 us
    all_to_all x1, blocking collectives, local(): lax.all_to_all(total.reshape(orb // 4, -1, bs, 2 * bs).astype(jnp.bfloat1...  10.5 us
    ppermute x6, starting transfers between devices, exchange(): return lax.ppermute(value, 'orb', [(i, i ^ flip) for i in range(orb)])  9.57 us
    pallas_call x4, Pallas kernels, relayout(): pl.pallas_call(functools.partial(relayout_kernel, part), in_specs=[hidden...  9.49 us
    ppermute x6, waiting for transfers between devices, exchange(): return lax.ppermute(value, 'orb', [(i, i ^ flip) for i in range(orb)])  5.77 us
    pallas_call x1, Pallas kernels, packed(): pl.pallas_call(functools.partial(pack_kernel, 1 << bits - 2, gather_round...  1.44 us
  transfers between devices with their start and end apart: 6, of which 3 were waited for; matrix products, arithmetic and copies ran while one was open for 0% of the time, Pallas kernels for 15%

profile of v9, /device:TPU:0, one launch (start us, length us, event | category | flops | bytes accessed | tf_op | source)
XLA Modules:
  0.0 63.4 jit_solution(17537413009402777243)
XLA Ops:
  0.7 1.4 %shard_map.64 = (bf16[1,64,128]{2,1,0:T(8,128)(2,1)}, s32[1,2]{1,0:T(1,128)}, s32[1,256]{1,0:T(1,128)}) custom-call(s32[1]{0:T(128)} %bitcast.me_ref, s32[1]{0:T(128)S(6)} %copy.8.count_ref, s32[1,2]{1,0:T(1,128)} %refs_0_.1, s32[1,256]{1,0:T(1,128)} %refs_1_.1, bf16[1,4096]{1,0:T(2,128)(2,1)} %refs_2_.1, bf16[1,4096]{1,0:T(2,128)(2,1)} %refs_3_.1), custom_call_target="tpu_custom_call" | custom-call | tf_op jit(solution)/shard_map/pallas_call | solution.py:52
  2.1 4.1 %collective-permute-start = (bf16[1,64,128]{2,1,0:T(8,128)(2,1)}, bf16[1,64,128]{2,1,0:T(8,128)(2,1)S(1)}, u32[]{:S(2)}, u32[]{:S(2)}) collective-permute-start(bf16[1,64,128]{2,1,0:T(8,128)(2,1)} %get-tuple-element.20), channel_id=1, source_target_pairs={{0,8},{1,9},{2,10},{3,11},{4,12},{5,13},{6,14},{7,15},{8,0},{9,1},... | collective-permute-start | bytes 49160 | tf_op jit(solution)/shard_map/ppermute | solution.py:324
  6.2 0.0 copy-start.2
  6.2 2.4 %shard_map.65.refs_2_ = bf16[64,8,16,128]{3,2,1,0:T(8,128)(2,1)S(1)} custom-call(bf16[64,16,4096]{2,1,0:T(8,128)(2,1)} %bitcast.10), custom_call_target="tpu_custom_call" | custom-call | flops 536870912 | bytes 4194304 | tf_op jit(solution)/shard_map/pallas_call | solution.py:118
  8.6 0.0 collective-permute-done.refs_0_
  8.6 0.0 copy-done.2
  8.6 1.6 %collective-permute-start.1 = (bf16[2,64,128]{2,1,0:T(8,128)(2,1)S(1)}, bf16[2,64,128]{2,1,0:T(8,128)(2,1)S(1)}, u32[]{:S(2)}, u32[]{:S(2)}) collective-permute-start(bf16[2,64,128]{2,1,0:T(8,128)(2,1)S(1)} %pad_maximum_fusion.2), channel_id=1, source_target_pairs={{0,4},{1,5},{2,6},{3,7},{4,0},{5,1},{6,2},{7,3},{8,12},{9,13},{10,... | collective-permute-start | bytes 98312 | tf_op jit(solution)/shard_map/ppermute | solution.py:324
  10.3 2.4 %shard_map.66.refs_3_ = bf16[64,8,16,128]{3,2,1,0:T(8,128)(2,1)S(1)} custom-call(bf16[64,16,4096]{2,1,0:T(8,128)(2,1)} %bitcast.11, bf16[1,64,128]{2,1,0:T(8,128)(2,1)S(1)} %collective-permute-done.refs_0_), custom_call_target="tpu_custom_call" | custom-call | flops 536870912 | bytes 4194304 | tf_op jit(solution)/shard_map/pallas_call | solution.py:118
  12.6 0.0 collective-permute-done.1.refs_0_
  12.7 1.6 %collective-permute-start.2 = (bf16[4,64,128]{2,1,0:T(8,128)(2,1)S(1)}, bf16[4,64,128]{2,1,0:T(8,128)(2,1)S(1)}, u32[]{:S(2)}, u32[]{:S(2)}) collective-permute-start(bf16[4,64,128]{2,1,0:T(8,128)(2,1)S(1)} %pad_maximum_fusion.1), channel_id=1, source_target_pairs={{0,2},{1,3},{2,0},{3,1},{4,6},{5,7},{6,4},{7,5},{8,10},{9,11},{10,... | collective-permute-start | bytes 196616 | tf_op jit(solution)/shard_map/ppermute | solution.py:324
  14.3 2.4 %shard_map.67.refs_4_ = bf16[64,8,16,128]{3,2,1,0:T(8,128)(2,1)S(1)} custom-call(bf16[64,16,4096]{2,1,0:T(8,128)(2,1)} %bitcast.12, bf16[2,64,128]{2,1,0:T(8,128)(2,1)S(1)} %collective-permute-done.1.refs_0_), custom_call_target="tpu_custom_call" | custom-call | flops 536870912 | bytes 4194304 | tf_op jit(solution)/shard_map/pallas_call | solution.py:118
  16.6 0.4 collective-permute-done.2.refs_0_
  17.0 0.0 copy-start.1
  17.0 0.1 collective-permute-start.3
  17.1 2.4 %shard_map.68.refs_5_ = bf16[64,8,16,128]{3,2,1,0:T(8,128)(2,1)S(1)} custom-call(bf16[64,16,4096]{2,1,0:T(8,128)(2,1)} %bitcast.13, bf16[4,64,128]{2,1,0:T(8,128)(2,1)S(1)} %collective-permute-done.2.refs_0_), custom_call_target="tpu_custom_call" | custom-call | flops 536870912 | bytes 4194304 | tf_op jit(solution)/shard_map/pallas_call | solution.py:118
  19.5 0.0 collective-permute-done.3.refs_1_
  19.5 0.0 copy-done.1
  19.5 0.0 copy-start
  19.5 13.0 %shard_map.69 = (bf16[64,32,16,128]{3,2,1,0:T(8,128)(2,1)S(1)}, bf16[64,32,16,128]{3,2,1,0:T(8,128)(2,1)S(1)}) custom-call(s32[2]{0:T(128)S(1)} %bitcast.9, bf16[8,64,128]{2,1,0:T(8,128)(2,1)S(1)} %pad_maximum_fusion.refs_0_, bf16[8,64,128]{2,1,0:T(8,128)(2,1)S(1)} %collective-permute-done.3.refs_1_, bf16[64,8,16,128]{3,2,1,0:T(8,128)(2,1)S(1)} %shard_map.65.refs_2_, ...), custom_call_target="tpu_custom_call" | custom-call | flops 8589934592 | bytes 16777216 | tf_op jit(solution)/shard_map/pallas_call | solution.py:286
  32.6 0.0 copy-done
  32.6 11.7 %shard_map.70 = (f32[16,64,128]{2,1,0:T(8,128)S(1)}, bf16[16,64,128]{2,1,0:T(8,128)(2,1)S(1)}) custom-call(s32[256]{0:T(256)S(1)} %bitcast.8, bf16[64,32,16,128]{3,2,1,0:T(8,128)(2,1)S(1)} %get-tuple-element.27.o_ref, bf16[64,32,16,128]{3,2,1,0:T(8,128)(2,1)S(1)} %get-tuple-element.28.v_ref), custom_call_target="tpu_custom_call" | custom-call | flops 8589934592 | bytes 16777216 | tf_op jit(solution)/shard_map/pallas_call | solution.py:302
  44.3 0.6 collective-permute-start.4
  44.8 1.2 %collective-permute-done.4 = bf16[16,64,128]{2,1,0:T(8,128)(2,1)S(1)} collective-permute-done((bf16[16,64,128]{2,1,0:T(8,128)(2,1)S(1)}, bf16[16,64,128]{2,1,0:T(8,128)(2,1)S(1)}, u32[]{:S(2)}, u32[]{:S(2)}) %collective-permute-start.4) | collective-permute-done | bytes 262176 | tf_op jit(solution)/shard_map/ppermute | solution.py:324
  46.0 0.1 convert_add_fusion
  46.1 1.6 %collective-permute-start.5 = (bf16[8,64,128]{2,1,0:T(8,128)(2,1)S(1)}, bf16[8,64,128]{2,1,0:T(8,128)(2,1)S(1)}, u32[]{:S(2)}, u32[]{:S(2)}) collective-permute-start(bf16[8,64,128]{2,1,0:T(8,128)(2,1)S(1)} %slice.15), channel_id=1, source_target_pairs={{0,2},{1,3},{2,0},{3,1},{4,6},{5,7},{6,4},{7,5},{8,10},{9,11},{10,... | collective-permute-start | bytes 393224 | tf_op jit(solution)/shard_map/ppermute | solution.py:324
  47.7 4.2 %collective-permute-done.5 = bf16[8,64,128]{2,1,0:T(8,128)(2,1)S(1)} collective-permute-done((bf16[8,64,128]{2,1,0:T(8,128)(2,1)S(1)}, bf16[8,64,128]{2,1,0:T(8,128)(2,1)S(1)}, u32[]{:S(2)}, u32[]{:S(2)}) %collective-permute-start.5) | collective-permute-done | bytes 131104 | tf_op jit(solution)/shard_map/ppermute | solution.py:324
  52.0 10.5 %all_to_all.5 = bf16[4,2,64,128]{3,2,1,0:T(8,128)(2,1)S(1)} all-to-all(bf16[4,2,64,128]{3,2,1,0:T(8,128)(2,1)S(1)} %bitcast.16), channel_id=1, replica_groups={{0,4,8,12},{1,5,9,13},{2,6,10,14},{3,7,11,15},{16,20,24,28},{17,21,25,2..., dimensions={0} | all-to-all | bytes 262144 | tf_op jit(solution)/shard_map/all_to_all | solution.py:345
  62.5 0.1 reshape.8
  62.6 0.7 %reshape.9 = f32[4,4096]{1,0:T(4,128)} reshape(f32[2,2,64,64]{3,2,1,0:T(8,128)S(1)} %copy.7) | data formatting | bytes 131072 | tf_op jit(solution)/shard_map/reshape | solution.py:350
  (7 shorter events, 0.1 us)
Async XLA Ops:
  2.1 6.5 %collective-permute-start = (bf16[1,64,128]{2,1,0:T(8,128)(2,1)}, bf16[1,64,128]{2,1,0:T(8,128)(2,1)S(1)}, u32[]{:S(2)}, u32[]{:S(2)}) collective-permute-start(bf16[1,64,128]{2,1,0:T(8,128)(2,1)} %get-tuple-element.20), channel_id=1, source_target_pairs={{0,8},{1,9},{2,10},{3,11},{4,12},{5,13},{6,14},{7,15},{8,0},{9,1},... | collective-permute-start | bytes 49160 | tf_op jit(solution)/shard_map/ppermute | solution.py:324
  6.2 2.4 %copy-start.2 = (bf16[1,64,128]{2,1,0:T(8,128)(2,1)S(1)}, bf16[1,64,128]{2,1,0:T(8,128)(2,1)}, u32[]{:S(2)}) copy-start(bf16[1,64,128]{2,1,0:T(8,128)(2,1)} %get-tuple-element.20) | copy-start | bytes 49156
  8.6 4.0 %collective-permute-start.1 = (bf16[2,64,128]{2,1,0:T(8,128)(2,1)S(1)}, bf16[2,64,128]{2,1,0:T(8,128)(2,1)S(1)}, u32[]{:S(2)}, u32[]{:S(2)}) collective-permute-start(bf16[2,64,128]{2,1,0:T(8,128)(2,1)S(1)} %pad_maximum_fusion.2), channel_id=1, source_target_pairs={{0,4},{1,5},{2,6},{3,7},{4,0},{5,1},{6,2},{7,3},{8,12},{9,13},{10,... | collective-permute-start | bytes 98312 | tf_op jit(solution)/shard_map/ppermute | solution.py:324
  12.7 4.3 %collective-permute-start.2 = (bf16[4,64,128]{2,1,0:T(8,128)(2,1)S(1)}, bf16[4,64,128]{2,1,0:T(8,128)(2,1)S(1)}, u32[]{:S(2)}, u32[]{:S(2)}) collective-permute-start(bf16[4,64,128]{2,1,0:T(8,128)(2,1)S(1)} %pad_maximum_fusion.1), channel_id=1, source_target_pairs={{0,2},{1,3},{2,0},{3,1},{4,6},{5,7},{6,4},{7,5},{8,10},{9,11},{10,... | collective-permute-start | bytes 196616 | tf_op jit(solution)/shard_map/ppermute | solution.py:324
  17.0 2.5 %copy-start.1 = (s32[1,2]{1,0:T(1,128)S(1)}, s32[1,2]{1,0:T(1,128)}, u32[]{:S(2)}) copy-start(s32[1,2]{1,0:T(1,128)} %get-tuple-element.19) | copy-start | bytes 28
  17.0 2.5 %collective-permute-start.3 = (bf16[8,64,128]{2,1,0:T(8,128)(2,1)S(1)}, bf16[8,64,128]{2,1,0:T(8,128)(2,1)S(1)}, u32[]{:S(2)}, u32[]{:S(2)}) collective-permute-start(bf16[8,64,128]{2,1,0:T(8,128)(2,1)S(1)} %pad_maximum_fusion.refs_0_), channel_id=1, source_target_pairs={{0,1},{1,0},{2,3},{3,2},{4,5},{5,4},{6,7},{7,6},{8,9},{9,8},{10,11... | collective-permute-start | bytes 393224 | tf_op jit(solution)/shard_map/ppermute | solution.py:324
  19.5 13.1 %copy-start = (s32[1,256]{1,0:T(1,128)S(1)}, s32[1,256]{1,0:T(1,128)}, u32[]{:S(2)}) copy-start(s32[1,256]{1,0:T(1,128)} %get-tuple-element.18) | copy-start | bytes 3076
  44.3 1.7 %collective-permute-start.4 = (bf16[16,64,128]{2,1,0:T(8,128)(2,1)S(1)}, bf16[16,64,128]{2,1,0:T(8,128)(2,1)S(1)}, u32[]{:S(2)}, u32[]{:S(2)}) collective-permute-start(bf16[16,64,128]{2,1,0:T(8,128)(2,1)S(1)} %get-tuple-element.30), channel_id=1, source_target_pairs={{0,1},{1,0},{2,3},{3,2},{4,5},{5,4},{6,7},{7,6},{8,9},{9,8},{10,11... | collective-permute-start | bytes 786440 | tf_op jit(solution)/shard_map/ppermute | solution.py:324
  46.1 5.8 %collective-permute-start.5 = (bf16[8,64,128]{2,1,0:T(8,128)(2,1)S(1)}, bf16[8,64,128]{2,1,0:T(8,128)(2,1)S(1)}, u32[]{:S(2)}, u32[]{:S(2)}) collective-permute-start(bf16[8,64,128]{2,1,0:T(8,128)(2,1)S(1)} %slice.15), channel_id=1, source_target_pairs={{0,2},{1,3},{2,0},{3,1},{4,6},{5,7},{6,4},{7,5},{8,10},{9,11},{10,... | collective-permute-start | bytes 393224 | tf_op jit(solution)/shard_map/ppermute | solution.py:324

commit v10 on v9

--- a/solution.py
+++ b/solution.py
@@ -9,11 +9,10 @@
 
 CB_DEV = 4
 LAM = 4
-PARTS = 4
 GRANT = 8 << 20
 
 
-def pack_kernel(quarter, table_rounds, me_ref, count_ref, *refs):
+def pack_kernel(place_rounds, table_rounds, me_ref, count_ref, *refs):
     sources, (out_ref, ids_ref, place_ref), (rows_ref, *held, sems) = refs[:4], refs[4:7], refs[7:]
     copies = [pltpu.make_async_copy(src, dst, sems.at[k]) for k, (src, dst) in enumerate(zip(sources, held))]
     for copy in copies:
@@ -42,15 +41,16 @@
     ids_ref[...] = ids
 
     targets = tgt_ref[...]
-    owner = targets // CB_DEV
-    rel = owner ^ me
-    place = ((rel & 1) * 2 + ((rel >> 1) & 1)) * quarter + (owner >> 2)
+    rel = (targets // CB_DEV) ^ me
+    place = jnp.zeros_like(targets)
+    for shift, step in place_rounds:
+        place = (place << step) | ((rel >> shift) & ((1 << step) - 1))
     place_ref[...] = place * CB_DEV + targets % CB_DEV
 
 
 def packed(me, basis_count, pair_atoms, chi_target, green_occ, green_virt, bs, bits):
     return pl.pallas_call(
-        functools.partial(pack_kernel, 1 << (bits - 2), gather_rounds(bits)),
+        functools.partial(pack_kernel, owner_rounds(bits), gather_rounds(bits)),
         in_specs=in_smem(2) + [pl.BlockSpec(memory_space=pl.ANY)] * 4,
         out_specs=in_vmem(3),
         out_shape=[
@@ -70,68 +70,12 @@
     return jnp.where(low, one, turned), jnp.where(low, turned, two)
 
 
-def relayout_kernel(part, b_hbm, *refs):
-    d_ref, b_ref, sems, *turns = refs[-5:]
-    lams, aux, width = b_ref.shape
-    lanes = d_ref.shape[3]
-    tiles, half, bs = width // lanes, aux // 2, lanes // 2
-
-    def copy(i):
-        held = pl.ds(2 * i, 2)
-        return pltpu.make_async_copy(b_hbm.at[pl.ds(part * lams + 2 * i, 2)], b_ref.at[held], sems.at[i])
-
-    for i in range(lams // 2):
-        copy(i).start()
-    low = lax.broadcasted_iota(jnp.int32, (aux, lanes), 1) < bs
-
-    def turned(i, turn):
-        for c in range(tiles):
-            one, two = [b_ref[2 * i + k, :, c * lanes:(c + 1) * lanes].astype(jnp.float32) for k in range(2)]
-            for k, joined in enumerate(halves_joined(one, two, low, lanes)):
-                for h in range(2):
-                    at = (h * bs + 2 * c + k) * half
-                    turn[at:at + half, :] = joined[h * half:(h + 1) * half]
-        for a in range(aux):
-            rows = turn[pl.ds(a // half * (bs * half) + a % half, bs, stride=half), :].astype(jnp.bfloat16)
-            d_ref[a * (bs // aux):(a + 1) * (bs // aux), i] = rows.reshape(bs // aux, aux, lanes)
-
-    @pl.loop(0, lams // 4)
-    def _(i):
-        for k, turn in enumerate(turns):
-            copy(2 * i + k).wait()
-        for k, turn in enumerate(turns):
-            turned(2 * i + k, turn)
-
-
 def in_vmem(count):
     return [pl.BlockSpec(memory_space=pltpu.VMEM)] * count
 
 
 def in_smem(count):
     return [pl.BlockSpec(memory_space=pltpu.SMEM)] * count
-
-
-def relayout(integrals, part, after):
-    bs, aux, width = integrals.shape
-    lams = bs // PARTS
-    hidden = pl.BlockSpec(memory_space=pl.ANY)
-    return pl.pallas_call(
-        functools.partial(relayout_kernel, part),
-        in_specs=[hidden] * (1 + len(after)),
-        out_specs=in_vmem(1)[0],
-        out_shape=jax.ShapeDtypeStruct((bs, lams // 2, aux, 2 * bs), jnp.bfloat16),
-        scratch_shapes=[
-            pltpu.VMEM((lams, aux, width), integrals.dtype),
-            pltpu.SemaphoreType.DMA((lams // 2,)),
-        ]
-        + [pltpu.VMEM((aux * bs, 2 * bs), jnp.float32)] * 2,
-        compiler_params=pltpu.CompilerParams(vmem_limit_bytes=48 << 20),
-        cost_estimate=pl.CostEstimate(
-            flops=2 * bs * aux * width * 256 // PARTS,
-            bytes_accessed=4 * bs * aux * width // PARTS,
-            transcendentals=0,
-        ),
-    )(integrals, *after)
 
 
 def spread_rows(block, of_row, count, bs):
@@ -156,35 +100,29 @@
 
 
 def sides_kernel(pieces, ids_ref, *refs):
-    tables, d_parts, refs = refs[:pieces], refs[pieces:pieces + PARTS], refs[pieces + PARTS:]
-    b_hbm, v_ref, o_ref, b_ref, sems, *results = refs
+    tables, (b_hbm, v_ref, o_ref, b_ref, sems, virt_res, turn, *occ_res) = refs[:pieces], refs[pieces:]
     bs, aux, width = b_ref.shape
     half, lanes = aux // 2, 2 * bs
     tiles = width // lanes
+    wide = LAM * bs
+    steps = width // wide
+    group = aux // LAM
 
     def columns(j):
-        return pl.ds(pl.multiple_of(j * (2 * lanes), 2 * lanes), 2 * lanes)
+        return pl.ds(pl.multiple_of(j * wide, wide), wide)
 
     def copy(j):
         return pltpu.make_async_copy(b_hbm.at[:, :, columns(j)], b_ref.at[:, :, columns(j)], sems.at[j])
 
-    for j in range(tiles // 2):
+    for j in range(steps):
         copy(j).start()
 
-    wide = LAM * bs
     spread = spread_rows(green_block(tables, ids_ref[1])[bs // 2:], lambda i: i % bs, wide, bs)
     spread = jnp.concatenate([spread] * LAM, axis=1)
     same = (
         lax.broadcasted_iota(jnp.int32, (wide, wide), 0) // bs == lax.broadcasted_iota(jnp.int32, (wide, wide), 1) // bs
     )
     virt_w = jnp.where(same, spread, 0.0).astype(jnp.bfloat16)
-    each = d_parts[0].shape[1]
-    for part in range(PARTS):
-        for at in range(0, each, 2):
-            got = jnp.dot(flat(d_parts[part], slice(None), [at, at + 1]), virt_w, preferred_element_type=jnp.float32)
-            got = got.astype(jnp.bfloat16)
-            for t in range(2):
-                v_ref[:, part * each + at + t] = got[:, t * lanes:(t + 1) * lanes].reshape(v_ref.shape[:1] + (aux, lanes))
 
     tall = bs * half
     rep_t = (
@@ -199,31 +137,52 @@
     occ_w = jnp.where(same, spread, 0.0).astype(jnp.bfloat16)
     low = lax.broadcasted_iota(jnp.int32, (bs // 2, half, lanes), 2) < lanes // 2
 
-    def product(j, h):
+    def occ_product(j, h):
         block = b_ref[:, :, columns(j)].astype(jnp.float32)[:, h * half:(h + 1) * half]
-        side = block.reshape(tall, 2 * lanes).astype(jnp.bfloat16)
-        results[h][...] = jnp.dot(occ_w, side, preferred_element_type=jnp.float32)
-
-    def placed(j, h):
-        for t in range(2):
-            got = results[h][:, t * lanes:(t + 1) * lanes].reshape(bs // 2, 2, half, lanes)
+        side = block.reshape(tall, wide).astype(jnp.bfloat16)
+        occ_res[h][...] = jnp.dot(occ_w, side, preferred_element_type=jnp.float32)
+
+    def occ_placed(j, h):
+        for t in range(wide // lanes):
+            got = occ_res[h][:, t * lanes:(t + 1) * lanes].reshape(bs // 2, 2, half, lanes)
             pair = halves_joined(got[:, 0], got[:, 1], low, lanes)
             o_ref[h * tiles + 2 * j + t] = jnp.concatenate(pair, axis=1).astype(jnp.bfloat16)
 
-    copy(0).wait()
-    product(0, 0)
-    product(0, 1)
-    placed(0, 0)
-
-    @pl.loop(1, tiles // 2)
+    def virt_product(j):
+        block = b_ref[:, :, columns(j)].reshape(bs * aux, wide)
+        virt_res[...] = jnp.dot(block, virt_w, preferred_element_type=jnp.float32)
+
+    def virt_turned(j):
+        for t in range(wide // lanes):
+            got = virt_res[:, t * lanes:(t + 1) * lanes].reshape(bs // 2, 2, 2, half, lanes)
+            for h in range(2):
+                for k, joined in enumerate(halves_joined(got[:, 0, h], got[:, 1, h], low, lanes)):
+                    at = ((j % group) * LAM + 2 * t + k) * half
+                    turn[j // group % 2, :, h, pl.ds(pl.multiple_of(at, half), half), :] = joined
+
+    def virt_placed(block, tile):
+        for a in range(aux):
+            rows = turn[block % 2, tile, a // half, pl.ds(a % half, aux, stride=half), :]
+            v_ref[a * (bs // aux) + block, tile] = rows.astype(jnp.bfloat16)
+
+    @pl.loop(0, steps)
     def _(j):
+        before = jnp.maximum(j - 1, 0)
+        block = jnp.maximum(j // group - 1, 0)
         copy(j).wait()
-        placed(j - 1, 1)
-        product(j, 0)
-        placed(j, 0)
-        product(j, 1)
-
-    placed(tiles // 2 - 1, 1)
+        occ_placed(before, 1)
+        occ_product(j, 0)
+        virt_turned(before)
+        virt_product(j)
+        occ_placed(j, 0)
+        occ_product(j, 1)
+        for tile in range(tiles // group):
+            virt_placed(block, (j % group) * (tiles // group) + tile)
+
+    occ_placed(steps - 1, 1)
+    virt_turned(steps - 1)
+    for tile in range(tiles):
+        virt_placed(steps // group - 1, tile)
 
 
 def chi_kernel(bs, sends, tgt_ref, o_ref, v_ref, *refs):
@@ -278,24 +237,26 @@
             send_ref[i] = joined((k + 1) * pairs + i).astype(jnp.bfloat16)
 
 
-def chi_blocks_of(ids, targets, tables, integrals, d_parts, blocks, sends):
+def chi_blocks_of(ids, targets, tables, integrals, blocks, sends):
     bs, aux, width = integrals.shape
     pairs = blocks // 2 // (sends + 1)
     side = jax.ShapeDtypeStruct((bs, bs // 2, aux, 2 * bs), jnp.bfloat16)
     cost = pl.CostEstimate(flops=2 * (aux * bs) ** 2 * width, bytes_accessed=4 * aux * bs * width, transcendentals=0)
     virt_side, occ_side = pl.pallas_call(
         functools.partial(sides_kernel, len(tables)),
-        in_specs=in_smem(1) + in_vmem(len(tables) + PARTS) + [pl.BlockSpec(memory_space=pl.ANY)],
+        in_specs=in_smem(1) + in_vmem(len(tables)) + [pl.BlockSpec(memory_space=pl.ANY)],
         out_specs=in_vmem(2),
         out_shape=[side, side],
         scratch_shapes=[
             pltpu.VMEM(integrals.shape, integrals.dtype),
-            pltpu.SemaphoreType.DMA((bs // 4,)),
+            pltpu.SemaphoreType.DMA((bs // LAM,)),
+            pltpu.VMEM((bs * aux, LAM * bs), jnp.float32),
+            pltpu.VMEM((2, bs // 2, 2, aux * aux // 2, 2 * bs), jnp.float32),
         ]
-        + [pltpu.VMEM((bs * aux // 2, 4 * bs), jnp.float32)] * 2,
-        compiler_params=pltpu.CompilerParams(vmem_limit_bytes=24 << 20),
+        + [pltpu.VMEM((bs * aux // 2, LAM * bs), jnp.float32)] * 2,
+        compiler_params=pltpu.CompilerParams(vmem_limit_bytes=32 << 20),
         cost_estimate=cost,
-    )(ids, *tables, *d_parts, integrals)
+    )(ids, *tables, integrals)
     accs = 2 if blocks <= 128 else 1
     acc = pltpu.VMEM((blocks, bs, 2 * bs), jnp.float32)
     out = pltpu.VMEM((2, aux * bs, 2 * bs), jnp.float32)
@@ -315,6 +276,15 @@
     return [(bit, 1) for bit in reversed(range(bits))]
 
 
+def owner_rounds(bits):
+    rounds, at = [], 0
+    while at < bits:
+        step = 1 if at < 2 else min(2, bits - at)
+        rounds.append((at, step))
+        at += step
+    return rounds
+
+
 def local(orb, three_centre, green_occ, green_virt, pair_atoms, basis_count, chi_target):
     bs = three_centre.shape[1]
     bits = orb.bit_length() - 1
@@ -327,25 +297,18 @@
     table, ids, place = packed(
         me[None].astype(jnp.int32), basis_count, pair_atoms, chi_target, green_occ, green_virt, bs, bits
     )
-    rounds = gather_rounds(bits)
-    tables, d_parts = [table], []
-    for k, (shift, step) in enumerate(rounds):
-        after = tables[-1:] if k else []
+    tables = [table]
+    for shift, step in gather_rounds(bits):
         table = tables[0] if len(tables) == 1 else jnp.concatenate(tables, axis=0)
-        if k and len(d_parts) == k:
-            table, d_parts[-1] = lax.optimization_barrier((table, d_parts[-1]))
         tables = [table] + [exchange(table, v << shift) for v in range(1, 1 << step)]
-        parts = [i for i in range(PARTS) if min(i, len(rounds) - 1) == k]
-        d_parts += [relayout(integrals, i, after) for i in parts]
-    total, send = chi_blocks_of(ids[0], place[0], tables, integrals, d_parts, orb * CB_DEV, 1)
-    total = total + exchange(send, 1).astype(jnp.float32)
-    rest = total.shape[0] // 2
-    total = total[:rest] + exchange(total[rest:].astype(jnp.bfloat16), 2).astype(jnp.float32)
-    groups = [list(range(low, orb, 4)) for low in range(4)]
-    came = lax.all_to_all(
-        total.reshape(orb // 4, -1, bs, 2 * bs).astype(jnp.bfloat16), "orb", 0, 0, axis_index_groups=groups, tiled=True
-    )
-    total = came.astype(jnp.float32).sum(axis=0)
+    total, *sends = chi_blocks_of(ids[0], place[0], tables, integrals, orb * CB_DEV, 1)
+    for k, (shift, step) in enumerate(owner_rounds(bits)):
+        if k:
+            rest = total.shape[0] >> step
+            sends = [total[v * rest:(v + 1) * rest].astype(jnp.bfloat16) for v in range(1, 1 << step)]
+            total = total[:rest]
+        for v, send in enumerate(sends):
+            total = total + exchange(send, (v + 1) << shift).astype(jnp.float32)
     total = total.reshape(CB_DEV // 2, bs, 2, bs).transpose(0, 2, 1, 3)
     return total.reshape(CB_DEV, bs * bs)
 

time: 63.7 us -> 69 us (1.083)
  waiting for transfers between devices: 5.77 us -> 17 us
  blocking collectives: 10.5 us -> 0 us
  starting transfers between devices: 9.57 us -> 14.6 us
  Pallas kernels: 35.7 us -> 32.2 us
  other arithmetic: 0.13 us -> 1.56 us
  local copies, waits for them, and re-layouts: 0.91 us -> 2.26 us
    ppermute x6 -> x9, waiting for transfers between devices: 5.77 us -> 17 us  [exchange(): return lax.ppermute(value, 'orb', [(i, i ^ flip) for i in range(orb)])]
    all_to_all x1 -> x0, blocking collectives: 10.5 us -> none  [local(): lax.all_to_all(total.reshape(orb // 4, -1, bs, 2 * bs).astype(jnp.bfloat1...]
    pallas_call x5 -> x1, Pallas kernels: 10.9 us -> 1.44 us  [packed(): pl.pallas_call(functools.partial(pack_kernel, owner_rounds(bits), gather_...]
    pallas_call x1, Pallas kernels: 13 us -> 19.1 us  [chi_blocks_of(): pl.pallas_call(functools.partial(sides_kernel, len(tables)), in_specs=in_...]
    ppermute x6 -> x9, starting transfers between devices: 9.57 us -> 14.6 us  [exchange(): return lax.ppermute(value, 'orb', [(i, i ^ flip) for i in range(orb)])]
    concatenate x3 -> x2, other arithmetic: 0.03 us -> 1.45 us  [local(): table = tables[0] if len(tables) == 1 else jnp.concatenate(tables, axis=0)]
    unnamed x6 -> x7, local copies, waits for them, and re-layouts: 0.01 us -> 1.35 us
  transfers between devices with their start and end apart: 6 -> 9, of which waited for: 3 -> 8; matrix products, arithmetic and copies ran while one was open for 0% -> 1% of each run, Pallas kernels for 15% -> 0%
where the time goes in v10:
time: 69 us; the launch traced here: 68.4 us
  Pallas kernels  32.2 us (47%)
  waiting for transfers between devices  17 us (25%)
  starting transfers between devices  14.6 us (21%)
  local copies, waits for them, and re-layouts  2.26 us (3%)
  other arithmetic  1.56 us (2%)
  between operations  0.75 us (1%)
    pallas_call x1, Pallas kernels, chi_blocks_of(): pl.pallas_call(functools.partial(sides_kernel, len(tables)), in_specs=in_...  19.1 us
    ppermute x9, waiting for transfers between devices, exchange(): return lax.ppermute(value, 'orb', [(i, i ^ flip) for i in range(orb)])  17 us
    ppermute x9, starting transfers between devices, exchange(): return lax.ppermute(value, 'orb', [(i, i ^ flip) for i in range(orb)])  14.6 us
    pallas_call x1, Pallas kernels, chi_blocks_of(): pl.pallas_call(functools.partial(chi_kernel, bs, sends), in_specs=in_smem...  11.7 us
    concatenate x2, other arithmetic, local(): table = tables[0] if len(tables) == 1 else jnp.concatenate(tables, axis=0)  1.45 us
    pallas_call x1, Pallas kernels, packed(): pl.pallas_call(functools.partial(pack_kernel, owner_rounds(bits), gather_...  1.44 us
  transfers between devices with their start and end apart: 9, of which 8 were waited for; matrix products, arithmetic and copies ran while one was open for 1% of the time, Pallas kernels for 0%

profile of v10, /device:TPU:0, one launch (start us, length us, event | category | flops | bytes accessed | tf_op | source)
XLA Modules:
  0.0 68.4 jit_solution(8647404644670508755)
XLA Ops:
  0.7 1.4 %shard_map.64 = (bf16[1,64,128]{2,1,0:T(8,128)(2,1)}, s32[1,2]{1,0:T(1,128)}, s32[1,256]{1,0:T(1,128)}) custom-call(s32[1]{0:T(128)} %bitcast.me_ref, s32[1]{0:T(128)S(6)} %copy.11.count_ref, s32[1,2]{1,0:T(1,128)} %refs_0_.1, s32[1,256]{1,0:T(1,128)} %refs_1_.1, bf16[1,4096]{1,0:T(2,128)(2,1)} %refs_2_.1, bf16[1,4096]{1,0:T(2,128)(2,1)} %refs_3_.1), custom_call_target="tpu_custom_call" | custom-call | tf_op jit(solution)/shard_map/pallas_call | solution.py:52
  2.1 4.1 %collective-permute-start = (bf16[1,64,128]{2,1,0:T(8,128)(2,1)}, bf16[1,64,128]{2,1,0:T(8,128)(2,1)S(1)}, u32[]{:S(2)}, u32[]{:S(2)}) collective-permute-start(bf16[1,64,128]{2,1,0:T(8,128)(2,1)} %get-tuple-element.14), channel_id=1, source_target_pairs={{0,8},{1,9},{2,10},{3,11},{4,12},{5,13},{6,14},{7,15},{8,0},{9,1},... | collective-permute-start | bytes 49160 | tf_op jit(solution)/shard_map/ppermute | solution.py:294
  6.2 0.8 %constant_dynamic-update-slice_fusion.3 = bf16[8,64,128]{2,1,0:T(8,128)(2,1)S(1)} fusion(bf16[1,64,128]{2,1,0:T(8,128)(2,1)} %get-tuple-element.14), kind=kLoop, calls=%fused_computation.11 | loop fusion | bytes 32768
  7.0 1.2 %collective-permute-done = bf16[1,64,128]{2,1,0:T(8,128)(2,1)S(1)} collective-permute-done((bf16[1,64,128]{2,1,0:T(8,128)(2,1)}, bf16[1,64,128]{2,1,0:T(8,128)(2,1)S(1)}, u32[]{:S(2)}, u32[]{:S(2)}) %collective-permute-start) | collective-permute-done | bytes 16416 | tf_op jit(solution)/shard_map/ppermute | solution.py:294
  8.1 0.7 %pad_maximum_fusion.1 = bf16[2,64,128]{2,1,0:T(8,128)(2,1)S(1)} fusion(bf16[1,64,128]{2,1,0:T(8,128)(2,1)S(1)} %collective-permute-done, bf16[1,64,128]{2,1,0:T(8,128)(2,1)} %get-tuple-element.14), kind=kLoop, calls=%fused_computation.7 | loop fusion | flops 16384 | bytes 65536 | tf_op jit(solution)/shard_map/concatenate | solution.py:302
  8.9 1.9 %collective-permute-start.1 = (bf16[2,64,128]{2,1,0:T(8,128)(2,1)S(1)}, bf16[2,64,128]{2,1,0:T(8,128)(2,1)S(1)}, u32[]{:S(2)}, u32[]{:S(2)}) collective-permute-start(bf16[2,64,128]{2,1,0:T(8,128)(2,1)S(1)} %pad_maximum_fusion.1), channel_id=1, source_target_pairs={{0,4},{1,5},{2,6},{3,7},{4,0},{5,1},{6,2},{7,3},{8,12},{9,13},{10,... | collective-permute-start | bytes 98312 | tf_op jit(solution)/shard_map/ppermute | solution.py:294
  10.8 2.0 %collective-permute-done.1 = bf16[2,64,128]{2,1,0:T(8,128)(2,1)S(1)} collective-permute-done((bf16[2,64,128]{2,1,0:T(8,128)(2,1)S(1)}, bf16[2,64,128]{2,1,0:T(8,128)(2,1)S(1)}, u32[]{:S(2)}, u32[]{:S(2)}) %collective-permute-start.1) | collective-permute-done | bytes 32800 | tf_op jit(solution)/shard_map/ppermute | solution.py:294
  12.8 0.7 %pad_maximum_fusion = bf16[4,64,128]{2,1,0:T(8,128)(2,1)S(1)} fusion(bf16[2,64,128]{2,1,0:T(8,128)(2,1)S(1)} %collective-permute-done.1, bf16[1,64,128]{2,1,0:T(8,128)(2,1)S(1)} %collective-permute-done, bf16[1,64,128]{2,1,0:T(8,128)(2,1)} %get-tuple-element.14), kind=kLoop, calls=%fused_computation.6 | loop fusion | flops 65536 | bytes 131072 | tf_op jit(solution)/shard_map/concatenate | solution.py:302
  13.5 1.9 %collective-permute-start.2 = (bf16[4,64,128]{2,1,0:T(8,128)(2,1)S(1)}, bf16[4,64,128]{2,1,0:T(8,128)(2,1)S(1)}, u32[]{:S(2)}, u32[]{:S(2)}) collective-permute-start(bf16[4,64,128]{2,1,0:T(8,128)(2,1)S(1)} %pad_maximum_fusion), channel_id=1, source_target_pairs={{0,2},{1,3},{2,0},{3,1},{4,6},{5,7},{6,4},{7,5},{8,10},{9,11},{10,... | collective-permute-start | bytes 196616 | tf_op jit(solution)/shard_map/ppermute | solution.py:294
  15.4 2.4 %collective-permute-done.2 = bf16[4,64,128]{2,1,0:T(8,128)(2,1)S(1)} collective-permute-done((bf16[4,64,128]{2,1,0:T(8,128)(2,1)S(1)}, bf16[4,64,128]{2,1,0:T(8,128)(2,1)S(1)}, u32[]{:S(2)}, u32[]{:S(2)}) %collective-permute-start.2) | collective-permute-done | bytes 65568 | tf_op jit(solution)/shard_map/ppermute | solution.py:294
  17.8 0.1 collective-permute-start.3
  17.9 1.3 %collective-permute-done.3.refs_1_ = bf16[8,64,128]{2,1,0:T(8,128)(2,1)S(1)} collective-permute-done((bf16[8,64,128]{2,1,0:T(8,128)(2,1)S(1)}, bf16[8,64,128]{2,1,0:T(8,128)(2,1)S(1)}, u32[]{:S(2)}, u32[]{:S(2)}) %collective-permute-start.3) | collective-permute-done | bytes 131104 | tf_op jit(solution)/shard_map/ppermute | solution.py:294
  19.2 0.0 copy-start.1
  19.2 0.6 copy-done.1
  19.8 0.0 copy-start
  19.8 19.1 %shard_map.65 = (bf16[64,32,16,128]{3,2,1,0:T(8,128)(2,1)S(1)}, bf16[64,32,16,128]{3,2,1,0:T(8,128)(2,1)S(1)}) custom-call(s32[2]{0:T(128)S(1)} %bitcast.8, bf16[8,64,128]{2,1,0:T(8,128)(2,1)S(1)} %constant_dynamic-update-slice_fusion.refs_0_, bf16[8,64,128]{2,1,0:T(8,128)(2,1)S(1)} %collective-permute-done.3.refs_1_, bf16[64,16,4096]{2,1,0:T(8,128)(2,1)} %bitcast.10), custom_call_target="tpu_custom_call" | custom-call | flops 8589934592 | bytes 16777216 | tf_op jit(solution)/shard_map/pallas_call | solution.py:245
  38.8 0.0 copy-done
  38.9 11.7 %shard_map.66 = (f32[16,64,128]{2,1,0:T(8,128)S(1)}, bf16[16,64,128]{2,1,0:T(8,128)(2,1)S(1)}) custom-call(s32[256]{0:T(256)S(1)} %bitcast.7, bf16[64,32,16,128]{3,2,1,0:T(8,128)(2,1)S(1)} %get-tuple-element.15.o_ref, bf16[64,32,16,128]{3,2,1,0:T(8,128)(2,1)S(1)} %get-tuple-element.16.v_ref), custom_call_target="tpu_custom_call" | custom-call | flops 8589934592 | bytes 16777216 | tf_op jit(solution)/shard_map/pallas_call | solution.py:263
  50.5 0.2 collective-permute-start.4
  50.8 1.4 %collective-permute-done.4 = bf16[16,64,128]{2,1,0:T(8,128)(2,1)S(1)} collective-permute-done((bf16[16,64,128]{2,1,0:T(8,128)(2,1)S(1)}, bf16[16,64,128]{2,1,0:T(8,128)(2,1)S(1)}, u32[]{:S(2)}, u32[]{:S(2)}) %collective-permute-start.4) | collective-permute-done | bytes 262176 | tf_op jit(solution)/shard_map/ppermute | solution.py:294
  52.1 0.1 convert_add_fusion
  52.2 2.0 %collective-permute-start.5 = (bf16[8,64,128]{2,1,0:T(8,128)(2,1)S(1)}, bf16[8,64,128]{2,1,0:T(8,128)(2,1)S(1)}, u32[]{:S(2)}, u32[]{:S(2)}) collective-permute-start(bf16[8,64,128]{2,1,0:T(8,128)(2,1)S(1)} %slice.41), channel_id=1, source_target_pairs={{0,2},{1,3},{2,0},{3,1},{4,6},{5,7},{6,4},{7,5},{8,10},{9,11},{10,... | collective-permute-start | bytes 393224 | tf_op jit(solution)/shard_map/ppermute | solution.py:294
  54.2 3.8 %collective-permute-done.5 = bf16[8,64,128]{2,1,0:T(8,128)(2,1)S(1)} collective-permute-done((bf16[8,64,128]{2,1,0:T(8,128)(2,1)S(1)}, bf16[8,64,128]{2,1,0:T(8,128)(2,1)S(1)}, u32[]{:S(2)}, u32[]{:S(2)}) %collective-permute-start.5) | collective-permute-done | bytes 131104 | tf_op jit(solution)/shard_map/ppermute | solution.py:294
  58.1 1.8 %collective-permute-start.6 = (bf16[2,64,128]{2,1,0:T(8,128)(2,1)S(1)}, bf16[2,64,128]{2,1,0:T(8,128)(2,1)S(1)}, u32[]{:S(2)}, u32[]{:S(2)}) collective-permute-start(bf16[2,64,128]{2,1,0:T(8,128)(2,1)S(1)} %get-tuple-element.21), channel_id=1, source_target_pairs={{0,4},{1,5},{2,6},{3,7},{4,0},{5,1},{6,2},{7,3},{8,12},{9,13},{10,... | collective-permute-start | bytes 98312 | tf_op jit(solution)/shard_map/ppermute | solution.py:294
  59.9 2.5 %collective-permute-start.8 = (bf16[2,64,128]{2,1,0:T(8,128)(2,1)S(1)}, bf16[2,64,128]{2,1,0:T(8,128)(2,1)S(1)}, u32[]{:S(2)}, u32[]{:S(2)}) collective-permute-start(bf16[2,64,128]{2,1,0:T(8,128)(2,1)S(1)} %get-tuple-element.22), channel_id=1, source_target_pairs={{0,12},{1,13},{2,14},{3,15},{4,8},{5,9},{6,10},{7,11},{8,4},{9,5},... | collective-permute-start | bytes 98312 | tf_op jit(solution)/shard_map/ppermute | solution.py:294
  62.4 0.2 collective-permute-start.7
  62.5 0.0 collective-permute-done.6
  62.5 3.1 %collective-permute-done.8 = bf16[2,64,128]{2,1,0:T(8,128)(2,1)S(1)} collective-permute-done((bf16[2,64,128]{2,1,0:T(8,128)(2,1)S(1)}, bf16[2,64,128]{2,1,0:T(8,128)(2,1)S(1)}, u32[]{:S(2)}, u32[]{:S(2)}) %collective-permute-start.8) | collective-permute-done | bytes 32800 | tf_op jit(solution)/shard_map/ppermute | solution.py:294
  65.6 1.9 %collective-permute-done.7 = bf16[2,64,128]{2,1,0:T(8,128)(2,1)S(1)} collective-permute-done((bf16[2,64,128]{2,1,0:T(8,128)(2,1)S(1)}, bf16[2,64,128]{2,1,0:T(8,128)(2,1)S(1)}, u32[]{:S(2)}, u32[]{:S(2)}) %collective-permute-start.7) | collective-permute-done | bytes 32800 | tf_op jit(solution)/shard_map/ppermute | solution.py:294
  67.5 0.1 reshape.6
  67.7 0.7 %reshape.7 = f32[4,4096]{1,0:T(4,128)} reshape(f32[2,2,64,64]{3,2,1,0:T(8,128)S(1)} %copy.7) | data formatting | bytes 131072 | tf_op jit(solution)/shard_map/reshape | solution.py:313
  (8 shorter events, 0.1 us)
Async XLA Ops:
  2.1 6.0 %collective-permute-start = (bf16[1,64,128]{2,1,0:T(8,128)(2,1)}, bf16[1,64,128]{2,1,0:T(8,128)(2,1)S(1)}, u32[]{:S(2)}, u32[]{:S(2)}) collective-permute-start(bf16[1,64,128]{2,1,0:T(8,128)(2,1)} %get-tuple-element.14), channel_id=1, source_target_pairs={{0,8},{1,9},{2,10},{3,11},{4,12},{5,13},{6,14},{7,15},{8,0},{9,1},... | collective-permute-start | bytes 49160 | tf_op jit(solution)/shard_map/ppermute | solution.py:294
  8.9 3.9 %collective-permute-start.1 = (bf16[2,64,128]{2,1,0:T(8,128)(2,1)S(1)}, bf16[2,64,128]{2,1,0:T(8,128)(2,1)S(1)}, u32[]{:S(2)}, u32[]{:S(2)}) collective-permute-start(bf16[2,64,128]{2,1,0:T(8,128)(2,1)S(1)} %pad_maximum_fusion.1), channel_id=1, source_target_pairs={{0,4},{1,5},{2,6},{3,7},{4,0},{5,1},{6,2},{7,3},{8,12},{9,13},{10,... | collective-permute-start | bytes 98312 | tf_op jit(solution)/shard_map/ppermute | solution.py:294
  13.5 4.3 %collective-permute-start.2 = (bf16[4,64,128]{2,1,0:T(8,128)(2,1)S(1)}, bf16[4,64,128]{2,1,0:T(8,128)(2,1)S(1)}, u32[]{:S(2)}, u32[]{:S(2)}) collective-permute-start(bf16[4,64,128]{2,1,0:T(8,128)(2,1)S(1)} %pad_maximum_fusion), channel_id=1, source_target_pairs={{0,2},{1,3},{2,0},{3,1},{4,6},{5,7},{6,4},{7,5},{8,10},{9,11},{10,... | collective-permute-start | bytes 196616 | tf_op jit(solution)/shard_map/ppermute | solution.py:294
  17.8 1.4 %collective-permute-start.3 = (bf16[8,64,128]{2,1,0:T(8,128)(2,1)S(1)}, bf16[8,64,128]{2,1,0:T(8,128)(2,1)S(1)}, u32[]{:S(2)}, u32[]{:S(2)}) collective-permute-start(bf16[8,64,128]{2,1,0:T(8,128)(2,1)S(1)} %constant_dynamic-update-slice_fusion.refs_0_), channel_id=1, source_target_pairs={{0,1},{1,0},{2,3},{3,2},{4,5},{5,4},{6,7},{7,6},{8,9},{9,8},{10,11... | collective-permute-start | bytes 393224 | tf_op jit(solution)/shard_map/ppermute | solution.py:294
  19.2 0.6 copy-start.1
  19.8 19.1 %copy-start = (s32[1,256]{1,0:T(1,128)S(1)}, s32[1,256]{1,0:T(1,128)}, u32[]{:S(2)}) copy-start(s32[1,256]{1,0:T(1,128)} %get-tuple-element.12) | copy-start | bytes 3076
  50.5 1.6 %collective-permute-start.4 = (bf16[16,64,128]{2,1,0:T(8,128)(2,1)S(1)}, bf16[16,64,128]{2,1,0:T(8,128)(2,1)S(1)}, u32[]{:S(2)}, u32[]{:S(2)}) collective-permute-start(bf16[16,64,128]{2,1,0:T(8,128)(2,1)S(1)} %get-tuple-element.18), channel_id=1, source_target_pairs={{0,1},{1,0},{2,3},{3,2},{4,5},{5,4},{6,7},{7,6},{8,9},{9,8},{10,11... | collective-permute-start | bytes 786440 | tf_op jit(solution)/shard_map/ppermute | solution.py:294
  52.2 5.8 %collective-permute-start.5 = (bf16[8,64,128]{2,1,0:T(8,128)(2,1)S(1)}, bf16[8,64,128]{2,1,0:T(8,128)(2,1)S(1)}, u32[]{:S(2)}, u32[]{:S(2)}) collective-permute-start(bf16[8,64,128]{2,1,0:T(8,128)(2,1)S(1)} %slice.41), channel_id=1, source_target_pairs={{0,2},{1,3},{2,0},{3,1},{4,6},{5,7},{6,4},{7,5},{8,10},{9,11},{10,... | collective-permute-start | bytes 393224 | tf_op jit(solution)/shard_map/ppermute | solution.py:294
  58.1 4.5 %collective-permute-start.6 = (bf16[2,64,128]{2,1,0:T(8,128)(2,1)S(1)}, bf16[2,64,128]{2,1,0:T(8,128)(2,1)S(1)}, u32[]{:S(2)}, u32[]{:S(2)}) collective-permute-start(bf16[2,64,128]{2,1,0:T(8,128)(2,1)S(1)} %get-tuple-element.21), channel_id=1, source_target_pairs={{0,4},{1,5},{2,6},{3,7},{4,0},{5,1},{6,2},{7,3},{8,12},{9,13},{10,... | collective-permute-start | bytes 98312 | tf_op jit(solution)/shard_map/ppermute | solution.py:294
  59.9 5.7 %collective-permute-start.8 = (bf16[2,64,128]{2,1,0:T(8,128)(2,1)S(1)}, bf16[2,64,128]{2,1,0:T(8,128)(2,1)S(1)}, u32[]{:S(2)}, u32[]{:S(2)}) collective-permute-start(bf16[2,64,128]{2,1,0:T(8,128)(2,1)S(1)} %get-tuple-element.22), channel_id=1, source_target_pairs={{0,12},{1,13},{2,14},{3,15},{4,8},{5,9},{6,10},{7,11},{8,4},{9,5},... | collective-permute-start | bytes 98312 | tf_op jit(solution)/shard_map/ppermute | solution.py:294
  62.4 5.2 %collective-permute-start.7 = (bf16[2,64,128]{2,1,0:T(8,128)(2,1)S(1)}, bf16[2,64,128]{2,1,0:T(8,128)(2,1)S(1)}, u32[]{:S(2)}, u32[]{:S(2)}) collective-permute-start(bf16[2,64,128]{2,1,0:T(8,128)(2,1)S(1)} %get-tuple-element.23), channel_id=1, source_target_pairs={{0,8},{1,9},{2,10},{3,11},{4,12},{5,13},{6,14},{7,15},{8,0},{9,1},... | collective-permute-start | bytes 98312 | tf_op jit(solution)/shard_map/ppermute | solution.py:294

commit v11 on v9

--- a/solution.py
+++ b/solution.py
@@ -9,11 +9,12 @@
 
 CB_DEV = 4
 LAM = 4
+WIDE = 512
 PARTS = 4
-GRANT = 8 << 20
-
-
-def pack_kernel(quarter, table_rounds, me_ref, count_ref, *refs):
+GRANT = 3 << 20
+
+
+def pack_kernel(place_rounds, table_rounds, me_ref, count_ref, *refs):
     sources, (out_ref, ids_ref, place_ref), (rows_ref, *held, sems) = refs[:4], refs[4:7], refs[7:]
     copies = [pltpu.make_async_copy(src, dst, sems.at[k]) for k, (src, dst) in enumerate(zip(sources, held))]
     for copy in copies:
@@ -42,15 +43,16 @@
     ids_ref[...] = ids
 
     targets = tgt_ref[...]
-    owner = targets // CB_DEV
-    rel = owner ^ me
-    place = ((rel & 1) * 2 + ((rel >> 1) & 1)) * quarter + (owner >> 2)
+    rel = (targets // CB_DEV) ^ me
+    place = jnp.zeros_like(targets)
+    for shift, step in place_rounds:
+        place = (place << step) | ((rel >> shift) & ((1 << step) - 1))
     place_ref[...] = place * CB_DEV + targets % CB_DEV
 
 
 def packed(me, basis_count, pair_atoms, chi_target, green_occ, green_virt, bs, bits):
     return pl.pallas_call(
-        functools.partial(pack_kernel, 1 << (bits - 2), gather_rounds(bits)),
+        functools.partial(pack_kernel, owner_rounds(bits), gather_rounds(bits)),
         in_specs=in_smem(2) + [pl.BlockSpec(memory_space=pl.ANY)] * 4,
         out_specs=in_vmem(3),
         out_shape=[
@@ -162,13 +164,15 @@
     half, lanes = aux // 2, 2 * bs
     tiles = width // lanes
 
+    per = WIDE // lanes
+
     def columns(j):
-        return pl.ds(pl.multiple_of(j * (2 * lanes), 2 * lanes), 2 * lanes)
+        return pl.ds(pl.multiple_of(j * WIDE, WIDE), WIDE)
 
     def copy(j):
         return pltpu.make_async_copy(b_hbm.at[:, :, columns(j)], b_ref.at[:, :, columns(j)], sems.at[j])
 
-    for j in range(tiles // 2):
+    for j in range(tiles // per):
         copy(j).start()
 
     wide = LAM * bs
@@ -201,21 +205,21 @@
 
     def product(j, h):
         block = b_ref[:, :, columns(j)].astype(jnp.float32)[:, h * half:(h + 1) * half]
-        side = block.reshape(tall, 2 * lanes).astype(jnp.bfloat16)
+        side = block.reshape(tall, WIDE).astype(jnp.bfloat16)
         results[h][...] = jnp.dot(occ_w, side, preferred_element_type=jnp.float32)
 
     def placed(j, h):
-        for t in range(2):
+        for t in range(per):
             got = results[h][:, t * lanes:(t + 1) * lanes].reshape(bs // 2, 2, half, lanes)
             pair = halves_joined(got[:, 0], got[:, 1], low, lanes)
-            o_ref[h * tiles + 2 * j + t] = jnp.concatenate(pair, axis=1).astype(jnp.bfloat16)
+            o_ref[h * tiles + per * j + t] = jnp.concatenate(pair, axis=1).astype(jnp.bfloat16)
 
     copy(0).wait()
     product(0, 0)
     product(0, 1)
     placed(0, 0)
 
-    @pl.loop(1, tiles // 2)
+    @pl.loop(1, tiles // per)
     def _(j):
         copy(j).wait()
         placed(j - 1, 1)
@@ -223,7 +227,7 @@
         placed(j, 0)
         product(j, 1)
 
-    placed(tiles // 2 - 1, 1)
+    placed(tiles // per - 1, 1)
 
 
 def chi_kernel(bs, sends, tgt_ref, o_ref, v_ref, *refs):
@@ -237,29 +241,30 @@
     low = lax.broadcasted_iota(jnp.int32, (bs, lanes), 1) < bs
     shared = len(accs) == 1
     outs = (out0, out1)
-    group = 4 * bs
+    wide = WIDE // lanes
 
     def scatter(n):
         for a in range(aux):
-            for t in range(2):
+            for t in range(wide):
                 value = outs[n % 2][t, pl.ds(a // half * (half * bs) + a % half, bs, stride=half), :]
-                first = tgt_ref[a * aux + n * 4 + 2 * t]
-                second = tgt_ref[a * aux + n * 4 + 2 * t + 1]
+                at = a * aux + 2 * (n * wide + t)
+                first, second = tgt_ref[at], tgt_ref[at + 1]
                 low_acc[first] += jnp.where(low, value, 0.0) if shared else value
                 high_acc[second] += jnp.where(low, 0.0, value) if shared else value
 
-    for n in range(aux // 4):
+    last = aux * bs // WIDE - 1
+    for n in range(last + 1):
         if n:
             scatter(n - 1)
         got = lax.dot_general(
             flat(o_ref, slice(None), range(tiles)),
-            flat(v_ref, slice(n * group // aux, (n + 1) * group // aux), range(tiles)),
+            flat(v_ref, slice(n * WIDE // aux, (n + 1) * WIDE // aux), range(tiles)),
             (((1,), (1,)), ((), ())),
             preferred_element_type=jnp.float32,
         )
-        for t in range(2):
+        for t in range(wide):
             outs[n % 2][t] = got[:, t * lanes:(t + 1) * lanes]
-    scatter(aux // 4 - 1)
+    scatter(last)
 
     pairs = keep_ref.shape[0]
 
@@ -290,15 +295,15 @@
         out_shape=[side, side],
         scratch_shapes=[
             pltpu.VMEM(integrals.shape, integrals.dtype),
-            pltpu.SemaphoreType.DMA((bs // 4,)),
+            pltpu.SemaphoreType.DMA((width // WIDE,)),
         ]
-        + [pltpu.VMEM((bs * aux // 2, 4 * bs), jnp.float32)] * 2,
+        + [pltpu.VMEM((bs * aux // 2, WIDE), jnp.float32)] * 2,
         compiler_params=pltpu.CompilerParams(vmem_limit_bytes=24 << 20),
         cost_estimate=cost,
     )(ids, *tables, *d_parts, integrals)
     accs = 2 if blocks <= 128 else 1
     acc = pltpu.VMEM((blocks, bs, 2 * bs), jnp.float32)
-    out = pltpu.VMEM((2, aux * bs, 2 * bs), jnp.float32)
+    out = pltpu.VMEM((WIDE // (2 * bs), aux * bs, 2 * bs), jnp.float32)
     return pl.pallas_call(
         functools.partial(chi_kernel, bs, sends),
         in_specs=in_smem(1) + in_vmem(2),
@@ -306,13 +311,22 @@
         out_shape=[jax.ShapeDtypeStruct((pairs, bs, 2 * bs), jnp.float32)]
         + [jax.ShapeDtypeStruct((pairs, bs, 2 * bs), jnp.bfloat16)] * sends,
         scratch_shapes=[out, out] + [acc] * accs,
-        compiler_params=pltpu.CompilerParams(vmem_limit_bytes=GRANT + 4 * (accs * blocks + 2 * aux * 2) * bs * 2 * bs),
+        compiler_params=pltpu.CompilerParams(vmem_limit_bytes=GRANT + 4 * (accs * blocks * bs * 2 * bs + 2 * aux * bs * WIDE)),
         cost_estimate=cost,
     )(targets, occ_side, virt_side)
 
 
 def gather_rounds(bits):
     return [(bit, 1) for bit in reversed(range(bits))]
+
+
+def owner_rounds(bits):
+    rounds, at = [], 0
+    while at < bits:
+        step = 1 if at < 2 else min(2, bits - at)
+        rounds.append((at, step))
+        at += step
+    return rounds
 
 
 def local(orb, three_centre, green_occ, green_virt, pair_atoms, basis_count, chi_target):
@@ -337,15 +351,14 @@
         tables = [table] + [exchange(table, v << shift) for v in range(1, 1 << step)]
         parts = [i for i in range(PARTS) if min(i, len(rounds) - 1) == k]
         d_parts += [relayout(integrals, i, after) for i in parts]
-    total, send = chi_blocks_of(ids[0], place[0], tables, integrals, d_parts, orb * CB_DEV, 1)
-    total = total + exchange(send, 1).astype(jnp.float32)
-    rest = total.shape[0] // 2
-    total = total[:rest] + exchange(total[rest:].astype(jnp.bfloat16), 2).astype(jnp.float32)
-    groups = [list(range(low, orb, 4)) for low in range(4)]
-    came = lax.all_to_all(
-        total.reshape(orb // 4, -1, bs, 2 * bs).astype(jnp.bfloat16), "orb", 0, 0, axis_index_groups=groups, tiled=True
-    )
-    total = came.astype(jnp.float32).sum(axis=0)
+    total, *sends = chi_blocks_of(ids[0], place[0], tables, integrals, d_parts, orb * CB_DEV, 1)
+    for k, (shift, step) in enumerate(owner_rounds(bits)):
+        if k:
+            rest = total.shape[0] >> step
+            sends = [total[v * rest:(v + 1) * rest].astype(jnp.bfloat16) for v in range(1, 1 << step)]
+            total = total[:rest]
+        for v, send in enumerate(sends):
+            total = total + exchange(send, (v + 1) << shift).astype(jnp.float32)
     total = total.reshape(CB_DEV // 2, bs, 2, bs).transpose(0, 2, 1, 3)
     return total.reshape(CB_DEV, bs * bs)
 

time: 63.7 us -> 61 us (0.958)
  blocking collectives: 10.5 us -> 0 us
  waiting for transfers between devices: 5.77 us -> 10.9 us
  starting transfers between devices: 9.57 us -> 13.6 us
  Pallas kernels: 35.7 us -> 34.3 us
    all_to_all x1 -> x0, blocking collectives: 10.5 us -> none  [local(): lax.all_to_all(total.reshape(orb // 4, -1, bs, 2 * bs).astype(jnp.bfloat1...]
    ppermute x6 -> x9, waiting for transfers between devices: 5.77 us -> 10.9 us  [exchange(): return lax.ppermute(value, 'orb', [(i, i ^ flip) for i in range(orb)])]
    ppermute x6 -> x9, starting transfers between devices: 9.57 us -> 13.6 us  [exchange(): return lax.ppermute(value, 'orb', [(i, i ^ flip) for i in range(orb)])]
    pallas_call x1, Pallas kernels: 13 us -> 11.3 us  [chi_blocks_of(): pl.pallas_call(functools.partial(sides_kernel, len(tables)), in_specs=in_...]
  transfers between devices with their start and end apart: 6 -> 9, of which waited for: 3 -> 5; matrix products, arithmetic and copies ran while one was open for 0% -> 0% of each run, Pallas kernels for 15% -> 16%
where the time goes in v11:
time: 61 us; the launch traced here: 60.7 us
  Pallas kernels  34.3 us (56%)
  starting transfers between devices  13.6 us (22%)
  waiting for transfers between devices  10.9 us (18%)
  local copies, waits for them, and re-layouts  0.92 us (2%)
  between operations  0.85 us (1%)
    ppermute x9, starting transfers between devices, exchange(): return lax.ppermute(value, 'orb', [(i, i ^ flip) for i in range(orb)])  13.6 us
    pallas_call x1, Pallas kernels, chi_blocks_of(): pl.pallas_call(functools.partial(chi_kernel, bs, sends), in_specs=in_smem...  12.1 us
    pallas_call x1, Pallas kernels, chi_blocks_of(): pl.pallas_call(functools.partial(sides_kernel, len(tables)), in_specs=in_...  11.3 us
    ppermute x9, waiting for transfers between devices, exchange(): return lax.ppermute(value, 'orb', [(i, i ^ flip) for i in range(orb)])  10.9 us
    pallas_call x4, Pallas kernels, relayout(): pl.pallas_call(functools.partial(relayout_kernel, part), in_specs=[hidden...  9.49 us
    pallas_call x1, Pallas kernels, packed(): pl.pallas_call(functools.partial(pack_kernel, owner_rounds(bits), gather_...  1.44 us
  transfers between devices with their start and end apart: 9, of which 5 were waited for; matrix products, arithmetic and copies ran while one was open for 0% of the time, Pallas kernels for 16%

profile of v11, /device:TPU:0, one launch (start us, length us, event | category | flops | bytes accessed | tf_op | source)
XLA Modules:
  0.0 60.7 jit_solution(764483095737673213)
XLA Ops:
  0.7 1.4 %shard_map.64 = (bf16[1,64,128]{2,1,0:T(8,128)(2,1)}, s32[1,2]{1,0:T(1,128)}, s32[1,256]{1,0:T(1,128)}) custom-call(s32[1]{0:T(128)} %bitcast.me_ref, s32[1]{0:T(128)S(6)} %copy.8.count_ref, s32[1,2]{1,0:T(1,128)} %refs_0_.1, s32[1,256]{1,0:T(1,128)} %refs_1_.1, bf16[1,4096]{1,0:T(2,128)(2,1)} %refs_2_.1, bf16[1,4096]{1,0:T(2,128)(2,1)} %refs_3_.1), custom_call_target="tpu_custom_call" | custom-call | tf_op jit(solution)/shard_map/pallas_call | solution.py:54
  2.1 4.1 %collective-permute-start = (bf16[1,64,128]{2,1,0:T(8,128)(2,1)}, bf16[1,64,128]{2,1,0:T(8,128)(2,1)S(1)}, u32[]{:S(2)}, u32[]{:S(2)}) collective-permute-start(bf16[1,64,128]{2,1,0:T(8,128)(2,1)} %get-tuple-element.20), channel_id=1, source_target_pairs={{0,8},{1,9},{2,10},{3,11},{4,12},{5,13},{6,14},{7,15},{8,0},{9,1},... | collective-permute-start | bytes 49160 | tf_op jit(solution)/shard_map/ppermute | solution.py:338
  6.2 0.0 copy-start.2
  6.2 2.4 %shard_map.65.refs_2_ = bf16[64,8,16,128]{3,2,1,0:T(8,128)(2,1)S(1)} custom-call(bf16[64,16,4096]{2,1,0:T(8,128)(2,1)} %bitcast.9), custom_call_target="tpu_custom_call" | custom-call | flops 536870912 | bytes 4194304 | tf_op jit(solution)/shard_map/pallas_call | solution.py:120
  8.6 0.0 collective-permute-done.refs_0_
  8.6 0.0 copy-done.2
  8.6 1.6 %collective-permute-start.1 = (bf16[2,64,128]{2,1,0:T(8,128)(2,1)S(1)}, bf16[2,64,128]{2,1,0:T(8,128)(2,1)S(1)}, u32[]{:S(2)}, u32[]{:S(2)}) collective-permute-start(bf16[2,64,128]{2,1,0:T(8,128)(2,1)S(1)} %pad_maximum_fusion.2), channel_id=1, source_target_pairs={{0,4},{1,5},{2,6},{3,7},{4,0},{5,1},{6,2},{7,3},{8,12},{9,13},{10,... | collective-permute-start | bytes 98312 | tf_op jit(solution)/shard_map/ppermute | solution.py:338
  10.3 2.4 %shard_map.66.refs_3_ = bf16[64,8,16,128]{3,2,1,0:T(8,128)(2,1)S(1)} custom-call(bf16[64,16,4096]{2,1,0:T(8,128)(2,1)} %bitcast.10, bf16[1,64,128]{2,1,0:T(8,128)(2,1)S(1)} %collective-permute-done.refs_0_), custom_call_target="tpu_custom_call" | custom-call | flops 536870912 | bytes 4194304 | tf_op jit(solution)/shard_map/pallas_call | solution.py:120
  12.6 0.0 collective-permute-done.1.refs_0_
  12.7 1.6 %collective-permute-start.2 = (bf16[4,64,128]{2,1,0:T(8,128)(2,1)S(1)}, bf16[4,64,128]{2,1,0:T(8,128)(2,1)S(1)}, u32[]{:S(2)}, u32[]{:S(2)}) collective-permute-start(bf16[4,64,128]{2,1,0:T(8,128)(2,1)S(1)} %pad_maximum_fusion.1), channel_id=1, source_target_pairs={{0,2},{1,3},{2,0},{3,1},{4,6},{5,7},{6,4},{7,5},{8,10},{9,11},{10,... | collective-permute-start | bytes 196616 | tf_op jit(solution)/shard_map/ppermute | solution.py:338
  14.3 2.4 %shard_map.67.refs_4_ = bf16[64,8,16,128]{3,2,1,0:T(8,128)(2,1)S(1)} custom-call(bf16[64,16,4096]{2,1,0:T(8,128)(2,1)} %bitcast.11, bf16[2,64,128]{2,1,0:T(8,128)(2,1)S(1)} %collective-permute-done.1.refs_0_), custom_call_target="tpu_custom_call" | custom-call | flops 536870912 | bytes 4194304 | tf_op jit(solution)/shard_map/pallas_call | solution.py:120
  16.6 0.4 collective-permute-done.2.refs_0_
  17.0 0.0 copy-start.1
  17.0 0.1 collective-permute-start.3
  17.1 2.4 %shard_map.68.refs_5_ = bf16[64,8,16,128]{3,2,1,0:T(8,128)(2,1)S(1)} custom-call(bf16[64,16,4096]{2,1,0:T(8,128)(2,1)} %bitcast.12, bf16[4,64,128]{2,1,0:T(8,128)(2,1)S(1)} %collective-permute-done.2.refs_0_), custom_call_target="tpu_custom_call" | custom-call | flops 536870912 | bytes 4194304 | tf_op jit(solution)/shard_map/pallas_call | solution.py:120
  19.5 0.0 collective-permute-done.3.refs_1_
  19.5 0.0 copy-done.1
  19.5 0.0 copy-start
  19.5 11.3 %shard_map.69 = (bf16[64,32,16,128]{3,2,1,0:T(8,128)(2,1)S(1)}, bf16[64,32,16,128]{3,2,1,0:T(8,128)(2,1)S(1)}) custom-call(s32[2]{0:T(128)S(1)} %bitcast.8, bf16[8,64,128]{2,1,0:T(8,128)(2,1)S(1)} %pad_maximum_fusion.refs_0_, bf16[8,64,128]{2,1,0:T(8,128)(2,1)S(1)} %collective-permute-done.3.refs_1_, bf16[64,8,16,128]{3,2,1,0:T(8,128)(2,1)S(1)} %shard_map.65.refs_2_, ...), custom_call_target="tpu_custom_call" | custom-call | flops 8589934592 | bytes 16777216 | tf_op jit(solution)/shard_map/pallas_call | solution.py:291
  30.8 0.0 copy-done
  30.9 12.1 %shard_map.70 = (f32[16,64,128]{2,1,0:T(8,128)S(1)}, bf16[16,64,128]{2,1,0:T(8,128)(2,1)S(1)}) custom-call(s32[256]{0:T(256)S(1)} %bitcast.7, bf16[64,32,16,128]{3,2,1,0:T(8,128)(2,1)S(1)} %get-tuple-element.27.o_ref, bf16[64,32,16,128]{3,2,1,0:T(8,128)(2,1)S(1)} %get-tuple-element.28.v_ref), custom_call_target="tpu_custom_call" | custom-call | flops 8589934592 | bytes 16777216 | tf_op jit(solution)/shard_map/pallas_call | solution.py:307
  42.9 0.6 collective-permute-start.4
  43.5 1.2 %collective-permute-done.4 = bf16[16,64,128]{2,1,0:T(8,128)(2,1)S(1)} collective-permute-done((bf16[16,64,128]{2,1,0:T(8,128)(2,1)S(1)}, bf16[16,64,128]{2,1,0:T(8,128)(2,1)S(1)}, u32[]{:S(2)}, u32[]{:S(2)}) %collective-permute-start.4) | collective-permute-done | bytes 262176 | tf_op jit(solution)/shard_map/ppermute | solution.py:338
  44.6 0.1 convert_add_fusion
  44.7 1.6 %collective-permute-start.5 = (bf16[8,64,128]{2,1,0:T(8,128)(2,1)S(1)}, bf16[8,64,128]{2,1,0:T(8,128)(2,1)S(1)}, u32[]{:S(2)}, u32[]{:S(2)}) collective-permute-start(bf16[8,64,128]{2,1,0:T(8,128)(2,1)S(1)} %slice.41), channel_id=1, source_target_pairs={{0,2},{1,3},{2,0},{3,1},{4,6},{5,7},{6,4},{7,5},{8,10},{9,11},{10,... | collective-permute-start | bytes 393224 | tf_op jit(solution)/shard_map/ppermute | solution.py:338
  46.3 4.2 %collective-permute-done.5 = bf16[8,64,128]{2,1,0:T(8,128)(2,1)S(1)} collective-permute-done((bf16[8,64,128]{2,1,0:T(8,128)(2,1)S(1)}, bf16[8,64,128]{2,1,0:T(8,128)(2,1)S(1)}, u32[]{:S(2)}, u32[]{:S(2)}) %collective-permute-start.5) | collective-permute-done | bytes 131104 | tf_op jit(solution)/shard_map/ppermute | solution.py:338
  50.6 1.6 %collective-permute-start.6 = (bf16[2,64,128]{2,1,0:T(8,128)(2,1)S(1)}, bf16[2,64,128]{2,1,0:T(8,128)(2,1)S(1)}, u32[]{:S(2)}, u32[]{:S(2)}) collective-permute-start(bf16[2,64,128]{2,1,0:T(8,128)(2,1)S(1)} %get-tuple-element.33), channel_id=1, source_target_pairs={{0,4},{1,5},{2,6},{3,7},{4,0},{5,1},{6,2},{7,3},{8,12},{9,13},{10,... | collective-permute-start | bytes 98312 | tf_op jit(solution)/shard_map/ppermute | solution.py:338
  52.2 2.4 %collective-permute-start.8 = (bf16[2,64,128]{2,1,0:T(8,128)(2,1)S(1)}, bf16[2,64,128]{2,1,0:T(8,128)(2,1)S(1)}, u32[]{:S(2)}, u32[]{:S(2)}) collective-permute-start(bf16[2,64,128]{2,1,0:T(8,128)(2,1)S(1)} %get-tuple-element.34), channel_id=1, source_target_pairs={{0,12},{1,13},{2,14},{3,15},{4,8},{5,9},{6,10},{7,11},{8,4},{9,5},... | collective-permute-start | bytes 98312 | tf_op jit(solution)/shard_map/ppermute | solution.py:338
  54.7 0.1 collective-permute-start.7
  54.7 0.0 collective-permute-done.6
  54.7 3.3 %collective-permute-done.8 = bf16[2,64,128]{2,1,0:T(8,128)(2,1)S(1)} collective-permute-done((bf16[2,64,128]{2,1,0:T(8,128)(2,1)S(1)}, bf16[2,64,128]{2,1,0:T(8,128)(2,1)S(1)}, u32[]{:S(2)}, u32[]{:S(2)}) %collective-permute-start.8) | collective-permute-done | bytes 32800 | tf_op jit(solution)/shard_map/ppermute | solution.py:338
  58.0 1.8 %collective-permute-done.7 = bf16[2,64,128]{2,1,0:T(8,128)(2,1)S(1)} collective-permute-done((bf16[2,64,128]{2,1,0:T(8,128)(2,1)S(1)}, bf16[2,64,128]{2,1,0:T(8,128)(2,1)S(1)}, u32[]{:S(2)}, u32[]{:S(2)}) %collective-permute-start.7) | collective-permute-done | bytes 32800 | tf_op jit(solution)/shard_map/ppermute | solution.py:338
  59.9 0.1 reshape.6
  60.0 0.7 %reshape.7 = f32[4,4096]{1,0:T(4,128)} reshape(f32[2,2,64,64]{3,2,1,0:T(8,128)S(1)} %copy.7) | data formatting | bytes 131072 | tf_op jit(solution)/shard_map/reshape | solution.py:363
  (8 shorter events, 0.1 us)
Async XLA Ops:
  2.1 6.5 %collective-permute-start = (bf16[1,64,128]{2,1,0:T(8,128)(2,1)}, bf16[1,64,128]{2,1,0:T(8,128)(2,1)S(1)}, u32[]{:S(2)}, u32[]{:S(2)}) collective-permute-start(bf16[1,64,128]{2,1,0:T(8,128)(2,1)} %get-tuple-element.20), channel_id=1, source_target_pairs={{0,8},{1,9},{2,10},{3,11},{4,12},{5,13},{6,14},{7,15},{8,0},{9,1},... | collective-permute-start | bytes 49160 | tf_op jit(solution)/shard_map/ppermute | solution.py:338
  6.2 2.4 %copy-start.2 = (bf16[1,64,128]{2,1,0:T(8,128)(2,1)S(1)}, bf16[1,64,128]{2,1,0:T(8,128)(2,1)}, u32[]{:S(2)}) copy-start(bf16[1,64,128]{2,1,0:T(8,128)(2,1)} %get-tuple-element.20) | copy-start | bytes 49156
  8.6 4.0 %collective-permute-start.1 = (bf16[2,64,128]{2,1,0:T(8,128)(2,1)S(1)}, bf16[2,64,128]{2,1,0:T(8,128)(2,1)S(1)}, u32[]{:S(2)}, u32[]{:S(2)}) collective-permute-start(bf16[2,64,128]{2,1,0:T(8,128)(2,1)S(1)} %pad_maximum_fusion.2), channel_id=1, source_target_pairs={{0,4},{1,5},{2,6},{3,7},{4,0},{5,1},{6,2},{7,3},{8,12},{9,13},{10,... | collective-permute-start | bytes 98312 | tf_op jit(solution)/shard_map/ppermute | solution.py:338
  12.7 4.3 %collective-permute-start.2 = (bf16[4,64,128]{2,1,0:T(8,128)(2,1)S(1)}, bf16[4,64,128]{2,1,0:T(8,128)(2,1)S(1)}, u32[]{:S(2)}, u32[]{:S(2)}) collective-permute-start(bf16[4,64,128]{2,1,0:T(8,128)(2,1)S(1)} %pad_maximum_fusion.1), channel_id=1, source_target_pairs={{0,2},{1,3},{2,0},{3,1},{4,6},{5,7},{6,4},{7,5},{8,10},{9,11},{10,... | collective-permute-start | bytes 196616 | tf_op jit(solution)/shard_map/ppermute | solution.py:338
  17.0 2.5 %copy-start.1 = (s32[1,2]{1,0:T(1,128)S(1)}, s32[1,2]{1,0:T(1,128)}, u32[]{:S(2)}) copy-start(s32[1,2]{1,0:T(1,128)} %get-tuple-element.19) | copy-start | bytes 28
  17.0 2.5 %collective-permute-start.3 = (bf16[8,64,128]{2,1,0:T(8,128)(2,1)S(1)}, bf16[8,64,128]{2,1,0:T(8,128)(2,1)S(1)}, u32[]{:S(2)}, u32[]{:S(2)}) collective-permute-start(bf16[8,64,128]{2,1,0:T(8,128)(2,1)S(1)} %pad_maximum_fusion.refs_0_), channel_id=1, source_target_pairs={{0,1},{1,0},{2,3},{3,2},{4,5},{5,4},{6,7},{7,6},{8,9},{9,8},{10,11... | collective-permute-start | bytes 393224 | tf_op jit(solution)/shard_map/ppermute | solution.py:338
  19.5 11.3 %copy-start = (s32[1,256]{1,0:T(1,128)S(1)}, s32[1,256]{1,0:T(1,128)}, u32[]{:S(2)}) copy-start(s32[1,256]{1,0:T(1,128)} %get-tuple-element.18) | copy-start | bytes 3076
  42.9 1.7 %collective-permute-start.4 = (bf16[16,64,128]{2,1,0:T(8,128)(2,1)S(1)}, bf16[16,64,128]{2,1,0:T(8,128)(2,1)S(1)}, u32[]{:S(2)}, u32[]{:S(2)}) collective-permute-start(bf16[16,64,128]{2,1,0:T(8,128)(2,1)S(1)} %get-tuple-element.30), channel_id=1, source_target_pairs={{0,1},{1,0},{2,3},{3,2},{4,5},{5,4},{6,7},{7,6},{8,9},{9,8},{10,11... | collective-permute-start | bytes 786440 | tf_op jit(solution)/shard_map/ppermute | solution.py:338
  44.7 5.8 %collective-permute-start.5 = (bf16[8,64,128]{2,1,0:T(8,128)(2,1)S(1)}, bf16[8,64,128]{2,1,0:T(8,128)(2,1)S(1)}, u32[]{:S(2)}, u32[]{:S(2)}) collective-permute-start(bf16[8,64,128]{2,1,0:T(8,128)(2,1)S(1)} %slice.41), channel_id=1, source_target_pairs={{0,2},{1,3},{2,0},{3,1},{4,6},{5,7},{6,4},{7,5},{8,10},{9,11},{10,... | collective-permute-start | bytes 393224 | tf_op jit(solution)/shard_map/ppermute | solution.py:338
  50.6 4.1 %collective-permute-start.6 = (bf16[2,64,128]{2,1,0:T(8,128)(2,1)S(1)}, bf16[2,64,128]{2,1,0:T(8,128)(2,1)S(1)}, u32[]{:S(2)}, u32[]{:S(2)}) collective-permute-start(bf16[2,64,128]{2,1,0:T(8,128)(2,1)S(1)} %get-tuple-element.33), channel_id=1, source_target_pairs={{0,4},{1,5},{2,6},{3,7},{4,0},{5,1},{6,2},{7,3},{8,12},{9,13},{10,... | collective-permute-start | bytes 98312 | tf_op jit(solution)/shard_map/ppermute | solution.py:338
  52.2 5.8 %collective-permute-start.8 = (bf16[2,64,128]{2,1,0:T(8,128)(2,1)S(1)}, bf16[2,64,128]{2,1,0:T(8,128)(2,1)S(1)}, u32[]{:S(2)}, u32[]{:S(2)}) collective-permute-start(bf16[2,64,128]{2,1,0:T(8,128)(2,1)S(1)} %get-tuple-element.34), channel_id=1, source_target_pairs={{0,12},{1,13},{2,14},{3,15},{4,8},{5,9},{6,10},{7,11},{8,4},{9,5},... | collective-permute-start | bytes 98312 | tf_op jit(solution)/shard_map/ppermute | solution.py:338
  54.7 5.2 %collective-permute-start.7 = (bf16[2,64,128]{2,1,0:T(8,128)(2,1)S(1)}, bf16[2,64,128]{2,1,0:T(8,128)(2,1)S(1)}, u32[]{:S(2)}, u32[]{:S(2)}) collective-permute-start(bf16[2,64,128]{2,1,0:T(8,128)(2,1)S(1)} %get-tuple-element.35), channel_id=1, source_target_pairs={{0,8},{1,9},{2,10},{3,11},{4,12},{5,13},{6,14},{7,15},{8,0},{9,1},... | collective-permute-start | bytes 98312 | tf_op jit(solution)/shard_map/ppermute | solution.py:338

commit v12 on v11

--- a/solution.py
+++ b/solution.py
@@ -10,7 +10,7 @@
 CB_DEV = 4
 LAM = 4
 WIDE = 512
-PARTS = 4
+PARTS = (32, 16, 16)
 GRANT = 3 << 20
 
 
@@ -52,7 +52,7 @@
 
 def packed(me, basis_count, pair_atoms, chi_target, green_occ, green_virt, bs, bits):
     return pl.pallas_call(
-        functools.partial(pack_kernel, owner_rounds(bits), gather_rounds(bits)),
+        functools.partial(pack_kernel, owner_rounds(bits), owner_rounds(bits)[::-1]),
         in_specs=in_smem(2) + [pl.BlockSpec(memory_space=pl.ANY)] * 4,
         out_specs=in_vmem(3),
         out_shape=[
@@ -72,7 +72,7 @@
     return jnp.where(low, one, turned), jnp.where(low, turned, two)
 
 
-def relayout_kernel(part, b_hbm, *refs):
+def relayout_kernel(first, b_hbm, *refs):
     d_ref, b_ref, sems, *turns = refs[-5:]
     lams, aux, width = b_ref.shape
     lanes = d_ref.shape[3]
@@ -80,7 +80,7 @@
 
     def copy(i):
         held = pl.ds(2 * i, 2)
-        return pltpu.make_async_copy(b_hbm.at[pl.ds(part * lams + 2 * i, 2)], b_ref.at[held], sems.at[i])
+        return pltpu.make_async_copy(b_hbm.at[pl.ds(first + 2 * i, 2)], b_ref.at[held], sems.at[i])
 
     for i in range(lams // 2):
         copy(i).start()
@@ -115,10 +115,10 @@
 
 def relayout(integrals, part, after):
     bs, aux, width = integrals.shape
-    lams = bs // PARTS
+    lams = PARTS[part]
     hidden = pl.BlockSpec(memory_space=pl.ANY)
     return pl.pallas_call(
-        functools.partial(relayout_kernel, part),
+        functools.partial(relayout_kernel, sum(PARTS[:part])),
         in_specs=[hidden] * (1 + len(after)),
         out_specs=in_vmem(1)[0],
         out_shape=jax.ShapeDtypeStruct((bs, lams // 2, aux, 2 * bs), jnp.bfloat16),
@@ -129,8 +129,8 @@
         + [pltpu.VMEM((aux * bs, 2 * bs), jnp.float32)] * 2,
         compiler_params=pltpu.CompilerParams(vmem_limit_bytes=48 << 20),
         cost_estimate=pl.CostEstimate(
-            flops=2 * bs * aux * width * 256 // PARTS,
-            bytes_accessed=4 * bs * aux * width // PARTS,
+            flops=2 * lams * aux * width * 256,
+            bytes_accessed=4 * lams * aux * width,
             transcendentals=0,
         ),
     )(integrals, *after)
@@ -158,7 +158,8 @@
 
 
 def sides_kernel(pieces, ids_ref, *refs):
-    tables, d_parts, refs = refs[:pieces], refs[pieces:pieces + PARTS], refs[pieces + PARTS:]
+    tables, refs = refs[:pieces], refs[pieces:]
+    d_parts, refs = refs[:len(PARTS)], refs[len(PARTS):]
     b_hbm, v_ref, o_ref, b_ref, sems, *results = refs
     bs, aux, width = b_ref.shape
     half, lanes = aux // 2, 2 * bs
@@ -182,13 +183,12 @@
         lax.broadcasted_iota(jnp.int32, (wide, wide), 0) // bs == lax.broadcasted_iota(jnp.int32, (wide, wide), 1) // bs
     )
     virt_w = jnp.where(same, spread, 0.0).astype(jnp.bfloat16)
-    each = d_parts[0].shape[1]
-    for part in range(PARTS):
-        for at in range(0, each, 2):
-            got = jnp.dot(flat(d_parts[part], slice(None), [at, at + 1]), virt_w, preferred_element_type=jnp.float32)
-            got = got.astype(jnp.bfloat16)
-            for t in range(2):
-                v_ref[:, part * each + at + t] = got[:, t * lanes:(t + 1) * lanes].reshape(v_ref.shape[:1] + (aux, lanes))
+
+    def virt_product(part, before, step):
+        got = jnp.dot(flat(d_parts[part], slice(None), [2 * step, 2 * step + 1]), virt_w, preferred_element_type=jnp.float32)
+        got = got.astype(jnp.bfloat16)
+        for t in range(2):
+            v_ref[:, before + 2 * step + t] = got[:, t * lanes:(t + 1) * lanes].reshape(v_ref.shape[:1] + (aux, lanes))
 
     tall = bs * half
     rep_t = (
@@ -214,20 +214,24 @@
             pair = halves_joined(got[:, 0], got[:, 1], low, lanes)
             o_ref[h * tiles + per * j + t] = jnp.concatenate(pair, axis=1).astype(jnp.bfloat16)
 
-    copy(0).wait()
-    product(0, 0)
-    product(0, 1)
-    placed(0, 0)
-
-    @pl.loop(1, tiles // per)
-    def _(j):
-        copy(j).wait()
-        placed(j - 1, 1)
-        product(j, 0)
-        placed(j, 0)
-        product(j, 1)
-
-    placed(tiles // per - 1, 1)
+    done = 0
+    for part, d_ref in enumerate(d_parts):
+        steps = d_ref.shape[1] // per
+
+        @pl.loop(0, steps)
+        def _(i):
+            j = done + i
+            copy(j).wait()
+            placed(jnp.maximum(j - 1, 0), 1)
+            product(j, 0)
+            for k in range(per // 2):
+                virt_product(part, done * per, i * (per // 2) + k)
+            placed(j, 0)
+            product(j, 1)
+
+        done += steps
+
+    placed(done - 1, 1)
 
 
 def chi_kernel(bs, sends, tgt_ref, o_ref, v_ref, *refs):
@@ -241,30 +245,29 @@
     low = lax.broadcasted_iota(jnp.int32, (bs, lanes), 1) < bs
     shared = len(accs) == 1
     outs = (out0, out1)
-    wide = WIDE // lanes
+    columns = [(0, WIDE)] + [(at, WIDE // 2) for at in range(WIDE, aux * bs, WIDE // 2)]
 
     def scatter(n):
         for a in range(aux):
-            for t in range(wide):
+            for t in range(columns[n][1] // lanes):
                 value = outs[n % 2][t, pl.ds(a // half * (half * bs) + a % half, bs, stride=half), :]
-                at = a * aux + 2 * (n * wide + t)
+                at = a * aux + 2 * (columns[n][0] // lanes + t)
                 first, second = tgt_ref[at], tgt_ref[at + 1]
                 low_acc[first] += jnp.where(low, value, 0.0) if shared else value
                 high_acc[second] += jnp.where(low, 0.0, value) if shared else value
 
-    last = aux * bs // WIDE - 1
-    for n in range(last + 1):
+    for n, (at, wide) in enumerate(columns):
         if n:
             scatter(n - 1)
         got = lax.dot_general(
             flat(o_ref, slice(None), range(tiles)),
-            flat(v_ref, slice(n * WIDE // aux, (n + 1) * WIDE // aux), range(tiles)),
+            flat(v_ref, slice(at // aux, (at + wide) // aux), range(tiles)),
             (((1,), (1,)), ((), ())),
             preferred_element_type=jnp.float32,
         )
-        for t in range(wide):
+        for t in range(wide // lanes):
             outs[n % 2][t] = got[:, t * lanes:(t + 1) * lanes]
-    scatter(last)
+    scatter(len(columns) - 1)
 
     pairs = keep_ref.shape[0]
 
@@ -276,7 +279,7 @@
         right = jnp.where(low, low_acc[2 * i + 1], high_acc[2 * i])
         return left + pltpu.roll(right, bs, 1)
 
-    @pl.loop(0, pairs)
+    @pl.loop(0, pairs, unroll=4)
     def _(i):
         keep_ref[i] = joined(i)
         for k, send_ref in enumerate(send_refs):
@@ -290,7 +293,7 @@
     cost = pl.CostEstimate(flops=2 * (aux * bs) ** 2 * width, bytes_accessed=4 * aux * bs * width, transcendentals=0)
     virt_side, occ_side = pl.pallas_call(
         functools.partial(sides_kernel, len(tables)),
-        in_specs=in_smem(1) + in_vmem(len(tables) + PARTS) + [pl.BlockSpec(memory_space=pl.ANY)],
+        in_specs=in_smem(1) + in_vmem(len(tables) + len(PARTS)) + [pl.BlockSpec(memory_space=pl.ANY)],
         out_specs=in_vmem(2),
         out_shape=[side, side],
         scratch_shapes=[
@@ -316,10 +319,6 @@
     )(targets, occ_side, virt_side)
 
 
-def gather_rounds(bits):
-    return [(bit, 1) for bit in reversed(range(bits))]
-
-
 def owner_rounds(bits):
     rounds, at = [], 0
     while at < bits:
@@ -341,7 +340,7 @@
     table, ids, place = packed(
         me[None].astype(jnp.int32), basis_count, pair_atoms, chi_target, green_occ, green_virt, bs, bits
     )
-    rounds = gather_rounds(bits)
+    rounds = owner_rounds(bits)[::-1]
     tables, d_parts = [table], []
     for k, (shift, step) in enumerate(rounds):
         after = tables[-1:] if k else []
@@ -349,7 +348,7 @@
         if k and len(d_parts) == k:
             table, d_parts[-1] = lax.optimization_barrier((table, d_parts[-1]))
         tables = [table] + [exchange(table, v << shift) for v in range(1, 1 << step)]
-        parts = [i for i in range(PARTS) if min(i, len(rounds) - 1) == k]
+        parts = [i for i in range(len(PARTS)) if min(i, len(rounds) - 1) == k]
         d_parts += [relayout(integrals, i, after) for i in parts]
     total, *sends = chi_blocks_of(ids[0], place[0], tables, integrals, d_parts, orb * CB_DEV, 1)
     for k, (shift, step) in enumerate(owner_rounds(bits)):

time: 61 us -> 58.6 us (0.961)
  Pallas kernels: 34.3 us -> 32.3 us
    pallas_call x5 -> x4, Pallas kernels: 10.9 us -> 9.89 us  [the longest x3 8.45 us: relayout(): pl.pallas_call(functools.partial(relayout_kernel, sum(PARTS[:part])), in_...]
    pallas_call x1, Pallas kernels: 12.1 us -> 11.2 us  [chi_blocks_of(): pl.pallas_call(functools.partial(chi_kernel, bs, sends), in_specs=in_smem...]
    ppermute x9 -> x10, waiting for transfers between devices: 10.9 us -> 10.7 us  [exchange(): return lax.ppermute(value, 'orb', [(i, i ^ flip) for i in range(orb)])]
    ppermute x9 -> x10, starting transfers between devices: 13.6 us -> 13.5 us  [exchange(): return lax.ppermute(value, 'orb', [(i, i ^ flip) for i in range(orb)])]
  transfers between devices with their start and end apart: 9 -> 10, of which waited for: 5 -> 6; matrix products, arithmetic and copies ran while one was open for 0% -> 0% of each run, Pallas kernels for 16% -> 14%
where the time goes in v12:
time: 58.6 us; the launch traced here: 58.3 us
  Pallas kernels  32.3 us (55%)
  starting transfers between devices  13.5 us (23%)
  waiting for transfers between devices  10.7 us (18%)
  local copies, waits for them, and re-layouts  0.92 us (2%)
  between operations  0.82 us (1%)
    ppermute x10, starting transfers between devices, exchange(): return lax.ppermute(value, 'orb', [(i, i ^ flip) for i in range(orb)])  13.5 us
    pallas_call x1, Pallas kernels, chi_blocks_of(): pl.pallas_call(functools.partial(sides_kernel, len(tables)), in_specs=in_...  11.2 us
    pallas_call x1, Pallas kernels, chi_blocks_of(): pl.pallas_call(functools.partial(chi_kernel, bs, sends), in_specs=in_smem...  11.2 us
    ppermute x10, waiting for transfers between devices, exchange(): return lax.ppermute(value, 'orb', [(i, i ^ flip) for i in range(orb)])  10.7 us
    pallas_call x3, Pallas kernels, relayout(): pl.pallas_call(functools.partial(relayout_kernel, sum(PARTS[:part])), in_...  8.45 us
    pallas_call x1, Pallas kernels, packed(): pl.pallas_call(functools.partial(pack_kernel, owner_rounds(bits), owner_r...  1.44 us
  transfers between devices with their start and end apart: 10, of which 6 were waited for; matrix products, arithmetic and copies ran while one was open for 0% of the time, Pallas kernels for 14%

profile of v12, /device:TPU:0, one launch (start us, length us, event | category | flops | bytes accessed | tf_op | source)
XLA Modules:
  0.0 58.3 jit_solution(2852288312698546665)
XLA Ops:
  0.7 1.4 %shard_map.64 = (bf16[1,64,128]{2,1,0:T(8,128)(2,1)}, s32[1,2]{1,0:T(1,128)}, s32[1,256]{1,0:T(1,128)}) custom-call(s32[1]{0:T(128)} %bitcast.me_ref, s32[1]{0:T(128)S(6)} %copy.8.count_ref, s32[1,2]{1,0:T(1,128)} %refs_0_.1, s32[1,256]{1,0:T(1,128)} %refs_1_.1, bf16[1,4096]{1,0:T(2,128)(2,1)} %refs_2_.1, bf16[1,4096]{1,0:T(2,128)(2,1)} %refs_3_.1), custom_call_target="tpu_custom_call" | custom-call | tf_op jit(solution)/shard_map/pallas_call | solution.py:54
  2.1 0.0 copy-start.2
  2.1 5.1 %collective-permute-start.2 = (bf16[1,64,128]{2,1,0:T(8,128)(2,1)}, bf16[1,64,128]{2,1,0:T(8,128)(2,1)S(1)}, u32[]{:S(2)}, u32[]{:S(2)}) collective-permute-start(bf16[1,64,128]{2,1,0:T(8,128)(2,1)} %get-tuple-element.18), channel_id=1, source_target_pairs={{0,12},{1,13},{2,14},{3,15},{4,8},{5,9},{6,10},{7,11},{8,4},{9,5},... | collective-permute-start | bytes 49160 | tf_op jit(solution)/shard_map/ppermute | solution.py:337
  7.2 0.0 collective-permute-start.1
  7.2 0.6 %collective-permute-start = (bf16[1,64,128]{2,1,0:T(8,128)(2,1)}, bf16[1,64,128]{2,1,0:T(8,128)(2,1)S(1)}, u32[]{:S(2)}, u32[]{:S(2)}) collective-permute-start(bf16[1,64,128]{2,1,0:T(8,128)(2,1)} %get-tuple-element.18), channel_id=1, source_target_pairs={{0,4},{1,5},{2,6},{3,7},{4,0},{5,1},{6,2},{7,3},{8,12},{9,13},{10,... | collective-permute-start | bytes 49160 | tf_op jit(solution)/shard_map/ppermute | solution.py:337
  7.9 3.7 %shard_map.65.refs_2_ = bf16[64,16,16,128]{3,2,1,0:T(8,128)(2,1)S(1)} custom-call(bf16[64,16,4096]{2,1,0:T(8,128)(2,1)} %bitcast.9), custom_call_target="tpu_custom_call" | custom-call | flops 1073741824 | bytes 8388608 | tf_op jit(solution)/shard_map/pallas_call | solution.py:120
  11.6 0.0 collective-permute-done.2.refs_0_
  11.6 0.5 collective-permute-done.1
  12.1 0.0 collective-permute-done
  12.1 0.0 copy-done.2
  12.1 0.0 copy-start.1
  12.1 1.6 %collective-permute-start.3 = (bf16[4,64,128]{2,1,0:T(8,128)(2,1)S(1)}, bf16[4,64,128]{2,1,0:T(8,128)(2,1)S(1)}, u32[]{:S(2)}, u32[]{:S(2)}) collective-permute-start(bf16[4,64,128]{2,1,0:T(8,128)(2,1)S(1)} %pad_maximum_fusion.1), channel_id=1, source_target_pairs={{0,2},{1,3},{2,0},{3,1},{4,6},{5,7},{6,4},{7,5},{8,10},{9,11},{10,... | collective-permute-start | bytes 196616 | tf_op jit(solution)/shard_map/ppermute | solution.py:337
  13.7 2.4 %shard_map.66.refs_3_ = bf16[64,8,16,128]{3,2,1,0:T(8,128)(2,1)S(1)} custom-call(bf16[64,16,4096]{2,1,0:T(8,128)(2,1)} %bitcast.10, bf16[1,64,128]{2,1,0:T(8,128)(2,1)S(1)} %collective-permute-done.2.refs_0_), custom_call_target="tpu_custom_call" | custom-call | flops 536870912 | bytes 4194304 | tf_op jit(solution)/shard_map/pallas_call | solution.py:120
  16.1 0.4 collective-permute-done.3.refs_0_
  16.5 0.1 collective-permute-start.4
  16.5 2.4 %shard_map.67.refs_4_ = bf16[64,8,16,128]{3,2,1,0:T(8,128)(2,1)S(1)} custom-call(bf16[64,16,4096]{2,1,0:T(8,128)(2,1)} %bitcast.11, bf16[4,64,128]{2,1,0:T(8,128)(2,1)S(1)} %collective-permute-done.3.refs_0_), custom_call_target="tpu_custom_call" | custom-call | flops 536870912 | bytes 4194304 | tf_op jit(solution)/shard_map/pallas_call | solution.py:120
  18.9 0.0 collective-permute-done.4.refs_1_
  18.9 0.0 copy-done.1
  18.9 0.0 copy-start
  18.9 11.2 %shard_map.68 = (bf16[64,32,16,128]{3,2,1,0:T(8,128)(2,1)S(1)}, bf16[64,32,16,128]{3,2,1,0:T(8,128)(2,1)S(1)}) custom-call(s32[2]{0:T(128)S(1)} %bitcast.8, bf16[8,64,128]{2,1,0:T(8,128)(2,1)S(1)} %pad_maximum_fusion.refs_0_, bf16[8,64,128]{2,1,0:T(8,128)(2,1)S(1)} %collective-permute-done.4.refs_1_, bf16[64,16,16,128]{3,2,1,0:T(8,128)(2,1)S(1)} %shard_map.65.refs_2_, ...), custom_call_target="tpu_custom_call" | custom-call | flops 8589934592 | bytes 16777216 | tf_op jit(solution)/shard_map/pallas_call | solution.py:294
  30.1 0.0 copy-done
  30.2 11.2 %shard_map.69 = (f32[16,64,128]{2,1,0:T(8,128)S(1)}, bf16[16,64,128]{2,1,0:T(8,128)(2,1)S(1)}) custom-call(s32[256]{0:T(256)S(1)} %bitcast.7, bf16[64,32,16,128]{3,2,1,0:T(8,128)(2,1)S(1)} %get-tuple-element.23.o_ref, bf16[64,32,16,128]{3,2,1,0:T(8,128)(2,1)S(1)} %get-tuple-element.24.v_ref), custom_call_target="tpu_custom_call" | custom-call | flops 8589934592 | bytes 16777216 | tf_op jit(solution)/shard_map/pallas_call | solution.py:310
  41.4 0.5 collective-permute-start.5
  41.9 1.2 %collective-permute-done.5 = bf16[16,64,128]{2,1,0:T(8,128)(2,1)S(1)} collective-permute-done((bf16[16,64,128]{2,1,0:T(8,128)(2,1)S(1)}, bf16[16,64,128]{2,1,0:T(8,128)(2,1)S(1)}, u32[]{:S(2)}, u32[]{:S(2)}) %collective-permute-start.5) | collective-permute-done | bytes 262176 | tf_op jit(solution)/shard_map/ppermute | solution.py:337
  43.1 0.1 convert_add_fusion
  43.1 1.6 %collective-permute-start.6 = (bf16[8,64,128]{2,1,0:T(8,128)(2,1)S(1)}, bf16[8,64,128]{2,1,0:T(8,128)(2,1)S(1)}, u32[]{:S(2)}, u32[]{:S(2)}) collective-permute-start(bf16[8,64,128]{2,1,0:T(8,128)(2,1)S(1)} %slice.41), channel_id=1, source_target_pairs={{0,2},{1,3},{2,0},{3,1},{4,6},{5,7},{6,4},{7,5},{8,10},{9,11},{10,... | collective-permute-start | bytes 393224 | tf_op jit(solution)/shard_map/ppermute | solution.py:337
  44.7 4.2 %collective-permute-done.6 = bf16[8,64,128]{2,1,0:T(8,128)(2,1)S(1)} collective-permute-done((bf16[8,64,128]{2,1,0:T(8,128)(2,1)S(1)}, bf16[8,64,128]{2,1,0:T(8,128)(2,1)S(1)}, u32[]{:S(2)}, u32[]{:S(2)}) %collective-permute-start.6) | collective-permute-done | bytes 131104 | tf_op jit(solution)/shard_map/ppermute | solution.py:337
  49.1 1.0 %collective-permute-start.7 = (bf16[2,64,128]{2,1,0:T(8,128)(2,1)S(1)}, bf16[2,64,128]{2,1,0:T(8,128)(2,1)S(1)}, u32[]{:S(2)}, u32[]{:S(2)}) collective-permute-start(bf16[2,64,128]{2,1,0:T(8,128)(2,1)S(1)} %get-tuple-element.29), channel_id=1, source_target_pairs={{0,4},{1,5},{2,6},{3,7},{4,0},{5,1},{6,2},{7,3},{8,12},{9,13},{10,... | collective-permute-start | bytes 98312 | tf_op jit(solution)/shard_map/ppermute | solution.py:337
  50.1 2.5 %collective-permute-start.9 = (bf16[2,64,128]{2,1,0:T(8,128)(2,1)S(1)}, bf16[2,64,128]{2,1,0:T(8,128)(2,1)S(1)}, u32[]{:S(2)}, u32[]{:S(2)}) collective-permute-start(bf16[2,64,128]{2,1,0:T(8,128)(2,1)S(1)} %get-tuple-element.30), channel_id=1, source_target_pairs={{0,12},{1,13},{2,14},{3,15},{4,8},{5,9},{6,10},{7,11},{8,4},{9,5},... | collective-permute-start | bytes 98312 | tf_op jit(solution)/shard_map/ppermute | solution.py:337
  52.6 0.4 collective-permute-start.8
  53.0 0.0 collective-permute-done.7
  53.0 3.2 %collective-permute-done.9 = bf16[2,64,128]{2,1,0:T(8,128)(2,1)S(1)} collective-permute-done((bf16[2,64,128]{2,1,0:T(8,128)(2,1)S(1)}, bf16[2,64,128]{2,1,0:T(8,128)(2,1)S(1)}, u32[]{:S(2)}, u32[]{:S(2)}) %collective-permute-start.9) | collective-permute-done | bytes 32800 | tf_op jit(solution)/shard_map/ppermute | solution.py:337
  56.2 1.2 %collective-permute-done.8 = bf16[2,64,128]{2,1,0:T(8,128)(2,1)S(1)} collective-permute-done((bf16[2,64,128]{2,1,0:T(8,128)(2,1)S(1)}, bf16[2,64,128]{2,1,0:T(8,128)(2,1)S(1)}, u32[]{:S(2)}, u32[]{:S(2)}) %collective-permute-start.8) | collective-permute-done | bytes 32800 | tf_op jit(solution)/shard_map/ppermute | solution.py:337
  57.4 0.1 reshape.6
  57.6 0.7 %reshape.7 = f32[4,4096]{1,0:T(4,128)} reshape(f32[2,2,64,64]{3,2,1,0:T(8,128)S(1)} %copy.7) | data formatting | bytes 131072 | tf_op jit(solution)/shard_map/reshape | solution.py:362
  (7 shorter events, 0.1 us)
Async XLA Ops:
  2.1 10.0 %copy-start.2 = (bf16[1,64,128]{2,1,0:T(8,128)(2,1)S(1)}, bf16[1,64,128]{2,1,0:T(8,128)(2,1)}, u32[]{:S(2)}) copy-start(bf16[1,64,128]{2,1,0:T(8,128)(2,1)} %get-tuple-element.18) | copy-start | bytes 49156
  2.1 9.5 %collective-permute-start.2 = (bf16[1,64,128]{2,1,0:T(8,128)(2,1)}, bf16[1,64,128]{2,1,0:T(8,128)(2,1)S(1)}, u32[]{:S(2)}, u32[]{:S(2)}) collective-permute-start(bf16[1,64,128]{2,1,0:T(8,128)(2,1)} %get-tuple-element.18), channel_id=1, source_target_pairs={{0,12},{1,13},{2,14},{3,15},{4,8},{5,9},{6,10},{7,11},{8,4},{9,5},... | collective-permute-start | bytes 49160 | tf_op jit(solution)/shard_map/ppermute | solution.py:337
  7.2 4.8 %collective-permute-start.1 = (bf16[1,64,128]{2,1,0:T(8,128)(2,1)}, bf16[1,64,128]{2,1,0:T(8,128)(2,1)S(1)}, u32[]{:S(2)}, u32[]{:S(2)}) collective-permute-start(bf16[1,64,128]{2,1,0:T(8,128)(2,1)} %get-tuple-element.18), channel_id=1, source_target_pairs={{0,8},{1,9},{2,10},{3,11},{4,12},{5,13},{6,14},{7,15},{8,0},{9,1},... | collective-permute-start | bytes 49160 | tf_op jit(solution)/shard_map/ppermute | solution.py:337
  7.2 4.8 %collective-permute-start = (bf16[1,64,128]{2,1,0:T(8,128)(2,1)}, bf16[1,64,128]{2,1,0:T(8,128)(2,1)S(1)}, u32[]{:S(2)}, u32[]{:S(2)}) collective-permute-start(bf16[1,64,128]{2,1,0:T(8,128)(2,1)} %get-tuple-element.18), channel_id=1, source_target_pairs={{0,4},{1,5},{2,6},{3,7},{4,0},{5,1},{6,2},{7,3},{8,12},{9,13},{10,... | collective-permute-start | bytes 49160 | tf_op jit(solution)/shard_map/ppermute | solution.py:337
  12.1 6.8 %copy-start.1 = (s32[1,2]{1,0:T(1,128)S(1)}, s32[1,2]{1,0:T(1,128)}, u32[]{:S(2)}) copy-start(s32[1,2]{1,0:T(1,128)} %get-tuple-element.17) | copy-start | bytes 28
  12.1 4.3 %collective-permute-start.3 = (bf16[4,64,128]{2,1,0:T(8,128)(2,1)S(1)}, bf16[4,64,128]{2,1,0:T(8,128)(2,1)S(1)}, u32[]{:S(2)}, u32[]{:S(2)}) collective-permute-start(bf16[4,64,128]{2,1,0:T(8,128)(2,1)S(1)} %pad_maximum_fusion.1), channel_id=1, source_target_pairs={{0,2},{1,3},{2,0},{3,1},{4,6},{5,7},{6,4},{7,5},{8,10},{9,11},{10,... | collective-permute-start | bytes 196616 | tf_op jit(solution)/shard_map/ppermute | solution.py:337
  16.5 2.5 %collective-permute-start.4 = (bf16[8,64,128]{2,1,0:T(8,128)(2,1)S(1)}, bf16[8,64,128]{2,1,0:T(8,128)(2,1)S(1)}, u32[]{:S(2)}, u32[]{:S(2)}) collective-permute-start(bf16[8,64,128]{2,1,0:T(8,128)(2,1)S(1)} %pad_maximum_fusion.refs_0_), channel_id=1, source_target_pairs={{0,1},{1,0},{2,3},{3,2},{4,5},{5,4},{6,7},{7,6},{8,9},{9,8},{10,11... | collective-permute-start | bytes 393224 | tf_op jit(solution)/shard_map/ppermute | solution.py:337
  18.9 11.2 %copy-start = (s32[1,256]{1,0:T(1,128)S(1)}, s32[1,256]{1,0:T(1,128)}, u32[]{:S(2)}) copy-start(s32[1,256]{1,0:T(1,128)} %get-tuple-element.16) | copy-start | bytes 3076
  41.4 1.7 %collective-permute-start.5 = (bf16[16,64,128]{2,1,0:T(8,128)(2,1)S(1)}, bf16[16,64,128]{2,1,0:T(8,128)(2,1)S(1)}, u32[]{:S(2)}, u32[]{:S(2)}) collective-permute-start(bf16[16,64,128]{2,1,0:T(8,128)(2,1)S(1)} %get-tuple-element.26), channel_id=1, source_target_pairs={{0,1},{1,0},{2,3},{3,2},{4,5},{5,4},{6,7},{7,6},{8,9},{9,8},{10,11... | collective-permute-start | bytes 786440 | tf_op jit(solution)/shard_map/ppermute | solution.py:337
  43.1 5.8 %collective-permute-start.6 = (bf16[8,64,128]{2,1,0:T(8,128)(2,1)S(1)}, bf16[8,64,128]{2,1,0:T(8,128)(2,1)S(1)}, u32[]{:S(2)}, u32[]{:S(2)}) collective-permute-start(bf16[8,64,128]{2,1,0:T(8,128)(2,1)S(1)} %slice.41), channel_id=1, source_target_pairs={{0,2},{1,3},{2,0},{3,1},{4,6},{5,7},{6,4},{7,5},{8,10},{9,11},{10,... | collective-permute-start | bytes 393224 | tf_op jit(solution)/shard_map/ppermute | solution.py:337
  49.1 4.0 %collective-permute-start.7 = (bf16[2,64,128]{2,1,0:T(8,128)(2,1)S(1)}, bf16[2,64,128]{2,1,0:T(8,128)(2,1)S(1)}, u32[]{:S(2)}, u32[]{:S(2)}) collective-permute-start(bf16[2,64,128]{2,1,0:T(8,128)(2,1)S(1)} %get-tuple-element.29), channel_id=1, source_target_pairs={{0,4},{1,5},{2,6},{3,7},{4,0},{5,1},{6,2},{7,3},{8,12},{9,13},{10,... | collective-permute-start | bytes 98312 | tf_op jit(solution)/shard_map/ppermute | solution.py:337
  50.1 6.1 %collective-permute-start.9 = (bf16[2,64,128]{2,1,0:T(8,128)(2,1)S(1)}, bf16[2,64,128]{2,1,0:T(8,128)(2,1)S(1)}, u32[]{:S(2)}, u32[]{:S(2)}) collective-permute-start(bf16[2,64,128]{2,1,0:T(8,128)(2,1)S(1)} %get-tuple-element.30), channel_id=1, source_target_pairs={{0,12},{1,13},{2,14},{3,15},{4,8},{5,9},{6,10},{7,11},{8,4},{9,5},... | collective-permute-start | bytes 98312 | tf_op jit(solution)/shard_map/ppermute | solution.py:337
  52.6 4.8 %collective-permute-start.8 = (bf16[2,64,128]{2,1,0:T(8,128)(2,1)S(1)}, bf16[2,64,128]{2,1,0:T(8,128)(2,1)S(1)}, u32[]{:S(2)}, u32[]{:S(2)}) collective-permute-start(bf16[2,64,128]{2,1,0:T(8,128)(2,1)S(1)} %get-tuple-element.31), channel_id=1, source_target_pairs={{0,8},{1,9},{2,10},{3,11},{4,12},{5,13},{6,14},{7,15},{8,0},{9,1},... | collective-permute-start | bytes 98312 | tf_op jit(solution)/shard_map/ppermute | solution.py:337

commit v13 on v12

--- a/solution.py
+++ b/solution.py
@@ -10,11 +10,11 @@
 CB_DEV = 4
 LAM = 4
 WIDE = 512
-PARTS = (32, 16, 16)
+PARTS = (40, 16, 8)
 GRANT = 3 << 20
 
 
-def pack_kernel(place_rounds, table_rounds, me_ref, count_ref, *refs):
+def pack_kernel(place_rounds, slot_rounds, me_ref, count_ref, *refs):
     sources, (out_ref, ids_ref, place_ref), (rows_ref, *held, sems) = refs[:4], refs[4:7], refs[7:]
     copies = [pltpu.make_async_copy(src, dst, sems.at[k]) for k, (src, dst) in enumerate(zip(sources, held))]
     for copy in copies:
@@ -37,7 +37,7 @@
     me = me_ref[0]
     rel = pair_ref[...] ^ me
     ids, weight = jnp.zeros_like(rel), 1
-    for shift, step in table_rounds:
+    for shift, step in slot_rounds:
         ids = ids + ((rel >> shift) & ((1 << step) - 1)) * weight
         weight <<= step
     ids_ref[...] = ids
@@ -52,7 +52,7 @@
 
 def packed(me, basis_count, pair_atoms, chi_target, green_occ, green_virt, bs, bits):
     return pl.pallas_call(
-        functools.partial(pack_kernel, owner_rounds(bits), owner_rounds(bits)[::-1]),
+        functools.partial(pack_kernel, owner_rounds(bits), table_rounds(bits)),
         in_specs=in_smem(2) + [pl.BlockSpec(memory_space=pl.ANY)] * 4,
         out_specs=in_vmem(3),
         out_shape=[
@@ -185,10 +185,12 @@
     virt_w = jnp.where(same, spread, 0.0).astype(jnp.bfloat16)
 
     def virt_product(part, before, step):
-        got = jnp.dot(flat(d_parts[part], slice(None), [2 * step, 2 * step + 1]), virt_w, preferred_element_type=jnp.float32)
-        got = got.astype(jnp.bfloat16)
-        for t in range(2):
-            v_ref[:, before + 2 * step + t] = got[:, t * lanes:(t + 1) * lanes].reshape(v_ref.shape[:1] + (aux, lanes))
+        held = [flat(d_parts[part], slice(None), [per * step + t, per * step + t + 1]) for t in range(0, per, 2)]
+        got = jnp.dot(jnp.concatenate(held, axis=0), virt_w, preferred_element_type=jnp.float32).astype(jnp.bfloat16)
+        count = held[0].shape[0]
+        for t in range(per):
+            side = got[t // 2 * count:(t // 2 + 1) * count, t % 2 * lanes:(t % 2 + 1) * lanes]
+            v_ref[:, before + per * step + t] = side.reshape(v_ref.shape[:1] + (aux, lanes))
 
     tall = bs * half
     rep_t = (
@@ -224,8 +226,7 @@
             copy(j).wait()
             placed(jnp.maximum(j - 1, 0), 1)
             product(j, 0)
-            for k in range(per // 2):
-                virt_product(part, done * per, i * (per // 2) + k)
+            virt_product(part, done * per, i)
             placed(j, 0)
             product(j, 1)
 
@@ -319,13 +320,17 @@
     )(targets, occ_side, virt_side)
 
 
-def owner_rounds(bits):
+def table_rounds(bits):
     rounds, at = [], 0
     while at < bits:
         step = 1 if at < 2 else min(2, bits - at)
         rounds.append((at, step))
         at += step
-    return rounds
+    return rounds[::-1]
+
+
+def owner_rounds(bits):
+    return [(0, 1)] + [(at, min(3, bits - at)) for at in range(1, bits, 3)]
 
 
 def local(orb, three_centre, green_occ, green_virt, pair_atoms, basis_count, chi_target):
@@ -340,7 +345,7 @@
     table, ids, place = packed(
         me[None].astype(jnp.int32), basis_count, pair_atoms, chi_target, green_occ, green_virt, bs, bits
     )
-    rounds = owner_rounds(bits)[::-1]
+    rounds = table_rounds(bits)
     tables, d_parts = [table], []
     for k, (shift, step) in enumerate(rounds):
         after = tables[-1:] if k else []

time: 58.6 us -> 58.5 us (level)
  waiting for transfers between devices: 10.7 us -> 4.75 us
  starting transfers between devices: 13.5 us -> 19.3 us
    ppermute x10 -> x13, waiting for transfers between devices: 10.7 us -> 4.75 us  [exchange(): return lax.ppermute(value, 'orb', [(i, i ^ flip) for i in range(orb)])]
    ppermute x10 -> x13, starting transfers between devices: 13.5 us -> 19.3 us  [exchange(): return lax.ppermute(value, 'orb', [(i, i ^ flip) for i in range(orb)])]
  transfers between devices with their start and end apart: 10 -> 13, of which waited for: 6 -> 6; matrix products, arithmetic and copies ran while one was open for 0% -> 0% of each run, Pallas kernels for 14% -> 15%
where the time goes in v13:
time: 58.5 us; the launch traced here: 58.2 us
  Pallas kernels  32.3 us (55%)
  starting transfers between devices  19.3 us (33%)
  waiting for transfers between devices  4.75 us (8%)
  local copies, waits for them, and re-layouts  0.91 us (2%)
  between operations  0.84 us (1%)
    ppermute x13, starting transfers between devices, exchange(): return lax.ppermute(value, 'orb', [(i, i ^ flip) for i in range(orb)])  19.3 us
    pallas_call x1, Pallas kernels, chi_blocks_of(): pl.pallas_call(functools.partial(chi_kernel, bs, sends), in_specs=in_smem...  11.2 us
    pallas_call x1, Pallas kernels, chi_blocks_of(): pl.pallas_call(functools.partial(sides_kernel, len(tables)), in_specs=in_...  11.2 us
    pallas_call x3, Pallas kernels, relayout(): pl.pallas_call(functools.partial(relayout_kernel, sum(PARTS[:part])), in_...  8.45 us
    ppermute x13, waiting for transfers between devices, exchange(): return lax.ppermute(value, 'orb', [(i, i ^ flip) for i in range(orb)])  4.75 us
    pallas_call x1, Pallas kernels, packed(): pl.pallas_call(functools.partial(pack_kernel, owner_rounds(bits), table_r...  1.44 us
  transfers between devices with their start and end apart: 13, of which 6 were waited for; matrix products, arithmetic and copies ran while one was open for 0% of the time, Pallas kernels for 15%

profile of v13, /device:TPU:0, one launch (start us, length us, event | category | flops | bytes accessed | tf_op | source)
XLA Modules:
  0.0 58.2 jit_solution(6495399843160510751)
XLA Ops:
  0.7 1.4 %shard_map.64 = (bf16[1,64,128]{2,1,0:T(8,128)(2,1)}, s32[1,2]{1,0:T(1,128)}, s32[1,256]{1,0:T(1,128)}) custom-call(s32[1]{0:T(128)} %bitcast.me_ref, s32[1]{0:T(128)S(6)} %copy.8.count_ref, s32[1,2]{1,0:T(1,128)} %refs_0_.1, s32[1,256]{1,0:T(1,128)} %refs_1_.1, bf16[1,4096]{1,0:T(2,128)(2,1)} %refs_2_.1, bf16[1,4096]{1,0:T(2,128)(2,1)} %refs_3_.1), custom_call_target="tpu_custom_call" | custom-call | tf_op jit(solution)/shard_map/pallas_call | solution.py:54
  2.1 0.0 copy-start.2
  2.1 5.1 %collective-permute-start.2 = (bf16[1,64,128]{2,1,0:T(8,128)(2,1)}, bf16[1,64,128]{2,1,0:T(8,128)(2,1)S(1)}, u32[]{:S(2)}, u32[]{:S(2)}) collective-permute-start(bf16[1,64,128]{2,1,0:T(8,128)(2,1)} %get-tuple-element.18), channel_id=1, source_target_pairs={{0,12},{1,13},{2,14},{3,15},{4,8},{5,9},{6,10},{7,11},{8,4},{9,5},... | collective-permute-start | bytes 49160 | tf_op jit(solution)/shard_map/ppermute | solution.py:342
  7.2 0.0 collective-permute-start.1
  7.2 0.6 %collective-permute-start = (bf16[1,64,128]{2,1,0:T(8,128)(2,1)}, bf16[1,64,128]{2,1,0:T(8,128)(2,1)S(1)}, u32[]{:S(2)}, u32[]{:S(2)}) collective-permute-start(bf16[1,64,128]{2,1,0:T(8,128)(2,1)} %get-tuple-element.18), channel_id=1, source_target_pairs={{0,4},{1,5},{2,6},{3,7},{4,0},{5,1},{6,2},{7,3},{8,12},{9,13},{10,... | collective-permute-start | bytes 49160 | tf_op jit(solution)/shard_map/ppermute | solution.py:342
  7.9 4.4 %shard_map.65.refs_2_ = bf16[64,20,16,128]{3,2,1,0:T(8,128)(2,1)S(1)} custom-call(bf16[64,16,4096]{2,1,0:T(8,128)(2,1)} %bitcast.9), custom_call_target="tpu_custom_call" | custom-call | flops 1342177280 | bytes 10485760 | tf_op jit(solution)/shard_map/pallas_call | solution.py:120
  12.3 0.0 collective-permute-done.2.refs_0_
  12.3 0.0 collective-permute-done.1
  12.3 0.0 collective-permute-done
  12.3 0.0 copy-done.2
  12.3 0.0 copy-start.1
  12.3 1.7 %collective-permute-start.3 = (bf16[4,64,128]{2,1,0:T(8,128)(2,1)S(1)}, bf16[4,64,128]{2,1,0:T(8,128)(2,1)S(1)}, u32[]{:S(2)}, u32[]{:S(2)}) collective-permute-start(bf16[4,64,128]{2,1,0:T(8,128)(2,1)S(1)} %pad_maximum_fusion.1), channel_id=1, source_target_pairs={{0,2},{1,3},{2,0},{3,1},{4,6},{5,7},{6,4},{7,5},{8,10},{9,11},{10,... | collective-permute-start | bytes 196616 | tf_op jit(solution)/shard_map/ppermute | solution.py:342
  14.1 2.4 %shard_map.66.refs_3_ = bf16[64,8,16,128]{3,2,1,0:T(8,128)(2,1)S(1)} custom-call(bf16[64,16,4096]{2,1,0:T(8,128)(2,1)} %bitcast.10, bf16[1,64,128]{2,1,0:T(8,128)(2,1)S(1)} %collective-permute-done.2.refs_0_), custom_call_target="tpu_custom_call" | custom-call | flops 536870912 | bytes 4194304 | tf_op jit(solution)/shard_map/pallas_call | solution.py:120
  16.4 0.2 collective-permute-done.3.refs_0_
  16.7 0.1 collective-permute-start.4
  16.8 1.7 %shard_map.67.refs_4_ = bf16[64,4,16,128]{3,2,1,0:T(8,128)(2,1)S(1)} custom-call(bf16[64,16,4096]{2,1,0:T(8,128)(2,1)} %bitcast.11, bf16[4,64,128]{2,1,0:T(8,128)(2,1)S(1)} %collective-permute-done.3.refs_0_), custom_call_target="tpu_custom_call" | custom-call | flops 268435456 | bytes 2097152 | tf_op jit(solution)/shard_map/pallas_call | solution.py:120
  18.5 0.0 collective-permute-done.4.refs_1_
  18.5 0.0 copy-done.1
  18.5 0.0 copy-start
  18.5 11.2 %shard_map.68 = (bf16[64,32,16,128]{3,2,1,0:T(8,128)(2,1)S(1)}, bf16[64,32,16,128]{3,2,1,0:T(8,128)(2,1)S(1)}) custom-call(s32[2]{0:T(128)S(1)} %bitcast.8, bf16[8,64,128]{2,1,0:T(8,128)(2,1)S(1)} %pad_maximum_fusion.refs_0_, bf16[8,64,128]{2,1,0:T(8,128)(2,1)S(1)} %collective-permute-done.4.refs_1_, bf16[64,20,16,128]{3,2,1,0:T(8,128)(2,1)S(1)} %shard_map.65.refs_2_, ...), custom_call_target="tpu_custom_call" | custom-call | flops 8589934592 | bytes 16777216 | tf_op jit(solution)/shard_map/pallas_call | solution.py:295
  29.7 0.0 copy-done
  29.7 11.2 %shard_map.69 = (f32[16,64,128]{2,1,0:T(8,128)S(1)}, bf16[16,64,128]{2,1,0:T(8,128)(2,1)S(1)}) custom-call(s32[256]{0:T(256)S(1)} %bitcast.7, bf16[64,32,16,128]{3,2,1,0:T(8,128)(2,1)S(1)} %get-tuple-element.23.o_ref, bf16[64,32,16,128]{3,2,1,0:T(8,128)(2,1)S(1)} %get-tuple-element.24.v_ref), custom_call_target="tpu_custom_call" | custom-call | flops 8589934592 | bytes 16777216 | tf_op jit(solution)/shard_map/pallas_call | solution.py:311
  40.9 0.6 collective-permute-start.5
  41.4 1.2 %collective-permute-done.5 = bf16[16,64,128]{2,1,0:T(8,128)(2,1)S(1)} collective-permute-done((bf16[16,64,128]{2,1,0:T(8,128)(2,1)S(1)}, bf16[16,64,128]{2,1,0:T(8,128)(2,1)S(1)}, u32[]{:S(2)}, u32[]{:S(2)}) %collective-permute-start.5) | collective-permute-done | bytes 262176 | tf_op jit(solution)/shard_map/ppermute | solution.py:342
  42.6 0.1 fusion.6
  42.7 1.7 %collective-permute-start.6 = (bf16[2,64,128]{2,1,0:T(8,128)(2,1)S(1)}, bf16[2,64,128]{2,1,0:T(8,128)(2,1)S(1)}, u32[]{:S(2)}, u32[]{:S(2)}) collective-permute-start(bf16[2,64,128]{2,1,0:T(8,128)(2,1)S(1)} %get-tuple-element.29), channel_id=1, source_target_pairs={{0,2},{1,3},{2,0},{3,1},{4,6},{5,7},{6,4},{7,5},{8,10},{9,11},{10,... | collective-permute-start | bytes 98312 | tf_op jit(solution)/shard_map/ppermute | solution.py:342
  44.5 3.5 %collective-permute-start.12 = (bf16[2,64,128]{2,1,0:T(8,128)(2,1)S(1)}, bf16[2,64,128]{2,1,0:T(8,128)(2,1)S(1)}, u32[]{:S(2)}, u32[]{:S(2)}) collective-permute-start(bf16[2,64,128]{2,1,0:T(8,128)(2,1)S(1)} %get-tuple-element.30), channel_id=1, source_target_pairs={{0,14},{1,15},{2,12},{3,13},{4,10},{5,11},{6,8},{7,9},{8,6},{9,7},... | collective-permute-start | bytes 98312 | tf_op jit(solution)/shard_map/ppermute | solution.py:342
  48.0 0.1 collective-permute-start.11
  48.1 1.5 %collective-permute-start.10 = (bf16[2,64,128]{2,1,0:T(8,128)(2,1)S(1)}, bf16[2,64,128]{2,1,0:T(8,128)(2,1)S(1)}, u32[]{:S(2)}, u32[]{:S(2)}) collective-permute-start(bf16[2,64,128]{2,1,0:T(8,128)(2,1)S(1)} %get-tuple-element.32), channel_id=1, source_target_pairs={{0,10},{1,11},{2,8},{3,9},{4,14},{5,15},{6,12},{7,13},{8,2},{9,3},... | collective-permute-start | bytes 98312 | tf_op jit(solution)/shard_map/ppermute | solution.py:342
  49.5 2.6 %collective-permute-start.9 = (bf16[2,64,128]{2,1,0:T(8,128)(2,1)S(1)}, bf16[2,64,128]{2,1,0:T(8,128)(2,1)S(1)}, u32[]{:S(2)}, u32[]{:S(2)}) collective-permute-start(bf16[2,64,128]{2,1,0:T(8,128)(2,1)S(1)} %get-tuple-element.33), channel_id=1, source_target_pairs={{0,8},{1,9},{2,10},{3,11},{4,12},{5,13},{6,14},{7,15},{8,0},{9,1},... | collective-permute-start | bytes 98312 | tf_op jit(solution)/shard_map/ppermute | solution.py:342
  52.1 0.0 collective-permute-done.6
  52.1 1.3 %collective-permute-start.8 = (bf16[2,64,128]{2,1,0:T(8,128)(2,1)S(1)}, bf16[2,64,128]{2,1,0:T(8,128)(2,1)S(1)}, u32[]{:S(2)}, u32[]{:S(2)}) collective-permute-start(bf16[2,64,128]{2,1,0:T(8,128)(2,1)S(1)} %get-tuple-element.34), channel_id=1, source_target_pairs={{0,6},{1,7},{2,4},{3,5},{4,2},{5,3},{6,0},{7,1},{8,14},{9,15},{10,... | collective-permute-start | bytes 98312 | tf_op jit(solution)/shard_map/ppermute | solution.py:342
  53.4 0.0 collective-permute-done.12
  53.4 0.6 collective-permute-start.7
  53.9 0.0 collective-permute-done.11
  54.0 0.3 collective-permute-done.10
  54.2 0.8 %collective-permute-done.9 = bf16[2,64,128]{2,1,0:T(8,128)(2,1)S(1)} collective-permute-done((bf16[2,64,128]{2,1,0:T(8,128)(2,1)S(1)}, bf16[2,64,128]{2,1,0:T(8,128)(2,1)S(1)}, u32[]{:S(2)}, u32[]{:S(2)}) %collective-permute-start.9) | collective-permute-done | bytes 32800 | tf_op jit(solution)/shard_map/ppermute | solution.py:342
  55.0 1.9 %collective-permute-done.8 = bf16[2,64,128]{2,1,0:T(8,128)(2,1)S(1)} collective-permute-done((bf16[2,64,128]{2,1,0:T(8,128)(2,1)S(1)}, bf16[2,64,128]{2,1,0:T(8,128)(2,1)S(1)}, u32[]{:S(2)}, u32[]{:S(2)}) %collective-permute-start.8) | collective-permute-done | bytes 32800 | tf_op jit(solution)/shard_map/ppermute | solution.py:342
  56.9 0.4 collective-permute-done.7
  57.3 0.1 reshape.6
  57.5 0.7 %reshape.7 = f32[4,4096]{1,0:T(4,128)} reshape(f32[2,2,64,64]{3,2,1,0:T(8,128)S(1)} %copy.7) | data formatting | bytes 131072 | tf_op jit(solution)/shard_map/reshape | solution.py:367
  (5 shorter events, 0.1 us)
Async XLA Ops:
  2.1 10.2 %copy-start.2 = (bf16[1,64,128]{2,1,0:T(8,128)(2,1)S(1)}, bf16[1,64,128]{2,1,0:T(8,128)(2,1)}, u32[]{:S(2)}) copy-start(bf16[1,64,128]{2,1,0:T(8,128)(2,1)} %get-tuple-element.18) | copy-start | bytes 49156
  2.1 10.2 %collective-permute-start.2 = (bf16[1,64,128]{2,1,0:T(8,128)(2,1)}, bf16[1,64,128]{2,1,0:T(8,128)(2,1)S(1)}, u32[]{:S(2)}, u32[]{:S(2)}) collective-permute-start(bf16[1,64,128]{2,1,0:T(8,128)(2,1)} %get-tuple-element.18), channel_id=1, source_target_pairs={{0,12},{1,13},{2,14},{3,15},{4,8},{5,9},{6,10},{7,11},{8,4},{9,5},... | collective-permute-start | bytes 49160 | tf_op jit(solution)/shard_map/ppermute | solution.py:342
  7.2 5.0 %collective-permute-start.1 = (bf16[1,64,128]{2,1,0:T(8,128)(2,1)}, bf16[1,64,128]{2,1,0:T(8,128)(2,1)S(1)}, u32[]{:S(2)}, u32[]{:S(2)}) collective-permute-start(bf16[1,64,128]{2,1,0:T(8,128)(2,1)} %get-tuple-element.18), channel_id=1, source_target_pairs={{0,8},{1,9},{2,10},{3,11},{4,12},{5,13},{6,14},{7,15},{8,0},{9,1},... | collective-permute-start | bytes 49160 | tf_op jit(solution)/shard_map/ppermute | solution.py:342
  7.2 5.1 %collective-permute-start = (bf16[1,64,128]{2,1,0:T(8,128)(2,1)}, bf16[1,64,128]{2,1,0:T(8,128)(2,1)S(1)}, u32[]{:S(2)}, u32[]{:S(2)}) collective-permute-start(bf16[1,64,128]{2,1,0:T(8,128)(2,1)} %get-tuple-element.18), channel_id=1, source_target_pairs={{0,4},{1,5},{2,6},{3,7},{4,0},{5,1},{6,2},{7,3},{8,12},{9,13},{10,... | collective-permute-start | bytes 49160 | tf_op jit(solution)/shard_map/ppermute | solution.py:342
  12.3 6.2 %copy-start.1 = (s32[1,2]{1,0:T(1,128)S(1)}, s32[1,2]{1,0:T(1,128)}, u32[]{:S(2)}) copy-start(s32[1,2]{1,0:T(1,128)} %get-tuple-element.17) | copy-start | bytes 28
  12.3 4.3 %collective-permute-start.3 = (bf16[4,64,128]{2,1,0:T(8,128)(2,1)S(1)}, bf16[4,64,128]{2,1,0:T(8,128)(2,1)S(1)}, u32[]{:S(2)}, u32[]{:S(2)}) collective-permute-start(bf16[4,64,128]{2,1,0:T(8,128)(2,1)S(1)} %pad_maximum_fusion.1), channel_id=1, source_target_pairs={{0,2},{1,3},{2,0},{3,1},{4,6},{5,7},{6,4},{7,5},{8,10},{9,11},{10,... | collective-permute-start | bytes 196616 | tf_op jit(solution)/shard_map/ppermute | solution.py:342
  16.7 1.8 %collective-permute-start.4 = (bf16[8,64,128]{2,1,0:T(8,128)(2,1)S(1)}, bf16[8,64,128]{2,1,0:T(8,128)(2,1)S(1)}, u32[]{:S(2)}, u32[]{:S(2)}) collective-permute-start(bf16[8,64,128]{2,1,0:T(8,128)(2,1)S(1)} %pad_maximum_fusion.refs_0_), channel_id=1, source_target_pairs={{0,1},{1,0},{2,3},{3,2},{4,5},{5,4},{6,7},{7,6},{8,9},{9,8},{10,11... | collective-permute-start | bytes 393224 | tf_op jit(solution)/shard_map/ppermute | solution.py:342
  18.5 11.2 %copy-start = (s32[1,256]{1,0:T(1,128)S(1)}, s32[1,256]{1,0:T(1,128)}, u32[]{:S(2)}) copy-start(s32[1,256]{1,0:T(1,128)} %get-tuple-element.16) | copy-start | bytes 3076
  40.9 1.7 %collective-permute-start.5 = (bf16[16,64,128]{2,1,0:T(8,128)(2,1)S(1)}, bf16[16,64,128]{2,1,0:T(8,128)(2,1)S(1)}, u32[]{:S(2)}, u32[]{:S(2)}) collective-permute-start(bf16[16,64,128]{2,1,0:T(8,128)(2,1)S(1)} %get-tuple-element.26), channel_id=1, source_target_pairs={{0,1},{1,0},{2,3},{3,2},{4,5},{5,4},{6,7},{7,6},{8,9},{9,8},{10,11... | collective-permute-start | bytes 786440 | tf_op jit(solution)/shard_map/ppermute | solution.py:342
  42.7 9.4 %collective-permute-start.6 = (bf16[2,64,128]{2,1,0:T(8,128)(2,1)S(1)}, bf16[2,64,128]{2,1,0:T(8,128)(2,1)S(1)}, u32[]{:S(2)}, u32[]{:S(2)}) collective-permute-start(bf16[2,64,128]{2,1,0:T(8,128)(2,1)S(1)} %get-tuple-element.29), channel_id=1, source_target_pairs={{0,2},{1,3},{2,0},{3,1},{4,6},{5,7},{6,4},{7,5},{8,10},{9,11},{10,... | collective-permute-start | bytes 98312 | tf_op jit(solution)/shard_map/ppermute | solution.py:342
  44.5 8.9 %collective-permute-start.12 = (bf16[2,64,128]{2,1,0:T(8,128)(2,1)S(1)}, bf16[2,64,128]{2,1,0:T(8,128)(2,1)S(1)}, u32[]{:S(2)}, u32[]{:S(2)}) collective-permute-start(bf16[2,64,128]{2,1,0:T(8,128)(2,1)S(1)} %get-tuple-element.30), channel_id=1, source_target_pairs={{0,14},{1,15},{2,12},{3,13},{4,10},{5,11},{6,8},{7,9},{8,6},{9,7},... | collective-permute-start | bytes 98312 | tf_op jit(solution)/shard_map/ppermute | solution.py:342
  48.0 5.9 %collective-permute-start.11 = (bf16[2,64,128]{2,1,0:T(8,128)(2,1)S(1)}, bf16[2,64,128]{2,1,0:T(8,128)(2,1)S(1)}, u32[]{:S(2)}, u32[]{:S(2)}) collective-permute-start(bf16[2,64,128]{2,1,0:T(8,128)(2,1)S(1)} %get-tuple-element.31), channel_id=1, source_target_pairs={{0,12},{1,13},{2,14},{3,15},{4,8},{5,9},{6,10},{7,11},{8,4},{9,5},... | collective-permute-start | bytes 98312 | tf_op jit(solution)/shard_map/ppermute | solution.py:342
  48.1 6.1 %collective-permute-start.10 = (bf16[2,64,128]{2,1,0:T(8,128)(2,1)S(1)}, bf16[2,64,128]{2,1,0:T(8,128)(2,1)S(1)}, u32[]{:S(2)}, u32[]{:S(2)}) collective-permute-start(bf16[2,64,128]{2,1,0:T(8,128)(2,1)S(1)} %get-tuple-element.32), channel_id=1, source_target_pairs={{0,10},{1,11},{2,8},{3,9},{4,14},{5,15},{6,12},{7,13},{8,2},{9,3},... | collective-permute-start | bytes 98312 | tf_op jit(solution)/shard_map/ppermute | solution.py:342
  49.5 5.5 %collective-permute-start.9 = (bf16[2,64,128]{2,1,0:T(8,128)(2,1)S(1)}, bf16[2,64,128]{2,1,0:T(8,128)(2,1)S(1)}, u32[]{:S(2)}, u32[]{:S(2)}) collective-permute-start(bf16[2,64,128]{2,1,0:T(8,128)(2,1)S(1)} %get-tuple-element.33), channel_id=1, source_target_pairs={{0,8},{1,9},{2,10},{3,11},{4,12},{5,13},{6,14},{7,15},{8,0},{9,1},... | collective-permute-start | bytes 98312 | tf_op jit(solution)/shard_map/ppermute | solution.py:342
  52.1 4.8 %collective-permute-start.8 = (bf16[2,64,128]{2,1,0:T(8,128)(2,1)S(1)}, bf16[2,64,128]{2,1,0:T(8,128)(2,1)S(1)}, u32[]{:S(2)}, u32[]{:S(2)}) collective-permute-start(bf16[2,64,128]{2,1,0:T(8,128)(2,1)S(1)} %get-tuple-element.34), channel_id=1, source_target_pairs={{0,6},{1,7},{2,4},{3,5},{4,2},{5,3},{6,0},{7,1},{8,14},{9,15},{10,... | collective-permute-start | bytes 98312 | tf_op jit(solution)/shard_map/ppermute | solution.py:342
  53.4 3.9 %collective-permute-start.7 = (bf16[2,64,128]{2,1,0:T(8,128)(2,1)S(1)}, bf16[2,64,128]{2,1,0:T(8,128)(2,1)S(1)}, u32[]{:S(2)}, u32[]{:S(2)}) collective-permute-start(bf16[2,64,128]{2,1,0:T(8,128)(2,1)S(1)} %get-tuple-element.35), channel_id=1, source_target_pairs={{0,4},{1,5},{2,6},{3,7},{4,0},{5,1},{6,2},{7,3},{8,12},{9,13},{10,... | collective-permute-start | bytes 98312 | tf_op jit(solution)/shard_map/ppermute | solution.py:342

commit v14 on v13

--- a/solution.py
+++ b/solution.py
@@ -168,7 +168,7 @@
     per = WIDE // lanes
 
     def columns(j):
-        return pl.ds(pl.multiple_of(j * WIDE, WIDE), WIDE)
+        return slice(j * WIDE, (j + 1) * WIDE)
 
     def copy(j):
         return pltpu.make_async_copy(b_hbm.at[:, :, columns(j)], b_ref.at[:, :, columns(j)], sems.at[j])
@@ -216,23 +216,19 @@
             pair = halves_joined(got[:, 0], got[:, 1], low, lanes)
             o_ref[h * tiles + per * j + t] = jnp.concatenate(pair, axis=1).astype(jnp.bfloat16)
 
-    done = 0
+    j = 0
     for part, d_ref in enumerate(d_parts):
-        steps = d_ref.shape[1] // per
-
-        @pl.loop(0, steps)
-        def _(i):
-            j = done + i
+        before = j * per
+        for i in range(d_ref.shape[1] // per):
             copy(j).wait()
-            placed(jnp.maximum(j - 1, 0), 1)
+            if j:
+                placed(j - 1, 1)
             product(j, 0)
-            virt_product(part, done * per, i)
+            virt_product(part, before, i)
             placed(j, 0)
             product(j, 1)
-
-        done += steps
-
-    placed(done - 1, 1)
+            j += 1
+    placed(j - 1, 1)
 
 
 def chi_kernel(bs, sends, tgt_ref, o_ref, v_ref, *refs):
@@ -330,7 +326,7 @@
 
 
 def owner_rounds(bits):
-    return [(0, 1)] + [(at, min(3, bits - at)) for at in range(1, bits, 3)]
+    return table_rounds(bits)[::-1]
 
 
 def local(orb, three_centre, green_occ, green_virt, pair_atoms, basis_count, chi_target):

time: 58.5 us -> 57.7 us (0.986)
  starting transfers between devices: 19.3 us -> 14.2 us
  waiting for transfers between devices: 4.75 us -> 9.82 us
  Pallas kernels: 32.3 us -> 31.5 us
    ppermute x13 -> x10, starting transfers between devices: 19.3 us -> 14.2 us  [exchange(): return lax.ppermute(value, 'orb', [(i, i ^ flip) for i in range(orb)])]
    ppermute x13 -> x10, waiting for transfers between devices: 4.75 us -> 9.82 us  [exchange(): return lax.ppermute(value, 'orb', [(i, i ^ flip) for i in range(orb)])]
    pallas_call x1, Pallas kernels: 11.2 us -> 10.2 us  [chi_blocks_of(): pl.pallas_call(functools.partial(sides_kernel, len(tables)), in_specs=in_...]
  transfers between devices with their start and end apart: 13 -> 10, of which waited for: 6 -> 5; matrix products, arithmetic and copies ran while one was open for 0% -> 0% of each run, Pallas kernels for 15% -> 15%
where the time goes in v14:
time: 57.7 us; the launch traced here: 57.5 us
  Pallas kernels  31.5 us (55%)
  starting transfers between devices  14.2 us (25%)
  waiting for transfers between devices  9.82 us (17%)
  local copies, waits for them, and re-layouts  0.92 us (2%)
  between operations  0.85 us (1%)
    ppermute x10, starting transfers between devices, exchange(): return lax.ppermute(value, 'orb', [(i, i ^ flip) for i in range(orb)])  14.2 us
    pallas_call x1, Pallas kernels, chi_blocks_of(): pl.pallas_call(functools.partial(chi_kernel, bs, sends), in_specs=in_smem...  11.4 us
    pallas_call x1, Pallas kernels, chi_blocks_of(): pl.pallas_call(functools.partial(sides_kernel, len(tables)), in_specs=in_...  10.2 us
    ppermute x10, waiting for transfers between devices, exchange(): return lax.ppermute(value, 'orb', [(i, i ^ flip) for i in range(orb)])  9.82 us
    pallas_call x3, Pallas kernels, relayout(): pl.pallas_call(functools.partial(relayout_kernel, sum(PARTS[:part])), in_...  8.45 us
    pallas_call x1, Pallas kernels, packed(): pl.pallas_call(functools.partial(pack_kernel, owner_rounds(bits), table_r...  1.44 us
  transfers between devices with their start and end apart: 10, of which 5 were waited for; matrix products, arithmetic and copies ran while one was open for 0% of the time, Pallas kernels for 15%

profile of v14, /device:TPU:0, one launch (start us, length us, event | category | flops | bytes accessed | tf_op | source)
XLA Modules:
  0.0 57.5 jit_solution(2051748278935753061)
XLA Ops:
  0.7 1.4 %shard_map.64 = (bf16[1,64,128]{2,1,0:T(8,128)(2,1)}, s32[1,2]{1,0:T(1,128)}, s32[1,256]{1,0:T(1,128)}) custom-call(s32[1]{0:T(128)} %bitcast.me_ref, s32[1]{0:T(128)S(6)} %copy.8.count_ref, s32[1,2]{1,0:T(1,128)} %refs_0_.1, s32[1,256]{1,0:T(1,128)} %refs_1_.1, bf16[1,4096]{1,0:T(2,128)(2,1)} %refs_2_.1, bf16[1,4096]{1,0:T(2,128)(2,1)} %refs_3_.1), custom_call_target="tpu_custom_call" | custom-call | tf_op jit(solution)/shard_map/pallas_call | solution.py:54
  2.1 0.0 copy-start.2
  2.1 5.1 %collective-permute-start.2 = (bf16[1,64,128]{2,1,0:T(8,128)(2,1)}, bf16[1,64,128]{2,1,0:T(8,128)(2,1)S(1)}, u32[]{:S(2)}, u32[]{:S(2)}) collective-permute-start(bf16[1,64,128]{2,1,0:T(8,128)(2,1)} %get-tuple-element.18), channel_id=1, source_target_pairs={{0,12},{1,13},{2,14},{3,15},{4,8},{5,9},{6,10},{7,11},{8,4},{9,5},... | collective-permute-start | bytes 49160 | tf_op jit(solution)/shard_map/ppermute | solution.py:338
  7.2 0.0 collective-permute-start.1
  7.2 0.6 %collective-permute-start = (bf16[1,64,128]{2,1,0:T(8,128)(2,1)}, bf16[1,64,128]{2,1,0:T(8,128)(2,1)S(1)}, u32[]{:S(2)}, u32[]{:S(2)}) collective-permute-start(bf16[1,64,128]{2,1,0:T(8,128)(2,1)} %get-tuple-element.18), channel_id=1, source_target_pairs={{0,4},{1,5},{2,6},{3,7},{4,0},{5,1},{6,2},{7,3},{8,12},{9,13},{10,... | collective-permute-start | bytes 49160 | tf_op jit(solution)/shard_map/ppermute | solution.py:338
  7.9 4.4 %shard_map.65.refs_2_ = bf16[64,20,16,128]{3,2,1,0:T(8,128)(2,1)S(1)} custom-call(bf16[64,16,4096]{2,1,0:T(8,128)(2,1)} %bitcast.9), custom_call_target="tpu_custom_call" | custom-call | flops 1342177280 | bytes 10485760 | tf_op jit(solution)/shard_map/pallas_call | solution.py:120
  12.3 0.0 collective-permute-done.2.refs_0_
  12.3 0.0 collective-permute-done.1
  12.3 0.0 collective-permute-done
  12.3 0.0 copy-done.2
  12.3 0.0 copy-start.1
  12.3 1.7 %collective-permute-start.3 = (bf16[4,64,128]{2,1,0:T(8,128)(2,1)S(1)}, bf16[4,64,128]{2,1,0:T(8,128)(2,1)S(1)}, u32[]{:S(2)}, u32[]{:S(2)}) collective-permute-start(bf16[4,64,128]{2,1,0:T(8,128)(2,1)S(1)} %pad_maximum_fusion.1), channel_id=1, source_target_pairs={{0,2},{1,3},{2,0},{3,1},{4,6},{5,7},{6,4},{7,5},{8,10},{9,11},{10,... | collective-permute-start | bytes 196616 | tf_op jit(solution)/shard_map/ppermute | solution.py:338
  14.1 2.4 %shard_map.66.refs_3_ = bf16[64,8,16,128]{3,2,1,0:T(8,128)(2,1)S(1)} custom-call(bf16[64,16,4096]{2,1,0:T(8,128)(2,1)} %bitcast.10, bf16[1,64,128]{2,1,0:T(8,128)(2,1)S(1)} %collective-permute-done.2.refs_0_), custom_call_target="tpu_custom_call" | custom-call | flops 536870912 | bytes 4194304 | tf_op jit(solution)/shard_map/pallas_call | solution.py:120
  16.4 0.2 collective-permute-done.3.refs_0_
  16.7 0.1 collective-permute-start.4
  16.8 1.7 %shard_map.67.refs_4_ = bf16[64,4,16,128]{3,2,1,0:T(8,128)(2,1)S(1)} custom-call(bf16[64,16,4096]{2,1,0:T(8,128)(2,1)} %bitcast.11, bf16[4,64,128]{2,1,0:T(8,128)(2,1)S(1)} %collective-permute-done.3.refs_0_), custom_call_target="tpu_custom_call" | custom-call | flops 268435456 | bytes 2097152 | tf_op jit(solution)/shard_map/pallas_call | solution.py:120
  18.5 0.0 collective-permute-done.4.refs_1_
  18.5 0.0 copy-done.1
  18.5 0.0 copy-start
  18.5 10.2 %shard_map.68 = (bf16[64,32,16,128]{3,2,1,0:T(8,128)(2,1)S(1)}, bf16[64,32,16,128]{3,2,1,0:T(8,128)(2,1)S(1)}) custom-call(s32[2]{0:T(128)S(1)} %bitcast.8, bf16[8,64,128]{2,1,0:T(8,128)(2,1)S(1)} %pad_maximum_fusion.refs_0_, bf16[8,64,128]{2,1,0:T(8,128)(2,1)S(1)} %collective-permute-done.4.refs_1_, bf16[64,20,16,128]{3,2,1,0:T(8,128)(2,1)S(1)} %shard_map.65.refs_2_, ...), custom_call_target="tpu_custom_call" | custom-call | flops 8589934592 | bytes 16777216 | tf_op jit(solution)/shard_map/pallas_call | solution.py:291
  28.7 0.0 copy-done
  28.8 11.4 %shard_map.69 = (f32[16,64,128]{2,1,0:T(8,128)S(1)}, bf16[16,64,128]{2,1,0:T(8,128)(2,1)S(1)}) custom-call(s32[256]{0:T(256)S(1)} %bitcast.7, bf16[64,32,16,128]{3,2,1,0:T(8,128)(2,1)S(1)} %get-tuple-element.23.o_ref, bf16[64,32,16,128]{3,2,1,0:T(8,128)(2,1)S(1)} %get-tuple-element.24.v_ref), custom_call_target="tpu_custom_call" | custom-call | flops 8589934592 | bytes 16777216 | tf_op jit(solution)/shard_map/pallas_call | solution.py:307
  40.1 0.6 collective-permute-start.5
  40.7 1.2 %collective-permute-done.5 = bf16[16,64,128]{2,1,0:T(8,128)(2,1)S(1)} collective-permute-done((bf16[16,64,128]{2,1,0:T(8,128)(2,1)S(1)}, bf16[16,64,128]{2,1,0:T(8,128)(2,1)S(1)}, u32[]{:S(2)}, u32[]{:S(2)}) %collective-permute-start.5) | collective-permute-done | bytes 262176 | tf_op jit(solution)/shard_map/ppermute | solution.py:338
  41.9 0.1 convert_add_fusion
  41.9 1.7 %collective-permute-start.6 = (bf16[8,64,128]{2,1,0:T(8,128)(2,1)S(1)}, bf16[8,64,128]{2,1,0:T(8,128)(2,1)S(1)}, u32[]{:S(2)}, u32[]{:S(2)}) collective-permute-start(bf16[8,64,128]{2,1,0:T(8,128)(2,1)S(1)} %slice.41), channel_id=1, source_target_pairs={{0,2},{1,3},{2,0},{3,1},{4,6},{5,7},{6,4},{7,5},{8,10},{9,11},{10,... | collective-permute-start | bytes 393224 | tf_op jit(solution)/shard_map/ppermute | solution.py:338
  43.7 4.1 %collective-permute-done.6 = bf16[8,64,128]{2,1,0:T(8,128)(2,1)S(1)} collective-permute-done((bf16[8,64,128]{2,1,0:T(8,128)(2,1)S(1)}, bf16[8,64,128]{2,1,0:T(8,128)(2,1)S(1)}, u32[]{:S(2)}, u32[]{:S(2)}) %collective-permute-start.6) | collective-permute-done | bytes 131104 | tf_op jit(solution)/shard_map/ppermute | solution.py:338
  47.8 1.4 %collective-permute-start.7 = (bf16[2,64,128]{2,1,0:T(8,128)(2,1)S(1)}, bf16[2,64,128]{2,1,0:T(8,128)(2,1)S(1)}, u32[]{:S(2)}, u32[]{:S(2)}) collective-permute-start(bf16[2,64,128]{2,1,0:T(8,128)(2,1)S(1)} %get-tuple-element.29), channel_id=1, source_target_pairs={{0,4},{1,5},{2,6},{3,7},{4,0},{5,1},{6,2},{7,3},{8,12},{9,13},{10,... | collective-permute-start | bytes 98312 | tf_op jit(solution)/shard_map/ppermute | solution.py:338
  49.3 2.4 %collective-permute-start.9 = (bf16[2,64,128]{2,1,0:T(8,128)(2,1)S(1)}, bf16[2,64,128]{2,1,0:T(8,128)(2,1)S(1)}, u32[]{:S(2)}, u32[]{:S(2)}) collective-permute-start(bf16[2,64,128]{2,1,0:T(8,128)(2,1)S(1)} %get-tuple-element.30), channel_id=1, source_target_pairs={{0,12},{1,13},{2,14},{3,15},{4,8},{5,9},{6,10},{7,11},{8,4},{9,5},... | collective-permute-start | bytes 98312 | tf_op jit(solution)/shard_map/ppermute | solution.py:338
  51.7 0.5 collective-permute-start.8
  52.2 0.0 collective-permute-done.7
  52.2 3.2 %collective-permute-done.9 = bf16[2,64,128]{2,1,0:T(8,128)(2,1)S(1)} collective-permute-done((bf16[2,64,128]{2,1,0:T(8,128)(2,1)S(1)}, bf16[2,64,128]{2,1,0:T(8,128)(2,1)S(1)}, u32[]{:S(2)}, u32[]{:S(2)}) %collective-permute-start.9) | collective-permute-done | bytes 32800 | tf_op jit(solution)/shard_map/ppermute | solution.py:338
  55.4 1.2 %collective-permute-done.8 = bf16[2,64,128]{2,1,0:T(8,128)(2,1)S(1)} collective-permute-done((bf16[2,64,128]{2,1,0:T(8,128)(2,1)S(1)}, bf16[2,64,128]{2,1,0:T(8,128)(2,1)S(1)}, u32[]{:S(2)}, u32[]{:S(2)}) %collective-permute-start.8) | collective-permute-done | bytes 32800 | tf_op jit(solution)/shard_map/ppermute | solution.py:338
  56.6 0.1 reshape.6
  56.7 0.7 %reshape.7 = f32[4,4096]{1,0:T(4,128)} reshape(f32[2,2,64,64]{3,2,1,0:T(8,128)S(1)} %copy.7) | data formatting | bytes 131072 | tf_op jit(solution)/shard_map/reshape | solution.py:363
  (7 shorter events, 0.1 us)
Async XLA Ops:
  2.1 10.2 %copy-start.2 = (bf16[1,64,128]{2,1,0:T(8,128)(2,1)S(1)}, bf16[1,64,128]{2,1,0:T(8,128)(2,1)}, u32[]{:S(2)}) copy-start(bf16[1,64,128]{2,1,0:T(8,128)(2,1)} %get-tuple-element.18) | copy-start | bytes 49156
  2.1 10.2 %collective-permute-start.2 = (bf16[1,64,128]{2,1,0:T(8,128)(2,1)}, bf16[1,64,128]{2,1,0:T(8,128)(2,1)S(1)}, u32[]{:S(2)}, u32[]{:S(2)}) collective-permute-start(bf16[1,64,128]{2,1,0:T(8,128)(2,1)} %get-tuple-element.18), channel_id=1, source_target_pairs={{0,12},{1,13},{2,14},{3,15},{4,8},{5,9},{6,10},{7,11},{8,4},{9,5},... | collective-permute-start | bytes 49160 | tf_op jit(solution)/shard_map/ppermute | solution.py:338
  7.2 5.0 %collective-permute-start.1 = (bf16[1,64,128]{2,1,0:T(8,128)(2,1)}, bf16[1,64,128]{2,1,0:T(8,128)(2,1)S(1)}, u32[]{:S(2)}, u32[]{:S(2)}) collective-permute-start(bf16[1,64,128]{2,1,0:T(8,128)(2,1)} %get-tuple-element.18), channel_id=1, source_target_pairs={{0,8},{1,9},{2,10},{3,11},{4,12},{5,13},{6,14},{7,15},{8,0},{9,1},... | collective-permute-start | bytes 49160 | tf_op jit(solution)/shard_map/ppermute | solution.py:338
  7.2 5.1 %collective-permute-start = (bf16[1,64,128]{2,1,0:T(8,128)(2,1)}, bf16[1,64,128]{2,1,0:T(8,128)(2,1)S(1)}, u32[]{:S(2)}, u32[]{:S(2)}) collective-permute-start(bf16[1,64,128]{2,1,0:T(8,128)(2,1)} %get-tuple-element.18), channel_id=1, source_target_pairs={{0,4},{1,5},{2,6},{3,7},{4,0},{5,1},{6,2},{7,3},{8,12},{9,13},{10,... | collective-permute-start | bytes 49160 | tf_op jit(solution)/shard_map/ppermute | solution.py:338
  12.3 6.2 %copy-start.1 = (s32[1,2]{1,0:T(1,128)S(1)}, s32[1,2]{1,0:T(1,128)}, u32[]{:S(2)}) copy-start(s32[1,2]{1,0:T(1,128)} %get-tuple-element.17) | copy-start | bytes 28
  12.3 4.3 %collective-permute-start.3 = (bf16[4,64,128]{2,1,0:T(8,128)(2,1)S(1)}, bf16[4,64,128]{2,1,0:T(8,128)(2,1)S(1)}, u32[]{:S(2)}, u32[]{:S(2)}) collective-permute-start(bf16[4,64,128]{2,1,0:T(8,128)(2,1)S(1)} %pad_maximum_fusion.1), channel_id=1, source_target_pairs={{0,2},{1,3},{2,0},{3,1},{4,6},{5,7},{6,4},{7,5},{8,10},{9,11},{10,... | collective-permute-start | bytes 196616 | tf_op jit(solution)/shard_map/ppermute | solution.py:338
  16.7 1.8 %collective-permute-start.4 = (bf16[8,64,128]{2,1,0:T(8,128)(2,1)S(1)}, bf16[8,64,128]{2,1,0:T(8,128)(2,1)S(1)}, u32[]{:S(2)}, u32[]{:S(2)}) collective-permute-start(bf16[8,64,128]{2,1,0:T(8,128)(2,1)S(1)} %pad_maximum_fusion.refs_0_), channel_id=1, source_target_pairs={{0,1},{1,0},{2,3},{3,2},{4,5},{5,4},{6,7},{7,6},{8,9},{9,8},{10,11... | collective-permute-start | bytes 393224 | tf_op jit(solution)/shard_map/ppermute | solution.py:338
  18.5 10.3 %copy-start = (s32[1,256]{1,0:T(1,128)S(1)}, s32[1,256]{1,0:T(1,128)}, u32[]{:S(2)}) copy-start(s32[1,256]{1,0:T(1,128)} %get-tuple-element.16) | copy-start | bytes 3076
  40.1 1.7 %collective-permute-start.5 = (bf16[16,64,128]{2,1,0:T(8,128)(2,1)S(1)}, bf16[16,64,128]{2,1,0:T(8,128)(2,1)S(1)}, u32[]{:S(2)}, u32[]{:S(2)}) collective-permute-start(bf16[16,64,128]{2,1,0:T(8,128)(2,1)S(1)} %get-tuple-element.26), channel_id=1, source_target_pairs={{0,1},{1,0},{2,3},{3,2},{4,5},{5,4},{6,7},{7,6},{8,9},{9,8},{10,11... | collective-permute-start | bytes 786440 | tf_op jit(solution)/shard_map/ppermute | solution.py:338
  41.9 5.8 %collective-permute-start.6 = (bf16[8,64,128]{2,1,0:T(8,128)(2,1)S(1)}, bf16[8,64,128]{2,1,0:T(8,128)(2,1)S(1)}, u32[]{:S(2)}, u32[]{:S(2)}) collective-permute-start(bf16[8,64,128]{2,1,0:T(8,128)(2,1)S(1)} %slice.41), channel_id=1, source_target_pairs={{0,2},{1,3},{2,0},{3,1},{4,6},{5,7},{6,4},{7,5},{8,10},{9,11},{10,... | collective-permute-start | bytes 393224 | tf_op jit(solution)/shard_map/ppermute | solution.py:338
  47.8 4.4 %collective-permute-start.7 = (bf16[2,64,128]{2,1,0:T(8,128)(2,1)S(1)}, bf16[2,64,128]{2,1,0:T(8,128)(2,1)S(1)}, u32[]{:S(2)}, u32[]{:S(2)}) collective-permute-start(bf16[2,64,128]{2,1,0:T(8,128)(2,1)S(1)} %get-tuple-element.29), channel_id=1, source_target_pairs={{0,4},{1,5},{2,6},{3,7},{4,0},{5,1},{6,2},{7,3},{8,12},{9,13},{10,... | collective-permute-start | bytes 98312 | tf_op jit(solution)/shard_map/ppermute | solution.py:338
  49.3 6.1 %collective-permute-start.9 = (bf16[2,64,128]{2,1,0:T(8,128)(2,1)S(1)}, bf16[2,64,128]{2,1,0:T(8,128)(2,1)S(1)}, u32[]{:S(2)}, u32[]{:S(2)}) collective-permute-start(bf16[2,64,128]{2,1,0:T(8,128)(2,1)S(1)} %get-tuple-element.30), channel_id=1, source_target_pairs={{0,12},{1,13},{2,14},{3,15},{4,8},{5,9},{6,10},{7,11},{8,4},{9,5},... | collective-permute-start | bytes 98312 | tf_op jit(solution)/shard_map/ppermute | solution.py:338
  51.7 4.8 %collective-permute-start.8 = (bf16[2,64,128]{2,1,0:T(8,128)(2,1)S(1)}, bf16[2,64,128]{2,1,0:T(8,128)(2,1)S(1)}, u32[]{:S(2)}, u32[]{:S(2)}) collective-permute-start(bf16[2,64,128]{2,1,0:T(8,128)(2,1)S(1)} %get-tuple-element.31), channel_id=1, source_target_pairs={{0,8},{1,9},{2,10},{3,11},{4,12},{5,13},{6,14},{7,15},{8,0},{9,1},... | collective-permute-start | bytes 98312 | tf_op jit(solution)/shard_map/ppermute | solution.py:338

commit v15 on v14

--- a/solution.py
+++ b/solution.py
@@ -242,7 +242,7 @@
     low = lax.broadcasted_iota(jnp.int32, (bs, lanes), 1) < bs
     shared = len(accs) == 1
     outs = (out0, out1)
-    columns = [(0, WIDE)] + [(at, WIDE // 2) for at in range(WIDE, aux * bs, WIDE // 2)]
+    columns = [(at, WIDE // 2) for at in range(0, aux * bs, WIDE // 2)]
 
     def scatter(n):
         for a in range(aux):
@@ -276,7 +276,7 @@
         right = jnp.where(low, low_acc[2 * i + 1], high_acc[2 * i])
         return left + pltpu.roll(right, bs, 1)
 
-    @pl.loop(0, pairs, unroll=4)
+    @pl.loop(0, pairs, unroll=8)
     def _(i):
         keep_ref[i] = joined(i)
         for k, send_ref in enumerate(send_refs):

time: 57.7 us -> 57.3 us (level)
  no operation moved by 1% of the time
where the time goes in v15:
time: 57.3 us; the launch traced here: 57 us
  Pallas kernels  31 us (54%)
  starting transfers between devices  14.3 us (25%)
  waiting for transfers between devices  9.82 us (17%)
  local copies, waits for them, and re-layouts  0.92 us (2%)
  between operations  0.85 us (1%)
    ppermute x10, starting transfers between devices, exchange(): return lax.ppermute(value, 'orb', [(i, i ^ flip) for i in range(orb)])  14.3 us
    pallas_call x1, Pallas kernels, chi_blocks_of(): pl.pallas_call(functools.partial(chi_kernel, bs, sends), in_specs=in_smem...  10.9 us
    pallas_call x1, Pallas kernels, chi_blocks_of(): pl.pallas_call(functools.partial(sides_kernel, len(tables)), in_specs=in_...  10.2 us
    ppermute x10, waiting for transfers between devices, exchange(): return lax.ppermute(value, 'orb', [(i, i ^ flip) for i in range(orb)])  9.82 us
    pallas_call x3, Pallas kernels, relayout(): pl.pallas_call(functools.partial(relayout_kernel, sum(PARTS[:part])), in_...  8.45 us
    pallas_call x1, Pallas kernels, packed(): pl.pallas_call(functools.partial(pack_kernel, owner_rounds(bits), table_r...  1.44 us
  transfers between devices with their start and end apart: 10, of which 5 were waited for; matrix products, arithmetic and copies ran while one was open for 0% of the time, Pallas kernels for 15%

profile of v15, /device:TPU:0, one launch (start us, length us, event | category | flops | bytes accessed | tf_op | source)
XLA Modules:
  0.0 57.0 jit_solution(3534299894509587935)
XLA Ops:
  0.7 1.4 %shard_map.64 = (bf16[1,64,128]{2,1,0:T(8,128)(2,1)}, s32[1,2]{1,0:T(1,128)}, s32[1,256]{1,0:T(1,128)}) custom-call(s32[1]{0:T(128)} %bitcast.me_ref, s32[1]{0:T(128)S(6)} %copy.8.count_ref, s32[1,2]{1,0:T(1,128)} %refs_0_.1, s32[1,256]{1,0:T(1,128)} %refs_1_.1, bf16[1,4096]{1,0:T(2,128)(2,1)} %refs_2_.1, bf16[1,4096]{1,0:T(2,128)(2,1)} %refs_3_.1), custom_call_target="tpu_custom_call" | custom-call | tf_op jit(solution)/shard_map/pallas_call | solution.py:54
  2.1 0.0 copy-start.2
  2.1 5.1 %collective-permute-start.2 = (bf16[1,64,128]{2,1,0:T(8,128)(2,1)}, bf16[1,64,128]{2,1,0:T(8,128)(2,1)S(1)}, u32[]{:S(2)}, u32[]{:S(2)}) collective-permute-start(bf16[1,64,128]{2,1,0:T(8,128)(2,1)} %get-tuple-element.18), channel_id=1, source_target_pairs={{0,12},{1,13},{2,14},{3,15},{4,8},{5,9},{6,10},{7,11},{8,4},{9,5},... | collective-permute-start | bytes 49160 | tf_op jit(solution)/shard_map/ppermute | solution.py:338
  7.2 0.0 collective-permute-start.1
  7.2 0.6 %collective-permute-start = (bf16[1,64,128]{2,1,0:T(8,128)(2,1)}, bf16[1,64,128]{2,1,0:T(8,128)(2,1)S(1)}, u32[]{:S(2)}, u32[]{:S(2)}) collective-permute-start(bf16[1,64,128]{2,1,0:T(8,128)(2,1)} %get-tuple-element.18), channel_id=1, source_target_pairs={{0,4},{1,5},{2,6},{3,7},{4,0},{5,1},{6,2},{7,3},{8,12},{9,13},{10,... | collective-permute-start | bytes 49160 | tf_op jit(solution)/shard_map/ppermute | solution.py:338
  7.9 4.4 %shard_map.65.refs_2_ = bf16[64,20,16,128]{3,2,1,0:T(8,128)(2,1)S(1)} custom-call(bf16[64,16,4096]{2,1,0:T(8,128)(2,1)} %bitcast.9), custom_call_target="tpu_custom_call" | custom-call | flops 1342177280 | bytes 10485760 | tf_op jit(solution)/shard_map/pallas_call | solution.py:120
  12.3 0.0 collective-permute-done.2.refs_0_
  12.3 0.0 collective-permute-done.1
  12.3 0.0 collective-permute-done
  12.3 0.0 copy-done.2
  12.3 0.0 copy-start.1
  12.3 1.7 %collective-permute-start.3 = (bf16[4,64,128]{2,1,0:T(8,128)(2,1)S(1)}, bf16[4,64,128]{2,1,0:T(8,128)(2,1)S(1)}, u32[]{:S(2)}, u32[]{:S(2)}) collective-permute-start(bf16[4,64,128]{2,1,0:T(8,128)(2,1)S(1)} %pad_maximum_fusion.1), channel_id=1, source_target_pairs={{0,2},{1,3},{2,0},{3,1},{4,6},{5,7},{6,4},{7,5},{8,10},{9,11},{10,... | collective-permute-start | bytes 196616 | tf_op jit(solution)/shard_map/ppermute | solution.py:338
  14.1 2.4 %shard_map.66.refs_3_ = bf16[64,8,16,128]{3,2,1,0:T(8,128)(2,1)S(1)} custom-call(bf16[64,16,4096]{2,1,0:T(8,128)(2,1)} %bitcast.10, bf16[1,64,128]{2,1,0:T(8,128)(2,1)S(1)} %collective-permute-done.2.refs_0_), custom_call_target="tpu_custom_call" | custom-call | flops 536870912 | bytes 4194304 | tf_op jit(solution)/shard_map/pallas_call | solution.py:120
  16.4 0.2 collective-permute-done.3.refs_0_
  16.7 0.1 collective-permute-start.4
  16.8 1.7 %shard_map.67.refs_4_ = bf16[64,4,16,128]{3,2,1,0:T(8,128)(2,1)S(1)} custom-call(bf16[64,16,4096]{2,1,0:T(8,128)(2,1)} %bitcast.11, bf16[4,64,128]{2,1,0:T(8,128)(2,1)S(1)} %collective-permute-done.3.refs_0_), custom_call_target="tpu_custom_call" | custom-call | flops 268435456 | bytes 2097152 | tf_op jit(solution)/shard_map/pallas_call | solution.py:120
  18.5 0.0 collective-permute-done.4.refs_1_
  18.5 0.0 copy-done.1
  18.5 0.0 copy-start
  18.5 10.2 %shard_map.68 = (bf16[64,32,16,128]{3,2,1,0:T(8,128)(2,1)S(1)}, bf16[64,32,16,128]{3,2,1,0:T(8,128)(2,1)S(1)}) custom-call(s32[2]{0:T(128)S(1)} %bitcast.8, bf16[8,64,128]{2,1,0:T(8,128)(2,1)S(1)} %pad_maximum_fusion.refs_0_, bf16[8,64,128]{2,1,0:T(8,128)(2,1)S(1)} %collective-permute-done.4.refs_1_, bf16[64,20,16,128]{3,2,1,0:T(8,128)(2,1)S(1)} %shard_map.65.refs_2_, ...), custom_call_target="tpu_custom_call" | custom-call | flops 8589934592 | bytes 16777216 | tf_op jit(solution)/shard_map/pallas_call | solution.py:291
  28.7 0.0 copy-done
  28.8 10.9 %shard_map.69 = (f32[16,64,128]{2,1,0:T(8,128)S(1)}, bf16[16,64,128]{2,1,0:T(8,128)(2,1)S(1)}) custom-call(s32[256]{0:T(256)S(1)} %bitcast.7, bf16[64,32,16,128]{3,2,1,0:T(8,128)(2,1)S(1)} %get-tuple-element.23.o_ref, bf16[64,32,16,128]{3,2,1,0:T(8,128)(2,1)S(1)} %get-tuple-element.24.v_ref), custom_call_target="tpu_custom_call" | custom-call | flops 8589934592 | bytes 16777216 | tf_op jit(solution)/shard_map/pallas_call | solution.py:307
  39.7 0.6 collective-permute-start.5
  40.2 1.2 %collective-permute-done.5 = bf16[16,64,128]{2,1,0:T(8,128)(2,1)S(1)} collective-permute-done((bf16[16,64,128]{2,1,0:T(8,128)(2,1)S(1)}, bf16[16,64,128]{2,1,0:T(8,128)(2,1)S(1)}, u32[]{:S(2)}, u32[]{:S(2)}) %collective-permute-start.5) | collective-permute-done | bytes 262176 | tf_op jit(solution)/shard_map/ppermute | solution.py:338
  41.4 0.1 convert_add_fusion
  41.5 1.7 %collective-permute-start.6 = (bf16[8,64,128]{2,1,0:T(8,128)(2,1)S(1)}, bf16[8,64,128]{2,1,0:T(8,128)(2,1)S(1)}, u32[]{:S(2)}, u32[]{:S(2)}) collective-permute-start(bf16[8,64,128]{2,1,0:T(8,128)(2,1)S(1)} %slice.41), channel_id=1, source_target_pairs={{0,2},{1,3},{2,0},{3,1},{4,6},{5,7},{6,4},{7,5},{8,10},{9,11},{10,... | collective-permute-start | bytes 393224 | tf_op jit(solution)/shard_map/ppermute | solution.py:338
  43.2 4.1 %collective-permute-done.6 = bf16[8,64,128]{2,1,0:T(8,128)(2,1)S(1)} collective-permute-done((bf16[8,64,128]{2,1,0:T(8,128)(2,1)S(1)}, bf16[8,64,128]{2,1,0:T(8,128)(2,1)S(1)}, u32[]{:S(2)}, u32[]{:S(2)}) %collective-permute-start.6) | collective-permute-done | bytes 131104 | tf_op jit(solution)/shard_map/ppermute | solution.py:338
  47.4 1.4 %collective-permute-start.7 = (bf16[2,64,128]{2,1,0:T(8,128)(2,1)S(1)}, bf16[2,64,128]{2,1,0:T(8,128)(2,1)S(1)}, u32[]{:S(2)}, u32[]{:S(2)}) collective-permute-start(bf16[2,64,128]{2,1,0:T(8,128)(2,1)S(1)} %get-tuple-element.29), channel_id=1, source_target_pairs={{0,4},{1,5},{2,6},{3,7},{4,0},{5,1},{6,2},{7,3},{8,12},{9,13},{10,... | collective-permute-start | bytes 98312 | tf_op jit(solution)/shard_map/ppermute | solution.py:338
  48.8 2.5 %collective-permute-start.9 = (bf16[2,64,128]{2,1,0:T(8,128)(2,1)S(1)}, bf16[2,64,128]{2,1,0:T(8,128)(2,1)S(1)}, u32[]{:S(2)}, u32[]{:S(2)}) collective-permute-start(bf16[2,64,128]{2,1,0:T(8,128)(2,1)S(1)} %get-tuple-element.30), channel_id=1, source_target_pairs={{0,12},{1,13},{2,14},{3,15},{4,8},{5,9},{6,10},{7,11},{8,4},{9,5},... | collective-permute-start | bytes 98312 | tf_op jit(solution)/shard_map/ppermute | solution.py:338
  51.3 0.5 collective-permute-start.8
  51.8 0.0 collective-permute-done.7
  51.8 3.1 %collective-permute-done.9 = bf16[2,64,128]{2,1,0:T(8,128)(2,1)S(1)} collective-permute-done((bf16[2,64,128]{2,1,0:T(8,128)(2,1)S(1)}, bf16[2,64,128]{2,1,0:T(8,128)(2,1)S(1)}, u32[]{:S(2)}, u32[]{:S(2)}) %collective-permute-start.9) | collective-permute-done | bytes 32800 | tf_op jit(solution)/shard_map/ppermute | solution.py:338
  54.9 1.2 %collective-permute-done.8 = bf16[2,64,128]{2,1,0:T(8,128)(2,1)S(1)} collective-permute-done((bf16[2,64,128]{2,1,0:T(8,128)(2,1)S(1)}, bf16[2,64,128]{2,1,0:T(8,128)(2,1)S(1)}, u32[]{:S(2)}, u32[]{:S(2)}) %collective-permute-start.8) | collective-permute-done | bytes 32800 | tf_op jit(solution)/shard_map/ppermute | solution.py:338
  56.1 0.1 reshape.6
  56.3 0.7 %reshape.7 = f32[4,4096]{1,0:T(4,128)} reshape(f32[2,2,64,64]{3,2,1,0:T(8,128)S(1)} %copy.7) | data formatting | bytes 131072 | tf_op jit(solution)/shard_map/reshape | solution.py:363
  (7 shorter events, 0.1 us)
Async XLA Ops:
  2.1 10.2 %copy-start.2 = (bf16[1,64,128]{2,1,0:T(8,128)(2,1)S(1)}, bf16[1,64,128]{2,1,0:T(8,128)(2,1)}, u32[]{:S(2)}) copy-start(bf16[1,64,128]{2,1,0:T(8,128)(2,1)} %get-tuple-element.18) | copy-start | bytes 49156
  2.1 10.2 %collective-permute-start.2 = (bf16[1,64,128]{2,1,0:T(8,128)(2,1)}, bf16[1,64,128]{2,1,0:T(8,128)(2,1)S(1)}, u32[]{:S(2)}, u32[]{:S(2)}) collective-permute-start(bf16[1,64,128]{2,1,0:T(8,128)(2,1)} %get-tuple-element.18), channel_id=1, source_target_pairs={{0,12},{1,13},{2,14},{3,15},{4,8},{5,9},{6,10},{7,11},{8,4},{9,5},... | collective-permute-start | bytes 49160 | tf_op jit(solution)/shard_map/ppermute | solution.py:338
  7.2 5.0 %collective-permute-start.1 = (bf16[1,64,128]{2,1,0:T(8,128)(2,1)}, bf16[1,64,128]{2,1,0:T(8,128)(2,1)S(1)}, u32[]{:S(2)}, u32[]{:S(2)}) collective-permute-start(bf16[1,64,128]{2,1,0:T(8,128)(2,1)} %get-tuple-element.18), channel_id=1, source_target_pairs={{0,8},{1,9},{2,10},{3,11},{4,12},{5,13},{6,14},{7,15},{8,0},{9,1},... | collective-permute-start | bytes 49160 | tf_op jit(solution)/shard_map/ppermute | solution.py:338
  7.2 5.1 %collective-permute-start = (bf16[1,64,128]{2,1,0:T(8,128)(2,1)}, bf16[1,64,128]{2,1,0:T(8,128)(2,1)S(1)}, u32[]{:S(2)}, u32[]{:S(2)}) collective-permute-start(bf16[1,64,128]{2,1,0:T(8,128)(2,1)} %get-tuple-element.18), channel_id=1, source_target_pairs={{0,4},{1,5},{2,6},{3,7},{4,0},{5,1},{6,2},{7,3},{8,12},{9,13},{10,... | collective-permute-start | bytes 49160 | tf_op jit(solution)/shard_map/ppermute | solution.py:338
  12.3 6.2 %copy-start.1 = (s32[1,2]{1,0:T(1,128)S(1)}, s32[1,2]{1,0:T(1,128)}, u32[]{:S(2)}) copy-start(s32[1,2]{1,0:T(1,128)} %get-tuple-element.17) | copy-start | bytes 28
  12.3 4.3 %collective-permute-start.3 = (bf16[4,64,128]{2,1,0:T(8,128)(2,1)S(1)}, bf16[4,64,128]{2,1,0:T(8,128)(2,1)S(1)}, u32[]{:S(2)}, u32[]{:S(2)}) collective-permute-start(bf16[4,64,128]{2,1,0:T(8,128)(2,1)S(1)} %pad_maximum_fusion.1), channel_id=1, source_target_pairs={{0,2},{1,3},{2,0},{3,1},{4,6},{5,7},{6,4},{7,5},{8,10},{9,11},{10,... | collective-permute-start | bytes 196616 | tf_op jit(solution)/shard_map/ppermute | solution.py:338
  16.7 1.8 %collective-permute-start.4 = (bf16[8,64,128]{2,1,0:T(8,128)(2,1)S(1)}, bf16[8,64,128]{2,1,0:T(8,128)(2,1)S(1)}, u32[]{:S(2)}, u32[]{:S(2)}) collective-permute-start(bf16[8,64,128]{2,1,0:T(8,128)(2,1)S(1)} %pad_maximum_fusion.refs_0_), channel_id=1, source_target_pairs={{0,1},{1,0},{2,3},{3,2},{4,5},{5,4},{6,7},{7,6},{8,9},{9,8},{10,11... | collective-permute-start | bytes 393224 | tf_op jit(solution)/shard_map/ppermute | solution.py:338
  18.5 10.3 %copy-start = (s32[1,256]{1,0:T(1,128)S(1)}, s32[1,256]{1,0:T(1,128)}, u32[]{:S(2)}) copy-start(s32[1,256]{1,0:T(1,128)} %get-tuple-element.16) | copy-start | bytes 3076
  39.7 1.7 %collective-permute-start.5 = (bf16[16,64,128]{2,1,0:T(8,128)(2,1)S(1)}, bf16[16,64,128]{2,1,0:T(8,128)(2,1)S(1)}, u32[]{:S(2)}, u32[]{:S(2)}) collective-permute-start(bf16[16,64,128]{2,1,0:T(8,128)(2,1)S(1)} %get-tuple-element.26), channel_id=1, source_target_pairs={{0,1},{1,0},{2,3},{3,2},{4,5},{5,4},{6,7},{7,6},{8,9},{9,8},{10,11... | collective-permute-start | bytes 786440 | tf_op jit(solution)/shard_map/ppermute | solution.py:338
  41.5 5.8 %collective-permute-start.6 = (bf16[8,64,128]{2,1,0:T(8,128)(2,1)S(1)}, bf16[8,64,128]{2,1,0:T(8,128)(2,1)S(1)}, u32[]{:S(2)}, u32[]{:S(2)}) collective-permute-start(bf16[8,64,128]{2,1,0:T(8,128)(2,1)S(1)} %slice.41), channel_id=1, source_target_pairs={{0,2},{1,3},{2,0},{3,1},{4,6},{5,7},{6,4},{7,5},{8,10},{9,11},{10,... | collective-permute-start | bytes 393224 | tf_op jit(solution)/shard_map/ppermute | solution.py:338
  47.4 4.4 %collective-permute-start.7 = (bf16[2,64,128]{2,1,0:T(8,128)(2,1)S(1)}, bf16[2,64,128]{2,1,0:T(8,128)(2,1)S(1)}, u32[]{:S(2)}, u32[]{:S(2)}) collective-permute-start(bf16[2,64,128]{2,1,0:T(8,128)(2,1)S(1)} %get-tuple-element.29), channel_id=1, source_target_pairs={{0,4},{1,5},{2,6},{3,7},{4,0},{5,1},{6,2},{7,3},{8,12},{9,13},{10,... | collective-permute-start | bytes 98312 | tf_op jit(solution)/shard_map/ppermute | solution.py:338
  48.8 6.1 %collective-permute-start.9 = (bf16[2,64,128]{2,1,0:T(8,128)(2,1)S(1)}, bf16[2,64,128]{2,1,0:T(8,128)(2,1)S(1)}, u32[]{:S(2)}, u32[]{:S(2)}) collective-permute-start(bf16[2,64,128]{2,1,0:T(8,128)(2,1)S(1)} %get-tuple-element.30), channel_id=1, source_target_pairs={{0,12},{1,13},{2,14},{3,15},{4,8},{5,9},{6,10},{7,11},{8,4},{9,5},... | collective-permute-start | bytes 98312 | tf_op jit(solution)/shard_map/ppermute | solution.py:338
  51.3 4.8 %collective-permute-start.8 = (bf16[2,64,128]{2,1,0:T(8,128)(2,1)S(1)}, bf16[2,64,128]{2,1,0:T(8,128)(2,1)S(1)}, u32[]{:S(2)}, u32[]{:S(2)}) collective-permute-start(bf16[2,64,128]{2,1,0:T(8,128)(2,1)S(1)} %get-tuple-element.31), channel_id=1, source_target_pairs={{0,8},{1,9},{2,10},{3,11},{4,12},{5,13},{6,14},{7,15},{8,0},{9,1},... | collective-permute-start | bytes 98312 | tf_op jit(solution)/shard_map/ppermute | solution.py:338
